TPU v7x, 128 devices: a whole 4x4x4 slice. The times are simulated.
128 devices in a mesh: section: 2 (over y_lo), dp: 16 (over z, x), seq: 4 (over y_hi, core).
Axes of the slice: x: 4, y: 4 (y_hi: 2, y_lo: 2; y = y_hi * 2 + y_lo), z: 4, core: 2. Of those that a mesh axis runs over, the one named last changes fastest.
Arguments:
- states: bfloat16 [2, 16, 1024, 1024], P('section', 'dp', 'seq'), may hold values from -6 to 6
- mirror: bfloat16 [2, 16, 1024, 1024], P('section', 'dp', 'seq'), may hold values from -6 to 6
- w_skip: bfloat16 [2048, 1024], replicated, may hold values from -0.125 to 0.125
- norm1_gain: bfloat16 [1024], replicated, may hold values from 0.099609375 to 1.8984375
- norm1_bias: bfloat16 [1024], replicated, may hold values from -1.5 to 1.5
- w_query: bfloat16 [1024, 1024], replicated, may hold values from -0.1875 to 0.1875
- w_key: bfloat16 [1024, 1024], replicated, may hold values from -0.1875 to 0.1875
- w_value: bfloat16 [1024, 1024], replicated, may hold values from -0.1875 to 0.1875
- w_out: bfloat16 [1024, 1024], replicated, may hold values from -0.75 to 0.75
- norm2_gain: bfloat16 [1024], replicated, may hold values from 0.099609375 to 1.8984375
- norm2_bias: bfloat16 [1024], replicated, may hold values from -1.5 to 1.5
- w_up: bfloat16 [1024, 4096], replicated, may hold values from -0.1875 to 0.1875
- w_down: bfloat16 [4096, 1024], replicated, may hold values from -0.09375 to 0.09375
- out_grad: bfloat16 [2, 16, 1024, 1024], P('section', 'dp', 'seq'), may hold values from -6 to 6
- lengths: int32 [2, 16, 4], P('section', 'dp'), may hold values from 1 to 896, as said below
- infill_spans: int32 [2, 16, 4, 2], P('section', 'dp'), may hold values from 0 to 896, as said below
Outputs:
- output: bfloat16 [2, 16, 1024, 1024], P('section', 'dp', 'seq')
- grad_states: bfloat16 [2, 16, 1024, 1024], P('section', 'dp', 'seq')
- grad_mirror: bfloat16 [2, 16, 1024, 1024], P('section', 'dp', 'seq')
- grad_w_skip: float32 [2, 2048, 1024], P('section', ('dp', 'seq'))
- grad_norm1_gain: float32 [2, 1024], P('section', ('dp', 'seq'))
- grad_norm1_bias: float32 [2, 1024], P('section', ('dp', 'seq'))
- grad_w_query: float32 [2, 1024, 1024], P('section', ('dp', 'seq'))
- grad_w_key: float32 [2, 1024, 1024], P('section', ('dp', 'seq'))
- grad_w_value: float32 [2, 1024, 1024], P('section', ('dp', 'seq'))
- grad_w_out: float32 [2, 1024, 1024], P('section', ('dp', 'seq'))
- grad_norm2_gain: float32 [2, 1024], P('section', ('dp', 'seq'))
- grad_norm2_bias: float32 [2, 1024], P('section', ('dp', 'seq'))
- grad_w_up: float32 [2, 1024, 4096], P('section', ('dp', 'seq'))
- grad_w_down: float32 [2, 4096, 1024], P('section', ('dp', 'seq'))
Inputs may be any that keep to these rules, and one draw needn't show every extreme that they name: Per packed row, 4 utterance lengths that sum to 1024; one of them is exactly 896. `infill_spans`: per utterance, offsets start < end within it whose span covers up to 100 percent of its frames (at least one frame).
All inputs are finite; a program needn't handle non-finite values.
Results may differ from a plain program's by a relative error of at most 0.019.
Values may be sent and summed in bfloat16 or wider, within the bound.
A program may use at most 256 MiB of HBM per device.

v0:
```python
import jax
import jax.numpy as jnp
from jax import lax
from jax.sharding import PartitionSpec as P

HEADS = 16


EPS = 1e-05


def from_partner(value, axis, stride):
    mask = 2**stride
    pairs = [(source, source ^ mask) for source in range(lax.axis_size(axis))]
    return lax.ppermute(value, axis, pairs)


def project(left, right):
    return jnp.dot(left, right, preferred_element_type=jnp.float32)


def rows_product(left, right):
    return lax.dot_general(
        left, right, (((0,), (0,)), ((), ())), preferred_element_type=jnp.float32
    )


def back_product(left, right):
    return lax.dot_general(
        left, right, (((1,), (1,)), ((), ())), preferred_element_type=jnp.float32
    )


def gelu_exact(values):
    return jax.nn.gelu(values, approximate=False)


def norm_forward(hidden, gain, bias):
    center = hidden - jnp.mean(hidden, axis=-1, keepdims=True)
    variance = jnp.mean(center * center, axis=-1, keepdims=True)
    inverse = lax.rsqrt(variance + EPS)
    unit = center * inverse
    return (unit * gain + bias, unit, inverse)


def norm_backward(grad, unit, inverse, gain):
    scaled = grad * gain
    mean_one = jnp.mean(scaled, axis=-1, keepdims=True)
    mean_two = jnp.mean(scaled * unit, axis=-1, keepdims=True)
    grad_input = inverse * (scaled - mean_one - unit * mean_two)
    return (grad_input, jnp.sum(grad * unit, axis=0), jnp.sum(grad, axis=0))


def segment_tables(lengths_row, spans_row, places):
    ends = jnp.cumsum(lengths_row, dtype=jnp.int32)
    starts = ends - lengths_row
    segment = jnp.sum((places[:, None] >= ends[None, :]).astype(jnp.int32), axis=1)
    lower = starts + spans_row[:, 0]
    upper = starts + spans_row[:, 1]
    inside = jnp.any(
        (places[:, None] >= lower[None, :]) & (places[:, None] < upper[None, :]), axis=1
    )
    return (segment, inside)


def on_device(
    states,
    mirror,
    w_skip,
    norm1_gain,
    norm1_bias,
    w_query,
    w_key,
    w_value,
    w_out,
    norm2_gain,
    norm2_bias,
    w_up,
    w_down,
    out_grad,
    lengths,
    infill_spans,
):
    rows_here = states.shape[2]
    model_width = states.shape[3]
    head_count = HEADS
    head_dim = model_width // head_count
    score_scale = head_dim ** (-0.5)
    own_rows = states.reshape(rows_here, model_width)
    stored = mirror.reshape(rows_here, model_width)
    partner = from_partner(stored, "section", 0)
    lengths_row = lengths.reshape(-1)
    spans_row = infill_spans.reshape(-1, 2)
    row_length = rows_here * lax.axis_size("seq")
    offset = lax.axis_index("seq") * rows_here
    query_place = offset + jnp.arange(rows_here, dtype=jnp.int32)
    key_place = jnp.arange(row_length, dtype=jnp.int32)
    query_segment, inside = segment_tables(lengths_row, spans_row, query_place)
    key_segment = segment_tables(lengths_row, spans_row, key_place)[0]
    allowed = query_segment[:, None] == key_segment[None, :]
    distance = jnp.abs(query_place[:, None] - key_place[None, :]).astype(jnp.float32)
    slopes = 2.0 ** (-8.0 * (jnp.arange(head_count, dtype=jnp.float32) + 1.0) / head_count)
    gain_one = norm1_gain.astype(jnp.float32)
    bias_one = norm1_bias.astype(jnp.float32)
    gain_two = norm2_gain.astype(jnp.float32)
    bias_two = norm2_bias.astype(jnp.float32)
    w_first = w_skip[:model_width]
    w_second = w_skip[model_width:]
    hidden = project(own_rows, w_first) + project(partner, w_second)
    normed_one, unit_one, inverse_one = norm_forward(hidden, gain_one, bias_one)
    normed_one = normed_one.astype(jnp.bfloat16)
    query = project(normed_one, w_query).astype(jnp.bfloat16)
    key_rows = project(normed_one, w_key).astype(jnp.bfloat16)
    value_rows = project(normed_one, w_value).astype(jnp.bfloat16)
    keys_all, values_all = (
        lax.all_gather(key_rows, "seq", axis=0, tiled=True),
        lax.all_gather(value_rows, "seq", axis=0, tiled=True),
    )
    query3 = query.reshape(rows_here, head_count, head_dim)
    keys3 = keys_all.reshape(row_length, head_count, head_dim)
    values3 = values_all.reshape(row_length, head_count, head_dim)

    def scores_of():
        raw = jnp.einsum("qhd,khd->hqk", query3, keys3, preferred_element_type=jnp.float32)
        scores = raw * score_scale - slopes[:, None, None] * distance[None]
        return jnp.where(allowed[None], scores, -1e30)

    scores = scores_of()
    row_top = jnp.max(scores, axis=-1, keepdims=True)
    exponent = jnp.exp(scores - row_top)
    row_total = jnp.sum(exponent, axis=-1, keepdims=True)
    log_total = row_top + jnp.log(row_total)
    softmax_low = (exponent / row_total).astype(jnp.bfloat16)
    mixed_rows = jnp.einsum(
        "hqk,khd->qhd", softmax_low, values3, preferred_element_type=jnp.float32
    )
    mixed_rows = mixed_rows.reshape(rows_here, model_width).astype(jnp.bfloat16)
    residual = hidden + project(mixed_rows, w_out)
    normed_two, unit_two, inverse_two = norm_forward(residual, gain_two, bias_two)
    normed_two = normed_two.astype(jnp.bfloat16)
    upward = project(normed_two, w_up)
    activated, gelu_pull = jax.vjp(gelu_exact, upward)
    act_low = activated.astype(jnp.bfloat16)
    result = residual + project(act_low, w_down)
    output = result.astype(jnp.bfloat16).reshape(states.shape)
    grad_rows = (
        out_grad.reshape(rows_here, model_width).astype(jnp.float32)
        * inside.astype(jnp.float32)[:, None]
    )
    grad_low = grad_rows.astype(jnp.bfloat16)
    grad_down = rows_product(act_low, grad_low)
    grad_act = back_product(grad_low, w_down)
    grad_upward = gelu_pull(grad_act)[0].astype(jnp.bfloat16)
    grad_up = rows_product(normed_two, grad_upward)
    grad_normed_two = back_product(grad_upward, w_up)
    grad_resid_norm, grad_gain_two, grad_bias_two = norm_backward(
        grad_normed_two, unit_two, inverse_two, gain_two
    )
    grad_residual = grad_rows + grad_resid_norm
    ffn_shares = (grad_gain_two, grad_bias_two, grad_up, grad_down)
    grad_attn = grad_residual.astype(jnp.bfloat16)
    grad_wout = rows_product(mixed_rows, grad_attn)
    grad_mixed = back_product(grad_attn, w_out).astype(jnp.bfloat16)
    grad_mixed3 = grad_mixed.reshape(rows_here, head_count, head_dim)
    softmax_again = jnp.exp(scores_of() - log_total)
    grad_softmax = jnp.einsum(
        "qhd,khd->hqk", grad_mixed3, values3, preferred_element_type=jnp.float32
    )
    centre = jnp.sum(softmax_again * grad_softmax, axis=-1, keepdims=True)
    grad_scores = (softmax_again * (grad_softmax - centre)).astype(jnp.bfloat16)
    grad_query = (
        jnp.einsum("hqk,khd->qhd", grad_scores, keys3, preferred_element_type=jnp.float32)
        * score_scale
    )
    grad_query = grad_query.reshape(rows_here, model_width).astype(jnp.bfloat16)
    key_part = (
        jnp.einsum("hqk,qhd->khd", grad_scores, query3, preferred_element_type=jnp.float32)
        * score_scale
    )
    value_part = jnp.einsum(
        "hqk,qhd->khd",
        softmax_again.astype(jnp.bfloat16),
        grad_mixed3,
        preferred_element_type=jnp.float32,
    )
    key_grad, value_grad = (
        lax.psum_scatter(
            key_part.reshape(row_length, model_width).astype(jnp.bfloat16),
            "seq",
            scatter_dimension=0,
            tiled=True,
        ).astype(jnp.float32),
        lax.psum_scatter(
            value_part.reshape(row_length, model_width).astype(jnp.bfloat16),
            "seq",
            scatter_dimension=0,
            tiled=True,
        ).astype(jnp.float32),
    )
    key_grad = key_grad.astype(jnp.bfloat16)
    value_grad = value_grad.astype(jnp.bfloat16)
    grad_wquery = rows_product(normed_one, grad_query)
    grad_wkey = rows_product(normed_one, key_grad)
    grad_wvalue = rows_product(normed_one, value_grad)
    grad_normed_one = (
        back_product(grad_query, w_query)
        + back_product(key_grad, w_key)
        + back_product(value_grad, w_value)
    )
    grad_hidden_norm, grad_gain_one, grad_bias_one = norm_backward(
        grad_normed_one, unit_one, inverse_one, gain_one
    )
    grad_hidden = (grad_residual + grad_hidden_norm).astype(jnp.bfloat16)
    grad_wskip = jnp.concatenate(
        [rows_product(own_rows, grad_hidden), rows_product(partner, grad_hidden)], axis=0
    )
    grad_own = back_product(grad_hidden, w_first).astype(jnp.bfloat16)
    grad_partner = back_product(grad_hidden, w_second).astype(jnp.bfloat16)
    grad_stored = from_partner(grad_partner, "section", 0)
    final = (
        lax.psum_scatter(grad_wskip, ("dp", "seq"), scatter_dimension=0, tiled=True),
        lax.psum_scatter(grad_gain_one, ("dp", "seq"), scatter_dimension=0, tiled=True),
        lax.psum_scatter(grad_bias_one, ("dp", "seq"), scatter_dimension=0, tiled=True),
        lax.psum_scatter(grad_wquery, ("dp", "seq"), scatter_dimension=0, tiled=True),
        lax.psum_scatter(grad_wkey, ("dp", "seq"), scatter_dimension=0, tiled=True),
        lax.psum_scatter(grad_wvalue, ("dp", "seq"), scatter_dimension=0, tiled=True),
        lax.psum_scatter(grad_wout, ("dp", "seq"), scatter_dimension=0, tiled=True),
        lax.psum_scatter(ffn_shares[0], ("dp", "seq"), scatter_dimension=0, tiled=True),
        lax.psum_scatter(ffn_shares[1], ("dp", "seq"), scatter_dimension=0, tiled=True),
        lax.psum_scatter(ffn_shares[2], ("dp", "seq"), scatter_dimension=0, tiled=True),
        lax.psum_scatter(ffn_shares[3], ("dp", "seq"), scatter_dimension=0, tiled=True),
    )
    shares = tuple((piece[None] for piece in final))
    return (
        output,
        grad_own.reshape(states.shape),
        grad_stored.reshape(states.shape),
        shares[0],
        shares[1],
        shares[2],
        shares[3],
        shares[4],
        shares[5],
        shares[6],
        shares[7],
        shares[8],
        shares[9],
        shares[10],
    )


def solution(mesh):
    in_specs = (
        P("section", "dp", "seq", None),
        P("section", "dp", "seq", None),
        P(),
        P(),
        P(),
        P(),
        P(),
        P(),
        P(),
        P(),
        P(),
        P(),
        P(),
        P("section", "dp", "seq", None),
        P("section", "dp", None),
        P("section", "dp", None, None),
    )
    out_specs = (
        P("section", "dp", "seq", None),
        P("section", "dp", "seq", None),
        P("section", "dp", "seq", None),
        P("section", ("dp", "seq"), None),
        P("section", ("dp", "seq")),
        P("section", ("dp", "seq")),
        P("section", ("dp", "seq"), None),
        P("section", ("dp", "seq"), None),
        P("section", ("dp", "seq"), None),
        P("section", ("dp", "seq"), None),
        P("section", ("dp", "seq")),
        P("section", ("dp", "seq")),
        P("section", ("dp", "seq"), None),
        P("section", ("dp", "seq"), None),
    )
    return jax.shard_map(
        on_device, mesh=mesh, in_specs=in_specs, out_specs=out_specs, check_vma=False
    )
```

profile of v0, /device:TPU:0, one launch (start us, length us, event | category | flops | bytes accessed | tf_op | source)
XLA Modules:
  0.0 2644.4 jit_solution(13512626009532326625)
XLA Ops:
  12.8 8.3 collective-permute-done
  36.6 19.4 all-gather.5.cloned.1.call-done
  56.0 4.1 copy.48
  60.1 6.3 fusion.56
  72.5 11.8 all-gather.3.cloned.1.call-done
  88.2 8.4 fusion.34
  97.7 15.4 multiply_convert_fusion.2
  113.1 11.0 add_convert_fusion
  124.1 6.9 multiply_reduce_fusion.1
  136.1 10.1 fusion.12
  146.2 13.0 multiply_reduce_fusion
  159.3 12.2 multiply_convert_fusion
  179.6 6.8 fusion.33
  194.0 30.6 %reduce-scatter.10.cloned.1.call-done = bf16[256,1024]{0,1:T(8,128)(2,1)} async-done(((bf16[1024,1024]{0,1:T(8,128)(2,1)}), bf16[256,1024]{0,1:T(8,128)(2,1)}) %reduce-scatter.10.cloned.1.call-update) | async-done | bytes 524304 | tf_op jit(solution)/shard_map/reduce_scatter | solution.py:187
  242.3 9.8 fusion.52
  252.4 9.8 fusion.46
  264.1 7.3 fusion.38
  273.6 329.1 %all-reduce.4 = (f32[1024]{0:T(1024)S(1)}, f32[1024]{0:T(1024)S(1)}, f32[1024]{0:T(1024)S(1)}, f32[1024]{0:T(1024)S(1)}) all-reduce(f32[1024]{0:T(1024)S(1)} %get-tuple-element.16, f32[1024]{0:T(1024)S(1)} %get-tuple-element.21, f32[1024]{0:T(1024)S(1)} %get-tuple-element.14, ...), channel_id=5, replica_groups=mesh['section'=2,'dp'=16,'seq'=4] {'dp','seq'}, use_global_device_ids=true, to_apply=%region_19.20.clone | all-reduce | flops 4096 | bytes 32768
  608.2 294.3 %reduce-scatter.16.cloned.1.call-done = f32[16,1024]{1,0:T(8,128)} async-done(((f32[1024,1024]{1,0:T(8,128)}), f32[16,1024]{1,0:T(8,128)}) %reduce-scatter.16.cloned.1.call-update) | async-done | bytes 65552 | tf_op jit(solution)/shard_map/reduce_scatter | solution.py:224
  902.5 336.3 %reduce-scatter.20.cloned.1.call-done = f32[16,1024]{1,0:T(8,128)} async-done(((f32[1024,1024]{1,0:T(8,128)}), f32[16,1024]{1,0:T(8,128)}) %reduce-scatter.20.cloned.1.call-update) | async-done | bytes 65552 | tf_op jit(solution)/shard_map/reduce_scatter | solution.py:226
  1238.7 336.5 %reduce-scatter.18.cloned.1.call-done = f32[16,1024]{1,0:T(8,128)} async-done(((f32[1024,1024]{1,0:T(8,128)}), f32[16,1024]{1,0:T(8,128)}) %reduce-scatter.18.cloned.1.call-update) | async-done | bytes 65552 | tf_op jit(solution)/shard_map/reduce_scatter | solution.py:225
  1575.2 344.1 %reduce-scatter.14.cloned.1.call-done = f32[32,1024]{1,0:T(8,128)} async-done(((f32[2048,1024]{1,0:T(8,128)}), f32[32,1024]{1,0:T(8,128)}) %reduce-scatter.14.cloned.1.call-update) | async-done | bytes 131088 | tf_op jit(solution)/shard_map/reduce_scatter | solution.py:221
  1919.3 359.1 %reduce-scatter.24.cloned.1.call-done = f32[16,4096]{1,0:T(8,128)} async-done(((f32[1024,4096]{1,0:T(8,128)}), f32[16,4096]{1,0:T(8,128)}) %reduce-scatter.24.cloned.1.call-update) | async-done | bytes 262160 | tf_op jit(solution)/shard_map/reduce_scatter | solution.py:230
  2278.4 358.4 %reduce-scatter.26.cloned.1.call-done = f32[64,1024]{1,0:T(8,128)} async-done(((f32[4096,1024]{1,0:T(8,128)}), f32[64,1024]{1,0:T(8,128)}) %reduce-scatter.26.cloned.1.call-update) | async-done | bytes 262160 | tf_op jit(solution)/shard_map/reduce_scatter | solution.py:231
  (144 shorter events, 80.3 us)
Async XLA Ops:
  7.2 19.7 copy-start
  7.2 48.8 %all-gather.5.cloned.1.call-start = ((), (), s32[]{:S(2)}) async-start(), calls=%async_computation.10 | async-start | bytes 2621440 | tf_op jit(solution)/shard_map/all_gather | solution.py:116
  7.2 13.9 collective-permute-start
  12.8 12.2 copy-start.17
  26.6 57.7 %all-gather.3.cloned.1.call-start = ((), (), s32[]{:S(2)}) async-start(), calls=%async_computation.9 | async-start | bytes 2621440 | tf_op jit(solution)/shard_map/all_gather | solution.py:117
  29.5 160.5 %reduce-scatter.12.cloned.1.call-start = ((), (), s32[]{:S(2)}) async-start(), calls=%async_computation.12 | async-start | bytes 2621440 | tf_op jit(solution)/shard_map/reduce_scatter | solution.py:193
  88.2 8.4 copy-start.12
  96.6 16.5 copy-start.21
  97.4 33.6 %copy-start.3 = (f32[256,1024]{1,0:T(8,128)}, f32[256,1024]{1,0:T(8,128)S(1)}, u32[]{:S(2)}) copy-start(f32[256,1024]{1,0:T(8,128)S(1)} %get-tuple-element.35) | copy-start | bytes 3145732
  97.7 15.4 copy-start.19
  146.2 78.4 %reduce-scatter.10.cloned.1.call-start = ((), (), s32[]{:S(2)}) async-start(), calls=%async_computation.11 | async-start | bytes 2621440 | tf_op jit(solution)/shard_map/reduce_scatter | solution.py:187
  159.3 12.2 copy-start.14
  175.4 432.8 %reduce-scatter.22.cloned.1.call-start = ((), (), s32[]{:S(2)}) async-start(), calls=%async_computation.17 | async-start | bytes 4259840 | tf_op jit(solution)/shard_map/reduce_scatter | solution.py:227
  179.5 722.9 %reduce-scatter.16.cloned.1.call-start = ((), (), s32[]{:S(2)}) async-start(), calls=%async_computation.14 | async-start | bytes 4259840 | tf_op jit(solution)/shard_map/reduce_scatter | solution.py:224
  179.6 7.6 copy-start.11
  189.9 1048.9 %reduce-scatter.20.cloned.1.call-start = ((), (), s32[]{:S(2)}) async-start(), calls=%async_computation.16 | async-start | bytes 4259840 | tf_op jit(solution)/shard_map/reduce_scatter | solution.py:226
  194.0 1381.2 %reduce-scatter.18.cloned.1.call-start = ((), (), s32[]{:S(2)}) async-start(), calls=%async_computation.15 | async-start | bytes 4259840 | tf_op jit(solution)/shard_map/reduce_scatter | solution.py:225
  228.5 1690.8 %reduce-scatter.14.cloned.1.call-start = ((), (), s32[]{:S(2)}) async-start(), calls=%async_computation.13 | async-start | bytes 8519680 | tf_op jit(solution)/shard_map/reduce_scatter | solution.py:221
  241.1 2037.3 %reduce-scatter.24.cloned.1.call-start = ((), (), s32[]{:S(2)}) async-start(), calls=%async_computation.18 | async-start | bytes 17039360 | tf_op jit(solution)/shard_map/reduce_scatter | solution.py:230
  252.1 2384.7 %reduce-scatter.26.cloned.1.call-start = ((), (), s32[]{:S(2)}) async-start(), calls=%async_computation.19 | async-start | bytes 17039360 | tf_op jit(solution)/shard_map/reduce_scatter | solution.py:231
  264.1 7.4 copy-start.8
  264.1 7.4 copy-start.23
  271.5 333.6 %copy-start.9 = (bf16[256,1024]{1,0:T(8,128)(2,1)S(1)}, bf16[256,1024]{1,0:T(8,128)(2,1)}, u32[]{:S(2)}) copy-start(bf16[256,1024]{1,0:T(8,128)(2,1)} %copy-done.7) | copy-start | bytes 1572868
  273.0 335.1 %collective-permute-start.1 = (bf16[256,1024]{1,0:T(8,128)(2,1)}, bf16[256,1024]{1,0:T(8,128)(2,1)S(1)}, u32[]{:S(2)}, u32[]{:S(2)}) collective-permute-start(bf16[256,1024]{1,0:T(8,128)(2,1)} %fusion.30), channel_id=1, source_target_pairs={{0,64},{64,0},{1,65},{65,1},{2,66},{66,2},{3,67},{67,3},{4,68},{68... | collective-permute-start | bytes 1572872 | tf_op jit(solution)/shard_map/ppermute | solution.py:15
  (19 other events, 53.6 us)
Sparse Core Ops, SparseCore 0:
  26.8 29.1 all-gather.4
  58.2 26.0 all-gather.2
  146.3 37.7 reduce-scatter.11
  186.8 37.7 reduce-scatter.9
  227.4 338.9 reduce-scatter.21
  569.3 333.1 reduce-scatter.15
  905.4 333.2 reduce-scatter.19
  1241.8 333.3 reduce-scatter.17
  1578.2 341.0 reduce-scatter.13
  1922.1 356.1 reduce-scatter.23
  2281.4 355.4 reduce-scatter.25
where the time goes:
time: 2650 us; the launch traced here: 2640 us
  waiting for transfers between devices  2100 us (79%)
  blocking collectives  329 us (12%)
  matrix products  150 us (6%)
    reduce_scatter x1, waiting for transfers between devices, on_device(): lax.psum_scatter(ffn_shares[2], ('dp', 'seq'), scatter_dimension=0, tiled...  359 us
    reduce_scatter x1, waiting for transfers between devices, on_device(): lax.psum_scatter(ffn_shares[3], ('dp', 'seq'), scatter_dimension=0, tiled...  358 us
    reduce_scatter x1, waiting for transfers between devices, on_device(): lax.psum_scatter(grad_wskip, ('dp', 'seq'), scatter_dimension=0, tiled=True)  344 us
    reduce_scatter x1, waiting for transfers between devices, on_device(): lax.psum_scatter(grad_wkey, ('dp', 'seq'), scatter_dimension=0, tiled=True)  336 us
    reduce_scatter x1, waiting for transfers between devices, on_device(): lax.psum_scatter(grad_wvalue, ('dp', 'seq'), scatter_dimension=0, tiled=T...  336 us
    unnamed x1, blocking collectives  329 us
    reduce_scatter x1, waiting for transfers between devices, on_device(): lax.psum_scatter(grad_wquery, ('dp', 'seq'), scatter_dimension=0, tiled=T...  294 us
  transfers between devices with their start and end apart: 13, of which 10 were waited for; matrix products, arithmetic and copies ran while one was open for 5% of the time, Pallas kernels for 0%

commit v1 on v0

v1 whole, which is shorter than its diff:
```python
import jax
import jax.numpy as jnp
import numpy as np
from jax import lax
from jax.sharding import PartitionSpec as P

HEADS = 16


EPS = 1e-05


def from_partner(value, axis, stride):
    mask = 2**stride
    pairs = [(source, source ^ mask) for source in range(lax.axis_size(axis))]
    return lax.ppermute(value, axis, pairs)


def project(left, right):
    return jnp.dot(left, right, preferred_element_type=jnp.float32)


def rows_product(left, right):
    return lax.dot_general(
        left, right, (((0,), (0,)), ((), ())), preferred_element_type=jnp.float32
    )


def back_product(left, right):
    return lax.dot_general(
        left, right, (((1,), (1,)), ((), ())), preferred_element_type=jnp.float32
    )


def gelu_exact(values):
    return jax.nn.gelu(values, approximate=False)


def norm_forward(hidden, gain, bias):
    center = hidden - jnp.mean(hidden, axis=-1, keepdims=True)
    variance = jnp.mean(center * center, axis=-1, keepdims=True)
    inverse = lax.rsqrt(variance + EPS)
    unit = center * inverse
    return (unit * gain + bias, unit, inverse)


def norm_backward(grad, unit, inverse, gain):
    scaled = grad * gain
    mean_one = jnp.mean(scaled, axis=-1, keepdims=True)
    mean_two = jnp.mean(scaled * unit, axis=-1, keepdims=True)
    grad_input = inverse * (scaled - mean_one - unit * mean_two)
    return (grad_input, jnp.sum(grad * unit, axis=0), jnp.sum(grad, axis=0))


def segment_tables(lengths_row, spans_row, places):
    ends = jnp.cumsum(lengths_row, dtype=jnp.int32)
    starts = ends - lengths_row
    segment = jnp.sum((places[:, None] >= ends[None, :]).astype(jnp.int32), axis=1)
    lower = starts + spans_row[:, 0]
    upper = starts + spans_row[:, 1]
    inside = jnp.any(
        (places[:, None] >= lower[None, :]) & (places[:, None] < upper[None, :]), axis=1
    )
    return (segment, inside)


ORDER_NEAR = (0, 3, 1, 2)
ORDER_WRAP = (0, 1, 3, 2)
QUARTERS = (("x", ORDER_NEAR), ("x", ORDER_WRAP), ("z", ORDER_NEAR), ("z", ORDER_WRAP))


def partner_of(value, axis, mask):
    pairs = [(source, source ^ mask) for source in range(lax.axis_size(axis))]
    return lax.ppermute(value, axis, pairs)


def quarter_masks(quarter):
    first, order = QUARTERS[quarter]
    ring = (1, 3) if order == ORDER_NEAR else (3, 1)
    x_masks = [("dp", mask) for mask in ring]
    z_masks = [("dp", mask * 4) for mask in ring]
    return x_masks + z_masks if first == "x" else z_masks + x_masks


def relative_blocks():
    shards, quarters = [], []
    for core in range(2):
        for quarter, (first, order) in enumerate(QUARTERS):
            for outer in order:
                for inner in order:
                    for high in range(2):
                        x, z = (outer, inner) if first == "x" else (inner, outer)
                        shards.append(z * 16 + x * 4 + high * 2 + core)
                        quarters.append(quarter)
    return np.asarray(shards, np.int32), np.asarray(quarters, np.int32)


def relative_rows(shard, rows):
    shards, quarters = relative_blocks()
    piece = rows // 256
    inner = np.arange(piece, dtype=np.int32)
    fixed = quarters[:, None] * piece + inner[None, :]
    return (((jnp.asarray(shards) ^ shard)[:, None] * (4 * piece)) + fixed).reshape(-1)


def selector(shard, rows):
    source = relative_rows(shard, rows)
    return (source[:, None] == jnp.arange(rows, dtype=jnp.int32)[None, :]).astype(jnp.bfloat16)


def reduce_rows(value):
    rows = value.shape[0] // 4
    kept = []
    for quarter in range(4):
        piece = value[quarter * rows : (quarter + 1) * rows]
        for axis, mask in quarter_masks(quarter):
            half = piece.shape[0] // 2
            other = partner_of(piece[half:], axis, mask)
            piece = (piece[:half].astype(jnp.float32) + other.astype(jnp.float32)).astype(
                jnp.bfloat16
            )
        kept.append(piece)
    half = kept[0].shape[0] // 2
    other = partner_of(jnp.concatenate([piece[half:] for piece in kept], axis=0), "seq", 2)
    mine = jnp.concatenate([piece[:half] for piece in kept], axis=0)
    return mine.astype(jnp.float32) + other.astype(jnp.float32)


def swap_core(value):
    return partner_of(value, "seq", 1)


def low(value):
    return value.astype(jnp.bfloat16)


def pair_product(kept, swapped, grad, grad_swapped):
    left = jnp.concatenate([kept, swapped], axis=1)
    right = jnp.concatenate([grad, grad_swapped], axis=0)
    return low(project(left, right))


def on_device(
    states,
    mirror,
    w_skip,
    norm1_gain,
    norm1_bias,
    w_query,
    w_key,
    w_value,
    w_out,
    norm2_gain,
    norm2_bias,
    w_up,
    w_down,
    out_grad,
    lengths,
    infill_spans,
):
    rows_here = states.shape[2]
    model_width = states.shape[3]
    head_count = HEADS
    head_dim = model_width // head_count
    score_scale = head_dim ** (-0.5)
    seq = lax.axis_index("seq")
    shard = lax.axis_index("dp") * 4 + seq
    own_rows = states.reshape(rows_here, model_width)
    stored = mirror.reshape(rows_here, model_width)
    partner = from_partner(stored, "section", 0)
    lengths_row = lengths.reshape(-1)
    spans_row = infill_spans.reshape(-1, 2)
    row_length = rows_here * lax.axis_size("seq")
    local = jnp.arange(rows_here, dtype=jnp.int32)
    query_place = seq * rows_here + local
    key_place = jnp.concatenate([(seq ^ step) * rows_here + local for step in range(4)])
    query_segment, inside = segment_tables(lengths_row, spans_row, query_place)
    key_segment = segment_tables(lengths_row, spans_row, key_place)[0]
    allowed = query_segment[:, None] == key_segment[None, :]
    distance = jnp.abs(query_place[:, None] - key_place[None, :]).astype(jnp.float32)
    slopes = 2.0 ** (-8.0 * (jnp.arange(head_count, dtype=jnp.float32) + 1.0) / head_count)
    gain_one = norm1_gain.astype(jnp.float32)
    bias_one = norm1_bias.astype(jnp.float32)
    gain_two = norm2_gain.astype(jnp.float32)
    bias_two = norm2_bias.astype(jnp.float32)
    w_first = w_skip[:model_width]
    w_second = w_skip[model_width:]
    select = selector(shard, model_width)
    half = model_width // 2

    grad_rows = (
        out_grad.reshape(rows_here, model_width).astype(jnp.float32)
        * inside.astype(jnp.float32)[:, None]
    )
    grad_low = low(grad_rows)
    grad_low_other = swap_core(grad_low)
    hidden = project(own_rows, w_first) + project(partner, w_second)
    normed_one, unit_one, inverse_one = norm_forward(hidden, gain_one, bias_one)
    normed_one = low(normed_one)
    far = partner_of(normed_one, "seq", 2)
    near = swap_core(normed_one)
    far_near = swap_core(far)
    normed_all = jnp.concatenate([normed_one, near, far, far_near], axis=0)
    query = low(project(normed_one, w_query))
    keys_all = low(project(normed_all, w_key))
    values_all = low(project(normed_all, w_value))
    query3 = query.reshape(rows_here, head_count, head_dim)
    keys3 = keys_all.reshape(row_length, head_count, head_dim)
    values3 = values_all.reshape(row_length, head_count, head_dim)

    def scores_of():
        raw = jnp.einsum("qhd,khd->hqk", query3, keys3, preferred_element_type=jnp.float32)
        scores = raw * score_scale - slopes[:, None, None] * distance[None]
        return jnp.where(allowed[None], scores, -1e30)

    scores = scores_of()
    row_top = jnp.max(scores, axis=-1, keepdims=True)
    exponent = jnp.exp(scores - row_top)
    row_total = jnp.sum(exponent, axis=-1, keepdims=True)
    log_total = row_top + jnp.log(row_total)
    softmax_low = (exponent / row_total).astype(jnp.bfloat16)
    mixed_rows = jnp.einsum(
        "hqk,khd->qhd", softmax_low, values3, preferred_element_type=jnp.float32
    )
    mixed_rows = low(mixed_rows.reshape(rows_here, model_width))
    residual = hidden + project(mixed_rows, w_out)
    normed_two, unit_two, inverse_two = norm_forward(residual, gain_two, bias_two)
    normed_two = low(normed_two)
    upward = project(normed_two, w_up)
    activated, gelu_pull = jax.vjp(gelu_exact, upward)
    act_low = low(activated)
    result = residual + project(act_low, w_down)
    output = low(result).reshape(states.shape)
    grad_act = back_product(grad_low, w_down)
    grad_upward = low(gelu_pull(grad_act)[0])
    grad_upward_other = swap_core(grad_upward)

    hidden_width = act_low.shape[1]
    piece = hidden_width // 256
    shards, quarters = relative_blocks()
    act_rows = act_low.T.reshape(256, piece, rows_here)
    act_rows = act_rows[(jnp.asarray(shards) ^ shard) * 4 + jnp.asarray(quarters)]
    act_rows = act_rows.reshape(2, hidden_width // 2, rows_here)
    act_other = swap_core(act_rows[1])
    down_sum = reduce_rows(pair_product(act_rows[0], act_other, grad_low, grad_low_other))

    two_rows = low(back_product(select, normed_two))
    two_other = swap_core(two_rows[half:])
    up_sum = reduce_rows(pair_product(two_rows[:half], two_other, grad_upward, grad_upward_other))

    grad_normed_two = back_product(grad_upward, w_up)
    grad_resid_norm, grad_gain_two, grad_bias_two = norm_backward(
        grad_normed_two, unit_two, inverse_two, gain_two
    )
    grad_residual = grad_rows + grad_resid_norm
    grad_attn = low(grad_residual)
    grad_attn_other = swap_core(grad_attn)
    mixed_cut = low(back_product(select, mixed_rows))
    mixed_other = swap_core(mixed_cut[half:])
    out_sum = reduce_rows(pair_product(mixed_cut[:half], mixed_other, grad_attn, grad_attn_other))

    grad_mixed = low(back_product(grad_attn, w_out))
    grad_mixed3 = grad_mixed.reshape(rows_here, head_count, head_dim)
    softmax_again = jnp.exp(scores_of() - log_total)
    grad_softmax = jnp.einsum(
        "qhd,khd->hqk", grad_mixed3, values3, preferred_element_type=jnp.float32
    )
    centre = jnp.sum(softmax_again * grad_softmax, axis=-1, keepdims=True)
    grad_scores = (softmax_again * (grad_softmax - centre)).astype(jnp.bfloat16)
    grad_query = (
        jnp.einsum("hqk,khd->qhd", grad_scores, keys3, preferred_element_type=jnp.float32)
        * score_scale
    )
    grad_query = low(grad_query.reshape(rows_here, model_width))
    key_part = (
        jnp.einsum("hqk,qhd->khd", grad_scores, query3, preferred_element_type=jnp.float32)
        * score_scale
    )
    value_part = jnp.einsum(
        "hqk,qhd->khd",
        softmax_again.astype(jnp.bfloat16),
        grad_mixed3,
        preferred_element_type=jnp.float32,
    )
    both_part = low(
        jnp.concatenate(
            [
                key_part.reshape(row_length, model_width),
                value_part.reshape(row_length, model_width),
            ],
            axis=1,
        )
    ).reshape(4, rows_here, 2 * model_width)
    both_other = swap_core(jnp.concatenate([both_part[1], both_part[3]], axis=0))
    both_mine = low(
        jnp.concatenate([both_part[0], both_part[2]], axis=0).astype(jnp.float32)
        + both_other.astype(jnp.float32)
    )
    both_far = swap_core(both_mine)
    grad_query_other = swap_core(grad_query)
    w_both = jnp.concatenate([w_key, w_value], axis=1)
    normed_part = back_product(both_mine, w_both)
    normed_far = partner_of(low(normed_part[rows_here:]), "seq", 2)
    grad_normed_one = (
        back_product(grad_query, w_query)
        + normed_part[:rows_here]
        + normed_far.astype(jnp.float32)
    )
    one_rows = low(back_product(select[:half], normed_all))
    query_share = low(
        project(one_rows[:, : 2 * rows_here], jnp.concatenate([grad_query, grad_query_other], axis=0))
    )
    both_rows = jnp.concatenate(
        [both_mine[:rows_here], both_far[:rows_here], both_mine[rows_here:], both_far[rows_here:]],
        axis=0,
    )
    both_share = low(project(one_rows, both_rows))
    query_sum = reduce_rows(query_share)
    both_sum = reduce_rows(both_share)

    grad_hidden_norm, grad_gain_one, grad_bias_one = norm_backward(
        grad_normed_one, unit_one, inverse_one, gain_one
    )
    grad_hidden = low(grad_residual + grad_hidden_norm)
    grad_hidden_other = swap_core(grad_hidden)
    grad_partner = low(back_product(grad_hidden, w_second))
    grad_stored = from_partner(grad_partner, "section", 0)
    grad_own = low(back_product(grad_hidden, w_first))
    select_joined = selector(shard, 2 * model_width)
    joined = jnp.concatenate([own_rows, partner], axis=1)
    joined_rows = low(back_product(select_joined, joined))
    joined_other = swap_core(joined_rows[model_width:])
    skip_sum = reduce_rows(
        pair_product(joined_rows[:model_width], joined_other, grad_hidden, grad_hidden_other)
    )

    sums = jnp.stack([grad_gain_one, grad_bias_one, grad_gain_two, grad_bias_two])
    for axis, mask in (("seq", 1), ("dp", 1), ("dp", 3), ("dp", 4), ("dp", 12), ("seq", 2)):
        sums = sums + partner_of(sums, axis, mask)
    sums = lax.dynamic_slice_in_dim(sums, shard * (model_width // 64), model_width // 64, axis=1)
    return (
        output,
        grad_own.reshape(states.shape),
        grad_stored.reshape(states.shape),
        skip_sum[None],
        sums[0][None],
        sums[1][None],
        query_sum[None],
        both_sum[None, :, :model_width],
        both_sum[None, :, model_width:],
        out_sum[None],
        sums[2][None],
        sums[3][None],
        up_sum[None],
        down_sum[None],
    )


def solution(mesh):
    in_specs = (
        P("section", "dp", "seq", None),
        P("section", "dp", "seq", None),
        P(),
        P(),
        P(),
        P(),
        P(),
        P(),
        P(),
        P(),
        P(),
        P(),
        P(),
        P("section", "dp", "seq", None),
        P("section", "dp", None),
        P("section", "dp", None, None),
    )
    out_specs = (
        P("section", "dp", "seq", None),
        P("section", "dp", "seq", None),
        P("section", "dp", "seq", None),
        P("section", ("dp", "seq"), None),
        P("section", ("dp", "seq")),
        P("section", ("dp", "seq")),
        P("section", ("dp", "seq"), None),
        P("section", ("dp", "seq"), None),
        P("section", ("dp", "seq"), None),
        P("section", ("dp", "seq"), None),
        P("section", ("dp", "seq")),
        P("section", ("dp", "seq")),
        P("section", ("dp", "seq"), None),
        P("section", ("dp", "seq"), None),
    )
    return jax.shard_map(
        on_device, mesh=mesh, in_specs=in_specs, out_specs=out_specs, check_vma=False
    )
```

time: 2650 us -> 479 us (0.18)
  waiting for transfers between devices: 2100 us -> 137 us
  blocking collectives: 329 us -> 0 us
  starting transfers between devices: 3.14 us -> 139 us
    reduce_scatter x9 -> x0, waiting for transfers between devices: 2060 us -> none  [the longest x1 359 us: on_device(): lax.psum_scatter(ffn_shares[2], ('dp', 'seq'), scatter_dimension=0, tiled...]
    unnamed x1 -> x0, blocking collectives: 329 us -> none
    ppermute x0 -> x123, waiting for transfers between devices: none -> 137 us  [partner_of(): return lax.ppermute(value, axis, pairs)]
    ppermute x0 -> x123, starting transfers between devices: none -> 137 us  [partner_of(): return lax.ppermute(value, axis, pairs)]
    dot_general x8 -> x0, matrix products: 35.8 us -> none  [rows_product(): lax.dot_general(left, right, (((0,), (0,)), ((), ())), preferred_element_...]
    all_gather x2 -> x0, waiting for transfers between devices: 31.2 us -> none  [the longest x1 19.4 us: on_device(): lax.all_gather(key_rows, 'seq', axis=0, tiled=True)]
    dot_general x8 -> x14, matrix products: 36 us -> 54.2 us  [project(): return jnp.dot(left, right, preferred_element_type=jnp.float32)]
  transfers between devices with their start and end apart: 13 -> 125, of which waited for: 10 -> 71; matrix products, arithmetic and copies ran while one was open for 5% -> 39% of each run, Pallas kernels for 0% -> 0%
where the time goes in v1:
time: 479 us; the launch traced here: 474 us
  starting transfers between devices  139 us (29%)
  waiting for transfers between devices  137 us (29%)
  matrix products  128 us (27%)
  other arithmetic  43.7 us (9%)
  local copies, waits for them, and re-layouts  21.6 us (5%)
    ppermute x123, waiting for transfers between devices, partner_of(): return lax.ppermute(value, axis, pairs)  137 us
    ppermute x123, starting transfers between devices, partner_of(): return lax.ppermute(value, axis, pairs)  137 us
    dot_general x14, matrix products, project(): return jnp.dot(left, right, preferred_element_type=jnp.float32)  54.2 us
    dot_general x11, matrix products, back_product(): lax.dot_general(left, right, (((1,), (1,)), ((), ())), preferred_element_...  39 us
    convert_element_type x1, other arithmetic, on_device(): grad_scores = (softmax_again * (grad_softmax - centre)).astype(jnp.bfloat16)  11.9 us
    dot_general x1, matrix products, on_device(): jnp.einsum('qhd,khd->hqk', grad_mixed3, values3, preferred_element_type=j...  11.2 us
  transfers between devices with their start and end apart: 125, of which 71 were waited for; matrix products, arithmetic and copies ran while one was open for 39% of the time, Pallas kernels for 0%

profile of v1, /device:TPU:0, one launch (start us, length us, event | category | flops | bytes accessed | tf_op | source)
XLA Modules:
  0.0 473.6 jit_solution(13931523736738459043)
XLA Ops:
  30.6 7.3 %collective-permute-done.2 = bf16[256,1024]{1,0:T(8,128)(2,1)} collective-permute-done((bf16[256,1024]{1,0:T(8,128)(2,1)}, bf16[256,1024]{1,0:T(8,128)(2,1)}, u32[]{:S(2)}, u32[]{:S(2)}) %collective-permute-start.2) | collective-permute-done | bytes 524320 | tf_op jit(solution)/shard_map/ppermute | solution.py:74
  38.0 4.9 %fusion.51 = bf16[2048,256]{0,1:T(8,128)(2,1)S(1)} fusion(s32[2048]{0:T(1024)S(1)} %eq.50, bf16[256,1024]{1,0:T(8,128)(2,1)} %collective-permute-done, bf16[256,1024]{1,0:T(8,128)(2,1)} %bitcast.196), kind=kOutput, calls=%fused_computation.84 | convolution fusion | flops 2154299392 | bytes 2105344 | tf_op jit(solution)/shard_map/dot_general | solution.py:30
  44.0 4.0 convolution_convert_fusion.3
  48.1 5.2 %fusion.184 = (f32[16,256]{1,0:T(8,128)S(1)}, f32[16,256,1024]{2,1,0:T(8,128)S(1)}) fusion(f32[256,1024]{1,0:T(8,128)S(1)} %copy-done.23, f32[16]{0:T(128)S(1)} %multiply_power_fusion, bf16[256,16,64]{0,2,1:T(8,128)(2,1)S(1)} %bitcast.166, bf16[1024,16,64]{0,2,1:T(8,128)(2,1)S(1)} %bitcast.170, pred[256,1024]{1,0:T(8,128)(4,1)S(1)} %broadcast_compare_fusion), kind=kOutput, calls=%fused_computation.370 | convolution fusion | flops 557838336 | bytes 20725824 | tf_op jit(solution)/shard_map/qhd,khd->hqk/dot_general | solution.py:212
  53.4 4.3 fusion.1
  57.7 5.0 %convolution_convert_fusion.4 = bf16[1024,1024]{0,1:T(8,128)(2,1)S(1)} fusion(bf16[1024,1024]{1,0:T(8,128)(2,1)S(1)} %copy-done.34, bf16[256,1024]{1,0:T(8,128)(2,1)S(1)} %collective-permute-done.3, bf16[256,1024]{1,0:T(8,128)(2,1)} %collective-permute-done.2, bf16[256,1024]{1,0:T(8,128)(2,1)} %collective-permute-done.1, ...), kind=kOutput, calls=%fused_computation.102 | convolution fusion | flops 2156920832 | bytes 6291456 | tf_op jit(solution)/shard_map/dot_general | solution.py:20
  62.6 4.3 fusion.93
  70.0 15.2 %fusion.11 = (bf16[4096,256]{0,1:T(8,128)(2,1)}, f32[256,4096]{1,0:T(8,128)S(1)}) fusion(bf16[1024,4096]{1,0:T(8,128)(2,1)} %param.33, f32[256,1024]{1,0:T(8,128)S(1)} %get-tuple-element.154, f32[1024]{0:T(1024)S(1)} %convert_element_type.1070, f32[1024]{0:T(1024)S(1)} %convert_element_type.1069, f32[256]{0:T(256)S(1)} %add_rsqrt_fusion, ...), kind=kOutput, calls=%fused_computation.27 | convolution fusion | flops 2216951808 | bytes 15738880 | tf_op jit(solution)/shard_map/dot_general | solution.py:20
  85.3 16.2 %add_convert_fusion.1 = (bf16[256,4096]{1,0:T(8,128)(2,1)S(1)}, f32[256,4096]{1,0:T(8,128)}) fusion(f32[256,4096]{1,0:T(8,128)S(1)} %get-tuple-element.159, bf16[256,1024]{1,0:T(8,128)(2,1)} %fusion.121, bf16[4096,1024]{1,0:T(8,128)(2,1)S(1)} %bitcast.163), kind=kOutput, calls=%fused_computation.66 | convolution fusion | flops 2222981120 | bytes 19398656 | tf_op jit(solution)/shard_map/dot_general | solution.py:30
  108.5 9.2 %fusion.65 = bf16[16,64,1024]{2,1,0:T(8,128)(2,1)} fusion(bf16[256,16,64]{0,2,1:T(8,128)(2,1)S(1)} %bitcast.164, f32[16,256,1024]{2,1,0:T(8,128)} %copy-done.2, f32[16,256]{1,0:T(8,128)S(1)} %log_add_fusion), kind=kOutput, calls=%fused_computation.99 | convolution fusion | flops 546308096 | bytes 19415040 | tf_op jit(solution)/shard_map/hqk,qhd->khd/dot_general | solution.py:279
  117.7 11.2 %multiply_reduce_fusion = (f32[16,256]{1,0:T(8,128)S(1)}, f32[16,256,1024]{2,1,0:T(8,128)}) fusion(f32[16,256,1024]{2,1,0:T(8,128)} %copy-done.2, f32[16,256]{1,0:T(8,128)S(1)} %log_add_fusion, bf16[256,16,64]{0,2,1:T(8,128)(2,1)S(1)} %bitcast.165, bf16[1024,16,64]{0,2,1:T(8,128)(2,1)S(1)} %bitcast.169), kind=kOutput, calls=%fused_computation.3 | convolution fusion | flops 549449728 | bytes 36208640 | tf_op jit(solution)/shard_map/qhd,khd->hqk/dot_general | solution.py:265
  128.9 11.9 %multiply_convert_fusion = bf16[16,256,1024]{2,1,0:T(8,128)(2,1)S(1)} fusion(f32[16,256,1024]{2,1,0:T(8,128)} %get-tuple-element.157, f32[16,256,1024]{2,1,0:T(8,128)} %copy-done.2, f32[16,256]{1,0:T(8,128)S(1)} %get-tuple-element.156, f32[16,256]{1,0:T(8,128)S(1)} %log_add_fusion), kind=kLoop, calls=%fused_computation.2 | loop fusion | flops 16777216 | bytes 41975808 | tf_op jit(solution)/shard_map/convert_element_type | solution.py:269
  150.0 4.5 copy.45
  154.4 3.9 gather_fusion
  161.2 8.0 %fusion.94 = bf16[1,1,256,1024]{3,2,1,0:T(8,128)(2,1)} fusion(f32[256,1024]{1,0:T(8,128)S(1)} %copy-done.7, bf16[4096,1024]{1,0:T(8,128)(2,1)} %param.34, f32[256,4096]{1,0:T(8,128)} %get-tuple-element.26, f32[256,4096]{1,0:T(8,128)S(1)} %copy-done.11), kind=kOutput, calls=%fused_computation.127 | convolution fusion | flops 2151153664 | bytes 18350080 | tf_op jit(solution)/shard_map/dot_general | solution.py:20
  178.7 4.0 collective-permute-start.82
  255.2 3.6 convolution_convert_fusion.1
  262.8 5.4 %collective-permute-done.108 = bf16[256,1024]{1,0:T(8,128)(2,1)S(1)} collective-permute-done((bf16[256,1024]{1,0:T(8,128)(2,1)S(1)}, bf16[256,1024]{1,0:T(8,128)(2,1)S(1)}, u32[]{:S(2)}, u32[]{:S(2)}) %collective-permute-start.108) | collective-permute-done | bytes 524320 | tf_op jit(solution)/shard_map/ppermute | solution.py:74
  330.8 5.5 %collective-permute-done.5 = bf16[256,1024]{1,0:T(8,128)(2,1)S(1)} collective-permute-done((bf16[256,1024]{1,0:T(8,128)(2,1)S(1)}, bf16[256,1024]{1,0:T(8,128)(2,1)S(1)}, u32[]{:S(2)}, u32[]{:S(2)}) %collective-permute-start.5) | collective-permute-done | bytes 524320 | tf_op jit(solution)/shard_map/ppermute | solution.py:74
  338.5 3.7 collective-permute-done.27
  362.9 4.0 collective-permute-done.94
  371.6 3.6 collective-permute-done.90
  386.7 3.9 collective-permute-done.100
  467.0 4.9 %collective-permute-done.67 = bf16[16,2048]{1,0:T(8,128)(2,1)S(1)} collective-permute-done((bf16[16,2048]{1,0:T(8,128)(2,1)S(1)}, bf16[16,2048]{1,0:T(8,128)(2,1)S(1)}, u32[]{:S(2)}, u32[]{:S(2)}) %collective-permute-start.67) | collective-permute-done | bytes 65568 | tf_op jit(solution)/shard_map/ppermute | solution.py:74
  (609 shorter events, 316.7 us)
Async XLA Ops:
  4.5 250.7 %collective-permute-start.107 = (bf16[256,1024]{1,0:T(8,128)(2,1)}, bf16[256,1024]{1,0:T(8,128)(2,1)}, u32[]{:S(2)}, u32[]{:S(2)}) collective-permute-start(bf16[256,1024]{1,0:T(8,128)(2,1)} %fusion.121), channel_id=1, source_target_pairs={{0,1},{1,0},{2,3},{3,2},{4,5},{5,4},{6,7},{7,6},{8,9},{9,8},{10,11... | collective-permute-start | bytes 1572872 | tf_op jit(solution)/shard_map/ppermute | solution.py:74
  4.5 14.7 %collective-permute-start = (bf16[256,1024]{1,0:T(8,128)(2,1)}, bf16[256,1024]{1,0:T(8,128)(2,1)}, u32[]{:S(2)}, u32[]{:S(2)}) collective-permute-start(bf16[256,1024]{1,0:T(8,128)(2,1)} %bitcast.195), channel_id=1, source_target_pairs={{0,64},{64,0},{1,65},{65,1},{2,66},{66,2},{3,67},{67,3},{4,68},{68... | collective-permute-start | bytes 1572872 | tf_op jit(solution)/shard_map/ppermute | solution.py:16
  22.4 15.5 %collective-permute-start.2 = (bf16[256,1024]{1,0:T(8,128)(2,1)}, bf16[256,1024]{1,0:T(8,128)(2,1)}, u32[]{:S(2)}, u32[]{:S(2)}) collective-permute-start(bf16[256,1024]{1,0:T(8,128)(2,1)} %add_convert_fusion.12), channel_id=1, source_target_pairs={{0,2},{1,3},{2,0},{3,1},{4,6},{5,7},{6,4},{7,5},{8,10},{9,11},{10,... | collective-permute-start | bytes 1572872 | tf_op jit(solution)/shard_map/ppermute | solution.py:74
  25.9 18.2 %collective-permute-start.1 = (bf16[256,1024]{1,0:T(8,128)(2,1)}, bf16[256,1024]{1,0:T(8,128)(2,1)}, u32[]{:S(2)}, u32[]{:S(2)}) collective-permute-start(bf16[256,1024]{1,0:T(8,128)(2,1)} %add_convert_fusion.12), channel_id=1, source_target_pairs={{0,1},{1,0},{2,3},{3,2},{4,5},{5,4},{6,7},{7,6},{8,9},{9,8},{10,11... | collective-permute-start | bytes 1572872 | tf_op jit(solution)/shard_map/ppermute | solution.py:74
  107.7 67.3 %collective-permute-start.69 = (bf16[256,1024]{1,0:T(8,128)(2,1)}, bf16[256,1024]{1,0:T(8,128)(2,1)}, u32[]{:S(2)}, u32[]{:S(2)}) collective-permute-start(bf16[256,1024]{1,0:T(8,128)(2,1)} %get-tuple-element.23), channel_id=1, source_target_pairs={{0,1},{1,0},{2,3},{3,2},{4,5},{5,4},{6,7},{7,6},{8,9},{9,8},{10,11... | collective-permute-start | bytes 1572872 | tf_op jit(solution)/shard_map/ppermute | solution.py:74
  145.9 36.9 %collective-permute-start.32 = (bf16[256,1024]{0,1:T(8,128)(2,1)}, bf16[256,1024]{0,1:T(8,128)(2,1)}, u32[]{:S(2)}, u32[]{:S(2)}) collective-permute-start(bf16[256,1024]{0,1:T(8,128)(2,1)} %bitcast.17), channel_id=1, source_target_pairs={{0,1},{1,0},{2,3},{3,2},{4,5},{5,4},{6,7},{7,6},{8,9},{9,8},{10,11... | collective-permute-start | bytes 1572872 | tf_op jit(solution)/shard_map/ppermute | solution.py:74
  149.5 25.4 %collective-permute-start.68 = (bf16[512,256]{0,1:T(8,128)(2,1)}, bf16[512,256]{0,1:T(8,128)(2,1)}, u32[]{:S(2)}, u32[]{:S(2)}) collective-permute-start(bf16[512,256]{0,1:T(8,128)(2,1)} %get-tuple-element.89), channel_id=1, source_target_pairs={{0,1},{1,0},{2,3},{3,2},{4,5},{5,4},{6,7},{7,6},{8,9},{9,8},{10,11... | collective-permute-start | bytes 786440 | tf_op jit(solution)/shard_map/ppermute | solution.py:74
  191.9 126.2 %collective-permute-start.88 = (bf16[256,4096]{1,0:T(8,128)(2,1)S(1)}, bf16[256,4096]{1,0:T(8,128)(2,1)S(1)}, u32[]{:S(2)}, u32[]{:S(2)}) collective-permute-start(bf16[256,4096]{1,0:T(8,128)(2,1)S(1)} %copy-done.39), channel_id=1, source_target_pairs={{0,1},{1,0},{2,3},{3,2},{4,5},{5,4},{6,7},{7,6},{8,9},{9,8},{10,11... | collective-permute-start | bytes 6291464 | tf_op jit(solution)/shard_map/ppermute | solution.py:74
  193.7 61.5 %collective-permute-start.106 = (bf16[2048,256]{1,0:T(8,128)(2,1)S(1)}, bf16[2048,256]{1,0:T(8,128)(2,1)S(1)}, u32[]{:S(2)}, u32[]{:S(2)}) collective-permute-start(bf16[2048,256]{1,0:T(8,128)(2,1)S(1)} %bitcast.173), channel_id=1, source_target_pairs={{0,1},{1,0},{2,3},{3,2},{4,5},{5,4},{6,7},{7,6},{8,9},{9,8},{10,11... | collective-permute-start | bytes 3145736 | tf_op jit(solution)/shard_map/ppermute | solution.py:74
  261.6 12.2 %collective-permute-start.112 = (bf16[256,1024]{1,0:T(8,128)(2,1)S(1)}, bf16[256,1024]{1,0:T(8,128)(2,1)S(1)}, u32[]{:S(2)}, u32[]{:S(2)}) collective-permute-start(bf16[256,1024]{1,0:T(8,128)(2,1)S(1)} %get-tuple-element.34), channel_id=1, source_target_pairs={{0,12},{4,8},{8,4},{12,0},{16,28},{20,24},{24,20},{28,16},{32,44},... | collective-permute-start | bytes 1572872 | tf_op jit(solution)/shard_map/ppermute | solution.py:74
  268.2 49.9 %collective-permute-start.87 = (bf16[512,256]{0,1:T(8,128)(2,1)S(1)}, bf16[512,256]{0,1:T(8,128)(2,1)S(1)}, u32[]{:S(2)}, u32[]{:S(2)}) collective-permute-start(bf16[512,256]{0,1:T(8,128)(2,1)S(1)} %get-tuple-element.87), channel_id=1, source_target_pairs={{0,1},{1,0},{2,3},{3,2},{4,5},{5,4},{6,7},{7,6},{8,9},{9,8},{10,11... | collective-permute-start | bytes 786440 | tf_op jit(solution)/shard_map/ppermute | solution.py:74
  269.5 51.3 %collective-permute-start.4 = (bf16[512,2048]{0,1:T(8,128)(2,1)S(1)}, bf16[512,2048]{0,1:T(8,128)(2,1)S(1)}, u32[]{:S(2)}, u32[]{:S(2)}) collective-permute-start(bf16[512,2048]{0,1:T(8,128)(2,1)S(1)} %fusion.56), channel_id=1, source_target_pairs={{0,1},{1,0},{2,3},{3,2},{4,5},{5,4},{6,7},{7,6},{8,9},{9,8},{10,11... | collective-permute-start | bytes 6291464 | tf_op jit(solution)/shard_map/ppermute | solution.py:74
  315.4 13.6 %collective-permute-start.124 = (bf16[64,1024]{1,0:T(8,128)(2,1)S(1)}, bf16[64,1024]{1,0:T(8,128)(2,1)S(1)}, u32[]{:S(2)}, u32[]{:S(2)}) collective-permute-start(bf16[64,1024]{1,0:T(8,128)(2,1)S(1)} %pad_maximum_fusion.2), channel_id=1, source_target_pairs={{0,2},{1,3},{2,0},{3,1},{4,6},{5,7},{6,4},{7,5},{8,10},{9,11},{10,... | collective-permute-start | bytes 393224 | tf_op jit(solution)/shard_map/ppermute | solution.py:74
  325.6 10.8 %collective-permute-start.5 = (bf16[256,1024]{1,0:T(8,128)(2,1)S(1)}, bf16[256,1024]{1,0:T(8,128)(2,1)S(1)}, u32[]{:S(2)}, u32[]{:S(2)}) collective-permute-start(bf16[256,1024]{1,0:T(8,128)(2,1)S(1)} %slice.1569), channel_id=1, source_target_pairs={{0,2},{1,3},{2,0},{3,1},{4,6},{5,7},{6,4},{7,5},{8,10},{9,11},{10,... | collective-permute-start | bytes 1572872 | tf_op jit(solution)/shard_map/ppermute | solution.py:74
  326.6 29.8 %collective-permute-start.89 = (bf16[64,4096]{1,0:T(8,128)(2,1)S(1)}, bf16[64,4096]{1,0:T(8,128)(2,1)S(1)}, u32[]{:S(2)}, u32[]{:S(2)}) collective-permute-start(bf16[64,4096]{1,0:T(8,128)(2,1)S(1)} %get-tuple-element.39), channel_id=1, source_target_pairs={{0,4},{4,0},{8,12},{12,8},{16,20},{20,16},{24,28},{28,24},{32,36},... | collective-permute-start | bytes 1572872 | tf_op jit(solution)/shard_map/ppermute | solution.py:74
  326.7 30.3 %collective-permute-start.101 = (bf16[64,4096]{1,0:T(8,128)(2,1)S(1)}, bf16[64,4096]{1,0:T(8,128)(2,1)S(1)}, u32[]{:S(2)}, u32[]{:S(2)}) collective-permute-start(bf16[64,4096]{1,0:T(8,128)(2,1)S(1)} %get-tuple-element.40), channel_id=1, source_target_pairs={{0,48},{4,52},{8,56},{12,60},{16,32},{20,36},{24,40},{28,44},{32,1... | collective-permute-start | bytes 1572872 | tf_op jit(solution)/shard_map/ppermute | solution.py:74
  328.9 28.9 %collective-permute-start.97 = (bf16[64,4096]{1,0:T(8,128)(2,1)S(1)}, bf16[64,4096]{1,0:T(8,128)(2,1)S(1)}, u32[]{:S(2)}, u32[]{:S(2)}) collective-permute-start(bf16[64,4096]{1,0:T(8,128)(2,1)S(1)} %get-tuple-element.41), channel_id=1, source_target_pairs={{0,16},{4,20},{8,24},{12,28},{16,0},{20,4},{24,8},{28,12},{32,48},... | collective-permute-start | bytes 1572872 | tf_op jit(solution)/shard_map/ppermute | solution.py:74
  328.9 28.9 %collective-permute-start.93 = (bf16[64,4096]{1,0:T(8,128)(2,1)S(1)}, bf16[64,4096]{1,0:T(8,128)(2,1)S(1)}, u32[]{:S(2)}, u32[]{:S(2)}) collective-permute-start(bf16[64,4096]{1,0:T(8,128)(2,1)S(1)} %get-tuple-element.42), channel_id=1, source_target_pairs={{0,12},{4,8},{8,4},{12,0},{16,28},{20,24},{24,20},{28,16},{32,44},... | collective-permute-start | bytes 1572872 | tf_op jit(solution)/shard_map/ppermute | solution.py:74
  356.4 40.1 %collective-permute-start.7 = (bf16[1024,256]{0,1:T(8,128)(2,1)S(1)}, bf16[1024,256]{0,1:T(8,128)(2,1)S(1)}, u32[]{:S(2)}, u32[]{:S(2)}) collective-permute-start(bf16[1024,256]{0,1:T(8,128)(2,1)S(1)} %copy-done.27), channel_id=1, source_target_pairs={{0,1},{1,0},{2,3},{3,2},{4,5},{5,4},{6,7},{7,6},{8,9},{9,8},{10,11... | collective-permute-start | bytes 1572872 | tf_op jit(solution)/shard_map/ppermute | solution.py:74
  356.4 40.1 %collective-permute-start.8 = (bf16[256,1024]{1,0:T(8,128)(2,1)S(1)}, bf16[256,1024]{1,0:T(8,128)(2,1)S(1)}, u32[]{:S(2)}, u32[]{:S(2)}) collective-permute-start(bf16[256,1024]{1,0:T(8,128)(2,1)S(1)} %add_convert_fusion.10), channel_id=1, source_target_pairs={{0,1},{1,0},{2,3},{3,2},{4,5},{5,4},{6,7},{7,6},{8,9},{9,8},{10,11... | collective-permute-start | bytes 1572872 | tf_op jit(solution)/shard_map/ppermute | solution.py:74
  368.2 33.2 %collective-permute-start.6 = (bf16[256,1024]{1,0:T(8,128)(2,1)S(1)}, bf16[256,1024]{1,0:T(8,128)(2,1)S(1)}, u32[]{:S(2)}, u32[]{:S(2)}) collective-permute-start(bf16[256,1024]{1,0:T(8,128)(2,1)S(1)} %fusion.87), channel_id=1, source_target_pairs={{0,64},{64,0},{1,65},{65,1},{2,66},{66,2},{3,67},{67,3},{4,68},{68... | collective-permute-start | bytes 1572872 | tf_op jit(solution)/shard_map/ppermute | solution.py:16
  401.4 27.4 %collective-permute-start.50 = (bf16[512,2048]{0,1:T(8,128)(2,1)S(1)}, bf16[512,2048]{0,1:T(8,128)(2,1)S(1)}, u32[]{:S(2)}, u32[]{:S(2)}) collective-permute-start(bf16[512,2048]{0,1:T(8,128)(2,1)S(1)} %add_convert_fusion), channel_id=1, source_target_pairs={{0,1},{1,0},{2,3},{3,2},{4,5},{5,4},{6,7},{7,6},{8,9},{9,8},{10,11... | collective-permute-start | bytes 6291464 | tf_op jit(solution)/shard_map/ppermute | solution.py:74
  425.7 10.5 %collective-permute-start.12 = (bf16[16,1024]{1,0:T(8,128)(2,1)S(1)}, bf16[16,1024]{1,0:T(8,128)(2,1)S(1)}, u32[]{:S(2)}, u32[]{:S(2)}) collective-permute-start(bf16[16,1024]{1,0:T(8,128)(2,1)S(1)} %slice.1178), channel_id=1, source_target_pairs={{0,48},{4,52},{8,56},{12,60},{16,32},{20,36},{24,40},{28,44},{32,1... | collective-permute-start | bytes 98312 | tf_op jit(solution)/shard_map/ppermute | solution.py:74
  443.0 23.4 %collective-permute-start.25 = (bf16[32,1024]{1,0:T(8,128)(2,1)S(1)}, bf16[32,1024]{1,0:T(8,128)(2,1)S(1)}, u32[]{:S(2)}, u32[]{:S(2)}) collective-permute-start(bf16[32,1024]{1,0:T(8,128)(2,1)S(1)} %pad_maximum_fusion.3), channel_id=1, source_target_pairs={{0,2},{1,3},{2,0},{3,1},{4,6},{5,7},{6,4},{7,5},{8,10},{9,11},{10,... | collective-permute-start | bytes 196616 | tf_op jit(solution)/shard_map/ppermute | solution.py:74
  (147 other events, 1164.4 us)

commit v2 on v1

--- a/solution.py
+++ b/solution.py
@@ -1,6 +1,9 @@
+import functools
+
 import jax
 import jax.numpy as jnp
-import numpy as np
+from jax.experimental import pallas as pl
+from jax.experimental.pallas import tpu as pltpu
 from jax import lax
 from jax.sharding import PartitionSpec as P
 
@@ -64,66 +67,16 @@
     return (segment, inside)
 
 
-ORDER_NEAR = (0, 3, 1, 2)
-ORDER_WRAP = (0, 1, 3, 2)
-QUARTERS = (("x", ORDER_NEAR), ("x", ORDER_WRAP), ("z", ORDER_NEAR), ("z", ORDER_WRAP))
-
-
 def partner_of(value, axis, mask):
     pairs = [(source, source ^ mask) for source in range(lax.axis_size(axis))]
     return lax.ppermute(value, axis, pairs)
 
 
-def quarter_masks(quarter):
-    first, order = QUARTERS[quarter]
-    ring = (1, 3) if order == ORDER_NEAR else (3, 1)
-    x_masks = [("dp", mask) for mask in ring]
-    z_masks = [("dp", mask * 4) for mask in ring]
-    return x_masks + z_masks if first == "x" else z_masks + x_masks
-
-
-def relative_blocks():
-    shards, quarters = [], []
-    for core in range(2):
-        for quarter, (first, order) in enumerate(QUARTERS):
-            for outer in order:
-                for inner in order:
-                    for high in range(2):
-                        x, z = (outer, inner) if first == "x" else (inner, outer)
-                        shards.append(z * 16 + x * 4 + high * 2 + core)
-                        quarters.append(quarter)
-    return np.asarray(shards, np.int32), np.asarray(quarters, np.int32)
-
-
-def relative_rows(shard, rows):
-    shards, quarters = relative_blocks()
-    piece = rows // 256
-    inner = np.arange(piece, dtype=np.int32)
-    fixed = quarters[:, None] * piece + inner[None, :]
-    return (((jnp.asarray(shards) ^ shard)[:, None] * (4 * piece)) + fixed).reshape(-1)
-
-
-def selector(shard, rows):
-    source = relative_rows(shard, rows)
+def core_selector(core, rows):
+    piece = rows // 64
+    target = jnp.arange(rows // 2, dtype=jnp.int32)
+    source = (target // piece) * (2 * piece) + core * piece + target % piece
     return (source[:, None] == jnp.arange(rows, dtype=jnp.int32)[None, :]).astype(jnp.bfloat16)
-
-
-def reduce_rows(value):
-    rows = value.shape[0] // 4
-    kept = []
-    for quarter in range(4):
-        piece = value[quarter * rows : (quarter + 1) * rows]
-        for axis, mask in quarter_masks(quarter):
-            half = piece.shape[0] // 2
-            other = partner_of(piece[half:], axis, mask)
-            piece = (piece[:half].astype(jnp.float32) + other.astype(jnp.float32)).astype(
-                jnp.bfloat16
-            )
-        kept.append(piece)
-    half = kept[0].shape[0] // 2
-    other = partner_of(jnp.concatenate([piece[half:] for piece in kept], axis=0), "seq", 2)
-    mine = jnp.concatenate([piece[:half] for piece in kept], axis=0)
-    return mine.astype(jnp.float32) + other.astype(jnp.float32)
 
 
 def swap_core(value):
@@ -137,7 +90,247 @@
 def pair_product(kept, swapped, grad, grad_swapped):
     left = jnp.concatenate([kept, swapped], axis=1)
     right = jnp.concatenate([grad, grad_swapped], axis=0)
-    return low(project(left, right))
+    return by_dp(low(project(left, right)))
+
+
+def by_dp(value):
+    return value.reshape(16, value.shape[0] // 16, value.shape[1])
+
+
+MESH = pl.DeviceIdType.MESH
+NEAR, WRAP = (0, 3, 1, 2), (0, 1, 3, 2)
+QUARTERS = (("x", NEAR), ("x", WRAP), ("z", NEAR), ("z", WRAP))
+
+
+def flip(value, mask):
+    if mask == 1:
+        return value + 1 - 2 * lax.rem(value, 2)
+    if mask == 2:
+        return lax.rem(value + 2, 4)
+    if mask == 3:
+        return 3 - value
+    return value
+
+
+def block_place(quarter, outer, inner, x, z):
+    first, order = QUARTERS[quarter]
+    if first == "x":
+        return flip(z, order[inner]) * 4 + flip(x, order[outer])
+    return flip(z, order[outer]) * 4 + flip(x, order[inner])
+
+
+def stage_partner(quarter, stage, x, z, seq):
+    if stage == 4:
+        return {"seq": lax.rem(seq + 2, 4)}
+    first, order = QUARTERS[quarter]
+    mask = order[2] if stage % 2 == 0 else order[1]
+    if (first == "x") == (stage < 2):
+        return {"dp": z * 4 + flip(x, mask)}
+    return {"dp": flip(z, mask) * 4 + x}
+
+
+def remote(source, target, send, recv, device):
+    return pltpu.make_async_remote_copy(
+        src_ref=source,
+        dst_ref=target,
+        send_sem=send,
+        recv_sem=recv,
+        device_id=device,
+        device_id_type=MESH,
+    )
+
+
+def enter(devices):
+    barrier = pltpu.get_barrier_semaphore()
+    for device in devices:
+        pl.semaphore_signal(barrier, inc=1, device_id=device, device_id_type=MESH)
+    pl.semaphore_wait(barrier, len(devices))
+
+
+def add_blocks(count, total, other):
+    def one(index, carry):
+        total[index] = (
+            total[index].astype(jnp.float32) + other[index].astype(jnp.float32)
+        ).astype(jnp.bfloat16)
+        return carry
+
+    lax.fori_loop(0, count, one, 0)
+
+
+def reduce_kernel(shapes, with_vectors, *refs):
+    count = len(shapes)
+    refs = list(refs)
+    take = lambda n: [refs.pop(0) for _ in range(n)]
+    sources = take(count)
+    vector = take(1)[0] if with_vectors else None
+    results = take(count)
+    vector_result = take(1)[0] if with_vectors else None
+    totals = take(count)
+    landings = [take(5) for _ in range(count)]
+    local_sem, send_sem, recv_sem = take(3)
+    if with_vectors:
+        vector_total, vector_landing, vector_send, vector_recv = take(4)
+
+    dp, seq = lax.axis_index("dp"), lax.axis_index("seq")
+    z, x = lax.div(dp, 4), lax.rem(dp, 4)
+    y = lax.div(seq, 2)
+    partners = [stage_partner(0, 0, x, z, seq), stage_partner(0, 1, x, z, seq)]
+    partners += [stage_partner(2, 0, x, z, seq), stage_partner(2, 1, x, z, seq)]
+    partners += [stage_partner(0, 4, x, z, seq)]
+    core = {"seq": flip(seq, 1)}
+    if with_vectors:
+        partners += [core]
+    enter(partners)
+
+    vector_stages = [(core, 0, 0, 16)]
+    if with_vectors:
+        vector_stages += [(stage_partner(0, 0, x, z, seq), 8, 16, 8)]
+        vector_stages += [(stage_partner(0, 1, x, z, seq), 4, 24, 4)]
+        vector_stages += [(stage_partner(0, 2, x, z, seq), 2, 28, 2)]
+        vector_stages += [(stage_partner(0, 3, x, z, seq), 1, 30, 1)]
+        vector_stages += [(stage_partner(0, 4, x, z, seq), 0, 31, 1)]
+
+    def vector_copy(step):
+        device, first, landing, size = vector_stages[step]
+        return remote(
+            vector_total.at[pl.ds(first, size)],
+            vector_landing.at[pl.ds(landing, size)],
+            vector_send.at[step],
+            vector_recv.at[step],
+            device,
+        )
+
+    def vector_finish(step):
+        _, _, landing, size = vector_stages[step]
+        copy = vector_copy(step)
+        copy.wait()
+        vector_total[pl.ds(0, size)] += vector_landing[pl.ds(landing, size)]
+
+    if with_vectors:
+        for index in range(16):
+            outer, inner = index // 4, index % 4
+            vector_total[index] = vector[block_place(0, outer, inner, x, z)]
+        vector_copy(0).start()
+
+    def first_blocks(job, quarter):
+        rows, width = shapes[job]
+        columns = pl.ds(quarter * (width // 4), width // 4)
+        for index in range(8):
+            outer, inner = index // 4, index % 4
+            there = block_place(quarter, outer + 2, inner, x, z)
+            here = block_place(quarter, outer, inner, x, z)
+            remote(
+                sources[job].at[there, :, columns],
+                landings[job][0].at[quarter, index],
+                send_sem.at[job, quarter, 0],
+                recv_sem.at[job, quarter, 0],
+                stage_partner(quarter, 0, x, z, seq),
+            ).start()
+            pltpu.make_async_copy(
+                sources[job].at[here, :, columns],
+                totals[job].at[quarter, index],
+                local_sem.at[job, quarter],
+            ).start()
+
+    def stage_copy(job, quarter, stage):
+        rows, width = shapes[job]
+        if stage == 0:
+            source = landings[job][0].at[quarter]
+            target = landings[job][0].at[quarter]
+        elif stage < 4:
+            size = 8 >> stage
+            source = totals[job].at[quarter, pl.ds(size, size)]
+            target = landings[job][stage].at[quarter]
+        else:
+            away = pl.multiple_of((1 - y) * rows, 16)
+            source = totals[job].at[quarter, 0, pl.ds(away, rows)]
+            target = landings[job][4].at[quarter]
+        return remote(
+            source,
+            target,
+            send_sem.at[job, quarter, stage],
+            recv_sem.at[job, quarter, stage],
+            stage_partner(quarter, stage, x, z, seq),
+        )
+
+    def finish(job, quarter, stage):
+        rows, width = shapes[job]
+        stage_copy(job, quarter, stage).wait_recv()
+        if stage == 0:
+            pltpu.make_async_copy(
+                totals[job].at[quarter], totals[job].at[quarter], local_sem.at[job, quarter]
+            ).wait()
+        if stage < 4:
+            add_blocks(8 >> stage, totals[job].at[quarter], landings[job][stage].at[quarter])
+            stage_copy(job, quarter, stage + 1).start()
+        else:
+            mine = pl.multiple_of(y * rows, 16)
+            columns = pl.ds(quarter * (width // 4), width // 4)
+            results[job][:, columns] = totals[job][quarter, 0, pl.ds(mine, rows)].astype(
+                jnp.float32
+            ) + landings[job][4][quarter].astype(jnp.float32)
+
+    for job in range(count):
+        for quarter in range(4):
+            first_blocks(job, quarter)
+    for stage in range(5):
+        for job in range(count):
+            for quarter in range(4):
+                finish(job, quarter, stage)
+        if with_vectors:
+            vector_finish(stage)
+            vector_copy(stage + 1).start()
+    if with_vectors:
+        vector_finish(5)
+        vector_result[...] = vector_total[0]
+    for job in range(count):
+        for quarter in range(4):
+            for stage in range(5):
+                stage_copy(job, quarter, stage).wait_send()
+
+
+def reduce_shares(shares, vectors, collective_id):
+    shapes = [(share.shape[1] // 2, share.shape[2]) for share in shares]
+    count = len(shares)
+    scratch = [
+        pltpu.VMEM((4, 8, 2 * rows, width // 4), jnp.bfloat16) for rows, width in shapes
+    ]
+    for rows, width in shapes:
+        for blocks in (8, 4, 2, 1):
+            scratch.append(pltpu.VMEM((4, blocks, 2 * rows, width // 4), jnp.bfloat16))
+        scratch.append(pltpu.VMEM((4, rows, width // 4), jnp.bfloat16))
+    scratch += [
+        pltpu.SemaphoreType.DMA((count, 4)),
+        pltpu.SemaphoreType.DMA((count, 4, 5)),
+        pltpu.SemaphoreType.DMA((count, 4, 5)),
+    ]
+    in_specs = [pl.BlockSpec(memory_space=pl.ANY)] * count
+    out_specs = [pl.BlockSpec(memory_space=pltpu.VMEM)] * count
+    out_shape = [jax.ShapeDtypeStruct(shape, jnp.float32) for shape in shapes]
+    operands = list(shares)
+    if vectors is not None:
+        in_specs.append(pl.BlockSpec(memory_space=pltpu.VMEM))
+        out_specs.append(pl.BlockSpec(memory_space=pltpu.VMEM))
+        out_shape.append(jax.ShapeDtypeStruct(vectors.shape[1:], jnp.float32))
+        operands.append(vectors)
+        scratch += [
+            pltpu.VMEM(vectors.shape, jnp.float32),
+            pltpu.VMEM((32,) + vectors.shape[1:], jnp.float32),
+            pltpu.SemaphoreType.DMA((6,)),
+            pltpu.SemaphoreType.DMA((6,)),
+        ]
+    return pl.pallas_call(
+        functools.partial(reduce_kernel, shapes, vectors is not None),
+        out_shape=out_shape,
+        in_specs=in_specs,
+        out_specs=out_specs,
+        scratch_shapes=scratch,
+        compiler_params=pltpu.CompilerParams(
+            collective_id=collective_id,
+            has_side_effects=True,
+            vmem_limit_bytes=56 * 2**20,
+        ),
+    )(*operands)
 
 
 def on_device(
@@ -164,7 +357,6 @@
     head_dim = model_width // head_count
     score_scale = head_dim ** (-0.5)
     seq = lax.axis_index("seq")
-    shard = lax.axis_index("dp") * 4 + seq
     own_rows = states.reshape(rows_here, model_width)
     stored = mirror.reshape(rows_here, model_width)
     partner = from_partner(stored, "section", 0)
@@ -185,8 +377,9 @@
     bias_two = norm2_bias.astype(jnp.float32)
     w_first = w_skip[:model_width]
     w_second = w_skip[model_width:]
-    select = selector(shard, model_width)
-    half = model_width // 2
+    core = seq % 2
+    select_mine = core_selector(core, model_width)
+    select_other = core_selector(1 - core, model_width)
 
     grad_rows = (
         out_grad.reshape(rows_here, model_width).astype(jnp.float32)
@@ -236,17 +429,15 @@
     grad_upward_other = swap_core(grad_upward)
 
     hidden_width = act_low.shape[1]
-    piece = hidden_width // 256
-    shards, quarters = relative_blocks()
-    act_rows = act_low.T.reshape(256, piece, rows_here)
-    act_rows = act_rows[(jnp.asarray(shards) ^ shard) * 4 + jnp.asarray(quarters)]
-    act_rows = act_rows.reshape(2, hidden_width // 2, rows_here)
-    act_other = swap_core(act_rows[1])
-    down_sum = reduce_rows(pair_product(act_rows[0], act_other, grad_low, grad_low_other))
-
-    two_rows = low(back_product(select, normed_two))
-    two_other = swap_core(two_rows[half:])
-    up_sum = reduce_rows(pair_product(two_rows[:half], two_other, grad_upward, grad_upward_other))
+    act_rows = act_low.T.reshape(32, 2, hidden_width // 64, rows_here)
+    act_mine = lax.dynamic_index_in_dim(act_rows, core, 1, False).reshape(-1, rows_here)
+    act_send = lax.dynamic_index_in_dim(act_rows, 1 - core, 1, False).reshape(-1, rows_here)
+    act_other = swap_core(act_send)
+    down_share = pair_product(act_mine, act_other, grad_low, grad_low_other)
+
+    two_mine = low(back_product(select_mine, normed_two))
+    two_other = swap_core(low(back_product(select_other, normed_two)))
+    up_share = pair_product(two_mine, two_other, grad_upward, grad_upward_other)
 
     grad_normed_two = back_product(grad_upward, w_up)
     grad_resid_norm, grad_gain_two, grad_bias_two = norm_backward(
@@ -255,9 +446,10 @@
     grad_residual = grad_rows + grad_resid_norm
     grad_attn = low(grad_residual)
     grad_attn_other = swap_core(grad_attn)
-    mixed_cut = low(back_product(select, mixed_rows))
-    mixed_other = swap_core(mixed_cut[half:])
-    out_sum = reduce_rows(pair_product(mixed_cut[:half], mixed_other, grad_attn, grad_attn_other))
+    mixed_mine = low(back_product(select_mine, mixed_rows))
+    mixed_other = swap_core(low(back_product(select_other, mixed_rows)))
+    out_share = pair_product(mixed_mine, mixed_other, grad_attn, grad_attn_other)
+    up_sum, down_sum, out_sum = reduce_shares([up_share, down_share, out_share], None, 1)
 
     grad_mixed = low(back_product(grad_attn, w_out))
     grad_mixed3 = grad_mixed.reshape(rows_here, head_count, head_dim)
@@ -306,7 +498,7 @@
         + normed_part[:rows_here]
         + normed_far.astype(jnp.float32)
     )
-    one_rows = low(back_product(select[:half], normed_all))
+    one_rows = low(back_product(select_mine, normed_all))
     query_share = low(
         project(one_rows[:, : 2 * rows_here], jnp.concatenate([grad_query, grad_query_other], axis=0))
     )
@@ -315,8 +507,6 @@
         axis=0,
     )
     both_share = low(project(one_rows, both_rows))
-    query_sum = reduce_rows(query_share)
-    both_sum = reduce_rows(both_share)
 
     grad_hidden_norm, grad_gain_one, grad_bias_one = norm_backward(
         grad_normed_one, unit_one, inverse_one, gain_one
@@ -326,18 +516,17 @@
     grad_partner = low(back_product(grad_hidden, w_second))
     grad_stored = from_partner(grad_partner, "section", 0)
     grad_own = low(back_product(grad_hidden, w_first))
-    select_joined = selector(shard, 2 * model_width)
     joined = jnp.concatenate([own_rows, partner], axis=1)
-    joined_rows = low(back_product(select_joined, joined))
-    joined_other = swap_core(joined_rows[model_width:])
-    skip_sum = reduce_rows(
-        pair_product(joined_rows[:model_width], joined_other, grad_hidden, grad_hidden_other)
-    )
-
-    sums = jnp.stack([grad_gain_one, grad_bias_one, grad_gain_two, grad_bias_two])
-    for axis, mask in (("seq", 1), ("dp", 1), ("dp", 3), ("dp", 4), ("dp", 12), ("seq", 2)):
-        sums = sums + partner_of(sums, axis, mask)
-    sums = lax.dynamic_slice_in_dim(sums, shard * (model_width // 64), model_width // 64, axis=1)
+    joined_mine = low(back_product(core_selector(core, 2 * model_width), joined))
+    joined_other = swap_core(low(back_product(core_selector(1 - core, 2 * model_width), joined)))
+    skip_share = pair_product(joined_mine, joined_other, grad_hidden, grad_hidden_other)
+    vectors = jnp.stack([grad_gain_one, grad_bias_one, grad_gain_two, grad_bias_two])
+    vectors = vectors.reshape(4, 16, 4, 16).transpose(1, 2, 0, 3).reshape(16, 4, 64)
+    vectors = jnp.pad(vectors, ((0, 0), (0, 4), (0, 64)))
+    query_sum, both_sum, skip_sum, sums = reduce_shares(
+        [by_dp(query_share), by_dp(both_share), skip_share], vectors, 2
+    )
+    sums = lax.dynamic_index_in_dim(sums, seq, 0, False)[:64].reshape(4, 16)
     return (
         output,
         grad_own.reshape(states.shape),

time: 479 us -> 355 us (0.74)
  starting transfers between devices: 139 us -> 14.1 us
  waiting for transfers between devices: 137 us -> 16.3 us
  Pallas kernels: 0 us -> 108 us
  matrix products: 128 us -> 148 us
  other arithmetic: 43.7 us -> 37.5 us
    ppermute x123 -> x15, starting transfers between devices: 137 us -> 10.9 us  [partner_of(): return lax.ppermute(value, axis, pairs)]
    ppermute x123 -> x15, waiting for transfers between devices: 137 us -> 15.8 us  [partner_of(): return lax.ppermute(value, axis, pairs)]
    pallas_call x0 -> x2, Pallas kernels: none -> 108 us  [reduce_shares(): pl.pallas_call(functools.partial(reduce_kernel, shapes, vectors is not No...]
    dot_general x14, matrix products: 54.2 us -> 63.9 us  [project(): return jnp.dot(left, right, preferred_element_type=jnp.float32)]
    dot_general x11 -> x14, matrix products: 39 us -> 47.3 us  [back_product(): lax.dot_general(left, right, (((1,), (1,)), ((), ())), preferred_element_...]
    slice x106 -> x0, local copies, waits for them, and re-layouts: 5.14 us -> none  [the longest x1 1.83 us: on_device(): act_rows[0]]
  transfers between devices with their start and end apart: 125 -> 17, of which waited for: 71 -> 3; matrix products, arithmetic and copies ran while one was open for 39% -> 38% of each run, Pallas kernels for 0% -> 19%
where the time goes in v2:
time: 355 us; the launch traced here: 350 us
  matrix products  148 us (42%)
  Pallas kernels  108 us (30%)
  other arithmetic  37.5 us (11%)
  local copies, waits for them, and re-layouts  25.4 us (7%)
  waiting for transfers between devices  16.3 us (5%)
  starting transfers between devices  14.1 us (4%)
    pallas_call x2, Pallas kernels, reduce_shares(): pl.pallas_call(functools.partial(reduce_kernel, shapes, vectors is not No...  108 us
    dot_general x14, matrix products, project(): return jnp.dot(left, right, preferred_element_type=jnp.float32)  63.9 us
    dot_general x14, matrix products, back_product(): lax.dot_general(left, right, (((1,), (1,)), ((), ())), preferred_element_...  47.3 us
    ppermute x15, waiting for transfers between devices, partner_of(): return lax.ppermute(value, axis, pairs)  15.8 us
    convert_element_type x1, other arithmetic, on_device(): grad_scores = (softmax_again * (grad_softmax - centre)).astype(jnp.bfloat16)  11.9 us
    dot_general x1, matrix products, on_device(): jnp.einsum('qhd,khd->hqk', grad_mixed3, values3, preferred_element_type=j...  11.1 us
    ppermute x15, starting transfers between devices, partner_of(): return lax.ppermute(value, axis, pairs)  10.9 us
    dot_general x1, matrix products, on_device(): jnp.einsum('hqk,qhd->khd', softmax_again.astype(jnp.bfloat16), grad_mixed...  9.35 us
  transfers between devices with their start and end apart: 17, of which 3 were waited for; matrix products, arithmetic and copies ran while one was open for 38% of the time, Pallas kernels for 19%

profile of v2, /device:TPU:0, one launch (start us, length us, event | category | flops | bytes accessed | tf_op | source)
XLA Modules:
  0.0 350.2 jit_solution(2653517334657115069)
XLA Ops:
  26.1 6.6 %collective-permute-done.2 = bf16[256,1024]{1,0:T(8,128)(2,1)} collective-permute-done((bf16[256,1024]{1,0:T(8,128)(2,1)}, bf16[256,1024]{1,0:T(8,128)(2,1)}, u32[]{:S(2)}, u32[]{:S(2)}) %collective-permute-start.2) | collective-permute-done | bytes 524320 | tf_op jit(solution)/shard_map/ppermute | solution.py:72
  33.0 3.9 %fusion.89 = bf16[1024,256]{0,1:T(8,128)(2,1)} fusion(s32[1024]{0:T(1024)S(1)} %fusion.140, bf16[256,1024]{1,0:T(8,128)(2,1)} %collective-permute-done, bf16[256,1024]{1,0:T(8,128)(2,1)} %bitcast.198), kind=kOutput, calls=%fused_computation.125 | convolution fusion | flops 1078198272 | bytes 1576960 | tf_op jit(solution)/shard_map/dot_general | solution.py:33
  37.0 3.9 %fusion.90 = bf16[1024,256]{0,1:T(8,128)(2,1)} fusion(s32[1024]{0:T(1024)S(1)} %fusion.141, bf16[256,1024]{1,0:T(8,128)(2,1)} %collective-permute-done, bf16[256,1024]{1,0:T(8,128)(2,1)S(1)} %bitcast.199), kind=kOutput, calls=%fused_computation.126 | convolution fusion | flops 1078198272 | bytes 1576960 | tf_op jit(solution)/shard_map/dot_general | solution.py:33
  40.9 4.0 %convolution_convert_fusion.3 = bf16[1024,1024]{0,1:T(8,128)(2,1)S(1)} fusion(bf16[1024,1024]{1,0:T(8,128)(2,1)S(1)} %copy-done.46, bf16[256,1024]{1,0:T(8,128)(2,1)S(1)} %collective-permute-done.3, bf16[256,1024]{1,0:T(8,128)(2,1)} %collective-permute-done.2, bf16[256,1024]{1,0:T(8,128)(2,1)} %collective-permute-done.1, ...), kind=kOutput, calls=%fused_computation.102 | convolution fusion | flops 2156920832 | bytes 6291456 | tf_op jit(solution)/shard_map/dot_general | solution.py:23
  44.9 5.2 %fusion.172 = (f32[16,256]{1,0:T(8,128)S(1)}, f32[16,256,1024]{2,1,0:T(8,128)S(1)}) fusion(f32[256,1024]{1,0:T(8,128)S(1)} %copy-done.25, f32[16]{0:T(128)S(1)} %multiply_power_fusion, bf16[256,16,64]{0,2,1:T(8,128)(2,1)S(1)} %bitcast.171, bf16[1024,16,64]{0,2,1:T(8,128)(2,1)S(1)} %bitcast.175, pred[256,1024]{1,0:T(8,128)(4,1)S(1)} %broadcast_compare_fusion), kind=kOutput, calls=%fused_computation.259 | convolution fusion | flops 557838336 | bytes 20725824 | tf_op jit(solution)/shard_map/qhd,khd->hqk/dot_general | solution.py:405
  50.2 4.4 %fusion = f32[16,256]{1,0:T(8,128)S(1)} fusion(f32[16,256,1024]{2,1,0:T(8,128)S(1)} %get-tuple-element.61, f32[16,256]{1,0:T(8,128)S(1)} %get-tuple-element.60), kind=kLoop, calls=%fused_computation.6 | loop fusion | flops 8384512 | bytes 16809984 | tf_op jit(solution)/shard_map/reduce_sum | solution.py:412
  54.6 5.0 %convolution_convert_fusion.4 = bf16[1024,1024]{0,1:T(8,128)(2,1)S(1)} fusion(bf16[1024,1024]{1,0:T(8,128)(2,1)S(1)} %copy-done.44, bf16[256,1024]{1,0:T(8,128)(2,1)S(1)} %collective-permute-done.3, bf16[256,1024]{1,0:T(8,128)(2,1)} %collective-permute-done.2, bf16[256,1024]{1,0:T(8,128)(2,1)} %collective-permute-done.1, ...), kind=kOutput, calls=%fused_computation.103 | convolution fusion | flops 2156920832 | bytes 6291456 | tf_op jit(solution)/shard_map/dot_general | solution.py:23
  59.6 4.3 %fusion.91 = bf16[16,64,256]{2,1,0:T(8,128)(2,1)S(1)} fusion(bf16[1024,16,64]{0,2,1:T(8,128)(2,1)S(1)} %bitcast.173, f32[16,256,1024]{2,1,0:T(8,128)S(1)} %get-tuple-element.61, f32[16,256]{1,0:T(8,128)S(1)} %fusion, f32[16,256]{1,0:T(8,128)S(1)} %get-tuple-element.60), kind=kOutput, calls=%fused_computation.127 | convolution fusion | flops 549715968 | bytes 19431424 | tf_op jit(solution)/shard_map/hqk,khd->qhd/dot_general | solution.py:415
  65.4 14.9 %fusion.11 = (bf16[4096,256]{0,1:T(8,128)(2,1)}, f32[256,4096]{1,0:T(8,128)S(1)}) fusion(bf16[256,1024]{1,0:T(8,128)(2,1)S(1)} %add_convert_fusion.3, bf16[1024,4096]{1,0:T(8,128)(2,1)} %param.27), kind=kOutput, calls=%fused_computation.27 | convolution fusion | flops 2215641088 | bytes 15204352 | tf_op jit(solution)/shard_map/dot_general | solution.py:23
  80.4 15.3 %add_convert_fusion.1 = (bf16[256,4096]{1,0:T(8,128)(2,1)S(1)}, f32[256,4096]{1,0:T(8,128)}) fusion(f32[256,4096]{1,0:T(8,128)S(1)} %get-tuple-element.68, bf16[256,1024]{1,0:T(8,128)(2,1)} %fusion.120, bf16[4096,1024]{1,0:T(8,128)(2,1)S(1)} %bitcast.166), kind=kOutput, calls=%fused_computation.67 | convolution fusion | flops 2222981120 | bytes 19398656 | tf_op jit(solution)/shard_map/dot_general | solution.py:33
  102.6 9.3 %fusion.65 = bf16[16,64,1024]{2,1,0:T(8,128)(2,1)} fusion(bf16[256,16,64]{0,2,1:T(8,128)(2,1)S(1)} %bitcast.167, f32[16,256,1024]{2,1,0:T(8,128)} %copy-done.1, f32[16,256]{1,0:T(8,128)S(1)} %log_add_fusion), kind=kOutput, calls=%fused_computation.100 | convolution fusion | flops 546308096 | bytes 19415040 | tf_op jit(solution)/shard_map/hqk,qhd->khd/dot_general | solution.py:471
  112.0 11.1 %multiply_reduce_fusion = (f32[16,256]{1,0:T(8,128)S(1)}, f32[16,256,1024]{2,1,0:T(8,128)}) fusion(f32[16,256,1024]{2,1,0:T(8,128)} %copy-done.1, f32[16,256]{1,0:T(8,128)S(1)} %log_add_fusion, bf16[256,16,64]{0,2,1:T(8,128)(2,1)S(1)} %bitcast.168, bf16[1024,16,64]{0,2,1:T(8,128)(2,1)S(1)} %bitcast.174), kind=kOutput, calls=%fused_computation.1 | convolution fusion | flops 549449728 | bytes 36208640 | tf_op jit(solution)/shard_map/qhd,khd->hqk/dot_general | solution.py:457
  123.1 11.9 %multiply_convert_fusion = bf16[16,256,1024]{2,1,0:T(8,128)(2,1)S(1)} fusion(f32[16,256,1024]{2,1,0:T(8,128)} %get-tuple-element.66, f32[16,256,1024]{2,1,0:T(8,128)} %copy-done.1, f32[16,256]{1,0:T(8,128)S(1)} %get-tuple-element.65, f32[16,256]{1,0:T(8,128)S(1)} %log_add_fusion), kind=kLoop, calls=%fused_computation | loop fusion | flops 16777216 | bytes 41975808 | tf_op jit(solution)/shard_map/convert_element_type | solution.py:461
  142.9 4.2 %copy.41 = bf16[4096,256]{1,0:T(8,128)(2,1)} copy(bf16[4096,256]{0,1:T(8,128)(2,1)} %get-tuple-element.67) | data formatting | bytes 4194304 | tf_op jit(solution)/shard_map/convert_element_type | solution.py:87
  150.8 8.0 %fusion.92 = bf16[1,1,256,1024]{3,2,1,0:T(8,128)(2,1)} fusion(f32[256,1024]{1,0:T(8,128)S(1)} %copy-done.6, bf16[4096,1024]{1,0:T(8,128)(2,1)} %param.28, f32[256,4096]{1,0:T(8,128)} %get-tuple-element.40, f32[256,4096]{1,0:T(8,128)S(1)} %copy-done.12), kind=kOutput, calls=%fused_computation.128 | convolution fusion | flops 2151153664 | bytes 18350080 | tf_op jit(solution)/shard_map/dot_general | solution.py:23
  165.0 3.7 %fusion.76 = bf16[512,1024]{1,0:T(8,128)(2,1)} fusion(s32[512]{0:T(512)S(1)} %copy-done.42, bf16[256,1024]{1,0:T(8,128)(2,1)S(1)} %copy-done.52, bf16[256,1024]{1,0:T(8,128)(2,1)} %collective-permute-done.2, bf16[256,1024]{1,0:T(8,128)(2,1)} %collective-permute-done.1, bf16[256,1024]{1,0:T(8,128)(2,1)} %add_convert_fusion.4), kind=kOutput, calls=%fused_computation.112 | convolution fusion | flops 1083179008 | bytes 3147776 | tf_op jit(solution)/shard_map/dot_general | solution.py:33
  180.5 6.0 %convolution_convert_fusion.1 = bf16[2048,1024]{1,0:T(8,128)(2,1)} fusion(bf16[2048,256]{1,0:T(8,128)(2,1)} %collective-permute-done.13, bf16[2048,256]{1,0:T(8,128)(2,1)S(1)} %bitcast.180, bf16[256,1024]{1,0:T(8,128)(2,1)} %collective-permute-done.14, bf16[256,1024]{1,0:T(8,128)(2,1)} %fusion.120), kind=kOutput, calls=%fused_computation.83 | convolution fusion | flops 2155872256 | bytes 7340032 | tf_op jit(solution)/shard_map/dot_general | solution.py:23
  190.2 4.0 %fusion.14 = f32[512,1024]{1,0:T(8,128)S(1)} fusion(bf16[512,2048]{0,1:T(8,128)(2,1)} %add_convert_fusion, bf16[1024,1024]{1,0:T(8,128)(2,1)S(1)} %copy-done.45, bf16[1024,1024]{1,0:T(8,128)(2,1)S(1)} %copy-done.47), kind=kOutput, calls=%fused_computation.31 | convolution fusion | flops 2155872256 | bytes 8388608 | tf_op jit(solution)/shard_map/dot_general | solution.py:33
  194.9 3.7 %collective-permute-start.5 = (bf16[256,1024]{1,0:T(8,128)(2,1)S(1)}, bf16[256,1024]{1,0:T(8,128)(2,1)S(1)}, u32[]{:S(2)}, u32[]{:S(2)}) collective-permute-start(bf16[256,1024]{1,0:T(8,128)(2,1)S(1)} %slice.156), channel_id=1, source_target_pairs={{0,2},{1,3},{2,0},{3,1},{4,6},{5,7},{6,4},{7,5},{8,10},{9,11},{10,... | collective-permute-start | bytes 1572872 | tf_op jit(solution)/shard_map/ppermute | solution.py:72
  201.6 9.1 %collective-permute-done.5 = bf16[256,1024]{1,0:T(8,128)(2,1)S(1)} collective-permute-done((bf16[256,1024]{1,0:T(8,128)(2,1)S(1)}, bf16[256,1024]{1,0:T(8,128)(2,1)S(1)}, u32[]{:S(2)}, u32[]{:S(2)}) %collective-permute-start.5) | collective-permute-done | bytes 524320 | tf_op jit(solution)/shard_map/ppermute | solution.py:72
  215.0 4.5 %convolution_convert_fusion = bf16[512,4096]{1,0:T(8,128)(2,1)} fusion(bf16[256,4096]{1,0:T(8,128)(2,1)S(1)} %collective-permute-done.12, bf16[256,4096]{1,0:T(8,128)(2,1)S(1)} %copy-done.49, bf16[512,256]{0,1:T(8,128)(2,1)S(1)} %collective-permute-done.11, bf16[512,256]{0,1:T(8,128)(2,1)S(1)} %copy-done.56), kind=kOutput, calls=%fused_computation.17 | convolution fusion | flops 2159017984 | bytes 8912896 | tf_op jit(solution)/shard_map/dot_general | solution.py:23
  219.4 65.1 %shard_map.264 = (f32[16,4096]{1,0:T(8,128)}, f32[64,1024]{1,0:T(8,128)}, f32[16,1024]{1,0:T(8,128)}) custom-call(bf16[16,32,4096]{2,1,0:T(8,128)(2,1)} %bitcast.170, bf16[16,128,1024]{2,1,0:T(8,128)(2,1)} %bitcast.169, bf16[16,32,1024]{2,1,0:T(8,128)(2,1)} %bitcast.179), custom_call_target="tpu_custom_call" | custom-call | tf_op jit(solution)/shard_map/pallas_call | solution.py:322
  288.9 3.9 %convolution_convert_fusion.2 = bf16[1024,1024]{1,0:T(8,128)(2,1)} fusion(bf16[1024,256]{0,1:T(8,128)(2,1)} %collective-permute-done.9, bf16[1024,256]{0,1:T(8,128)(2,1)S(1)} %copy-done.57, bf16[256,1024]{1,0:T(8,128)(2,1)} %collective-permute-done.10, bf16[256,1024]{1,0:T(8,128)(2,1)S(1)} %add_convert_fusion.2), kind=kOutput, calls=%fused_computation.101 | convolution fusion | flops 1078984704 | bytes 4194304 | tf_op jit(solution)/shard_map/dot_general | solution.py:23
  298.9 42.4 %shard_map.263 = (f32[16,1024]{1,0:T(8,128)}, f32[16,2048]{1,0:T(8,128)}, f32[32,1024]{1,0:T(8,128)}, f32[8,128]{1,0:T(8,128)}) custom-call(bf16[16,32,1024]{2,1,0:T(8,128)(2,1)} %bitcast.181, bf16[16,32,2048]{2,1,0:T(8,128)(2,1)} %bitcast.178, bf16[16,64,1024]{2,1,0:T(8,128)(2,1)} %bitcast.177, f32[16,8,128]{2,1,0:T(8,128)} %pad.4.refs_3_), custom_call_target="tpu_custom_call" | custom-call | tf_op jit(solution)/shard_map/pallas_call | solution.py:322
  (238 shorter events, 93.8 us)
Async XLA Ops:
  0.6 63.3 %copy-start = (bf16[1024,1024]{1,0:T(8,128)(2,1)S(1)}, bf16[1024,1024]{1,0:T(8,128)(2,1)}, u32[]{:S(2)}) copy-start(bf16[1024,1024]{1,0:T(8,128)(2,1)} %param.24) | copy-start | bytes 6291460
  0.7 14.0 %collective-permute-start = (bf16[256,1024]{1,0:T(8,128)(2,1)}, bf16[256,1024]{1,0:T(8,128)(2,1)}, u32[]{:S(2)}, u32[]{:S(2)}) collective-permute-start(bf16[256,1024]{1,0:T(8,128)(2,1)} %bitcast.197), channel_id=1, source_target_pairs={{0,64},{64,0},{1,65},{65,1},{2,66},{66,2},{3,67},{67,3},{4,68},{68... | collective-permute-start | bytes 1572872 | tf_op jit(solution)/shard_map/ppermute | solution.py:19
  16.6 47.4 %copy-start.2 = (f32[256,1024]{1,0:T(8,128)}, f32[256,1024]{1,0:T(8,128)S(1)}, u32[]{:S(2)}) copy-start(f32[256,1024]{1,0:T(8,128)S(1)} %get-tuple-element.59) | copy-start | bytes 3145732
  18.0 14.8 %collective-permute-start.2 = (bf16[256,1024]{1,0:T(8,128)(2,1)}, bf16[256,1024]{1,0:T(8,128)(2,1)}, u32[]{:S(2)}, u32[]{:S(2)}) collective-permute-start(bf16[256,1024]{1,0:T(8,128)(2,1)} %add_convert_fusion.4), channel_id=1, source_target_pairs={{0,2},{1,3},{2,0},{3,1},{4,6},{5,7},{6,4},{7,5},{8,10},{9,11},{10,... | collective-permute-start | bytes 1572872 | tf_op jit(solution)/shard_map/ppermute | solution.py:72
  21.4 19.4 %collective-permute-start.1 = (bf16[256,1024]{1,0:T(8,128)(2,1)}, bf16[256,1024]{1,0:T(8,128)(2,1)}, u32[]{:S(2)}, u32[]{:S(2)}) collective-permute-start(bf16[256,1024]{1,0:T(8,128)(2,1)} %add_convert_fusion.4), channel_id=1, source_target_pairs={{0,1},{1,0},{2,3},{3,2},{4,5},{5,4},{6,7},{7,6},{8,9},{9,8},{10,11... | collective-permute-start | bytes 1572872 | tf_op jit(solution)/shard_map/ppermute | solution.py:72
  32.8 8.1 %collective-permute-start.3 = (bf16[256,1024]{1,0:T(8,128)(2,1)}, bf16[256,1024]{1,0:T(8,128)(2,1)S(1)}, u32[]{:S(2)}, u32[]{:S(2)}) collective-permute-start(bf16[256,1024]{1,0:T(8,128)(2,1)} %collective-permute-done.2), channel_id=1, source_target_pairs={{0,1},{1,0},{2,3},{3,2},{4,5},{5,4},{6,7},{7,6},{8,9},{9,8},{10,11... | collective-permute-start | bytes 1572872 | tf_op jit(solution)/shard_map/ppermute | solution.py:72
  64.8 33.6 %copy-start.5 = (f32[256,1024]{1,0:T(8,128)}, f32[256,1024]{1,0:T(8,128)S(1)}, u32[]{:S(2)}) copy-start(f32[256,1024]{1,0:T(8,128)S(1)} %get-tuple-element.63) | copy-start | bytes 3145732
  65.4 30.3 %slice-start.2 = ((s8[8388608]{0:T(1024)(128)(4,1)}), s8[4194304]{0:T(1024)(128)(4,1)S(1)}, s32[]{:S(2)}) async-start(s8[8388608]{0:T(1024)(128)(4,1)} %bitcast.195), calls=%async_computation.2 | async-start | bytes 8388608
  101.8 71.7 %collective-permute-start.16 = (bf16[256,1024]{1,0:T(8,128)(2,1)}, bf16[256,1024]{1,0:T(8,128)(2,1)}, u32[]{:S(2)}, u32[]{:S(2)}) collective-permute-start(bf16[256,1024]{1,0:T(8,128)(2,1)} %get-tuple-element.37), channel_id=1, source_target_pairs={{0,1},{1,0},{2,3},{3,2},{4,5},{5,4},{6,7},{7,6},{8,9},{9,8},{10,11... | collective-permute-start | bytes 1572872 | tf_op jit(solution)/shard_map/ppermute | solution.py:72
  142.8 28.6 %collective-permute-start.15 = (bf16[512,256]{0,1:T(8,128)(2,1)}, bf16[512,256]{0,1:T(8,128)(2,1)}, u32[]{:S(2)}, u32[]{:S(2)}) collective-permute-start(bf16[512,256]{0,1:T(8,128)(2,1)} %fusion.99), channel_id=1, source_target_pairs={{0,1},{1,0},{2,3},{3,2},{4,5},{5,4},{6,7},{7,6},{8,9},{9,8},{10,11... | collective-permute-start | bytes 786440 | tf_op jit(solution)/shard_map/ppermute | solution.py:72
  150.3 30.2 %collective-permute-start.13 = (bf16[2048,256]{1,0:T(8,128)(2,1)}, bf16[2048,256]{1,0:T(8,128)(2,1)}, u32[]{:S(2)}, u32[]{:S(2)}) collective-permute-start(bf16[2048,256]{1,0:T(8,128)(2,1)} %bitcast.38), channel_id=1, source_target_pairs={{0,1},{1,0},{2,3},{3,2},{4,5},{5,4},{6,7},{7,6},{8,9},{9,8},{10,11... | collective-permute-start | bytes 3145736 | tf_op jit(solution)/shard_map/ppermute | solution.py:72
  158.9 18.1 %collective-permute-start.7 = (bf16[256,1024]{0,1:T(8,128)(2,1)}, bf16[256,1024]{0,1:T(8,128)(2,1)}, u32[]{:S(2)}, u32[]{:S(2)}) collective-permute-start(bf16[256,1024]{0,1:T(8,128)(2,1)} %bitcast.17), channel_id=1, source_target_pairs={{0,1},{1,0},{2,3},{3,2},{4,5},{5,4},{6,7},{7,6},{8,9},{9,8},{10,11... | collective-permute-start | bytes 1572872 | tf_op jit(solution)/shard_map/ppermute | solution.py:72
  162.4 24.1 %collective-permute-start.4 = (bf16[512,2048]{0,1:T(8,128)(2,1)}, bf16[512,2048]{0,1:T(8,128)(2,1)}, u32[]{:S(2)}, u32[]{:S(2)}) collective-permute-start(bf16[512,2048]{0,1:T(8,128)(2,1)} %fusion.55), channel_id=1, source_target_pairs={{0,1},{1,0},{2,3},{3,2},{4,5},{5,4},{6,7},{7,6},{8,9},{9,8},{10,11... | collective-permute-start | bytes 6291464 | tf_op jit(solution)/shard_map/ppermute | solution.py:72
  171.4 9.0 %collective-permute-start.14 = (bf16[256,1024]{1,0:T(8,128)(2,1)}, bf16[256,1024]{1,0:T(8,128)(2,1)}, u32[]{:S(2)}, u32[]{:S(2)}) collective-permute-start(bf16[256,1024]{1,0:T(8,128)(2,1)} %fusion.120), channel_id=1, source_target_pairs={{0,1},{1,0},{2,3},{3,2},{4,5},{5,4},{6,7},{7,6},{8,9},{9,8},{10,11... | collective-permute-start | bytes 1572872 | tf_op jit(solution)/shard_map/ppermute | solution.py:72
  173.5 115.3 %collective-permute-start.9 = (bf16[1024,256]{0,1:T(8,128)(2,1)}, bf16[1024,256]{0,1:T(8,128)(2,1)}, u32[]{:S(2)}, u32[]{:S(2)}) collective-permute-start(bf16[1024,256]{0,1:T(8,128)(2,1)} %fusion.89), channel_id=1, source_target_pairs={{0,1},{1,0},{2,3},{3,2},{4,5},{5,4},{6,7},{7,6},{8,9},{9,8},{10,11... | collective-permute-start | bytes 1572872 | tf_op jit(solution)/shard_map/ppermute | solution.py:72
  176.9 38.1 %collective-permute-start.12 = (bf16[256,4096]{1,0:T(8,128)(2,1)S(1)}, bf16[256,4096]{1,0:T(8,128)(2,1)S(1)}, u32[]{:S(2)}, u32[]{:S(2)}) collective-permute-start(bf16[256,4096]{1,0:T(8,128)(2,1)S(1)} %copy-done.49), channel_id=1, source_target_pairs={{0,1},{1,0},{2,3},{3,2},{4,5},{5,4},{6,7},{7,6},{8,9},{9,8},{10,11... | collective-permute-start | bytes 6291464 | tf_op jit(solution)/shard_map/ppermute | solution.py:72
  180.5 33.1 %collective-permute-start.11 = (bf16[512,256]{0,1:T(8,128)(2,1)S(1)}, bf16[512,256]{0,1:T(8,128)(2,1)S(1)}, u32[]{:S(2)}, u32[]{:S(2)}) collective-permute-start(bf16[512,256]{0,1:T(8,128)(2,1)S(1)} %copy-done.53), channel_id=1, source_target_pairs={{0,1},{1,0},{2,3},{3,2},{4,5},{5,4},{6,7},{7,6},{8,9},{9,8},{10,11... | collective-permute-start | bytes 786440 | tf_op jit(solution)/shard_map/ppermute | solution.py:72
  194.3 98.4 %collective-permute-start.8 = (bf16[512,2048]{0,1:T(8,128)(2,1)}, bf16[512,2048]{0,1:T(8,128)(2,1)}, u32[]{:S(2)}, u32[]{:S(2)}) collective-permute-start(bf16[512,2048]{0,1:T(8,128)(2,1)} %add_convert_fusion), channel_id=1, source_target_pairs={{0,1},{1,0},{2,3},{3,2},{4,5},{5,4},{6,7},{7,6},{8,9},{9,8},{10,11... | collective-permute-start | bytes 6291464 | tf_op jit(solution)/shard_map/ppermute | solution.py:72
  194.9 15.9 %collective-permute-start.5 = (bf16[256,1024]{1,0:T(8,128)(2,1)S(1)}, bf16[256,1024]{1,0:T(8,128)(2,1)S(1)}, u32[]{:S(2)}, u32[]{:S(2)}) collective-permute-start(bf16[256,1024]{1,0:T(8,128)(2,1)S(1)} %slice.156), channel_id=1, source_target_pairs={{0,2},{1,3},{2,0},{3,1},{4,6},{5,7},{6,4},{7,5},{8,10},{9,11},{10,... | collective-permute-start | bytes 1572872 | tf_op jit(solution)/shard_map/ppermute | solution.py:72
  211.9 77.0 %collective-permute-start.10 = (bf16[256,1024]{1,0:T(8,128)(2,1)S(1)}, bf16[256,1024]{1,0:T(8,128)(2,1)}, u32[]{:S(2)}, u32[]{:S(2)}) collective-permute-start(bf16[256,1024]{1,0:T(8,128)(2,1)S(1)} %add_convert_fusion.2), channel_id=1, source_target_pairs={{0,1},{1,0},{2,3},{3,2},{4,5},{5,4},{6,7},{7,6},{8,9},{9,8},{10,11... | collective-permute-start | bytes 1572872 | tf_op jit(solution)/shard_map/ppermute | solution.py:72
  213.5 75.3 %collective-permute-start.6 = (bf16[256,1024]{1,0:T(8,128)(2,1)}, bf16[256,1024]{1,0:T(8,128)(2,1)S(1)}, u32[]{:S(2)}, u32[]{:S(2)}) collective-permute-start(bf16[256,1024]{1,0:T(8,128)(2,1)} %fusion.85), channel_id=1, source_target_pairs={{0,64},{64,0},{1,65},{65,1},{2,66},{66,2},{3,67},{67,3},{4,68},{68... | collective-permute-start | bytes 1572872 | tf_op jit(solution)/shard_map/ppermute | solution.py:19
  298.9 49.1 %copy-start.37 = (f32[16,1024]{1,0:T(8,128)S(1)}, f32[16,1024]{1,0:T(8,128)}, u32[]{:S(2)}) copy-start(f32[16,1024]{1,0:T(8,128)} %get-tuple-element.25) | copy-start | bytes 196612
  298.9 49.7 %copy-start.34 = (f32[16,4096]{1,0:T(8,128)S(1)}, f32[16,4096]{1,0:T(8,128)}, u32[]{:S(2)}) copy-start(f32[16,4096]{1,0:T(8,128)} %get-tuple-element.26) | copy-start | bytes 786436
  298.9 50.4 %copy-start.33 = (f32[64,1024]{1,0:T(8,128)S(1)}, f32[64,1024]{1,0:T(8,128)}, u32[]{:S(2)}) copy-start(f32[64,1024]{1,0:T(8,128)} %get-tuple-element.27) | copy-start | bytes 786436
  (55 other events, 402.2 us)

commit v3 on v2

--- a/solution.py
+++ b/solution.py
@@ -8,6 +8,7 @@
 from jax.sharding import PartitionSpec as P
 
 HEADS = 16
+LOG2E = 1.4426950408889634
 
 
 EPS = 1e-05
@@ -33,10 +34,6 @@
     return lax.dot_general(
         left, right, (((1,), (1,)), ((), ())), preferred_element_type=jnp.float32
     )
-
-
-def gelu_exact(values):
-    return jax.nn.gelu(values, approximate=False)
 
 
 def norm_forward(hidden, gain, bias):
@@ -333,6 +330,289 @@
     )(*operands)
 
 
+def attention_forward_kernel(
+    query, keys, values, key_places, key_segments, query_places, query_segments, slopes,
+    shares, mixed, inverses, distance, scores,
+):
+    span = keys.shape[0]
+    chunk = 128
+    here = query.shape[0]
+
+    @pl.when(pl.program_id(0) == 0)
+    def _():
+        gap = jnp.abs(query_places[...] - key_places[...]).astype(jnp.float32)
+        same = query_segments[...] == key_segments[...]
+        distance[...] = jnp.where(same, gap, 1e30)
+
+    lane = lax.broadcasted_iota(jnp.int32, query.shape, 1)
+    zero = jnp.zeros(query.shape, query.dtype)
+    both = jnp.concatenate(
+        [jnp.where(lane < 64, query[...], zero), jnp.where(lane >= 64, query[...], zero)], axis=0
+    )
+    slope = slopes[0]
+
+    def raw(index, top):
+        rows = pl.ds(pl.multiple_of(index * chunk, chunk), chunk)
+        part = back_product(keys[rows], both)
+        gap = distance[rows]
+        part = part - slope * jnp.concatenate([gap, gap], axis=1)
+        scores[rows] = part
+        return jnp.maximum(top, jnp.max(part.reshape(chunk // 8, 8, 2 * here), axis=0))
+
+    top = lax.fori_loop(
+        0, span // chunk, raw, jnp.full((8, 2 * here), -jnp.inf, jnp.float32), unroll=True
+    )
+    top = jnp.max(top, axis=0, keepdims=True)
+
+    def exponent(index, carry):
+        rows = pl.ds(pl.multiple_of(index * chunk, chunk), chunk)
+        shares[0, rows] = jnp.exp2(scores[rows] - top).astype(jnp.bfloat16)
+        return carry
+
+    lax.fori_loop(0, span // chunk, exponent, 0, unroll=True)
+    turned = jnp.concatenate([values[...].T, jnp.ones((16, span), jnp.bfloat16)], axis=0)
+    out = project(turned, shares[0])
+    inverse = 1.0 / out[128:129]
+    inverses[0] = inverse
+    out = out[:128] * inverse
+    out = jnp.concatenate([out[:64, :here], out[64:, here:]], axis=0)
+    mixed[...] = out.T.astype(jnp.bfloat16)
+
+
+def attention_forward(query, keys, values, tables, slopes):
+    here, width = query.shape
+    span = keys.shape[0]
+    pairs = width // 128
+    whole = lambda a: pl.BlockSpec(a.shape, lambda i: (0,) * a.ndim)
+    return pl.pallas_call(
+        attention_forward_kernel,
+        grid=(pairs,),
+        in_specs=[
+            pl.BlockSpec((here, 128), lambda i: (0, i)),
+            pl.BlockSpec((span, 128), lambda i: (0, i)),
+            pl.BlockSpec((span, 128), lambda i: (0, i)),
+            *[whole(table) for table in tables],
+            pl.BlockSpec((1, 1, 2 * here), lambda i: (i, 0, 0)),
+        ],
+        out_specs=[
+            pl.BlockSpec((1, span, 2 * here), lambda i: (i, 0, 0)),
+            pl.BlockSpec((here, 128), lambda i: (0, i)),
+            pl.BlockSpec((1, 1, 2 * here), lambda i: (i, 0, 0)),
+        ],
+        out_shape=[
+            jax.ShapeDtypeStruct((pairs, span, 2 * here), jnp.bfloat16),
+            jax.ShapeDtypeStruct((here, width), jnp.bfloat16),
+            jax.ShapeDtypeStruct((pairs, 1, 2 * here), jnp.float32),
+        ],
+        scratch_shapes=[
+            pltpu.VMEM((span, here), jnp.float32),
+            pltpu.VMEM((span, 2 * here), jnp.float32),
+        ],
+        compiler_params=pltpu.CompilerParams(vmem_limit_bytes=40 * 2**20),
+    )(query, keys, values, *tables, slopes)
+
+
+def attention_backward_kernel(
+    query, keys, values, shares, inverses, grad, mixed, grad_query, grad_keys, grad_values, lows
+):
+    span = keys.shape[0]
+    chunk = 128
+    here = query.shape[0]
+    lane = lax.broadcasted_iota(jnp.int32, query.shape, 1)
+    zero = jnp.zeros(query.shape, query.dtype)
+
+    def stacked(value):
+        return jnp.concatenate(
+            [jnp.where(lane < 64, value, zero), jnp.where(lane >= 64, value, zero)], axis=0
+        )
+
+    queries = stacked(query[...])
+    inverse = inverses[0]
+    turned = grad[...].astype(jnp.float32).T
+    product = turned * mixed[...].astype(jnp.float32).T
+    top = turned[:64] * inverse[:, :here]
+    low_half = turned[64:] * inverse[:, here:]
+    none = jnp.zeros_like(top)
+    grads = jnp.concatenate(
+        [jnp.concatenate([top, none], axis=1), jnp.concatenate([none, low_half], axis=1)], axis=0
+    ).astype(jnp.bfloat16)
+    grads_back = grads.T
+    centre = inverse * jnp.concatenate(
+        [
+            jnp.sum(product[:64], axis=0, keepdims=True),
+            jnp.sum(product[64:], axis=0, keepdims=True),
+        ],
+        axis=1,
+    )
+
+    def part(index, carry):
+        rows = pl.ds(pl.multiple_of(index * chunk, chunk), chunk)
+        grad_share = project(values[rows], grads)
+        share = shares[0, rows]
+        grad_score = (share.astype(jnp.float32) * (grad_share - centre)).astype(jnp.bfloat16)
+        lows[rows] = grad_score
+        grad_keys[rows] = (project(grad_score, queries) * 0.6931471805599453).astype(jnp.bfloat16)
+        grad_values[rows] = project(share, grads_back).astype(jnp.bfloat16)
+        return carry
+
+    lax.fori_loop(0, span // chunk, part, 0, unroll=True)
+    out = rows_product(keys[...], lows[...])
+    out = jnp.concatenate([out[:64, :here], out[64:, here:]], axis=0)
+    grad_query[...] = (out.T * 0.125).astype(jnp.bfloat16)
+
+
+def attention_backward(query, keys, values, shares, inverses, grad, mixed):
+    here, width = query.shape
+    span = keys.shape[0]
+    pairs = width // 128
+    column = lambda rows: pl.BlockSpec((rows, 128), lambda i: (0, i))
+    return pl.pallas_call(
+        attention_backward_kernel,
+        grid=(pairs,),
+        in_specs=[
+            column(here),
+            column(span),
+            column(span),
+            pl.BlockSpec((1, span, 2 * here), lambda i: (i, 0, 0)),
+            pl.BlockSpec((1, 1, 2 * here), lambda i: (i, 0, 0)),
+            column(here),
+            column(here),
+        ],
+        out_specs=[column(here), column(span), column(span)],
+        out_shape=[
+            jax.ShapeDtypeStruct((here, width), jnp.bfloat16),
+            jax.ShapeDtypeStruct((span, width), jnp.bfloat16),
+            jax.ShapeDtypeStruct((span, width), jnp.bfloat16),
+        ],
+        scratch_shapes=[pltpu.VMEM((span, 2 * here), jnp.bfloat16)],
+        compiler_params=pltpu.CompilerParams(vmem_limit_bytes=40 * 2**20),
+    )(query, keys, values, shares, inverses, grad, mixed)
+
+
+def mean_rows(value):
+    return jnp.mean(value, axis=-1, keepdims=True)
+
+
+def ffn_kernel(
+    core, hidden, mixed, grad_low, w_out, gain, bias, w_up, w_down,
+    output, act_kept, act_sent, two_kept, two_sent, grad_up, grad_attn, grad_mixed, gain_sum, bias_sum,
+    residual, unit, inverse, normed, total, grad_normed, turned,
+):
+    step = pl.program_id(0)
+    last = pl.num_programs(0) - 1
+    here = hidden.shape[0]
+    mine = core[0]
+    root = 0.7071067811865476
+
+    @pl.when(step == 0)
+    def _():
+        value = hidden[...] + project(mixed[...], w_out[...])
+        center = value - mean_rows(value)
+        scale = lax.rsqrt(mean_rows(center * center) + EPS)
+        residual[...] = value
+        unit[...] = center * scale
+        inverse[...] = scale
+        two = (unit[...] * gain[...] + bias[...]).astype(jnp.bfloat16)
+        normed[...] = two
+        total[...] = jnp.zeros_like(total)
+        grad_normed[...] = jnp.zeros_like(grad_normed)
+        turned[...] = two.T
+
+        def split(index, carry):
+            place = pl.ds(pl.multiple_of(index * 16, 16), 16)
+            two_kept[place] = turned[pl.ds(pl.multiple_of(index * 32 + mine * 16, 16), 16)]
+            two_sent[place] = turned[pl.ds(pl.multiple_of(index * 32 + (1 - mine) * 16, 16), 16)]
+            return carry
+
+        lax.fori_loop(0, two_kept.shape[0] // 16, split, 0)
+
+    upward = project(normed[...], w_up[...])
+    cdf = 0.5 * (1.0 + lax.erf(upward * root))
+    act = (upward * cdf).astype(jnp.bfloat16)
+    density = jnp.exp(upward * upward * -0.5) * 0.3989422804014327
+    slope = cdf + upward * density
+    back = back_product(grad_low[...], w_down[...])
+    grad = (back * slope).astype(jnp.bfloat16)
+    grad_up[...] = grad
+    total[...] += project(act, w_down[...])
+    grad_normed[...] += back_product(grad, w_up[...])
+    width = act.shape[1]
+    turned[pl.ds(0, width)] = act.T
+    for index in range(width // 128):
+        place = pl.ds(index * 64, 64)
+        act_kept[place] = turned[pl.ds(pl.multiple_of(index * 128 + mine * 64, 64), 64)]
+        act_sent[place] = turned[pl.ds(pl.multiple_of(index * 128 + (1 - mine) * 64, 64), 64)]
+
+    @pl.when(step == last)
+    def _():
+        output[...] = (residual[...] + total[...]).astype(jnp.bfloat16)
+        grads = grad_normed[...]
+        scaled = grads * gain[...]
+        units = unit[...]
+        step_one = scaled - mean_rows(scaled) - units * mean_rows(scaled * units)
+        value = grad_low[...].astype(jnp.float32) + inverse[...] * step_one
+        gain_sum[...] = jnp.sum(grads * units, axis=0, keepdims=True)
+        bias_sum[...] = jnp.sum(grads, axis=0, keepdims=True)
+        grad_attn[...] = value
+        grad_mixed[...] = back_product(value.astype(jnp.bfloat16), w_out[...]).astype(jnp.bfloat16)
+
+
+def feed_forward(core, hidden, mixed, grad_low, w_out, gain, bias, w_up, w_down):
+    here, width = hidden.shape
+    full = w_up.shape[1]
+    block = 512
+    whole = lambda shape: pl.BlockSpec(shape, lambda i: (0,) * len(shape))
+    return pl.pallas_call(
+        ffn_kernel,
+        grid=(full // block,),
+        in_specs=[
+            pl.BlockSpec(memory_space=pltpu.SMEM),
+            whole((here, width)),
+            whole((here, width)),
+            whole((here, width)),
+            whole((width, width)),
+            whole((1, width)),
+            whole((1, width)),
+            pl.BlockSpec((width, block), lambda i: (0, i)),
+            pl.BlockSpec((block, width), lambda i: (i, 0)),
+        ],
+        out_specs=[
+            whole((here, width)),
+            pl.BlockSpec((block // 2, here), lambda i: (i, 0)),
+            pl.BlockSpec((block // 2, here), lambda i: (i, 0)),
+            whole((width // 2, here)),
+            whole((width // 2, here)),
+            pl.BlockSpec((here, block), lambda i: (0, i)),
+            whole((here, width)),
+            whole((here, width)),
+            whole((1, width)),
+            whole((1, width)),
+        ],
+        out_shape=[
+            jax.ShapeDtypeStruct((here, width), jnp.bfloat16),
+            jax.ShapeDtypeStruct((full // 2, here), jnp.bfloat16),
+            jax.ShapeDtypeStruct((full // 2, here), jnp.bfloat16),
+            jax.ShapeDtypeStruct((width // 2, here), jnp.bfloat16),
+            jax.ShapeDtypeStruct((width // 2, here), jnp.bfloat16),
+            jax.ShapeDtypeStruct((here, full), jnp.bfloat16),
+            jax.ShapeDtypeStruct((here, width), jnp.float32),
+            jax.ShapeDtypeStruct((here, width), jnp.bfloat16),
+            jax.ShapeDtypeStruct((1, width), jnp.float32),
+            jax.ShapeDtypeStruct((1, width), jnp.float32),
+        ],
+        scratch_shapes=[
+            pltpu.VMEM((here, width), jnp.float32),
+            pltpu.VMEM((here, width), jnp.float32),
+            pltpu.VMEM((here, 1), jnp.float32),
+            pltpu.VMEM((here, width), jnp.bfloat16),
+            pltpu.VMEM((here, width), jnp.float32),
+            pltpu.VMEM((here, width), jnp.float32),
+            pltpu.VMEM((width, here), jnp.bfloat16),
+        ],
+        compiler_params=pltpu.CompilerParams(vmem_limit_bytes=48 * 2**20),
+    )(core, hidden, mixed, grad_low, w_out, gain, bias, w_up, w_down)
+
+
 def on_device(
     states,
     mirror,
@@ -355,7 +635,7 @@
     model_width = states.shape[3]
     head_count = HEADS
     head_dim = model_width // head_count
-    score_scale = head_dim ** (-0.5)
+    query_scale = head_dim ** (-0.5) * LOG2E
     seq = lax.axis_index("seq")
     own_rows = states.reshape(rows_here, model_width)
     stored = mirror.reshape(rows_here, model_width)
@@ -368,24 +648,20 @@
     key_place = jnp.concatenate([(seq ^ step) * rows_here + local for step in range(4)])
     query_segment, inside = segment_tables(lengths_row, spans_row, query_place)
     key_segment = segment_tables(lengths_row, spans_row, key_place)[0]
-    allowed = query_segment[:, None] == key_segment[None, :]
-    distance = jnp.abs(query_place[:, None] - key_place[None, :]).astype(jnp.float32)
+    tables = (key_place[:, None], key_segment[:, None], query_place[None], query_segment[None])
     slopes = 2.0 ** (-8.0 * (jnp.arange(head_count, dtype=jnp.float32) + 1.0) / head_count)
+    slopes = jnp.repeat(LOG2E * slopes.reshape(-1, 2), rows_here, axis=1)[:, None, :]
     gain_one = norm1_gain.astype(jnp.float32)
     bias_one = norm1_bias.astype(jnp.float32)
-    gain_two = norm2_gain.astype(jnp.float32)
-    bias_two = norm2_bias.astype(jnp.float32)
     w_first = w_skip[:model_width]
     w_second = w_skip[model_width:]
     core = seq % 2
     select_mine = core_selector(core, model_width)
     select_other = core_selector(1 - core, model_width)
 
-    grad_rows = (
-        out_grad.reshape(rows_here, model_width).astype(jnp.float32)
-        * inside.astype(jnp.float32)[:, None]
-    )
-    grad_low = low(grad_rows)
+    grad_low = jnp.where(
+        inside[:, None], out_grad.reshape(rows_here, model_width), jnp.bfloat16(0)
+    )
     grad_low_other = swap_core(grad_low)
     hidden = project(own_rows, w_first) + project(partner, w_second)
     normed_one, unit_one, inverse_one = norm_forward(hidden, gain_one, bias_one)
@@ -394,56 +670,39 @@
     near = swap_core(normed_one)
     far_near = swap_core(far)
     normed_all = jnp.concatenate([normed_one, near, far, far_near], axis=0)
-    query = low(project(normed_one, w_query))
+    query = low(project(normed_one, w_query) * query_scale)
     keys_all = low(project(normed_all, w_key))
     values_all = low(project(normed_all, w_value))
-    query3 = query.reshape(rows_here, head_count, head_dim)
-    keys3 = keys_all.reshape(row_length, head_count, head_dim)
-    values3 = values_all.reshape(row_length, head_count, head_dim)
-
-    def scores_of():
-        raw = jnp.einsum("qhd,khd->hqk", query3, keys3, preferred_element_type=jnp.float32)
-        scores = raw * score_scale - slopes[:, None, None] * distance[None]
-        return jnp.where(allowed[None], scores, -1e30)
-
-    scores = scores_of()
-    row_top = jnp.max(scores, axis=-1, keepdims=True)
-    exponent = jnp.exp(scores - row_top)
-    row_total = jnp.sum(exponent, axis=-1, keepdims=True)
-    log_total = row_top + jnp.log(row_total)
-    softmax_low = (exponent / row_total).astype(jnp.bfloat16)
-    mixed_rows = jnp.einsum(
-        "hqk,khd->qhd", softmax_low, values3, preferred_element_type=jnp.float32
-    )
-    mixed_rows = low(mixed_rows.reshape(rows_here, model_width))
-    residual = hidden + project(mixed_rows, w_out)
-    normed_two, unit_two, inverse_two = norm_forward(residual, gain_two, bias_two)
-    normed_two = low(normed_two)
-    upward = project(normed_two, w_up)
-    activated, gelu_pull = jax.vjp(gelu_exact, upward)
-    act_low = low(activated)
-    result = residual + project(act_low, w_down)
-    output = low(result).reshape(states.shape)
-    grad_act = back_product(grad_low, w_down)
-    grad_upward = low(gelu_pull(grad_act)[0])
+    shares, mixed_rows, inverses = attention_forward(query, keys_all, values_all, tables, slopes)
+    (
+        output,
+        act_mine,
+        act_send,
+        two_mine,
+        two_send,
+        grad_upward,
+        grad_residual,
+        grad_mixed,
+        grad_gain_two,
+        grad_bias_two,
+    ) = feed_forward(
+        core.reshape(1),
+        hidden,
+        mixed_rows,
+        grad_low,
+        w_out,
+        norm2_gain.astype(jnp.float32)[None],
+        norm2_bias.astype(jnp.float32)[None],
+        w_up,
+        w_down,
+    )
+    output = output.reshape(states.shape)
     grad_upward_other = swap_core(grad_upward)
 
-    hidden_width = act_low.shape[1]
-    act_rows = act_low.T.reshape(32, 2, hidden_width // 64, rows_here)
-    act_mine = lax.dynamic_index_in_dim(act_rows, core, 1, False).reshape(-1, rows_here)
-    act_send = lax.dynamic_index_in_dim(act_rows, 1 - core, 1, False).reshape(-1, rows_here)
     act_other = swap_core(act_send)
     down_share = pair_product(act_mine, act_other, grad_low, grad_low_other)
-
-    two_mine = low(back_product(select_mine, normed_two))
-    two_other = swap_core(low(back_product(select_other, normed_two)))
+    two_other = swap_core(two_send)
     up_share = pair_product(two_mine, two_other, grad_upward, grad_upward_other)
-
-    grad_normed_two = back_product(grad_upward, w_up)
-    grad_resid_norm, grad_gain_two, grad_bias_two = norm_backward(
-        grad_normed_two, unit_two, inverse_two, gain_two
-    )
-    grad_residual = grad_rows + grad_resid_norm
     grad_attn = low(grad_residual)
     grad_attn_other = swap_core(grad_attn)
     mixed_mine = low(back_product(select_mine, mixed_rows))
@@ -451,38 +710,10 @@
     out_share = pair_product(mixed_mine, mixed_other, grad_attn, grad_attn_other)
     up_sum, down_sum, out_sum = reduce_shares([up_share, down_share, out_share], None, 1)
 
-    grad_mixed = low(back_product(grad_attn, w_out))
-    grad_mixed3 = grad_mixed.reshape(rows_here, head_count, head_dim)
-    softmax_again = jnp.exp(scores_of() - log_total)
-    grad_softmax = jnp.einsum(
-        "qhd,khd->hqk", grad_mixed3, values3, preferred_element_type=jnp.float32
-    )
-    centre = jnp.sum(softmax_again * grad_softmax, axis=-1, keepdims=True)
-    grad_scores = (softmax_again * (grad_softmax - centre)).astype(jnp.bfloat16)
-    grad_query = (
-        jnp.einsum("hqk,khd->qhd", grad_scores, keys3, preferred_element_type=jnp.float32)
-        * score_scale
-    )
-    grad_query = low(grad_query.reshape(rows_here, model_width))
-    key_part = (
-        jnp.einsum("hqk,qhd->khd", grad_scores, query3, preferred_element_type=jnp.float32)
-        * score_scale
-    )
-    value_part = jnp.einsum(
-        "hqk,qhd->khd",
-        softmax_again.astype(jnp.bfloat16),
-        grad_mixed3,
-        preferred_element_type=jnp.float32,
-    )
-    both_part = low(
-        jnp.concatenate(
-            [
-                key_part.reshape(row_length, model_width),
-                value_part.reshape(row_length, model_width),
-            ],
-            axis=1,
-        )
-    ).reshape(4, rows_here, 2 * model_width)
+    grad_query, key_part, value_part = attention_backward(
+        query, keys_all, values_all, shares, inverses, grad_mixed, mixed_rows
+    )
+    both_part = jnp.concatenate([key_part, value_part], axis=1).reshape(4, rows_here, -1)
     both_other = swap_core(jnp.concatenate([both_part[1], both_part[3]], axis=0))
     both_mine = low(
         jnp.concatenate([both_part[0], both_part[2]], axis=0).astype(jnp.float32)
@@ -520,7 +751,9 @@
     joined_mine = low(back_product(core_selector(core, 2 * model_width), joined))
     joined_other = swap_core(low(back_product(core_selector(1 - core, 2 * model_width), joined)))
     skip_share = pair_product(joined_mine, joined_other, grad_hidden, grad_hidden_other)
-    vectors = jnp.stack([grad_gain_one, grad_bias_one, grad_gain_two, grad_bias_two])
+    vectors = jnp.stack(
+        [grad_gain_one, grad_bias_one, grad_gain_two[0], grad_bias_two[0]]
+    )
     vectors = vectors.reshape(4, 16, 4, 16).transpose(1, 2, 0, 3).reshape(16, 4, 64)
     vectors = jnp.pad(vectors, ((0, 0), (0, 4), (0, 64)))
     query_sum, both_sum, skip_sum, sums = reduce_shares(

time: 355 us -> 292 us (0.82)
  matrix products: 148 us -> 61.3 us
  Pallas kernels: 108 us -> 158 us
  other arithmetic: 37.5 us -> 12.6 us
  local copies, waits for them, and re-layouts: 25.4 us -> 20.6 us
    pallas_call x0 -> x3, Pallas kernels: none -> 51.1 us  [the longest x1 21.1 us: attention_backward(): pl.pallas_call(attention_backward_kernel, grid=(pairs,), in_specs=[column...]
    dot_general x6 -> x0, matrix products: 36.5 us -> none  [the longest x1 11.1 us: on_device(): jnp.einsum('qhd,khd->hqk', grad_mixed3, values3, preferred_element_type=j...]
    dot_general x14 -> x11, matrix products: 63.9 us -> 38.8 us  [project(): return jnp.dot(left, right, preferred_element_type=jnp.float32)]
    dot_general x14 -> x9, matrix products: 47.3 us -> 22.5 us  [back_product(): lax.dot_general(left, right, (((1,), (1,)), ((), ())), preferred_element_...]
    convert_element_type x5 -> x0, other arithmetic: 14.5 us -> none  [the longest x1 11.9 us: on_device(): grad_scores = (softmax_again * (grad_softmax - centre)).astype(jnp.bfloat16)]
    convert_element_type x3 -> x0, local copies, waits for them, and re-layouts: 6.41 us -> none  [low(): return value.astype(jnp.bfloat16)]
    convert_element_type x6 -> x3, other arithmetic: 9.12 us -> 4.19 us  [low(): return value.astype(jnp.bfloat16)]
    reduce_sum x1 -> x0, other arithmetic: 4.37 us -> none  [on_device(): row_total = jnp.sum(exponent, axis=-1, keepdims=True)]
  transfers between devices with their start and end apart: 17 -> 17, of which waited for: 3 -> 4; matrix products, arithmetic and copies ran while one was open for 38% -> 27% of each run, Pallas kernels for 19% -> 40%
where the time goes in v3:
time: 292 us; the launch traced here: 288 us
  Pallas kernels  158 us (54%)
  matrix products  61.3 us (21%)
  local copies, waits for them, and re-layouts  20.6 us (7%)
  waiting for transfers between devices  19.8 us (7%)
  starting transfers between devices  14 us (5%)
  other arithmetic  12.6 us (4%)
    pallas_call x2, Pallas kernels, reduce_shares(): pl.pallas_call(functools.partial(reduce_kernel, shapes, vectors is not No...  107 us
    dot_general x11, matrix products, project(): return jnp.dot(left, right, preferred_element_type=jnp.float32)  38.8 us
    dot_general x9, matrix products, back_product(): lax.dot_general(left, right, (((1,), (1,)), ((), ())), preferred_element_...  22.5 us
    pallas_call x1, Pallas kernels, attention_backward(): pl.pallas_call(attention_backward_kernel, grid=(pairs,), in_specs=[column...  21.1 us
    pallas_call x1, Pallas kernels, feed_forward(): pl.pallas_call(ffn_kernel, grid=(full // block,), in_specs=[pl.BlockSpec(...  18.2 us
    ppermute x15, waiting for transfers between devices, partner_of(): return lax.ppermute(value, axis, pairs)  16.6 us
    pallas_call x1, Pallas kernels, attention_forward(): pl.pallas_call(attention_forward_kernel, grid=(pairs,), in_specs=[pl.Bloc...  11.8 us
    ppermute x15, starting transfers between devices, partner_of(): return lax.ppermute(value, axis, pairs)  10.4 us
  transfers between devices with their start and end apart: 17, of which 4 were waited for; matrix products, arithmetic and copies ran while one was open for 27% of the time, Pallas kernels for 40%

profile of v3, /device:TPU:0, one launch (start us, length us, event | category | flops | bytes accessed | tf_op | source)
XLA Modules:
  0.0 288.0 jit_solution(12576773125992306856)
XLA Ops:
  11.3 3.2 %collective-permute-done = bf16[256,1024]{1,0:T(8,128)(2,1)S(1)} collective-permute-done((bf16[256,1024]{1,0:T(8,128)(2,1)}, bf16[256,1024]{1,0:T(8,128)(2,1)S(1)}, u32[]{:S(2)}, u32[]{:S(2)}) %collective-permute-start) | collective-permute-done | bytes 524320 | tf_op jit(solution)/shard_map/ppermute | solution.py:20
  17.7 3.4 %collective-permute-start.2 = (bf16[256,1024]{1,0:T(8,128)(2,1)S(1)}, bf16[256,1024]{1,0:T(8,128)(2,1)}, u32[]{:S(2)}, u32[]{:S(2)}) collective-permute-start(bf16[256,1024]{1,0:T(8,128)(2,1)S(1)} %add_convert_fusion.2), channel_id=1, source_target_pairs={{0,2},{1,3},{2,0},{3,1},{4,6},{5,7},{6,4},{7,5},{8,10},{9,11},{10,... | collective-permute-start | bytes 1572872 | tf_op jit(solution)/shard_map/ppermute | solution.py:69
  21.5 10.8 %collective-permute-done.2 = bf16[256,1024]{1,0:T(8,128)(2,1)} collective-permute-done((bf16[256,1024]{1,0:T(8,128)(2,1)S(1)}, bf16[256,1024]{1,0:T(8,128)(2,1)}, u32[]{:S(2)}, u32[]{:S(2)}) %collective-permute-start.2) | collective-permute-done | bytes 524320 | tf_op jit(solution)/shard_map/ppermute | solution.py:69
  34.9 3.6 %convolution_convert_fusion.3.values = bf16[1024,1024]{1,0:T(8,128)(2,1)S(1)} fusion(bf16[1024,1024]{1,0:T(8,128)(2,1)S(1)} %copy-done.28, bf16[256,1024]{1,0:T(8,128)(2,1)S(1)} %collective-permute-done.3, bf16[256,1024]{1,0:T(8,128)(2,1)} %collective-permute-done.2, bf16[256,1024]{1,0:T(8,128)(2,1)S(1)} %collective-permute-done.1, ...), kind=kOutput, calls=%fused_computation.36 | convolution fusion | flops 2156920832 | bytes 6291456 | tf_op jit(solution)/shard_map/dot_general | solution.py:24
  38.6 3.5 %convolution_convert_fusion.4.keys = bf16[1024,1024]{1,0:T(8,128)(2,1)S(1)} fusion(bf16[1024,1024]{1,0:T(8,128)(2,1)S(1)} %copy-done.26, bf16[256,1024]{1,0:T(8,128)(2,1)S(1)} %collective-permute-done.3, bf16[256,1024]{1,0:T(8,128)(2,1)} %collective-permute-done.2, bf16[256,1024]{1,0:T(8,128)(2,1)S(1)} %collective-permute-done.1, ...), kind=kOutput, calls=%fused_computation.37 | convolution fusion | flops 2156920832 | bytes 6291456 | tf_op jit(solution)/shard_map/dot_general | solution.py:24
  42.1 11.8 %shard_map.263 = (bf16[8,1024,512]{2,1,0:T(8,128)(2,1)}, bf16[256,1024]{1,0:T(8,128)(2,1)S(1)}, f32[8,1,512]{2,1,0:T(1,128)S(1)}) custom-call(bf16[256,1024]{1,0:T(8,128)(2,1)S(1)} %fusion.46.query, bf16[1024,1024]{1,0:T(8,128)(2,1)S(1)} %convolution_convert_fusion.4.keys, bf16[1024,1024]{1,0:T(8,128)(2,1)S(1)} %convolution_convert_fusion.3.values, ...), custom_call_target="tpu_custom_call" | custom-call | tf_op jit(solution)/shard_map/pallas_call | solution.py:387
  53.8 18.2 %shard_map.264 = (bf16[256,1024]{1,0:T(8,128)(2,1)}, bf16[2048,256]{1,0:T(8,128)(2,1)S(1)}, bf16[2048,256]{1,0:T(8,128)(2,1)}, bf16[512,256]{1,0:T(8,128)(2,1)S(...) custom-call(s32[1]{0:T(128)} %bitcast.core, ...), custom_call_target="tpu_custom_call" | custom-call | tf_op jit(solution)/shard_map/pallas_call | solution.py:565
  72.1 21.1 %shard_map.265 = (bf16[256,1024]{1,0:T(8,128)(2,1)}, bf16[1024,1024]{1,0:T(8,128)(2,1)S(1)}, bf16[1024,1024]{1,0:T(8,128)(2,1)S(1)}) custom-call(bf16[256,1024]{1,0:T(8,128)(2,1)S(1)} %fusion.46.query, bf16[1024,1024]{1,0:T(8,128)(2,1)S(1)} %convolution_convert_fusion.4.keys, bf16[1024,1024]{1,0:T(8,128)(2,1)S(1)} %convolution_convert_fusion.3.values, ...), custom_call_target="tpu_custom_call" | custom-call | tf_op jit(solution)/shard_map/pallas_call | solution.py:469
  97.6 2.7 fusion.47
  100.3 2.7 fusion.48
  103.5 3.3 %fusion.36 = bf16[512,1024]{1,0:T(8,128)(2,1)} fusion(s32[512]{0:T(512)S(1)} %add_add_fusion.1, bf16[256,1024]{1,0:T(8,128)(2,1)S(1)} %copy-done.32, bf16[256,1024]{1,0:T(8,128)(2,1)} %collective-permute-done.2, bf16[256,1024]{1,0:T(8,128)(2,1)S(1)} %collective-permute-done.1, bf16[256,1024]{1,0:T(8,128)(2,1)S(1)} %copy-done.20), kind=kOutput, calls=%fused_computation.46 | convolution fusion | flops 1083179008 | bytes 3147776 | tf_op jit(solution)/shard_map/dot_general | solution.py:34
  106.8 2.8 fusion.117
  114.9 3.0 %convolution_convert_fusion.6 = bf16[512,1024]{1,0:T(8,128)(2,1)} fusion(bf16[256,1024]{1,0:T(8,128)(2,1)} %collective-permute-done.7, bf16[256,1024]{1,0:T(8,128)(2,1)} %get-tuple-element.43, bf16[512,1024]{1,0:T(8,128)(2,1)S(1)} %copy-done.33), kind=kOutput, calls=%fused_computation.48 | convolution fusion | flops 539492352 | bytes 2621440 | tf_op jit(solution)/shard_map/dot_general | solution.py:24
  118.6 5.8 %convolution_convert_fusion.1 = bf16[2048,1024]{1,0:T(8,128)(2,1)} fusion(bf16[2048,256]{1,0:T(8,128)(2,1)} %collective-permute-done.13, bf16[2048,256]{1,0:T(8,128)(2,1)S(1)} %copy-done.7, bf16[256,1024]{1,0:T(8,128)(2,1)} %collective-permute-done.14, bf16[256,1024]{1,0:T(8,128)(2,1)S(1)} %bitcast_select_fusion.grad_low), kind=kOutput, calls=%fused_computation.23 | convolution fusion | flops 2155872256 | bytes 7340032 | tf_op jit(solution)/shard_map/dot_general | solution.py:24
  130.2 3.3 %collective-permute-start.5 = (bf16[256,1024]{1,0:T(8,128)(2,1)S(1)}, bf16[256,1024]{1,0:T(8,128)(2,1)S(1)}, u32[]{:S(2)}, u32[]{:S(2)}) collective-permute-start(bf16[256,1024]{1,0:T(8,128)(2,1)S(1)} %slice.136), channel_id=1, source_target_pairs={{0,2},{1,3},{2,0},{3,1},{4,6},{5,7},{6,4},{7,5},{8,10},{9,11},{10,... | collective-permute-start | bytes 1572872 | tf_op jit(solution)/shard_map/ppermute | solution.py:69
  133.5 6.6 %convolution_convert_fusion = bf16[512,4096]{1,0:T(8,128)(2,1)} fusion(bf16[256,4096]{1,0:T(8,128)(2,1)} %collective-permute-done.12, bf16[256,4096]{1,0:T(8,128)(2,1)} %get-tuple-element.54, bf16[512,256]{1,0:T(8,128)(2,1)S(1)} %collective-permute-done.11, bf16[512,256]{1,0:T(8,128)(2,1)S(1)} %get-tuple-element.52), kind=kOutput, calls=%fused_computation.4 | convolution fusion | flops 2159017984 | bytes 8912896 | tf_op jit(solution)/shard_map/dot_general | solution.py:24
  141.3 4.5 %collective-permute-done.5 = bf16[256,1024]{1,0:T(8,128)(2,1)S(1)} collective-permute-done((bf16[256,1024]{1,0:T(8,128)(2,1)S(1)}, bf16[256,1024]{1,0:T(8,128)(2,1)S(1)}, u32[]{:S(2)}, u32[]{:S(2)}) %collective-permute-start.5) | collective-permute-done | bytes 524320 | tf_op jit(solution)/shard_map/ppermute | solution.py:69
  149.0 2.6 fusion.43
  154.7 3.3 %fusion.49 = bf16[1,1,256,1024]{3,2,1,0:T(8,128)(2,1)} fusion(bf16[256,1024]{1,0:T(8,128)(2,1)} %get-tuple-element.74, bf16[2048,1024]{1,0:T(8,128)(2,1)} %param.18), kind=kOutput, calls=%fused_computation.56 | convolution fusion | flops 537133056 | bytes 3145728 | tf_op jit(solution)/shard_map/dot_general | solution.py:34
  158.0 3.0 %convolution_convert_fusion.5 = bf16[512,1024]{1,0:T(8,128)(2,1)} fusion(bf16[256,1024]{1,0:T(8,128)(2,1)} %collective-permute-done.16, bf16[256,1024]{1,0:T(8,128)(2,1)} %get-tuple-element.73, bf16[512,256]{0,1:T(8,128)(2,1)} %collective-permute-done.15, bf16[512,256]{0,1:T(8,128)(2,1)S(1)} %copy-done.35), kind=kOutput, calls=%fused_computation.47 | convolution fusion | flops 540540928 | bytes 2621440 | tf_op jit(solution)/shard_map/dot_general | solution.py:24
  161.1 63.0 %shard_map.267 = (f32[16,4096]{1,0:T(8,128)}, f32[64,1024]{1,0:T(8,128)}, f32[16,1024]{1,0:T(8,128)}) custom-call(bf16[16,32,4096]{2,1,0:T(8,128)(2,1)} %bitcast.67, bf16[16,128,1024]{2,1,0:T(8,128)(2,1)} %bitcast.66, bf16[16,32,1024]{2,1,0:T(8,128)(2,1)} %bitcast.70), custom_call_target="tpu_custom_call" | custom-call | tf_op jit(solution)/shard_map/pallas_call | solution.py:319
  224.2 4.0 %convolution_convert_fusion.2 = bf16[1024,1024]{1,0:T(8,128)(2,1)} fusion(bf16[1024,256]{0,1:T(8,128)(2,1)} %collective-permute-done.9, bf16[1024,256]{0,1:T(8,128)(2,1)S(1)} %copy-done.36, bf16[256,1024]{1,0:T(8,128)(2,1)} %collective-permute-done.10, bf16[256,1024]{1,0:T(8,128)(2,1)} %get-tuple-element.74), kind=kOutput, calls=%fused_computation.35 | convolution fusion | flops 1078984704 | bytes 4194304 | tf_op jit(solution)/shard_map/dot_general | solution.py:24
  230.3 3.6 %fusion.19 = bf16[512,2048]{1,0:T(8,128)(2,1)} fusion(bf16[512,1024]{1,0:T(8,128)(2,1)S(1)} %copy-done.34, bf16[256,2048]{1,0:T(8,128)(2,1)S(1)} %get-tuple-element.72, bf16[256,2048]{1,0:T(8,128)(2,1)S(1)} %copy-done.16, bf16[256,2048]{1,0:T(8,128)(2,1)S(1)} %get-tuple-element.71, bf16[256,2048]{1,0:T(8,128)(2,1)S(1)} %get-tuple-element.69), kind=kOutput, calls=%fused_computation.24 | convolution fusion | flops 2165309440 | bytes 7340032 | tf_op jit(solution)/shard_map/dot_general | solution.py:24
  233.9 44.0 %shard_map.266 = (f32[16,1024]{1,0:T(8,128)}, f32[16,2048]{1,0:T(8,128)}, f32[32,1024]{1,0:T(8,128)}, f32[8,128]{1,0:T(8,128)}) custom-call(bf16[16,32,1024]{2,1,0:T(8,128)(2,1)} %bitcast.71, bf16[16,32,2048]{2,1,0:T(8,128)(2,1)} %bitcast.69, bf16[16,64,1024]{2,1,0:T(8,128)(2,1)} %bitcast.68, f32[16,8,128]{2,1,0:T(8,128)} %pad.4.refs_3_), custom_call_target="tpu_custom_call" | custom-call | tf_op jit(solution)/shard_map/pallas_call | solution.py:319
  (167 shorter events, 52.6 us)
Async XLA Ops:
  0.6 32.3 %copy-start = (bf16[1024,1024]{1,0:T(8,128)(2,1)S(1)}, bf16[1024,1024]{1,0:T(8,128)(2,1)}, u32[]{:S(2)}) copy-start(bf16[1024,1024]{1,0:T(8,128)(2,1)} %param.21) | copy-start | bytes 6291460
  0.7 13.9 %collective-permute-start = (bf16[256,1024]{1,0:T(8,128)(2,1)}, bf16[256,1024]{1,0:T(8,128)(2,1)S(1)}, u32[]{:S(2)}, u32[]{:S(2)}) collective-permute-start(bf16[256,1024]{1,0:T(8,128)(2,1)} %bitcast.85), channel_id=1, source_target_pairs={{0,64},{64,0},{1,65},{65,1},{2,66},{66,2},{3,67},{67,3},{4,68},{68... | collective-permute-start | bytes 1572872 | tf_op jit(solution)/shard_map/ppermute | solution.py:20
  5.2 112.6 %collective-permute-start.14 = (bf16[256,1024]{1,0:T(8,128)(2,1)S(1)}, bf16[256,1024]{1,0:T(8,128)(2,1)}, u32[]{:S(2)}, u32[]{:S(2)}) collective-permute-start(bf16[256,1024]{1,0:T(8,128)(2,1)S(1)} %bitcast_select_fusion.grad_low), channel_id=1, source_target_pairs={{0,1},{1,0},{2,3},{3,2},{4,5},{5,4},{6,7},{7,6},{8,9},{9,8},{10,11... | collective-permute-start | bytes 1572872 | tf_op jit(solution)/shard_map/ppermute | solution.py:69
  17.7 14.6 %collective-permute-start.2 = (bf16[256,1024]{1,0:T(8,128)(2,1)S(1)}, bf16[256,1024]{1,0:T(8,128)(2,1)}, u32[]{:S(2)}, u32[]{:S(2)}) collective-permute-start(bf16[256,1024]{1,0:T(8,128)(2,1)S(1)} %add_convert_fusion.2), channel_id=1, source_target_pairs={{0,2},{1,3},{2,0},{3,1},{4,6},{5,7},{6,4},{7,5},{8,10},{9,11},{10,... | collective-permute-start | bytes 1572872 | tf_op jit(solution)/shard_map/ppermute | solution.py:69
  21.4 12.3 %collective-permute-start.1 = (bf16[256,1024]{1,0:T(8,128)(2,1)S(1)}, bf16[256,1024]{1,0:T(8,128)(2,1)S(1)}, u32[]{:S(2)}, u32[]{:S(2)}) collective-permute-start(bf16[256,1024]{1,0:T(8,128)(2,1)S(1)} %add_convert_fusion.2), channel_id=1, source_target_pairs={{0,1},{1,0},{2,3},{3,2},{4,5},{5,4},{6,7},{7,6},{8,9},{9,8},{10,11... | collective-permute-start | bytes 1572872 | tf_op jit(solution)/shard_map/ppermute | solution.py:69
  32.3 2.6 collective-permute-start.3
  72.1 21.1 %copy-start.4 = (f32[256,1024]{1,0:T(8,128)}, f32[256,1024]{1,0:T(8,128)S(1)}, u32[]{:S(2)}) copy-start(f32[256,1024]{1,0:T(8,128)S(1)} %get-tuple-element.39) | copy-start | bytes 3145732
  72.1 21.1 %copy-start.6 = (bf16[2048,256]{1,0:T(8,128)(2,1)}, bf16[2048,256]{1,0:T(8,128)(2,1)S(1)}, u32[]{:S(2)}) copy-start(bf16[2048,256]{1,0:T(8,128)(2,1)S(1)} %get-tuple-element.55) | copy-start | bytes 3145732
  97.3 27.1 %collective-permute-start.4 = (bf16[512,2048]{1,0:T(8,128)(2,1)}, bf16[512,2048]{1,0:T(8,128)(2,1)}, u32[]{:S(2)}, u32[]{:S(2)}) collective-permute-start(bf16[512,2048]{1,0:T(8,128)(2,1)} %pad_maximum_fusion.1), channel_id=1, source_target_pairs={{0,1},{1,0},{2,3},{3,2},{4,5},{5,4},{6,7},{7,6},{8,9},{9,8},{10,11... | collective-permute-start | bytes 6291464 | tf_op jit(solution)/shard_map/ppermute | solution.py:69
  103.0 15.2 %collective-permute-start.13 = (bf16[2048,256]{1,0:T(8,128)(2,1)}, bf16[2048,256]{1,0:T(8,128)(2,1)}, u32[]{:S(2)}, u32[]{:S(2)}) collective-permute-start(bf16[2048,256]{1,0:T(8,128)(2,1)} %get-tuple-element.56), channel_id=1, source_target_pairs={{0,1},{1,0},{2,3},{3,2},{4,5},{5,4},{6,7},{7,6},{8,9},{9,8},{10,11... | collective-permute-start | bytes 3145736 | tf_op jit(solution)/shard_map/ppermute | solution.py:69
  103.3 11.4 %collective-permute-start.7 = (bf16[256,1024]{1,0:T(8,128)(2,1)}, bf16[256,1024]{1,0:T(8,128)(2,1)}, u32[]{:S(2)}, u32[]{:S(2)}) collective-permute-start(bf16[256,1024]{1,0:T(8,128)(2,1)} %get-tuple-element.43), channel_id=1, source_target_pairs={{0,1},{1,0},{2,3},{3,2},{4,5},{5,4},{6,7},{7,6},{8,9},{9,8},{10,11... | collective-permute-start | bytes 1572872 | tf_op jit(solution)/shard_map/ppermute | solution.py:69
  109.6 23.8 %collective-permute-start.12 = (bf16[256,4096]{1,0:T(8,128)(2,1)}, bf16[256,4096]{1,0:T(8,128)(2,1)}, u32[]{:S(2)}, u32[]{:S(2)}) collective-permute-start(bf16[256,4096]{1,0:T(8,128)(2,1)} %get-tuple-element.54), channel_id=1, source_target_pairs={{0,1},{1,0},{2,3},{3,2},{4,5},{5,4},{6,7},{7,6},{8,9},{9,8},{10,11... | collective-permute-start | bytes 6291464 | tf_op jit(solution)/shard_map/ppermute | solution.py:69
  114.7 109.4 %collective-permute-start.9 = (bf16[1024,256]{0,1:T(8,128)(2,1)}, bf16[1024,256]{0,1:T(8,128)(2,1)}, u32[]{:S(2)}, u32[]{:S(2)}) collective-permute-start(bf16[1024,256]{0,1:T(8,128)(2,1)} %fusion.47), channel_id=1, source_target_pairs={{0,1},{1,0},{2,3},{3,2},{4,5},{5,4},{6,7},{7,6},{8,9},{9,8},{10,11... | collective-permute-start | bytes 1572872 | tf_op jit(solution)/shard_map/ppermute | solution.py:69
  117.9 33.9 %collective-permute-start.15 = (bf16[512,256]{0,1:T(8,128)(2,1)}, bf16[512,256]{0,1:T(8,128)(2,1)}, u32[]{:S(2)}, u32[]{:S(2)}) collective-permute-start(bf16[512,256]{0,1:T(8,128)(2,1)} %fusion.52), channel_id=1, source_target_pairs={{0,1},{1,0},{2,3},{3,2},{4,5},{5,4},{6,7},{7,6},{8,9},{9,8},{10,11... | collective-permute-start | bytes 786440 | tf_op jit(solution)/shard_map/ppermute | solution.py:69
  118.2 12.0 %collective-permute-start.11 = (bf16[512,256]{1,0:T(8,128)(2,1)S(1)}, bf16[512,256]{1,0:T(8,128)(2,1)S(1)}, u32[]{:S(2)}, u32[]{:S(2)}) collective-permute-start(bf16[512,256]{1,0:T(8,128)(2,1)S(1)} %copy-done.9), channel_id=1, source_target_pairs={{0,1},{1,0},{2,3},{3,2},{4,5},{5,4},{6,7},{7,6},{8,9},{9,8},{10,11... | collective-permute-start | bytes 786440 | tf_op jit(solution)/shard_map/ppermute | solution.py:69
  129.7 98.5 %collective-permute-start.8 = (bf16[512,2048]{1,0:T(8,128)(2,1)S(1)}, bf16[512,2048]{1,0:T(8,128)(2,1)}, u32[]{:S(2)}, u32[]{:S(2)}) collective-permute-start(bf16[512,2048]{1,0:T(8,128)(2,1)S(1)} %add_convert_fusion), channel_id=1, source_target_pairs={{0,1},{1,0},{2,3},{3,2},{4,5},{5,4},{6,7},{7,6},{8,9},{9,8},{10,11... | collective-permute-start | bytes 6291464 | tf_op jit(solution)/shard_map/ppermute | solution.py:69
  130.2 15.6 %collective-permute-start.5 = (bf16[256,1024]{1,0:T(8,128)(2,1)S(1)}, bf16[256,1024]{1,0:T(8,128)(2,1)S(1)}, u32[]{:S(2)}, u32[]{:S(2)}) collective-permute-start(bf16[256,1024]{1,0:T(8,128)(2,1)S(1)} %slice.136), channel_id=1, source_target_pairs={{0,2},{1,3},{2,0},{3,1},{4,6},{5,7},{6,4},{7,5},{8,10},{9,11},{10,... | collective-permute-start | bytes 1572872 | tf_op jit(solution)/shard_map/ppermute | solution.py:69
  147.8 10.2 %collective-permute-start.16 = (bf16[256,1024]{1,0:T(8,128)(2,1)}, bf16[256,1024]{1,0:T(8,128)(2,1)}, u32[]{:S(2)}, u32[]{:S(2)}) collective-permute-start(bf16[256,1024]{1,0:T(8,128)(2,1)} %get-tuple-element.73), channel_id=1, source_target_pairs={{0,1},{1,0},{2,3},{3,2},{4,5},{5,4},{6,7},{7,6},{8,9},{9,8},{10,11... | collective-permute-start | bytes 1572872 | tf_op jit(solution)/shard_map/ppermute | solution.py:69
  147.8 76.3 %collective-permute-start.10 = (bf16[256,1024]{1,0:T(8,128)(2,1)}, bf16[256,1024]{1,0:T(8,128)(2,1)}, u32[]{:S(2)}, u32[]{:S(2)}) collective-permute-start(bf16[256,1024]{1,0:T(8,128)(2,1)} %get-tuple-element.74), channel_id=1, source_target_pairs={{0,1},{1,0},{2,3},{3,2},{4,5},{5,4},{6,7},{7,6},{8,9},{9,8},{10,11... | collective-permute-start | bytes 1572872 | tf_op jit(solution)/shard_map/ppermute | solution.py:69
  151.8 72.3 %collective-permute-start.6 = (bf16[256,1024]{1,0:T(8,128)(2,1)}, bf16[256,1024]{1,0:T(8,128)(2,1)}, u32[]{:S(2)}, u32[]{:S(2)}) collective-permute-start(bf16[256,1024]{1,0:T(8,128)(2,1)} %fusion.43), channel_id=1, source_target_pairs={{0,64},{64,0},{1,65},{65,1},{2,66},{66,2},{3,67},{67,3},{4,68},{68... | collective-permute-start | bytes 1572872 | tf_op jit(solution)/shard_map/ppermute | solution.py:20
  161.1 63.1 %copy-start.36 = (bf16[1024,256]{0,1:T(8,128)(2,1)S(1)}, bf16[1024,256]{0,1:T(8,128)(2,1)}, u32[]{:S(2)}) copy-start(bf16[1024,256]{0,1:T(8,128)(2,1)} %fusion.48) | copy-start | bytes 1572868
  233.9 51.8 %copy-start.23 = (f32[16,1024]{1,0:T(8,128)S(1)}, f32[16,1024]{1,0:T(8,128)}, u32[]{:S(2)}) copy-start(f32[16,1024]{1,0:T(8,128)} %get-tuple-element.57) | copy-start | bytes 196612
  233.9 52.4 %copy-start.22 = (f32[16,4096]{1,0:T(8,128)S(1)}, f32[16,4096]{1,0:T(8,128)}, u32[]{:S(2)}) copy-start(f32[16,4096]{1,0:T(8,128)} %get-tuple-element.58) | copy-start | bytes 786436
  233.9 53.8 %copy-start.1 = (bf16[1024,1024]{1,0:T(8,128)(2,1)S(1)}, bf16[1024,1024]{1,0:T(8,128)(2,1)}, u32[]{:S(2)}) copy-start(bf16[1024,1024]{1,0:T(8,128)(2,1)} %param.21) | copy-start | bytes 6291460
  (30 other events, 162.1 us)

commit v4 on v3

--- a/solution.py
+++ b/solution.py
@@ -9,6 +9,7 @@
 
 HEADS = 16
 LOG2E = 1.4426950408889634
+LN2 = 0.6931471805599453
 
 
 EPS = 1e-05
@@ -154,38 +155,121 @@
     lax.fori_loop(0, count, one, 0)
 
 
-def reduce_kernel(shapes, with_vectors, *refs):
+def place_here():
+    dp, seq = lax.axis_index("dp"), lax.axis_index("seq")
+    return lax.div(dp, 4), lax.rem(dp, 4), seq
+
+
+def ring_partners(z, x, seq):
+    pairs = ((0, 0), (0, 1), (2, 0), (2, 1), (0, 4))
+    return [stage_partner(quarter, stage, x, z, seq) for quarter, stage in pairs]
+
+
+class Halving:
+    def __init__(self, shapes, sources, results, scratch):
+        self.shapes, self.sources, self.results = shapes, sources, results
+        scratch = list(scratch)
+        count = len(shapes)
+        self.totals = scratch[:count]
+        self.landings = [scratch[count + 5 * job : count + 5 * job + 5] for job in range(count)]
+        self.local_sem, self.send_sem, self.recv_sem = scratch[6 * count :]
+        self.z, self.x, self.seq = place_here()
+        self.y = lax.div(self.seq, 2)
+
+    @staticmethod
+    def scratch(shapes):
+        count = len(shapes)
+        shapes_of = [(4, 8, 2 * rows, width // 4) for rows, width in shapes]
+        for rows, width in shapes:
+            shapes_of += [(4, blocks, 2 * rows, width // 4) for blocks in (8, 4, 2, 1)]
+            shapes_of.append((4, rows, width // 4))
+        return [pltpu.VMEM(shape, jnp.bfloat16) for shape in shapes_of] + [
+            pltpu.SemaphoreType.DMA((count, 4)),
+            pltpu.SemaphoreType.DMA((count, 4, 5)),
+            pltpu.SemaphoreType.DMA((count, 4, 5)),
+        ]
+
+    def columns(self, job, quarter):
+        width = self.shapes[job][1] // 4
+        return pl.ds(quarter * width, width)
+
+    def start(self, job):
+        for quarter in range(4):
+            columns = self.columns(job, quarter)
+            for index in range(8):
+                outer, inner = index // 4, index % 4
+                there = block_place(quarter, outer + 2, inner, self.x, self.z)
+                here = block_place(quarter, outer, inner, self.x, self.z)
+                remote(
+                    self.sources[job].at[there, :, columns],
+                    self.landings[job][0].at[quarter, index],
+                    self.send_sem.at[job, quarter, 0],
+                    self.recv_sem.at[job, quarter, 0],
+                    stage_partner(quarter, 0, self.x, self.z, self.seq),
+                ).start()
+                pltpu.make_async_copy(
+                    self.sources[job].at[here, :, columns],
+                    self.totals[job].at[quarter, index],
+                    self.local_sem.at[job, quarter],
+                ).start()
+
+    def copy(self, job, quarter, stage):
+        rows = self.shapes[job][0]
+        target = self.landings[job][stage].at[quarter]
+        if stage == 0:
+            source = target
+        elif stage < 4:
+            size = 8 >> stage
+            source = self.totals[job].at[quarter, pl.ds(size, size)]
+        else:
+            away = pl.multiple_of((1 - self.y) * rows, 16)
+            source = self.totals[job].at[quarter, 0, pl.ds(away, rows)]
+        return remote(
+            source,
+            target,
+            self.send_sem.at[job, quarter, stage],
+            self.recv_sem.at[job, quarter, stage],
+            stage_partner(quarter, stage, self.x, self.z, self.seq),
+        )
+
+    def finish(self, job, stage):
+        rows = self.shapes[job][0]
+        for quarter in range(4):
+            total = self.totals[job].at[quarter]
+            landing = self.landings[job][stage].at[quarter]
+            self.copy(job, quarter, stage).wait_recv()
+            if stage == 0:
+                pltpu.make_async_copy(total, total, self.local_sem.at[job, quarter]).wait()
+            if stage < 4:
+                add_blocks(8 >> stage, total, landing)
+                self.copy(job, quarter, stage + 1).start()
+            else:
+                mine = pl.multiple_of(self.y * rows, 16)
+                self.results[job][:, self.columns(job, quarter)] = total[
+                    0, pl.ds(mine, rows)
+                ].astype(jnp.float32) + landing[...].astype(jnp.float32)
+
+    def drain(self):
+        for job in range(len(self.shapes)):
+            for quarter in range(4):
+                for stage in range(5):
+                    self.copy(job, quarter, stage).wait_send()
+
+
+def reduce_kernel(shapes, *refs):
     count = len(shapes)
     refs = list(refs)
     take = lambda n: [refs.pop(0) for _ in range(n)]
-    sources = take(count)
-    vector = take(1)[0] if with_vectors else None
-    results = take(count)
-    vector_result = take(1)[0] if with_vectors else None
-    totals = take(count)
-    landings = [take(5) for _ in range(count)]
-    local_sem, send_sem, recv_sem = take(3)
-    if with_vectors:
-        vector_total, vector_landing, vector_send, vector_recv = take(4)
-
-    dp, seq = lax.axis_index("dp"), lax.axis_index("seq")
-    z, x = lax.div(dp, 4), lax.rem(dp, 4)
-    y = lax.div(seq, 2)
-    partners = [stage_partner(0, 0, x, z, seq), stage_partner(0, 1, x, z, seq)]
-    partners += [stage_partner(2, 0, x, z, seq), stage_partner(2, 1, x, z, seq)]
-    partners += [stage_partner(0, 4, x, z, seq)]
+    sources, vector = take(count), take(1)[0]
+    results, vector_result = take(count), take(1)[0]
+    vector_total, vector_landing, vector_send, vector_recv = take(4)
+    halving = Halving(shapes, sources, results, refs)
+    z, x, seq = place_here()
     core = {"seq": flip(seq, 1)}
-    if with_vectors:
-        partners += [core]
-    enter(partners)
-
-    vector_stages = [(core, 0, 0, 16)]
-    if with_vectors:
-        vector_stages += [(stage_partner(0, 0, x, z, seq), 8, 16, 8)]
-        vector_stages += [(stage_partner(0, 1, x, z, seq), 4, 24, 4)]
-        vector_stages += [(stage_partner(0, 2, x, z, seq), 2, 28, 2)]
-        vector_stages += [(stage_partner(0, 3, x, z, seq), 1, 30, 1)]
-        vector_stages += [(stage_partner(0, 4, x, z, seq), 0, 31, 1)]
+    enter(ring_partners(z, x, seq) + [core])
+
+    devices = [core] + [stage_partner(0, stage, x, z, seq) for stage in range(5)]
+    vector_stages = list(zip(devices, (0, 8, 4, 2, 1, 0), (0, 16, 24, 28, 30, 31), (16, 8, 4, 2, 1, 1)))
 
     def vector_copy(step):
         device, first, landing, size = vector_stages[step]
@@ -199,135 +283,196 @@
 
     def vector_finish(step):
         _, _, landing, size = vector_stages[step]
-        copy = vector_copy(step)
-        copy.wait()
+        vector_copy(step).wait()
         vector_total[pl.ds(0, size)] += vector_landing[pl.ds(landing, size)]
 
-    if with_vectors:
-        for index in range(16):
-            outer, inner = index // 4, index % 4
-            vector_total[index] = vector[block_place(0, outer, inner, x, z)]
-        vector_copy(0).start()
-
-    def first_blocks(job, quarter):
-        rows, width = shapes[job]
-        columns = pl.ds(quarter * (width // 4), width // 4)
-        for index in range(8):
-            outer, inner = index // 4, index % 4
-            there = block_place(quarter, outer + 2, inner, x, z)
-            here = block_place(quarter, outer, inner, x, z)
-            remote(
-                sources[job].at[there, :, columns],
-                landings[job][0].at[quarter, index],
-                send_sem.at[job, quarter, 0],
-                recv_sem.at[job, quarter, 0],
-                stage_partner(quarter, 0, x, z, seq),
-            ).start()
-            pltpu.make_async_copy(
-                sources[job].at[here, :, columns],
-                totals[job].at[quarter, index],
-                local_sem.at[job, quarter],
-            ).start()
-
-    def stage_copy(job, quarter, stage):
-        rows, width = shapes[job]
-        if stage == 0:
-            source = landings[job][0].at[quarter]
-            target = landings[job][0].at[quarter]
-        elif stage < 4:
-            size = 8 >> stage
-            source = totals[job].at[quarter, pl.ds(size, size)]
-            target = landings[job][stage].at[quarter]
-        else:
-            away = pl.multiple_of((1 - y) * rows, 16)
-            source = totals[job].at[quarter, 0, pl.ds(away, rows)]
-            target = landings[job][4].at[quarter]
-        return remote(
-            source,
-            target,
-            send_sem.at[job, quarter, stage],
-            recv_sem.at[job, quarter, stage],
-            stage_partner(quarter, stage, x, z, seq),
-        )
-
-    def finish(job, quarter, stage):
-        rows, width = shapes[job]
-        stage_copy(job, quarter, stage).wait_recv()
-        if stage == 0:
-            pltpu.make_async_copy(
-                totals[job].at[quarter], totals[job].at[quarter], local_sem.at[job, quarter]
-            ).wait()
-        if stage < 4:
-            add_blocks(8 >> stage, totals[job].at[quarter], landings[job][stage].at[quarter])
-            stage_copy(job, quarter, stage + 1).start()
-        else:
-            mine = pl.multiple_of(y * rows, 16)
-            columns = pl.ds(quarter * (width // 4), width // 4)
-            results[job][:, columns] = totals[job][quarter, 0, pl.ds(mine, rows)].astype(
-                jnp.float32
-            ) + landings[job][4][quarter].astype(jnp.float32)
-
+    for index in range(16):
+        vector_total[index] = vector[block_place(0, index // 4, index % 4, x, z)]
+    vector_copy(0).start()
     for job in range(count):
-        for quarter in range(4):
-            first_blocks(job, quarter)
+        halving.start(job)
     for stage in range(5):
         for job in range(count):
-            for quarter in range(4):
-                finish(job, quarter, stage)
-        if with_vectors:
-            vector_finish(stage)
-            vector_copy(stage + 1).start()
-    if with_vectors:
-        vector_finish(5)
-        vector_result[...] = vector_total[0]
-    for job in range(count):
-        for quarter in range(4):
-            for stage in range(5):
-                stage_copy(job, quarter, stage).wait_send()
+            halving.finish(job, stage)
+        vector_finish(stage)
+        vector_copy(stage + 1).start()
+    vector_finish(5)
+    vector_result[...] = vector_total[0]
+    halving.drain()
 
 
 def reduce_shares(shares, vectors, collective_id):
     shapes = [(share.shape[1] // 2, share.shape[2]) for share in shares]
     count = len(shares)
-    scratch = [
-        pltpu.VMEM((4, 8, 2 * rows, width // 4), jnp.bfloat16) for rows, width in shapes
-    ]
-    for rows, width in shapes:
-        for blocks in (8, 4, 2, 1):
-            scratch.append(pltpu.VMEM((4, blocks, 2 * rows, width // 4), jnp.bfloat16))
-        scratch.append(pltpu.VMEM((4, rows, width // 4), jnp.bfloat16))
-    scratch += [
-        pltpu.SemaphoreType.DMA((count, 4)),
-        pltpu.SemaphoreType.DMA((count, 4, 5)),
-        pltpu.SemaphoreType.DMA((count, 4, 5)),
-    ]
-    in_specs = [pl.BlockSpec(memory_space=pl.ANY)] * count
-    out_specs = [pl.BlockSpec(memory_space=pltpu.VMEM)] * count
-    out_shape = [jax.ShapeDtypeStruct(shape, jnp.float32) for shape in shapes]
-    operands = list(shares)
-    if vectors is not None:
-        in_specs.append(pl.BlockSpec(memory_space=pltpu.VMEM))
-        out_specs.append(pl.BlockSpec(memory_space=pltpu.VMEM))
-        out_shape.append(jax.ShapeDtypeStruct(vectors.shape[1:], jnp.float32))
-        operands.append(vectors)
-        scratch += [
+    return pl.pallas_call(
+        functools.partial(reduce_kernel, shapes),
+        out_shape=[jax.ShapeDtypeStruct(shape, jnp.float32) for shape in shapes]
+        + [jax.ShapeDtypeStruct(vectors.shape[1:], jnp.float32)],
+        in_specs=[pl.BlockSpec(memory_space=pl.ANY)] * count
+        + [pl.BlockSpec(memory_space=pltpu.VMEM)],
+        out_specs=[pl.BlockSpec(memory_space=pltpu.VMEM)] * (count + 1),
+        scratch_shapes=[
             pltpu.VMEM(vectors.shape, jnp.float32),
             pltpu.VMEM((32,) + vectors.shape[1:], jnp.float32),
             pltpu.SemaphoreType.DMA((6,)),
             pltpu.SemaphoreType.DMA((6,)),
         ]
-    return pl.pallas_call(
-        functools.partial(reduce_kernel, shapes, vectors is not None),
-        out_shape=out_shape,
-        in_specs=in_specs,
-        out_specs=out_specs,
-        scratch_shapes=scratch,
+        + Halving.scratch(shapes),
         compiler_params=pltpu.CompilerParams(
             collective_id=collective_id,
             has_side_effects=True,
             vmem_limit_bytes=56 * 2**20,
         ),
-    )(*operands)
+    )(*shares, vectors)
+
+
+def attention_backward_pair(query, keys, values, share, inverse, grad, mixed, lows):
+    span = keys.shape[0]
+    here = query.shape[0]
+    chunk = 128
+    lane = lax.broadcasted_iota(jnp.int32, query.shape, 1)
+    zero = jnp.zeros(query.shape, query.dtype)
+    queries = jnp.concatenate(
+        [jnp.where(lane < 64, query, zero), jnp.where(lane >= 64, query, zero)], axis=0
+    )
+    turned = grad.astype(jnp.float32).T
+    product = turned * mixed.astype(jnp.float32).T
+    first = turned[:64] * inverse[:, :here]
+    second = turned[64:] * inverse[:, here:]
+    none = jnp.zeros_like(first)
+    grads = jnp.concatenate(
+        [jnp.concatenate([first, none], axis=1), jnp.concatenate([none, second], axis=1)], axis=0
+    ).astype(jnp.bfloat16)
+    grads_back = grads.T
+    centre = inverse * jnp.concatenate(
+        [
+            jnp.sum(product[:64], axis=0, keepdims=True),
+            jnp.sum(product[64:], axis=0, keepdims=True),
+        ],
+        axis=1,
+    )
+    grad_keys, grad_values = [], []
+    for index in range(span // chunk):
+        rows = pl.ds(index * chunk, chunk)
+        part = share[rows]
+        grad_share = project(values[rows], grads)
+        grad_score = (part.astype(jnp.float32) * (grad_share - centre)).astype(jnp.bfloat16)
+        lows[rows] = grad_score
+        grad_keys.append((project(grad_score, queries) * LN2).astype(jnp.bfloat16))
+        grad_values.append(project(part, grads_back).astype(jnp.bfloat16))
+    out = rows_product(keys[...], lows[...])
+    out = jnp.concatenate([out[:64, :here], out[64:, here:]], axis=0)
+    return (out.T * 0.125).astype(jnp.bfloat16), grad_keys, grad_values
+
+
+def backward_kernel(
+    shapes, query, keys, values, shares, inverses, grad, mixed, share_one, share_two, share_three,
+    grad_query, both, result_one, result_two, result_three,
+    lows, held, held_sem, parts, landing, swap_send, swap_recv, *halving_refs,
+):
+    halving = Halving(
+        shapes,
+        (share_one, share_two, share_three),
+        (result_one, result_two, result_three),
+        halving_refs,
+    )
+    z, x, seq = place_here()
+    core = {"seq": flip(seq, 1)}
+    pairs = shares.shape[0]
+    here, width = query.shape
+
+    def fetch(pair):
+        slot = lax.rem(pair, 2)
+        return pltpu.make_async_copy(shares.at[pair], held.at[slot], held_sem.at[slot])
+
+    fetch(0).start()
+    enter(ring_partners(z, x, seq) + [core])
+    for job in range(3):
+        halving.start(job)
+
+    def one_pair(pair, carry):
+        @pl.when(pair + 1 < pairs)
+        def _():
+            fetch(pair + 1).start()
+
+        fetch(pair).wait()
+        columns = pl.ds(pl.multiple_of(pair * 128, 128), 128)
+        others = pl.ds(pl.multiple_of(width + pair * 128, 128), 128)
+        out, grad_keys, grad_values = attention_backward_pair(
+            query[:, columns],
+            keys.at[:, columns],
+            values.at[:, columns],
+            held.at[lax.rem(pair, 2)],
+            inverses[pair],
+            grad[:, columns],
+            mixed[:, columns],
+            lows,
+        )
+        grad_query[:, columns] = out
+        for index, (one, two) in enumerate(zip(grad_keys, grad_values)):
+            part, rows = index * 128 // here, pl.ds(index * 128 % here, 128)
+            parts[part, rows, columns] = one
+            parts[part, rows, others] = two
+        for step in range(2):
+            for place in (columns, others):
+                remote(
+                    parts.at[2 * step + 1, :, place],
+                    landing.at[step, :, place],
+                    swap_send,
+                    swap_recv,
+                    core,
+                ).start()
+        return carry
+
+    lax.fori_loop(0, 5, one_pair, 0)
+    halving.finish(0, 0)
+    lax.fori_loop(5, pairs, one_pair, 0)
+    swapped = remote(landing, landing, swap_send, swap_recv, core)
+    swapped.wait_recv()
+    for step in range(2):
+        both[step] = (
+            parts[2 * step].astype(jnp.float32) + landing[step].astype(jnp.float32)
+        ).astype(jnp.bfloat16)
+    for job in (1, 2):
+        halving.finish(job, 0)
+    for stage in range(1, 5):
+        for job in range(3):
+            halving.finish(job, stage)
+    halving.drain()
+    swapped.wait_send()
+
+
+def backward(query, keys, values, shares, inverses, grad, mixed, weights, collective_id):
+    here, width = query.shape
+    span = keys.shape[0]
+    shapes = [(share.shape[1] // 2, share.shape[2]) for share in weights]
+    inside = pl.BlockSpec(memory_space=pltpu.VMEM)
+    outside = pl.BlockSpec(memory_space=pl.ANY)
+    return pl.pallas_call(
+        functools.partial(backward_kernel, shapes),
+        in_specs=[inside, inside, inside, outside, inside, inside, inside] + [outside] * 3,
+        out_specs=[inside] * 5,
+        out_shape=[
+            jax.ShapeDtypeStruct((here, width), jnp.bfloat16),
+            jax.ShapeDtypeStruct((2, here, 2 * width), jnp.bfloat16),
+        ]
+        + [jax.ShapeDtypeStruct(shape, jnp.float32) for shape in shapes],
+        scratch_shapes=[
+            pltpu.VMEM((span, 2 * here), jnp.bfloat16),
+            pltpu.VMEM((2, span, 2 * here), jnp.bfloat16),
+            pltpu.SemaphoreType.DMA((2,)),
+            pltpu.VMEM((4, here, 2 * width), jnp.bfloat16),
+            pltpu.VMEM((2, here, 2 * width), jnp.bfloat16),
+            pltpu.SemaphoreType.DMA,
+            pltpu.SemaphoreType.DMA,
+        ]
+        + Halving.scratch(shapes),
+        compiler_params=pltpu.CompilerParams(
+            collective_id=collective_id,
+            has_side_effects=True,
+            vmem_limit_bytes=56 * 2**20,
+        ),
+    )(query, keys, values, shares, inverses, grad, mixed, *weights)
 
 
 def attention_forward_kernel(
@@ -410,83 +555,6 @@
         ],
         compiler_params=pltpu.CompilerParams(vmem_limit_bytes=40 * 2**20),
     )(query, keys, values, *tables, slopes)
-
-
-def attention_backward_kernel(
-    query, keys, values, shares, inverses, grad, mixed, grad_query, grad_keys, grad_values, lows
-):
-    span = keys.shape[0]
-    chunk = 128
-    here = query.shape[0]
-    lane = lax.broadcasted_iota(jnp.int32, query.shape, 1)
-    zero = jnp.zeros(query.shape, query.dtype)
-
-    def stacked(value):
-        return jnp.concatenate(
-            [jnp.where(lane < 64, value, zero), jnp.where(lane >= 64, value, zero)], axis=0
-        )
-
-    queries = stacked(query[...])
-    inverse = inverses[0]
-    turned = grad[...].astype(jnp.float32).T
-    product = turned * mixed[...].astype(jnp.float32).T
-    top = turned[:64] * inverse[:, :here]
-    low_half = turned[64:] * inverse[:, here:]
-    none = jnp.zeros_like(top)
-    grads = jnp.concatenate(
-        [jnp.concatenate([top, none], axis=1), jnp.concatenate([none, low_half], axis=1)], axis=0
-    ).astype(jnp.bfloat16)
-    grads_back = grads.T
-    centre = inverse * jnp.concatenate(
-        [
-            jnp.sum(product[:64], axis=0, keepdims=True),
-            jnp.sum(product[64:], axis=0, keepdims=True),
-        ],
-        axis=1,
-    )
-
-    def part(index, carry):
-        rows = pl.ds(pl.multiple_of(index * chunk, chunk), chunk)
-        grad_share = project(values[rows], grads)
-        share = shares[0, rows]
-        grad_score = (share.astype(jnp.float32) * (grad_share - centre)).astype(jnp.bfloat16)
-        lows[rows] = grad_score
-        grad_keys[rows] = (project(grad_score, queries) * 0.6931471805599453).astype(jnp.bfloat16)
-        grad_values[rows] = project(share, grads_back).astype(jnp.bfloat16)
-        return carry
-
-    lax.fori_loop(0, span // chunk, part, 0, unroll=True)
-    out = rows_product(keys[...], lows[...])
-    out = jnp.concatenate([out[:64, :here], out[64:, here:]], axis=0)
-    grad_query[...] = (out.T * 0.125).astype(jnp.bfloat16)
-
-
-def attention_backward(query, keys, values, shares, inverses, grad, mixed):
-    here, width = query.shape
-    span = keys.shape[0]
-    pairs = width // 128
-    column = lambda rows: pl.BlockSpec((rows, 128), lambda i: (0, i))
-    return pl.pallas_call(
-        attention_backward_kernel,
-        grid=(pairs,),
-        in_specs=[
-            column(here),
-            column(span),
-            column(span),
-            pl.BlockSpec((1, span, 2 * here), lambda i: (i, 0, 0)),
-            pl.BlockSpec((1, 1, 2 * here), lambda i: (i, 0, 0)),
-            column(here),
-            column(here),
-        ],
-        out_specs=[column(here), column(span), column(span)],
-        out_shape=[
-            jax.ShapeDtypeStruct((here, width), jnp.bfloat16),
-            jax.ShapeDtypeStruct((span, width), jnp.bfloat16),
-            jax.ShapeDtypeStruct((span, width), jnp.bfloat16),
-        ],
-        scratch_shapes=[pltpu.VMEM((span, 2 * here), jnp.bfloat16)],
-        compiler_params=pltpu.CompilerParams(vmem_limit_bytes=40 * 2**20),
-    )(query, keys, values, shares, inverses, grad, mixed)
 
 
 def mean_rows(value):
@@ -708,17 +776,18 @@
     mixed_mine = low(back_product(select_mine, mixed_rows))
     mixed_other = swap_core(low(back_product(select_other, mixed_rows)))
     out_share = pair_product(mixed_mine, mixed_other, grad_attn, grad_attn_other)
-    up_sum, down_sum, out_sum = reduce_shares([up_share, down_share, out_share], None, 1)
-
-    grad_query, key_part, value_part = attention_backward(
-        query, keys_all, values_all, shares, inverses, grad_mixed, mixed_rows
-    )
-    both_part = jnp.concatenate([key_part, value_part], axis=1).reshape(4, rows_here, -1)
-    both_other = swap_core(jnp.concatenate([both_part[1], both_part[3]], axis=0))
-    both_mine = low(
-        jnp.concatenate([both_part[0], both_part[2]], axis=0).astype(jnp.float32)
-        + both_other.astype(jnp.float32)
-    )
+    grad_query, both_mine, down_sum, up_sum, out_sum = backward(
+        query,
+        keys_all,
+        values_all,
+        shares,
+        inverses,
+        grad_mixed,
+        mixed_rows,
+        [down_share, up_share, out_share],
+        1,
+    )
+    both_mine = both_mine.reshape(2 * rows_here, 2 * model_width)
     both_far = swap_core(both_mine)
     grad_query_other = swap_core(grad_query)
     w_both = jnp.concatenate([w_key, w_value], axis=1)

time: 292 us -> 287 us (0.983)
  waiting for transfers between devices: 19.8 us -> 35.1 us
  Pallas kernels: 158 us -> 143 us
  starting transfers between devices: 14 us -> 9.15 us
    pallas_call x3 -> x2, Pallas kernels: 128 us -> 112 us  [the longest x1 69.3 us: backward(): pl.pallas_call(functools.partial(backward_kernel, shapes), in_specs=[insi...]
    ppermute x2, waiting for transfers between devices: 3.19 us -> 12.6 us  [from_partner(): return lax.ppermute(value, axis, pairs)]
    ppermute x15 -> x14, waiting for transfers between devices: 16.6 us -> 22.5 us  [partner_of(): return lax.ppermute(value, axis, pairs)]
    ppermute x15 -> x14, starting transfers between devices: 10.4 us -> 6.48 us  [partner_of(): return lax.ppermute(value, axis, pairs)]
    unnamed x81 -> x78, local copies, waits for them, and re-layouts: 8.5 us -> 10.1 us
  transfers between devices with their start and end apart: 17 -> 16, of which waited for: 4 -> 5; matrix products, arithmetic and copies ran while one was open for 27% -> 27% of each run, Pallas kernels for 40% -> 35%
where the time goes in v4:
time: 287 us; the launch traced here: 283 us
  Pallas kernels  143 us (50%)
  matrix products  63.2 us (22%)
  waiting for transfers between devices  35.1 us (12%)
  local copies, waits for them, and re-layouts  20.3 us (7%)
  other arithmetic  11.1 us (4%)
  starting transfers between devices  9.15 us (3%)
    pallas_call x1, Pallas kernels, backward(): pl.pallas_call(functools.partial(backward_kernel, shapes), in_specs=[insi...  69.3 us
    pallas_call x1, Pallas kernels, reduce_shares(): pl.pallas_call(functools.partial(reduce_kernel, shapes), out_shape=[jax.S...  42.8 us
    dot_general x11, matrix products, project(): return jnp.dot(left, right, preferred_element_type=jnp.float32)  40.4 us
    dot_general x9, matrix products, back_product(): lax.dot_general(left, right, (((1,), (1,)), ((), ())), preferred_element_...  22.8 us
    ppermute x14, waiting for transfers between devices, partner_of(): return lax.ppermute(value, axis, pairs)  22.5 us
    pallas_call x1, Pallas kernels, feed_forward(): pl.pallas_call(ffn_kernel, grid=(full // block,), in_specs=[pl.BlockSpec(...  18.6 us
    ppermute x2, waiting for transfers between devices, from_partner(): return lax.ppermute(value, axis, pairs)  12.6 us
    pallas_call x1, Pallas kernels, attention_forward(): pl.pallas_call(attention_forward_kernel, grid=(pairs,), in_specs=[pl.Bloc...  11.8 us
  transfers between devices with their start and end apart: 16, of which 5 were waited for; matrix products, arithmetic and copies ran while one was open for 27% of the time, Pallas kernels for 35%

profile of v4, /device:TPU:0, one launch (start us, length us, event | category | flops | bytes accessed | tf_op | source)
XLA Modules:
  0.0 282.8 jit_solution(9846978787040352698)
XLA Ops:
  9.9 4.7 %collective-permute-done = bf16[256,1024]{1,0:T(8,128)(2,1)S(1)} collective-permute-done((bf16[256,1024]{1,0:T(8,128)(2,1)}, bf16[256,1024]{1,0:T(8,128)(2,1)S(1)}, u32[]{:S(2)}, u32[]{:S(2)}) %collective-permute-start) | collective-permute-done | bytes 524320 | tf_op jit(solution)/shard_map/ppermute | solution.py:21
  14.5 2.6 fusion.112
  18.5 3.4 %collective-permute-start.2 = (bf16[256,1024]{1,0:T(8,128)(2,1)}, bf16[256,1024]{1,0:T(8,128)(2,1)}, u32[]{:S(2)}, u32[]{:S(2)}) collective-permute-start(bf16[256,1024]{1,0:T(8,128)(2,1)} %add_convert_fusion.1), channel_id=1, source_target_pairs={{0,2},{1,3},{2,0},{3,1},{4,6},{5,7},{6,4},{7,5},{8,10},{9,11},{10,... | collective-permute-start | bytes 1572872 | tf_op jit(solution)/shard_map/ppermute | solution.py:70
  22.7 10.5 %collective-permute-done.2 = bf16[256,1024]{1,0:T(8,128)(2,1)} collective-permute-done((bf16[256,1024]{1,0:T(8,128)(2,1)}, bf16[256,1024]{1,0:T(8,128)(2,1)}, u32[]{:S(2)}, u32[]{:S(2)}) %collective-permute-start.2) | collective-permute-done | bytes 524320 | tf_op jit(solution)/shard_map/ppermute | solution.py:70
  35.5 4.2 %convolution_convert_fusion.3.values = bf16[1024,1024]{1,0:T(8,128)(2,1)S(1)} fusion(bf16[1024,1024]{1,0:T(8,128)(2,1)S(1)} %copy-done.26, bf16[256,1024]{1,0:T(8,128)(2,1)S(1)} %collective-permute-done.3, bf16[256,1024]{1,0:T(8,128)(2,1)} %collective-permute-done.2, bf16[256,1024]{1,0:T(8,128)(2,1)S(1)} %collective-permute-done.1, ...), kind=kOutput, calls=%fused_computation.34 | convolution fusion | flops 2156920832 | bytes 6291456 | tf_op jit(solution)/shard_map/dot_general | solution.py:25
  39.8 4.3 %convolution_convert_fusion.4.keys = bf16[1024,1024]{1,0:T(8,128)(2,1)S(1)} fusion(bf16[1024,1024]{1,0:T(8,128)(2,1)S(1)} %copy-done.24, bf16[256,1024]{1,0:T(8,128)(2,1)S(1)} %collective-permute-done.3, bf16[256,1024]{1,0:T(8,128)(2,1)} %collective-permute-done.2, bf16[256,1024]{1,0:T(8,128)(2,1)S(1)} %collective-permute-done.1, ...), kind=kOutput, calls=%fused_computation.35 | convolution fusion | flops 2156920832 | bytes 6291456 | tf_op jit(solution)/shard_map/dot_general | solution.py:25
  44.1 11.8 %shard_map.263 = (bf16[8,1024,512]{2,1,0:T(8,128)(2,1)}, bf16[256,1024]{1,0:T(8,128)(2,1)S(1)}, f32[8,1,512]{2,1,0:T(1,128)S(1)}) custom-call(bf16[256,1024]{1,0:T(8,128)(2,1)S(1)} %fusion.46.query, bf16[1024,1024]{1,0:T(8,128)(2,1)S(1)} %convolution_convert_fusion.4.keys, bf16[1024,1024]{1,0:T(8,128)(2,1)S(1)} %convolution_convert_fusion.3.values, ...), custom_call_target="tpu_custom_call" | custom-call | tf_op jit(solution)/shard_map/pallas_call | solution.py:532
  56.5 18.6 %shard_map.264 = (bf16[256,1024]{1,0:T(8,128)(2,1)}, bf16[2048,256]{1,0:T(8,128)(2,1)S(1)}, bf16[2048,256]{1,0:T(8,128)(2,1)}, bf16[512,256]{1,0:T(8,128)(2,1)S(...) custom-call(s32[1]{0:T(128)} %bitcast.core, ...), custom_call_target="tpu_custom_call" | custom-call | tf_op jit(solution)/shard_map/pallas_call | solution.py:633
  77.9 3.9 %fusion.47 = bf16[1024,256]{0,1:T(8,128)(2,1)} fusion(s32[1024]{0:T(1024)S(1)} %fusion.86, bf16[256,1024]{1,0:T(8,128)(2,1)} %copy-done.16, bf16[256,1024]{1,0:T(8,128)(2,1)} %bitcast.92), kind=kOutput, calls=%fused_computation.53 | convolution fusion | flops 1078198272 | bytes 1576960 | tf_op jit(solution)/shard_map/dot_general | solution.py:35
  82.4 2.7 fusion.48
  87.8 3.6 %fusion.36 = bf16[512,1024]{1,0:T(8,128)(2,1)} fusion(s32[512]{0:T(512)S(1)} %add_add_fusion.1, bf16[256,1024]{1,0:T(8,128)(2,1)S(1)} %copy-done.33, bf16[256,1024]{1,0:T(8,128)(2,1)} %collective-permute-done.2, bf16[256,1024]{1,0:T(8,128)(2,1)S(1)} %copy-done.31, bf16[256,1024]{1,0:T(8,128)(2,1)} %add_convert_fusion.1), kind=kOutput, calls=%fused_computation.44 | convolution fusion | flops 1083179008 | bytes 3147776 | tf_op jit(solution)/shard_map/dot_general | solution.py:35
  95.7 3.1 %convolution_convert_fusion.6 = bf16[512,1024]{1,0:T(8,128)(2,1)} fusion(bf16[256,1024]{1,0:T(8,128)(2,1)} %collective-permute-done.9, bf16[256,1024]{1,0:T(8,128)(2,1)} %convert_element_type.93, bf16[512,256]{0,1:T(8,128)(2,1)} %collective-permute-done.8, bf16[512,256]{0,1:T(8,128)(2,1)S(1)} %fusion.53), kind=kOutput, calls=%fused_computation.46 | convolution fusion | flops 540540928 | bytes 2621440 | tf_op jit(solution)/shard_map/dot_general | solution.py:25
  98.8 6.0 %convolution_convert_fusion.1 = bf16[2048,1024]{1,0:T(8,128)(2,1)} fusion(bf16[2048,256]{1,0:T(8,128)(2,1)} %collective-permute-done.4, bf16[2048,256]{1,0:T(8,128)(2,1)S(1)} %copy-done.9, bf16[256,1024]{1,0:T(8,128)(2,1)} %collective-permute-done.5, bf16[256,1024]{1,0:T(8,128)(2,1)} %bitcast_select_fusion.grad_low), kind=kOutput, calls=%fused_computation.22 | convolution fusion | flops 2155872256 | bytes 7340032 | tf_op jit(solution)/shard_map/dot_general | solution.py:25
  104.8 5.9 %convolution_convert_fusion = bf16[512,4096]{1,0:T(8,128)(2,1)} fusion(bf16[256,4096]{1,0:T(8,128)(2,1)} %collective-permute-done.7, bf16[256,4096]{1,0:T(8,128)(2,1)S(1)} %copy-done.28, bf16[512,256]{1,0:T(8,128)(2,1)S(1)} %collective-permute-done.6, bf16[512,256]{1,0:T(8,128)(2,1)S(1)} %get-tuple-element.44), kind=kOutput, calls=%fused_computation.4 | convolution fusion | flops 2159017984 | bytes 8912896 | tf_op jit(solution)/shard_map/dot_general | solution.py:25
  110.7 69.3 %shard_map.265 = (bf16[256,1024]{1,0:T(8,128)(2,1)}, bf16[2,256,2048]{2,1,0:T(8,128)(2,1)}, f32[64,1024]{1,0:T(8,128)}, f32[16,4096]{1,0:T(8,128)}, f32[16,1024]{1,0:T(8,128)}) custom-call(bf16[256,1024]{1,0:T(8,128)(2,1)} %copy-done.5, bf16[1024,1024]{1,0:T(8,128)(2,1)} %copy-done.2, bf16[1024,1024]{1,0:T(8,128)(2,1)} %copy-done.1, ...), custom_call_target="tpu_custom_call" | custom-call | tf_op jit(solution)/shard_map/pallas_call | solution.py:451
  180.1 4.0 %fusion.5 = f32[512,1024]{1,0:T(8,128)S(1)} fusion(bf16[512,2048]{1,0:T(8,128)(2,1)} %bitcast.19, bf16[1024,1024]{1,0:T(8,128)(2,1)S(1)} %copy-done.27, bf16[1024,1024]{1,0:T(8,128)(2,1)S(1)} %copy-done.25), kind=kOutput, calls=%fused_computation.8 | convolution fusion | flops 2155872256 | bytes 8388608 | tf_op jit(solution)/shard_map/dot_general | solution.py:35
  185.1 3.2 %slice_bitcast_fusion.1 = (bf16[256,2048]{1,0:T(8,128)(2,1)}, bf16[256,2048]{1,0:T(8,128)(2,1)}) fusion(bf16[2,256,2048]{2,1,0:T(8,128)(2,1)} %get-tuple-element.48), kind=kLoop, calls=%fused_computation.77 | loop fusion | bytes 4194304 | tf_op jit(solution)/shard_map/slice | solution.py:806
  188.3 11.8 %collective-permute-done.10 = bf16[256,1024]{1,0:T(8,128)(2,1)S(1)} collective-permute-done((bf16[256,1024]{1,0:T(8,128)(2,1)S(1)}, bf16[256,1024]{1,0:T(8,128)(2,1)S(1)}, u32[]{:S(2)}, u32[]{:S(2)}) %collective-permute-start.10) | collective-permute-done | bytes 524320 | tf_op jit(solution)/shard_map/ppermute | solution.py:70
  200.1 3.3 %multiply_reduce_fusion = (f32[1024]{0:T(1024)S(1)}, f32[256]{0:T(256)S(1)}, f32[256]{0:T(256)S(1)}, f32[1024]{0:T(1024)S(1)}, f32[256,1024]{1,0:T(8,128)}) fusion(f32[256,1024]{1,0:T(8,128)S(1)} %copy-done.12, f32[256]{0:T(256)S(1)} %add_rsqrt_fusion, f32[256]{0:T(256)S(1)} %broadcast_multiply_fusion.2, bf16[256,1024]{1,0:T(8,128)(2,1)S(1)} %collective-permute-done.10, ...), kind=kOutput, calls=%fused_computation.75 | convolution fusion | flops 540014080 | bytes 6307840 | tf_op jit(solution)/shard_map/dot_general | solution.py:35
  209.3 2.9 %convolution_convert_fusion.5 = bf16[512,1024]{1,0:T(8,128)(2,1)} fusion(bf16[256,1024]{1,0:T(8,128)(2,1)} %collective-permute-done.12, bf16[256,1024]{1,0:T(8,128)(2,1)} %get-tuple-element.47, bf16[512,1024]{1,0:T(8,128)(2,1)S(1)} %copy-done.34), kind=kOutput, calls=%fused_computation.45 | convolution fusion | flops 539492352 | bytes 2621440 | tf_op jit(solution)/shard_map/dot_general | solution.py:25
  213.8 7.9 %collective-permute-done.11 = bf16[256,1024]{1,0:T(8,128)(2,1)S(1)} collective-permute-done((bf16[256,1024]{1,0:T(8,128)(2,1)S(1)}, bf16[256,1024]{1,0:T(8,128)(2,1)S(1)}, u32[]{:S(2)}, u32[]{:S(2)}) %collective-permute-start.11) | collective-permute-done | bytes 524320 | tf_op jit(solution)/shard_map/ppermute | solution.py:21
  221.7 3.6 %convolution_convert_fusion.2 = bf16[1024,1024]{1,0:T(8,128)(2,1)} fusion(bf16[1024,256]{0,1:T(8,128)(2,1)} %collective-permute-done.14, bf16[1024,256]{0,1:T(8,128)(2,1)S(1)} %copy-done.35, bf16[256,1024]{1,0:T(8,128)(2,1)S(1)} %collective-permute-done.15, bf16[256,1024]{1,0:T(8,128)(2,1)S(1)} %add_convert_fusion), kind=kOutput, calls=%fused_computation.33 | convolution fusion | flops 1078984704 | bytes 4194304 | tf_op jit(solution)/shard_map/dot_general | solution.py:25
  227.5 3.6 %fusion.19 = bf16[512,2048]{1,0:T(8,128)(2,1)} fusion(bf16[512,1024]{1,0:T(8,128)(2,1)S(1)} %copy-done.34, bf16[256,2048]{1,0:T(8,128)(2,1)S(1)} %get-tuple-element.65, bf16[256,2048]{1,0:T(8,128)(2,1)S(1)} %copy-done.15, bf16[256,2048]{1,0:T(8,128)(2,1)S(1)} %get-tuple-element.64, bf16[256,2048]{1,0:T(8,128)(2,1)S(1)} %copy-done.14), kind=kOutput, calls=%fused_computation.23 | convolution fusion | flops 2165309440 | bytes 7340032 | tf_op jit(solution)/shard_map/dot_general | solution.py:25
  231.1 42.8 %shard_map.266 = (f32[16,1024]{1,0:T(8,128)}, f32[16,2048]{1,0:T(8,128)}, f32[32,1024]{1,0:T(8,128)}, f32[8,128]{1,0:T(8,128)}) custom-call(bf16[16,32,1024]{2,1,0:T(8,128)(2,1)} %bitcast.76, bf16[16,32,2048]{2,1,0:T(8,128)(2,1)} %bitcast.74, bf16[16,64,1024]{2,1,0:T(8,128)(2,1)} %bitcast.73, f32[16,8,128]{2,1,0:T(8,128)} %pad.4.refs_3_), custom_call_target="tpu_custom_call" | custom-call | tf_op jit(solution)/shard_map/pallas_call | solution.py:307
  (157 shorter events, 43.8 us)
Async XLA Ops:
  0.6 32.8 %copy-start = (bf16[1024,1024]{1,0:T(8,128)(2,1)S(1)}, bf16[1024,1024]{1,0:T(8,128)(2,1)}, u32[]{:S(2)}) copy-start(bf16[1024,1024]{1,0:T(8,128)(2,1)} %param.21) | copy-start | bytes 6291460
  0.7 13.9 %collective-permute-start = (bf16[256,1024]{1,0:T(8,128)(2,1)}, bf16[256,1024]{1,0:T(8,128)(2,1)S(1)}, u32[]{:S(2)}, u32[]{:S(2)}) collective-permute-start(bf16[256,1024]{1,0:T(8,128)(2,1)} %bitcast.91), channel_id=1, source_target_pairs={{0,64},{64,0},{1,65},{65,1},{2,66},{66,2},{3,67},{67,3},{4,68},{68... | collective-permute-start | bytes 1572872 | tf_op jit(solution)/shard_map/ppermute | solution.py:21
  6.0 92.8 %collective-permute-start.5 = (bf16[256,1024]{1,0:T(8,128)(2,1)}, bf16[256,1024]{1,0:T(8,128)(2,1)}, u32[]{:S(2)}, u32[]{:S(2)}) collective-permute-start(bf16[256,1024]{1,0:T(8,128)(2,1)} %bitcast_select_fusion.grad_low), channel_id=1, source_target_pairs={{0,1},{1,0},{2,3},{3,2},{4,5},{5,4},{6,7},{7,6},{8,9},{9,8},{10,11... | collective-permute-start | bytes 1572872 | tf_op jit(solution)/shard_map/ppermute | solution.py:70
  18.5 14.7 %collective-permute-start.2 = (bf16[256,1024]{1,0:T(8,128)(2,1)}, bf16[256,1024]{1,0:T(8,128)(2,1)}, u32[]{:S(2)}, u32[]{:S(2)}) collective-permute-start(bf16[256,1024]{1,0:T(8,128)(2,1)} %add_convert_fusion.1), channel_id=1, source_target_pairs={{0,2},{1,3},{2,0},{3,1},{4,6},{5,7},{6,4},{7,5},{8,10},{9,11},{10,... | collective-permute-start | bytes 1572872 | tf_op jit(solution)/shard_map/ppermute | solution.py:70
  22.6 12.9 %copy-start.26 = (bf16[1024,1024]{1,0:T(8,128)(2,1)S(1)}, bf16[1024,1024]{1,0:T(8,128)(2,1)}, u32[]{:S(2)}) copy-start(bf16[1024,1024]{1,0:T(8,128)(2,1)} %param.23) | copy-start | bytes 6291460
  22.7 12.6 %collective-permute-start.1 = (bf16[256,1024]{1,0:T(8,128)(2,1)}, bf16[256,1024]{1,0:T(8,128)(2,1)S(1)}, u32[]{:S(2)}, u32[]{:S(2)}) collective-permute-start(bf16[256,1024]{1,0:T(8,128)(2,1)} %add_convert_fusion.1), channel_id=1, source_target_pairs={{0,1},{1,0},{2,3},{3,2},{4,5},{5,4},{6,7},{7,6},{8,9},{9,8},{10,11... | collective-permute-start | bytes 1572872 | tf_op jit(solution)/shard_map/ppermute | solution.py:70
  33.2 2.3 collective-permute-start.3
  56.5 18.6 %copy-start.3 = (bf16[256,1024]{1,0:T(8,128)(2,1)}, bf16[256,1024]{1,0:T(8,128)(2,1)S(1)}, u32[]{:S(2)}) copy-start(bf16[256,1024]{1,0:T(8,128)(2,1)S(1)} %get-tuple-element.36.mixed) | copy-start | bytes 1572868
  77.7 27.2 %collective-permute-start.7 = (bf16[256,4096]{1,0:T(8,128)(2,1)}, bf16[256,4096]{1,0:T(8,128)(2,1)}, u32[]{:S(2)}, u32[]{:S(2)}) collective-permute-start(bf16[256,4096]{1,0:T(8,128)(2,1)} %get-tuple-element.46), channel_id=1, source_target_pairs={{0,1},{1,0},{2,3},{3,2},{4,5},{5,4},{6,7},{7,6},{8,9},{9,8},{10,11... | collective-permute-start | bytes 6291464 | tf_op jit(solution)/shard_map/ppermute | solution.py:70
  81.8 17.0 %collective-permute-start.4 = (bf16[2048,256]{1,0:T(8,128)(2,1)}, bf16[2048,256]{1,0:T(8,128)(2,1)}, u32[]{:S(2)}, u32[]{:S(2)}) collective-permute-start(bf16[2048,256]{1,0:T(8,128)(2,1)} %get-tuple-element.43), channel_id=1, source_target_pairs={{0,1},{1,0},{2,3},{3,2},{4,5},{5,4},{6,7},{7,6},{8,9},{9,8},{10,11... | collective-permute-start | bytes 3145736 | tf_op jit(solution)/shard_map/ppermute | solution.py:70
  85.9 9.4 %collective-permute-start.9 = (bf16[256,1024]{1,0:T(8,128)(2,1)}, bf16[256,1024]{1,0:T(8,128)(2,1)}, u32[]{:S(2)}, u32[]{:S(2)}) collective-permute-start(bf16[256,1024]{1,0:T(8,128)(2,1)} %convert_element_type.93), channel_id=1, source_target_pairs={{0,1},{1,0},{2,3},{3,2},{4,5},{5,4},{6,7},{7,6},{8,9},{9,8},{10,11... | collective-permute-start | bytes 1572872 | tf_op jit(solution)/shard_map/ppermute | solution.py:70
  87.5 7.7 %collective-permute-start.8 = (bf16[512,256]{0,1:T(8,128)(2,1)}, bf16[512,256]{0,1:T(8,128)(2,1)}, u32[]{:S(2)}, u32[]{:S(2)}) collective-permute-start(bf16[512,256]{0,1:T(8,128)(2,1)} %fusion.52), channel_id=1, source_target_pairs={{0,1},{1,0},{2,3},{3,2},{4,5},{5,4},{6,7},{7,6},{8,9},{9,8},{10,11... | collective-permute-start | bytes 786440 | tf_op jit(solution)/shard_map/ppermute | solution.py:70
  95.1 126.6 %collective-permute-start.14 = (bf16[1024,256]{0,1:T(8,128)(2,1)}, bf16[1024,256]{0,1:T(8,128)(2,1)}, u32[]{:S(2)}, u32[]{:S(2)}) collective-permute-start(bf16[1024,256]{0,1:T(8,128)(2,1)} %fusion.47), channel_id=1, source_target_pairs={{0,1},{1,0},{2,3},{3,2},{4,5},{5,4},{6,7},{7,6},{8,9},{9,8},{10,11... | collective-permute-start | bytes 1572872 | tf_op jit(solution)/shard_map/ppermute | solution.py:70
  95.4 9.4 %collective-permute-start.6 = (bf16[512,256]{1,0:T(8,128)(2,1)}, bf16[512,256]{1,0:T(8,128)(2,1)S(1)}, u32[]{:S(2)}, u32[]{:S(2)}) collective-permute-start(bf16[512,256]{1,0:T(8,128)(2,1)} %copy-done.10), channel_id=1, source_target_pairs={{0,1},{1,0},{2,3},{3,2},{4,5},{5,4},{6,7},{7,6},{8,9},{9,8},{10,11... | collective-permute-start | bytes 786440 | tf_op jit(solution)/shard_map/ppermute | solution.py:70
  110.7 69.4 %copy-start.25 = (bf16[1024,1024]{1,0:T(8,128)(2,1)S(1)}, bf16[1024,1024]{1,0:T(8,128)(2,1)}, u32[]{:S(2)}) copy-start(bf16[1024,1024]{1,0:T(8,128)(2,1)} %param.22) | copy-start | bytes 6291460
  110.7 69.4 %copy-start.27 = (bf16[1024,1024]{1,0:T(8,128)(2,1)S(1)}, bf16[1024,1024]{1,0:T(8,128)(2,1)}, u32[]{:S(2)}) copy-start(bf16[1024,1024]{1,0:T(8,128)(2,1)} %param.23) | copy-start | bytes 6291460
  184.0 41.3 %collective-permute-start.13 = (bf16[512,2048]{1,0:T(8,128)(2,1)}, bf16[512,2048]{1,0:T(8,128)(2,1)}, u32[]{:S(2)}, u32[]{:S(2)}) collective-permute-start(bf16[512,2048]{1,0:T(8,128)(2,1)} %bitcast.19), channel_id=1, source_target_pairs={{0,1},{1,0},{2,3},{3,2},{4,5},{5,4},{6,7},{7,6},{8,9},{9,8},{10,11... | collective-permute-start | bytes 6291464 | tf_op jit(solution)/shard_map/ppermute | solution.py:70
  184.2 15.9 %collective-permute-start.10 = (bf16[256,1024]{1,0:T(8,128)(2,1)S(1)}, bf16[256,1024]{1,0:T(8,128)(2,1)S(1)}, u32[]{:S(2)}, u32[]{:S(2)}) collective-permute-start(bf16[256,1024]{1,0:T(8,128)(2,1)S(1)} %slice.118), channel_id=1, source_target_pairs={{0,2},{1,3},{2,0},{3,1},{4,6},{5,7},{6,4},{7,5},{8,10},{9,11},{10,... | collective-permute-start | bytes 1572872 | tf_op jit(solution)/shard_map/ppermute | solution.py:70
  184.9 24.4 %collective-permute-start.12 = (bf16[256,1024]{1,0:T(8,128)(2,1)}, bf16[256,1024]{1,0:T(8,128)(2,1)}, u32[]{:S(2)}, u32[]{:S(2)}) collective-permute-start(bf16[256,1024]{1,0:T(8,128)(2,1)} %get-tuple-element.47), channel_id=1, source_target_pairs={{0,1},{1,0},{2,3},{3,2},{4,5},{5,4},{6,7},{7,6},{8,9},{9,8},{10,11... | collective-permute-start | bytes 1572872 | tf_op jit(solution)/shard_map/ppermute | solution.py:70
  185.1 15.0 %copy-start.12 = (f32[256,1024]{1,0:T(8,128)S(1)}, f32[256,1024]{1,0:T(8,128)}, u32[]{:S(2)}) copy-start(f32[256,1024]{1,0:T(8,128)} %copy-done.11) | copy-start | bytes 3145732
  206.3 15.4 %collective-permute-start.15 = (bf16[256,1024]{1,0:T(8,128)(2,1)S(1)}, bf16[256,1024]{1,0:T(8,128)(2,1)S(1)}, u32[]{:S(2)}, u32[]{:S(2)}) collective-permute-start(bf16[256,1024]{1,0:T(8,128)(2,1)S(1)} %add_convert_fusion), channel_id=1, source_target_pairs={{0,1},{1,0},{2,3},{3,2},{4,5},{5,4},{6,7},{7,6},{8,9},{9,8},{10,11... | collective-permute-start | bytes 1572872 | tf_op jit(solution)/shard_map/ppermute | solution.py:70
  207.7 14.0 %collective-permute-start.11 = (bf16[256,1024]{1,0:T(8,128)(2,1)S(1)}, bf16[256,1024]{1,0:T(8,128)(2,1)S(1)}, u32[]{:S(2)}, u32[]{:S(2)}) collective-permute-start(bf16[256,1024]{1,0:T(8,128)(2,1)S(1)} %fusion.43), channel_id=1, source_target_pairs={{0,64},{64,0},{1,65},{65,1},{2,66},{66,2},{3,67},{67,3},{4,68},{68... | collective-permute-start | bytes 1572872 | tf_op jit(solution)/shard_map/ppermute | solution.py:21
  231.1 49.5 %copy-start.21 = (f32[16,1024]{1,0:T(8,128)S(1)}, f32[16,1024]{1,0:T(8,128)}, u32[]{:S(2)}) copy-start(f32[16,1024]{1,0:T(8,128)} %get-tuple-element.55) | copy-start | bytes 196612
  231.1 50.1 %copy-start.20 = (f32[16,4096]{1,0:T(8,128)S(1)}, f32[16,4096]{1,0:T(8,128)}, u32[]{:S(2)}) copy-start(f32[16,4096]{1,0:T(8,128)} %get-tuple-element.56) | copy-start | bytes 786436
  (28 other events, 118.7 us)

commit v5 on v4

--- a/solution.py
+++ b/solution.py
@@ -43,14 +43,6 @@
     inverse = lax.rsqrt(variance + EPS)
     unit = center * inverse
     return (unit * gain + bias, unit, inverse)
-
-
-def norm_backward(grad, unit, inverse, gain):
-    scaled = grad * gain
-    mean_one = jnp.mean(scaled, axis=-1, keepdims=True)
-    mean_two = jnp.mean(scaled * unit, axis=-1, keepdims=True)
-    grad_input = inverse * (scaled - mean_one - unit * mean_two)
-    return (grad_input, jnp.sum(grad * unit, axis=0), jnp.sum(grad, axis=0))
 
 
 def segment_tables(lengths_row, spans_row, places):
@@ -165,21 +157,35 @@
     return [stage_partner(quarter, stage, x, z, seq) for quarter, stage in pairs]
 
 
+def relative_place(quarter, z, x, z_there, x_there):
+    first, order = QUARTERS[quarter]
+
+    def position(value):
+        if order == NEAR:
+            return 2 * value - lax.div(value, 2) - 4 * lax.div(value, 3)
+        return value + lax.div(value, 2) * (1 - 2 * lax.rem(value, 2))
+
+    z_place, x_place = position(flip(z, z_there)), position(flip(x, x_there))
+    return x_place * 4 + z_place if first == "x" else z_place * 4 + x_place
+
+
 class Halving:
     def __init__(self, shapes, sources, results, scratch):
         self.shapes, self.sources, self.results = shapes, sources, results
         scratch = list(scratch)
         count = len(shapes)
-        self.totals = scratch[:count]
+        self.work = scratch[:count]
         self.landings = [scratch[count + 5 * job : count + 5 * job + 5] for job in range(count)]
         self.local_sem, self.send_sem, self.recv_sem = scratch[6 * count :]
         self.z, self.x, self.seq = place_here()
         self.y = lax.div(self.seq, 2)
 
     @staticmethod
-    def scratch(shapes):
+    def scratch(shapes, made):
         count = len(shapes)
-        shapes_of = [(4, 8, 2 * rows, width // 4) for rows, width in shapes]
+        shapes_of = [
+            (4, 16 if own else 8, 2 * rows, width // 4) for (rows, width), own in zip(shapes, made)
+        ]
         for rows, width in shapes:
             shapes_of += [(4, blocks, 2 * rows, width // 4) for blocks in (8, 4, 2, 1)]
             shapes_of.append((4, rows, width // 4))
@@ -189,13 +195,10 @@
             pltpu.SemaphoreType.DMA((count, 4, 5)),
         ]
 
-    def columns(self, job, quarter):
+    def start(self, job):
         width = self.shapes[job][1] // 4
-        return pl.ds(quarter * width, width)
-
-    def start(self, job):
         for quarter in range(4):
-            columns = self.columns(job, quarter)
+            columns = pl.ds(quarter * width, width)
             for index in range(8):
                 outer, inner = index // 4, index % 4
                 there = block_place(quarter, outer + 2, inner, self.x, self.z)
@@ -209,21 +212,31 @@
                 ).start()
                 pltpu.make_async_copy(
                     self.sources[job].at[here, :, columns],
-                    self.totals[job].at[quarter, index],
+                    self.work[job].at[quarter, index],
                     self.local_sem.at[job, quarter],
                 ).start()
+
+    def store(self, job, quarter, value):
+        rows = 2 * self.shapes[job][0]
+        for index in range(16):
+            place = relative_place(quarter, self.z, self.x, index // 4, index % 4)
+            self.work[job][quarter, place] = value[index * rows : (index + 1) * rows].astype(
+                jnp.bfloat16
+            )
+        self.copy(job, quarter, 0).start()
 
     def copy(self, job, quarter, stage):
         rows = self.shapes[job][0]
         target = self.landings[job][stage].at[quarter]
         if stage == 0:
-            source = target
+            made = self.sources[job] is None
+            source = self.work[job].at[quarter, pl.ds(8, 8)] if made else target
         elif stage < 4:
             size = 8 >> stage
-            source = self.totals[job].at[quarter, pl.ds(size, size)]
+            source = self.work[job].at[quarter, pl.ds(size, size)]
         else:
             away = pl.multiple_of((1 - self.y) * rows, 16)
-            source = self.totals[job].at[quarter, 0, pl.ds(away, rows)]
+            source = self.work[job].at[quarter, 0, pl.ds(away, rows)]
         return remote(
             source,
             target,
@@ -233,97 +246,30 @@
         )
 
     def finish(self, job, stage):
-        rows = self.shapes[job][0]
+        rows, width = self.shapes[job]
         for quarter in range(4):
-            total = self.totals[job].at[quarter]
+            work = self.work[job].at[quarter]
             landing = self.landings[job][stage].at[quarter]
             self.copy(job, quarter, stage).wait_recv()
-            if stage == 0:
-                pltpu.make_async_copy(total, total, self.local_sem.at[job, quarter]).wait()
+            if stage == 0 and self.sources[job] is not None:
+                pltpu.make_async_copy(landing, work, self.local_sem.at[job, quarter]).wait()
             if stage < 4:
-                add_blocks(8 >> stage, total, landing)
+                add_blocks(8 >> stage, work, landing)
                 self.copy(job, quarter, stage + 1).start()
             else:
                 mine = pl.multiple_of(self.y * rows, 16)
-                self.results[job][:, self.columns(job, quarter)] = total[
-                    0, pl.ds(mine, rows)
-                ].astype(jnp.float32) + landing[...].astype(jnp.float32)
+                total = work[0, pl.ds(mine, rows)].astype(jnp.float32)
+                first = quarter * width // 4
+                result = self.results[job][first // 4096 if width == 4096 else first // 1024]
+                result[:, pl.ds(first % result.shape[1], width // 4)] = total + landing[
+                    ...
+                ].astype(jnp.float32)
 
     def drain(self):
         for job in range(len(self.shapes)):
             for quarter in range(4):
                 for stage in range(5):
                     self.copy(job, quarter, stage).wait_send()
-
-
-def reduce_kernel(shapes, *refs):
-    count = len(shapes)
-    refs = list(refs)
-    take = lambda n: [refs.pop(0) for _ in range(n)]
-    sources, vector = take(count), take(1)[0]
-    results, vector_result = take(count), take(1)[0]
-    vector_total, vector_landing, vector_send, vector_recv = take(4)
-    halving = Halving(shapes, sources, results, refs)
-    z, x, seq = place_here()
-    core = {"seq": flip(seq, 1)}
-    enter(ring_partners(z, x, seq) + [core])
-
-    devices = [core] + [stage_partner(0, stage, x, z, seq) for stage in range(5)]
-    vector_stages = list(zip(devices, (0, 8, 4, 2, 1, 0), (0, 16, 24, 28, 30, 31), (16, 8, 4, 2, 1, 1)))
-
-    def vector_copy(step):
-        device, first, landing, size = vector_stages[step]
-        return remote(
-            vector_total.at[pl.ds(first, size)],
-            vector_landing.at[pl.ds(landing, size)],
-            vector_send.at[step],
-            vector_recv.at[step],
-            device,
-        )
-
-    def vector_finish(step):
-        _, _, landing, size = vector_stages[step]
-        vector_copy(step).wait()
-        vector_total[pl.ds(0, size)] += vector_landing[pl.ds(landing, size)]
-
-    for index in range(16):
-        vector_total[index] = vector[block_place(0, index // 4, index % 4, x, z)]
-    vector_copy(0).start()
-    for job in range(count):
-        halving.start(job)
-    for stage in range(5):
-        for job in range(count):
-            halving.finish(job, stage)
-        vector_finish(stage)
-        vector_copy(stage + 1).start()
-    vector_finish(5)
-    vector_result[...] = vector_total[0]
-    halving.drain()
-
-
-def reduce_shares(shares, vectors, collective_id):
-    shapes = [(share.shape[1] // 2, share.shape[2]) for share in shares]
-    count = len(shares)
-    return pl.pallas_call(
-        functools.partial(reduce_kernel, shapes),
-        out_shape=[jax.ShapeDtypeStruct(shape, jnp.float32) for shape in shapes]
-        + [jax.ShapeDtypeStruct(vectors.shape[1:], jnp.float32)],
-        in_specs=[pl.BlockSpec(memory_space=pl.ANY)] * count
-        + [pl.BlockSpec(memory_space=pltpu.VMEM)],
-        out_specs=[pl.BlockSpec(memory_space=pltpu.VMEM)] * (count + 1),
-        scratch_shapes=[
-            pltpu.VMEM(vectors.shape, jnp.float32),
-            pltpu.VMEM((32,) + vectors.shape[1:], jnp.float32),
-            pltpu.SemaphoreType.DMA((6,)),
-            pltpu.SemaphoreType.DMA((6,)),
-        ]
-        + Halving.scratch(shapes),
-        compiler_params=pltpu.CompilerParams(
-            collective_id=collective_id,
-            has_side_effects=True,
-            vmem_limit_bytes=56 * 2**20,
-        ),
-    )(*shares, vectors)
 
 
 def attention_backward_pair(query, keys, values, share, inverse, grad, mixed, lows):
@@ -363,116 +309,6 @@
     out = rows_product(keys[...], lows[...])
     out = jnp.concatenate([out[:64, :here], out[64:, here:]], axis=0)
     return (out.T * 0.125).astype(jnp.bfloat16), grad_keys, grad_values
-
-
-def backward_kernel(
-    shapes, query, keys, values, shares, inverses, grad, mixed, share_one, share_two, share_three,
-    grad_query, both, result_one, result_two, result_three,
-    lows, held, held_sem, parts, landing, swap_send, swap_recv, *halving_refs,
-):
-    halving = Halving(
-        shapes,
-        (share_one, share_two, share_three),
-        (result_one, result_two, result_three),
-        halving_refs,
-    )
-    z, x, seq = place_here()
-    core = {"seq": flip(seq, 1)}
-    pairs = shares.shape[0]
-    here, width = query.shape
-
-    def fetch(pair):
-        slot = lax.rem(pair, 2)
-        return pltpu.make_async_copy(shares.at[pair], held.at[slot], held_sem.at[slot])
-
-    fetch(0).start()
-    enter(ring_partners(z, x, seq) + [core])
-    for job in range(3):
-        halving.start(job)
-
-    def one_pair(pair, carry):
-        @pl.when(pair + 1 < pairs)
-        def _():
-            fetch(pair + 1).start()
-
-        fetch(pair).wait()
-        columns = pl.ds(pl.multiple_of(pair * 128, 128), 128)
-        others = pl.ds(pl.multiple_of(width + pair * 128, 128), 128)
-        out, grad_keys, grad_values = attention_backward_pair(
-            query[:, columns],
-            keys.at[:, columns],
-            values.at[:, columns],
-            held.at[lax.rem(pair, 2)],
-            inverses[pair],
-            grad[:, columns],
-            mixed[:, columns],
-            lows,
-        )
-        grad_query[:, columns] = out
-        for index, (one, two) in enumerate(zip(grad_keys, grad_values)):
-            part, rows = index * 128 // here, pl.ds(index * 128 % here, 128)
-            parts[part, rows, columns] = one
-            parts[part, rows, others] = two
-        for step in range(2):
-            for place in (columns, others):
-                remote(
-                    parts.at[2 * step + 1, :, place],
-                    landing.at[step, :, place],
-                    swap_send,
-                    swap_recv,
-                    core,
-                ).start()
-        return carry
-
-    lax.fori_loop(0, 5, one_pair, 0)
-    halving.finish(0, 0)
-    lax.fori_loop(5, pairs, one_pair, 0)
-    swapped = remote(landing, landing, swap_send, swap_recv, core)
-    swapped.wait_recv()
-    for step in range(2):
-        both[step] = (
-            parts[2 * step].astype(jnp.float32) + landing[step].astype(jnp.float32)
-        ).astype(jnp.bfloat16)
-    for job in (1, 2):
-        halving.finish(job, 0)
-    for stage in range(1, 5):
-        for job in range(3):
-            halving.finish(job, stage)
-    halving.drain()
-    swapped.wait_send()
-
-
-def backward(query, keys, values, shares, inverses, grad, mixed, weights, collective_id):
-    here, width = query.shape
-    span = keys.shape[0]
-    shapes = [(share.shape[1] // 2, share.shape[2]) for share in weights]
-    inside = pl.BlockSpec(memory_space=pltpu.VMEM)
-    outside = pl.BlockSpec(memory_space=pl.ANY)
-    return pl.pallas_call(
-        functools.partial(backward_kernel, shapes),
-        in_specs=[inside, inside, inside, outside, inside, inside, inside] + [outside] * 3,
-        out_specs=[inside] * 5,
-        out_shape=[
-            jax.ShapeDtypeStruct((here, width), jnp.bfloat16),
-            jax.ShapeDtypeStruct((2, here, 2 * width), jnp.bfloat16),
-        ]
-        + [jax.ShapeDtypeStruct(shape, jnp.float32) for shape in shapes],
-        scratch_shapes=[
-            pltpu.VMEM((span, 2 * here), jnp.bfloat16),
-            pltpu.VMEM((2, span, 2 * here), jnp.bfloat16),
-            pltpu.SemaphoreType.DMA((2,)),
-            pltpu.VMEM((4, here, 2 * width), jnp.bfloat16),
-            pltpu.VMEM((2, here, 2 * width), jnp.bfloat16),
-            pltpu.SemaphoreType.DMA,
-            pltpu.SemaphoreType.DMA,
-        ]
-        + Halving.scratch(shapes),
-        compiler_params=pltpu.CompilerParams(
-            collective_id=collective_id,
-            has_side_effects=True,
-            vmem_limit_bytes=56 * 2**20,
-        ),
-    )(query, keys, values, shares, inverses, grad, mixed, *weights)
 
 
 def attention_forward_kernel(
@@ -555,6 +391,327 @@
         ],
         compiler_params=pltpu.CompilerParams(vmem_limit_bytes=40 * 2**20),
     )(query, keys, values, *tables, slopes)
+
+
+def backward_kernel(
+    shapes, query, keys, values, shares, inverses, grad, mixed, share_one, share_two, share_three,
+    w_query, w_key, w_value, w_skip, one_rows, joined_kept, joined_other, unit, grad_residual,
+    inverse_one, gain_one, gain_two_sum, bias_two_sum,
+    grad_own, grad_stored, vectors, *refs,
+):
+    refs = list(refs)
+    take = lambda n: [refs.pop(0) for _ in range(n)]
+    results = [take(1), take(1), take(1), take(1), take(2), take(1)]
+    lows, held, held_sem, parts, landing, swap_send, swap_recv = take(7)
+    far_landing, grad_query, query_landing, side_send, side_recv = take(5)
+    columns_two, heads, load_sem, rows_one, kept, other, units, residuals = take(8)
+    grad_normed, normed_send, normed_landing, grad_hidden, hidden_landing = take(5)
+    stored_send, stored_landing, vector_landing, vector_send, vector_recv = take(5)
+    halving = Halving(shapes, (share_one, share_two, share_three, None, None, None), results, refs)
+    z, x, seq = place_here()
+    core = {"seq": flip(seq, 1)}
+    far = {"seq": flip(seq, 2)}
+    section = {"section": 1 - lax.axis_index("section")}
+    pairs = shares.shape[0]
+    here, width = query.shape
+
+    def fetch(pair):
+        slot = lax.rem(pair, 2)
+        return pltpu.make_async_copy(shares.at[pair], held.at[slot], held_sem.at[slot])
+
+    def load(index):
+        source, target = (
+            (keys, columns_two.at[pl.ds(0, width)]),
+            (values, columns_two.at[pl.ds(width, width)]),
+            (w_query, heads.at[0]),
+            (w_key, heads.at[1]),
+            (w_value, heads.at[2]),
+            (one_rows, rows_one),
+            (unit, units),
+            (grad_residual, residuals),
+            (joined_kept, kept),
+            (joined_other, other),
+            (w_skip, columns_two),
+        )[index]
+        return pltpu.make_async_copy(source, target, load_sem.at[index])
+
+    def side(index):
+        source, target, device = (
+            (parts.at[0], far_landing.at[0], core),
+            (parts.at[2], far_landing.at[1], core),
+            (grad_query, query_landing, core),
+            (normed_send, normed_landing, far),
+            (grad_hidden, hidden_landing, core),
+            (stored_send, stored_landing, section),
+        )[index]
+        return remote(source, target, side_send.at[index], side_recv.at[index], device)
+
+    vector_devices = [core] + [stage_partner(0, stage, x, z, seq) for stage in range(5)]
+
+    def vector_copy(step):
+        return remote(
+            vectors,
+            vector_landing.at[step],
+            vector_send.at[step],
+            vector_recv.at[step],
+            vector_devices[step],
+        )
+
+    def vector_finish(step):
+        vector_copy(step).wait()
+        vectors[...] += vector_landing[step]
+        if step < 5:
+            vector_copy(step + 1).start()
+
+    load(0).start()
+    load(1).start()
+    fetch(0).start()
+    enter(ring_partners(z, x, seq) + [core, section])
+    for job in range(3):
+        halving.start(job)
+    for index in range(2, 10):
+        load(index).start()
+    load(0).wait()
+    load(1).wait()
+
+    def one_pair(pair, carry):
+        @pl.when(pair + 1 < pairs)
+        def _():
+            fetch(pair + 1).start()
+
+        fetch(pair).wait()
+        columns = pl.ds(pl.multiple_of(pair * 128, 128), 128)
+        others = pl.ds(pl.multiple_of(width + pair * 128, 128), 128)
+        out, grad_keys, grad_values = attention_backward_pair(
+            query[:, columns],
+            columns_two.at[pl.ds(0, width), columns],
+            columns_two.at[pl.ds(width, width), columns],
+            held.at[lax.rem(pair, 2)],
+            inverses[pair],
+            grad[:, columns],
+            mixed[:, columns],
+            lows,
+        )
+        grad_query[:, columns] = out
+        for index, (one, two) in enumerate(zip(grad_keys, grad_values)):
+            part, rows = index * 128 // here, pl.ds(index * 128 % here, 128)
+            parts[part, rows, columns] = one
+            parts[part, rows, others] = two
+        for step in range(2):
+            for place in (columns, others):
+                remote(
+                    parts.at[2 * step + 1, :, place],
+                    landing.at[step, :, place],
+                    swap_send,
+                    swap_recv,
+                    core,
+                ).start()
+        return carry
+
+    lax.fori_loop(0, 5, one_pair, 0)
+    halving.finish(0, 0)
+    lax.fori_loop(5, pairs, one_pair, 0)
+    side(2).start()
+    load(10).start()
+    swapped = remote(landing, landing, swap_send, swap_recv, core)
+    swapped.wait_recv()
+    for step in (1, 0):
+
+        def add_rows(index, carry):
+            rows = pl.ds(pl.multiple_of(index * 64, 64), 64)
+            parts[2 * step, rows] = (
+                parts[2 * step, rows].astype(jnp.float32)
+                + landing[step, rows].astype(jnp.float32)
+            ).astype(jnp.bfloat16)
+            return carry
+
+        lax.fori_loop(0, here // 64, add_rows, 0)
+        side(step).start()
+    for index in range(2, 5):
+        load(index).wait()
+
+    def from_parts(part, rows):
+        return back_product(parts[part, :, pl.ds(0, width)], heads[1, rows]) + back_product(
+            parts[part, :, pl.ds(width, width)], heads[2, rows]
+        )
+
+    def far_rows(index, carry):
+        rows = pl.ds(pl.multiple_of(index * 256, 256), 256)
+        normed_send[:, rows] = from_parts(2, rows).astype(jnp.bfloat16)
+        return carry
+
+    lax.fori_loop(0, width // 256, far_rows, 0)
+    side(3).start()
+    halving.finish(1, 0)
+    halving.finish(2, 0)
+
+    def own_rows(index, carry):
+        rows = pl.ds(pl.multiple_of(index * 256, 256), 256)
+        grad_normed[:, rows] = from_parts(0, rows) + back_product(grad_query[...], heads[0, rows])
+        return carry
+
+    lax.fori_loop(0, width // 256, own_rows, 0)
+    load(5).wait()
+    side(2).wait_recv()
+    for quarter in range(4):
+        columns = pl.ds(quarter * 256, 256)
+        halving.store(
+            3,
+            quarter,
+            project(rows_one[:, pl.ds(0, here)], grad_query[:, columns])
+            + project(rows_one[:, pl.ds(here, here)], query_landing[:, columns]),
+        )
+    side(0).wait_recv()
+    side(1).wait_recv()
+    for quarter in range(4):
+        columns = pl.ds(quarter * 512, 512)
+        halving.store(
+            4,
+            quarter,
+            project(rows_one[:, pl.ds(0, here)], parts[0, :, columns])
+            + project(rows_one[:, pl.ds(here, here)], far_landing[0, :, columns])
+            + project(rows_one[:, pl.ds(2 * here, here)], parts[2, :, columns])
+            + project(rows_one[:, pl.ds(3 * here, here)], far_landing[1, :, columns]),
+        )
+    halving.finish(0, 1)
+    load(6).wait()
+    load(7).wait()
+    side(3).wait_recv()
+
+    def norm_rows(index, sums):
+        rows = pl.ds(pl.multiple_of(index * 32, 32), 32)
+        grads = grad_normed[rows] + normed_landing[rows].astype(jnp.float32)
+        ones = units[rows]
+        scaled = grads * gain_one[...]
+        value = scaled - mean_rows(scaled) - ones * mean_rows(scaled * ones)
+        grad_hidden[rows] = (residuals[rows] + inverse_one[rows] * value).astype(jnp.bfloat16)
+        return (
+            sums[0] + jnp.sum(grads * ones, axis=0, keepdims=True),
+            sums[1] + jnp.sum(grads, axis=0, keepdims=True),
+        )
+
+    nothing = jnp.zeros((1, width), jnp.float32)
+    gain_sum, bias_sum = lax.fori_loop(0, here // 32, norm_rows, (nothing, nothing))
+    side(4).start()
+    vectors[...] = jnp.concatenate(
+        [gain_sum, bias_sum, gain_two_sum[...], bias_two_sum[...], jnp.zeros((4, width), jnp.float32)],
+        axis=0,
+    )
+    vector_copy(0).start()
+    load(10).wait()
+
+    def stored_rows(index, carry):
+        rows = pl.ds(pl.multiple_of(index * 256, 256), 256)
+        below = pl.ds(pl.multiple_of(width + index * 256, 256), 256)
+        stored_send[:, rows] = back_product(grad_hidden[...], columns_two[below]).astype(
+            jnp.bfloat16
+        )
+        return carry
+
+    lax.fori_loop(0, width // 256, stored_rows, 0)
+    side(5).start()
+    halving.finish(1, 1)
+    halving.finish(2, 1)
+    load(8).wait()
+    load(9).wait()
+    side(4).wait_recv()
+    for quarter in range(4):
+        columns = pl.ds(quarter * 256, 256)
+        halving.store(
+            5,
+            quarter,
+            project(kept[...], grad_hidden[:, columns])
+            + project(other[...], hidden_landing[:, columns]),
+        )
+    vector_finish(0)
+
+    def own_grads(index, carry):
+        rows = pl.ds(pl.multiple_of(index * 256, 256), 256)
+        grad_own[:, rows] = back_product(grad_hidden[...], columns_two[rows]).astype(jnp.bfloat16)
+        return carry
+
+    lax.fori_loop(0, width // 256, own_grads, 0)
+    for stage in range(2, 7):
+        if stage < 5:
+            for job in range(3):
+                halving.finish(job, stage)
+        for job in range(3, 6):
+            halving.finish(job, stage - 2)
+        vector_finish(stage - 1)
+    side(5).wait_recv()
+    grad_stored[...] = stored_landing[...]
+    halving.drain()
+    swapped.wait_send()
+    for index in range(6):
+        side(index).wait_send()
+
+
+def backward(
+    query, keys, values, shares, inverses, grad, mixed, weights, tail, small, collective_id
+):
+    here, width = query.shape
+    span = keys.shape[0]
+    shapes = [(share.shape[1] // 2, share.shape[2]) for share in weights]
+    shapes += [(width // 64, width), (width // 64, 2 * width), (width // 32, width)]
+    made = (False, False, False, True, True, True)
+    inside = pl.BlockSpec(memory_space=pltpu.VMEM)
+    outside = pl.BlockSpec(memory_space=pl.ANY)
+    result_shapes = shapes[:4] + [shapes[3], shapes[3]] + shapes[5:]
+    rows_shape = (here, width)
+    low_rows = pltpu.VMEM(rows_shape, jnp.bfloat16)
+    full_rows = pltpu.VMEM(rows_shape, jnp.float32)
+    dma = pltpu.SemaphoreType.DMA
+    return pl.pallas_call(
+        functools.partial(backward_kernel, shapes),
+        in_specs=[inside, outside, outside, outside, inside, inside, inside]
+        + [outside] * (3 + len(tail))
+        + [inside] * len(small),
+        out_specs=[inside] * (3 + len(result_shapes)),
+        out_shape=[
+            jax.ShapeDtypeStruct(rows_shape, jnp.bfloat16),
+            jax.ShapeDtypeStruct(rows_shape, jnp.bfloat16),
+            jax.ShapeDtypeStruct((8, width), jnp.float32),
+        ]
+        + [jax.ShapeDtypeStruct(shape, jnp.float32) for shape in result_shapes],
+        scratch_shapes=[
+            pltpu.VMEM((span, 2 * here), jnp.bfloat16),
+            pltpu.VMEM((2, span, 2 * here), jnp.bfloat16),
+            dma((2,)),
+            pltpu.VMEM((4, here, 2 * width), jnp.bfloat16),
+            pltpu.VMEM((2, here, 2 * width), jnp.bfloat16),
+            dma,
+            dma,
+            pltpu.VMEM((2, here, 2 * width), jnp.bfloat16),
+            low_rows,
+            low_rows,
+            dma((6,)),
+            dma((6,)),
+            pltpu.VMEM((2 * width, width), jnp.bfloat16),
+            pltpu.VMEM((3, width, width), jnp.bfloat16),
+            dma((11,)),
+            pltpu.VMEM((width // 2, span), jnp.bfloat16),
+            pltpu.VMEM((width, here), jnp.bfloat16),
+            pltpu.VMEM((width, here), jnp.bfloat16),
+            full_rows,
+            full_rows,
+            full_rows,
+            low_rows,
+            low_rows,
+            low_rows,
+            low_rows,
+            low_rows,
+            low_rows,
+            pltpu.VMEM((6, 8, width), jnp.float32),
+            dma((6,)),
+            dma((6,)),
+        ]
+        + Halving.scratch(shapes, made),
+        compiler_params=pltpu.CompilerParams(
+            collective_id=collective_id,
+            has_side_effects=True,
+            vmem_limit_bytes=62 * 2**20,
+        ),
+    )(query, keys, values, shares, inverses, grad, mixed, *weights, *tail, *small)
 
 
 def mean_rows(value):
@@ -776,7 +933,22 @@
     mixed_mine = low(back_product(select_mine, mixed_rows))
     mixed_other = swap_core(low(back_product(select_other, mixed_rows)))
     out_share = pair_product(mixed_mine, mixed_other, grad_attn, grad_attn_other)
-    grad_query, both_mine, down_sum, up_sum, out_sum = backward(
+    one_rows = low(back_product(select_mine, normed_all))
+    joined = jnp.concatenate([own_rows, partner], axis=1)
+    joined_mine = low(back_product(core_selector(core, 2 * model_width), joined))
+    joined_other = swap_core(low(back_product(core_selector(1 - core, 2 * model_width), joined)))
+    (
+        grad_own,
+        grad_stored,
+        sums,
+        down_sum,
+        up_sum,
+        out_sum,
+        query_sum,
+        key_sum,
+        value_sum,
+        skip_sum,
+    ) = backward(
         query,
         keys_all,
         values_all,
@@ -785,50 +957,23 @@
         grad_mixed,
         mixed_rows,
         [down_share, up_share, out_share],
+        [
+            w_query,
+            w_key,
+            w_value,
+            w_skip,
+            one_rows,
+            joined_mine,
+            joined_other,
+            unit_one,
+            grad_residual,
+        ],
+        [inverse_one, gain_one[None], grad_gain_two, grad_bias_two],
         1,
     )
-    both_mine = both_mine.reshape(2 * rows_here, 2 * model_width)
-    both_far = swap_core(both_mine)
-    grad_query_other = swap_core(grad_query)
-    w_both = jnp.concatenate([w_key, w_value], axis=1)
-    normed_part = back_product(both_mine, w_both)
-    normed_far = partner_of(low(normed_part[rows_here:]), "seq", 2)
-    grad_normed_one = (
-        back_product(grad_query, w_query)
-        + normed_part[:rows_here]
-        + normed_far.astype(jnp.float32)
-    )
-    one_rows = low(back_product(select_mine, normed_all))
-    query_share = low(
-        project(one_rows[:, : 2 * rows_here], jnp.concatenate([grad_query, grad_query_other], axis=0))
-    )
-    both_rows = jnp.concatenate(
-        [both_mine[:rows_here], both_far[:rows_here], both_mine[rows_here:], both_far[rows_here:]],
-        axis=0,
-    )
-    both_share = low(project(one_rows, both_rows))
-
-    grad_hidden_norm, grad_gain_one, grad_bias_one = norm_backward(
-        grad_normed_one, unit_one, inverse_one, gain_one
-    )
-    grad_hidden = low(grad_residual + grad_hidden_norm)
-    grad_hidden_other = swap_core(grad_hidden)
-    grad_partner = low(back_product(grad_hidden, w_second))
-    grad_stored = from_partner(grad_partner, "section", 0)
-    grad_own = low(back_product(grad_hidden, w_first))
-    joined = jnp.concatenate([own_rows, partner], axis=1)
-    joined_mine = low(back_product(core_selector(core, 2 * model_width), joined))
-    joined_other = swap_core(low(back_product(core_selector(1 - core, 2 * model_width), joined)))
-    skip_share = pair_product(joined_mine, joined_other, grad_hidden, grad_hidden_other)
-    vectors = jnp.stack(
-        [grad_gain_one, grad_bias_one, grad_gain_two[0], grad_bias_two[0]]
-    )
-    vectors = vectors.reshape(4, 16, 4, 16).transpose(1, 2, 0, 3).reshape(16, 4, 64)
-    vectors = jnp.pad(vectors, ((0, 0), (0, 4), (0, 64)))
-    query_sum, both_sum, skip_sum, sums = reduce_shares(
-        [by_dp(query_share), by_dp(both_share), skip_share], vectors, 2
-    )
-    sums = lax.dynamic_index_in_dim(sums, seq, 0, False)[:64].reshape(4, 16)
+    shard = lax.axis_index("dp") * 4 + seq
+    piece = model_width // 64
+    sums = lax.dynamic_slice(sums, (0, shard * piece), (4, piece))
     return (
         output,
         grad_own.reshape(states.shape),
@@ -837,8 +982,8 @@
         sums[0][None],
         sums[1][None],
         query_sum[None],
-        both_sum[None, :, :model_width],
-        both_sum[None, :, model_width:],
+        key_sum[None],
+        value_sum[None],
         out_sum[None],
         sums[2][None],
         sums[3][None],

time: 287 us -> 209 us (0.73)
  matrix products: 63.2 us -> 35.4 us
  waiting for transfers between devices: 35.1 us -> 15.5 us
  Pallas kernels: 143 us -> 126 us
  local copies, waits for them, and re-layouts: 20.3 us -> 12.6 us
  other arithmetic: 11.1 us -> 5.99 us
    pallas_call x1 -> x0, Pallas kernels: 42.8 us -> none  [reduce_shares(): pl.pallas_call(functools.partial(reduce_kernel, shapes), out_shape=[jax.S...]
    pallas_call x1, Pallas kernels: 69.3 us -> 95.8 us  [backward(): pl.pallas_call(functools.partial(backward_kernel, shapes), in_specs=[insi...]
    dot_general x11 -> x8, matrix products: 40.4 us -> 25.5 us  [project(): return jnp.dot(left, right, preferred_element_type=jnp.float32)]
    dot_general x9 -> x5, matrix products: 22.8 us -> 9.88 us  [back_product(): lax.dot_general(left, right, (((1,), (1,)), ((), ())), preferred_element_...]
    ppermute x14 -> x10, waiting for transfers between devices: 22.5 us -> 10.2 us  [partner_of(): return lax.ppermute(value, axis, pairs)]
    ppermute x2 -> x1, waiting for transfers between devices: 12.6 us -> 5.33 us  [from_partner(): return lax.ppermute(value, axis, pairs)]
    slice x3 -> x0, local copies, waits for them, and re-layouts: 5.1 us -> none  [the longest x1 3.21 us: on_device(): both_mine[:rows_here]]
    convert_element_type x3 -> x2, other arithmetic: 4.17 us -> 1.29 us  [low(): return value.astype(jnp.bfloat16)]
  transfers between devices with their start and end apart: 16 -> 11, of which waited for: 5 -> 2; matrix products, arithmetic and copies ran while one was open for 27% -> 21% of each run, Pallas kernels for 35% -> 15%
where the time goes in v5:
time: 209 us; the launch traced here: 205 us
  Pallas kernels  126 us (60%)
  matrix products  35.4 us (17%)
  waiting for transfers between devices  15.5 us (7%)
  local copies, waits for them, and re-layouts  12.6 us (6%)
  starting transfers between devices  7.61 us (4%)
  other arithmetic  5.99 us (3%)
    pallas_call x1, Pallas kernels, backward(): pl.pallas_call(functools.partial(backward_kernel, shapes), in_specs=[insi...  95.8 us
    dot_general x8, matrix products, project(): return jnp.dot(left, right, preferred_element_type=jnp.float32)  25.5 us
    pallas_call x1, Pallas kernels, feed_forward(): pl.pallas_call(ffn_kernel, grid=(full // block,), in_specs=[pl.BlockSpec(...  18.5 us
    pallas_call x1, Pallas kernels, attention_forward(): pl.pallas_call(attention_forward_kernel, grid=(pairs,), in_specs=[pl.Bloc...  11.8 us
    ppermute x10, waiting for transfers between devices, partner_of(): return lax.ppermute(value, axis, pairs)  10.2 us
    dot_general x5, matrix products, back_product(): lax.dot_general(left, right, (((1,), (1,)), ((), ())), preferred_element_...  9.88 us
    unnamed x77, local copies, waits for them, and re-layouts  9.86 us
    ppermute x10, starting transfers between devices, partner_of(): return lax.ppermute(value, axis, pairs)  5.87 us
  transfers between devices with their start and end apart: 11, of which 2 were waited for; matrix products, arithmetic and copies ran while one was open for 21% of the time, Pallas kernels for 15%

profile of v5, /device:TPU:0, one launch (start us, length us, event | category | flops | bytes accessed | tf_op | source)
XLA Modules:
  0.0 204.8 jit_solution(18393758576748133940)
XLA Ops:
  0.6 1.7 collective-permute-start
  2.4 0.8 reduce-window.7
  4.1 1.1 bitcast_select_fusion.grad_low
  6.7 2.5 %fusion.14 = f32[256,1024]{1,0:T(8,128)S(1)} fusion(bf16[2048,1024]{1,0:T(8,128)(2,1)} %w_skip.1, bf16[1,1,256,1024]{3,2,1,0:T(8,128)(2,1)} %param.16), kind=kOutput, calls=%fused_computation.21 | convolution fusion | flops 536870912 | bytes 3670016 | tf_op jit(solution)/shard_map/dot_general | solution.py:25
  9.2 5.3 %collective-permute-done = bf16[256,1024]{1,0:T(8,128)(2,1)S(1)} collective-permute-done((bf16[256,1024]{1,0:T(8,128)(2,1)}, bf16[256,1024]{1,0:T(8,128)(2,1)S(1)}, u32[]{:S(2)}, u32[]{:S(2)}) %collective-permute-start) | collective-permute-done | bytes 524320 | tf_op jit(solution)/shard_map/ppermute | solution.py:21
  14.5 2.6 %fusion.68 = (f32[256]{0:T(256)S(1)}, f32[256,1024]{1,0:T(8,128)S(1)}) fusion(f32[256,1024]{1,0:T(8,128)S(1)} %fusion.14, bf16[256,1024]{1,0:T(8,128)(2,1)S(1)} %collective-permute-done, bf16[2048,1024]{1,0:T(8,128)(2,1)} %w_skip.1), kind=kOutput, calls=%fused_computation.108 | convolution fusion | flops 537394944 | bytes 4719616 | tf_op jit(solution)/shard_map/dot_general | solution.py:25
  17.4 1.2 add_convert_fusion
  18.7 3.4 %collective-permute-start.2 = (bf16[256,1024]{1,0:T(8,128)(2,1)S(1)}, bf16[256,1024]{1,0:T(8,128)(2,1)S(1)}, u32[]{:S(2)}, u32[]{:S(2)}) collective-permute-start(bf16[256,1024]{1,0:T(8,128)(2,1)S(1)} %get-tuple-element.60), channel_id=1, source_target_pairs={{0,2},{1,3},{2,0},{3,1},{4,6},{5,7},{6,4},{7,5},{8,10},{9,11},{10,... | collective-permute-start | bytes 1572872 | tf_op jit(solution)/shard_map/ppermute | solution.py:62
  22.9 10.2 %collective-permute-done.2 = bf16[256,1024]{1,0:T(8,128)(2,1)S(1)} collective-permute-done((bf16[256,1024]{1,0:T(8,128)(2,1)S(1)}, bf16[256,1024]{1,0:T(8,128)(2,1)S(1)}, u32[]{:S(2)}, u32[]{:S(2)}) %collective-permute-start.2) | collective-permute-done | bytes 524320 | tf_op jit(solution)/shard_map/ppermute | solution.py:62
  33.3 2.3 %fusion.21.query = bf16[256,1024]{1,0:T(8,128)(2,1)S(1)} fusion(bf16[256,1024]{1,0:T(8,128)(2,1)S(1)} %get-tuple-element.60, bf16[1024,1024]{1,0:T(8,128)(2,1)} %w_query.1), kind=kOutput, calls=%fused_computation.30 | convolution fusion | flops 537395200 | bytes 3145728 | tf_op jit(solution)/shard_map/dot_general | solution.py:25
  35.7 2.3 %convolution_convert_fusion.2.values = bf16[1024,1024]{1,0:T(8,128)(2,1)S(1)} fusion(bf16[1024,1024]{1,0:T(8,128)(2,1)S(1)} %copy-done.13, bf16[256,1024]{1,0:T(8,128)(2,1)S(1)} %collective-permute-done.3, bf16[256,1024]{1,0:T(8,128)(2,1)S(1)} %collective-permute-done.2, bf16[256,1024]{1,0:T(8,128)(2,1)S(1)} %collective-permute-done.1, ...), kind=kOutput, calls=%fused_computation.24 | convolution fusion | flops 2156920832 | bytes 6291456 | tf_op jit(solution)/shard_map/dot_general | solution.py:25
  38.1 2.3 %convolution_convert_fusion.3.keys = bf16[1024,1024]{1,0:T(8,128)(2,1)S(1)} fusion(bf16[1024,1024]{1,0:T(8,128)(2,1)S(1)} %copy-done.12, bf16[256,1024]{1,0:T(8,128)(2,1)S(1)} %collective-permute-done.3, bf16[256,1024]{1,0:T(8,128)(2,1)S(1)} %collective-permute-done.2, bf16[256,1024]{1,0:T(8,128)(2,1)S(1)} %collective-permute-done.1, ...), kind=kOutput, calls=%fused_computation.25 | convolution fusion | flops 2156920832 | bytes 6291456 | tf_op jit(solution)/shard_map/dot_general | solution.py:25
  40.5 11.8 %shard_map.263 = (bf16[8,1024,512]{2,1,0:T(8,128)(2,1)}, bf16[256,1024]{1,0:T(8,128)(2,1)S(1)}, f32[8,1,512]{2,1,0:T(1,128)S(1)}) custom-call(bf16[256,1024]{1,0:T(8,128)(2,1)S(1)} %fusion.21.query, bf16[1024,1024]{1,0:T(8,128)(2,1)S(1)} %convolution_convert_fusion.3.keys, bf16[1024,1024]{1,0:T(8,128)(2,1)S(1)} %convolution_convert_fusion.2.values, ...), custom_call_target="tpu_custom_call" | custom-call | tf_op jit(solution)/shard_map/pallas_call | solution.py:368
  52.9 18.5 %shard_map.264 = (bf16[256,1024]{1,0:T(8,128)(2,1)}, bf16[2048,256]{1,0:T(8,128)(2,1)S(1)}, bf16[2048,256]{1,0:T(8,128)(2,1)}, bf16[512,256]{1,0:T(8,128)(2,1)S(...) custom-call(s32[1]{0:T(128)} %bitcast.core, ...), custom_call_target="tpu_custom_call" | custom-call | tf_op jit(solution)/shard_map/pallas_call | solution.py:790
  72.0 2.4 %fusion.22 = bf16[1024,256]{1,0:T(8,128)(2,1)} fusion(s32[1024]{0:T(1024)S(1)} %fusion.48, bf16[256,1024]{1,0:T(8,128)(2,1)S(1)} %copy-done.16, bf16[256,1024]{1,0:T(8,128)(2,1)S(1)} %bitcast.73), kind=kOutput, calls=%fused_computation.31 | convolution fusion | flops 1078198272 | bytes 1576960 | tf_op jit(solution)/shard_map/dot_general | solution.py:35
  74.7 2.4 %fusion.23.joined_kept = bf16[1024,256]{1,0:T(8,128)(2,1)} fusion(s32[1024]{0:T(1024)S(1)} %fusion.49, bf16[256,1024]{1,0:T(8,128)(2,1)S(1)} %copy-done.16, bf16[256,1024]{1,0:T(8,128)(2,1)S(1)} %bitcast.74), kind=kOutput, calls=%fused_computation.32 | convolution fusion | flops 1078198272 | bytes 1576960 | tf_op jit(solution)/shard_map/dot_general | solution.py:35
  79.3 3.9 %fusion.17.one_rows = bf16[512,1024]{1,0:T(8,128)(2,1)} fusion(s32[512]{0:T(512)S(1)} %add_add_fusion.1, bf16[256,1024]{1,0:T(8,128)(2,1)} %copy-done.32, bf16[256,1024]{1,0:T(8,128)(2,1)} %copy-done.30, bf16[256,1024]{1,0:T(8,128)(2,1)} %copy-done.31, bf16[256,1024]{1,0:T(8,128)(2,1)} %copy-done.17), kind=kOutput, calls=%fused_computation.26 | convolution fusion | flops 1083179008 | bytes 3147776 | tf_op jit(solution)/shard_map/dot_general | solution.py:35
  84.5 1.7 convolution_convert_fusion.4
  86.2 5.9 %convolution_convert_fusion.1 = bf16[2048,1024]{1,0:T(8,128)(2,1)} fusion(bf16[2048,256]{1,0:T(8,128)(2,1)} %collective-permute-done.4, bf16[2048,256]{1,0:T(8,128)(2,1)S(1)} %copy-done.10, bf16[256,1024]{1,0:T(8,128)(2,1)} %collective-permute-done.5, bf16[256,1024]{1,0:T(8,128)(2,1)S(1)} %bitcast_select_fusion.grad_low), kind=kOutput, calls=%fused_computation.10 | convolution fusion | flops 2155872256 | bytes 7340032 | tf_op jit(solution)/shard_map/dot_general | solution.py:25
  92.1 5.9 %convolution_convert_fusion = bf16[512,4096]{1,0:T(8,128)(2,1)} fusion(bf16[256,4096]{1,0:T(8,128)(2,1)} %collective-permute-done.7, bf16[256,4096]{1,0:T(8,128)(2,1)S(1)} %copy-done.28, bf16[512,256]{1,0:T(8,128)(2,1)S(1)} %collective-permute-done.6, bf16[512,256]{1,0:T(8,128)(2,1)S(1)} %get-tuple-element.44), kind=kOutput, calls=%fused_computation.4 | convolution fusion | flops 2159017984 | bytes 8912896 | tf_op jit(solution)/shard_map/dot_general | solution.py:25
  98.8 95.8 %shard_map.265 = (bf16[256,1024]{1,0:T(8,128)(2,1)}, bf16[256,1024]{1,0:T(8,128)(2,1)}, f32[8,1024]{1,0:T(8,128)}, f32[64,1024]{1,0:T(8,128)}, f32[16,4096]{1,0:...) custom-call(bf16[256,1024]{1,0:T(8,128)(2,1)} %copy-done.4, ...), custom_call_target="tpu_custom_call" | custom-call | tf_op jit(solution)/shard_map/pallas_call | solution.py:664
  194.7 0.9 constant_dynamic-slice_fusion
  196.0 1.9 copy.47
  197.9 1.9 copy.48
  (122 shorter events, 14.6 us)
Async XLA Ops:
  0.6 13.9 %collective-permute-start = (bf16[256,1024]{1,0:T(8,128)(2,1)}, bf16[256,1024]{1,0:T(8,128)(2,1)S(1)}, u32[]{:S(2)}, u32[]{:S(2)}) collective-permute-start(bf16[256,1024]{1,0:T(8,128)(2,1)} %bitcast.72), channel_id=1, source_target_pairs={{0,64},{64,0},{1,65},{65,1},{2,66},{66,2},{3,67},{67,3},{4,68},{68... | collective-permute-start | bytes 1572872 | tf_op jit(solution)/shard_map/ppermute | solution.py:21
  5.2 81.0 %collective-permute-start.5 = (bf16[256,1024]{1,0:T(8,128)(2,1)S(1)}, bf16[256,1024]{1,0:T(8,128)(2,1)}, u32[]{:S(2)}, u32[]{:S(2)}) collective-permute-start(bf16[256,1024]{1,0:T(8,128)(2,1)S(1)} %bitcast_select_fusion.grad_low), channel_id=1, source_target_pairs={{0,1},{1,0},{2,3},{3,2},{4,5},{5,4},{6,7},{7,6},{8,9},{9,8},{10,11... | collective-permute-start | bytes 1572872 | tf_op jit(solution)/shard_map/ppermute | solution.py:62
  6.0 11.4 %copy-start.25 = (f32[1024]{0:T(1024)}, f32[1024]{0:T(1024)S(1)}, u32[]{:S(2)}) copy-start(f32[1024]{0:T(1024)S(1)} %convert_element_type.57) | copy-start | bytes 12292
  18.7 19.4 %copy-start.17 = (bf16[256,1024]{1,0:T(8,128)(2,1)}, bf16[256,1024]{1,0:T(8,128)(2,1)S(1)}, u32[]{:S(2)}) copy-start(bf16[256,1024]{1,0:T(8,128)(2,1)S(1)} %get-tuple-element.60) | copy-start | bytes 1572868
  18.7 14.4 %collective-permute-start.2 = (bf16[256,1024]{1,0:T(8,128)(2,1)S(1)}, bf16[256,1024]{1,0:T(8,128)(2,1)S(1)}, u32[]{:S(2)}, u32[]{:S(2)}) collective-permute-start(bf16[256,1024]{1,0:T(8,128)(2,1)S(1)} %get-tuple-element.60), channel_id=1, source_target_pairs={{0,2},{1,3},{2,0},{3,1},{4,6},{5,7},{6,4},{7,5},{8,10},{9,11},{10,... | collective-permute-start | bytes 1572872 | tf_op jit(solution)/shard_map/ppermute | solution.py:62
  22.8 12.9 %copy-start.13 = (bf16[1024,1024]{1,0:T(8,128)(2,1)S(1)}, bf16[1024,1024]{1,0:T(8,128)(2,1)}, u32[]{:S(2)}) copy-start(bf16[1024,1024]{1,0:T(8,128)(2,1)} %w_value.1) | copy-start | bytes 6291460
  22.8 12.9 %collective-permute-start.1 = (bf16[256,1024]{1,0:T(8,128)(2,1)S(1)}, bf16[256,1024]{1,0:T(8,128)(2,1)S(1)}, u32[]{:S(2)}, u32[]{:S(2)}) collective-permute-start(bf16[256,1024]{1,0:T(8,128)(2,1)S(1)} %get-tuple-element.60), channel_id=1, source_target_pairs={{0,1},{1,0},{2,3},{3,2},{4,5},{5,4},{6,7},{7,6},{8,9},{9,8},{10,11... | collective-permute-start | bytes 1572872 | tf_op jit(solution)/shard_map/ppermute | solution.py:62
  33.1 2.6 %collective-permute-start.3 = (bf16[256,1024]{1,0:T(8,128)(2,1)S(1)}, bf16[256,1024]{1,0:T(8,128)(2,1)S(1)}, u32[]{:S(2)}, u32[]{:S(2)}) collective-permute-start(bf16[256,1024]{1,0:T(8,128)(2,1)S(1)} %collective-permute-done.2), channel_id=1, source_target_pairs={{0,1},{1,0},{2,3},{3,2},{4,5},{5,4},{6,7},{7,6},{8,9},{9,8},{10,11... | collective-permute-start | bytes 1572872 | tf_op jit(solution)/shard_map/ppermute | solution.py:62
  40.5 11.8 %copy-start.1 = (bf16[1024,1024]{1,0:T(8,128)(2,1)}, bf16[1024,1024]{1,0:T(8,128)(2,1)S(1)}, u32[]{:S(2)}) copy-start(bf16[1024,1024]{1,0:T(8,128)(2,1)S(1)} %convolution_convert_fusion.3.keys) | copy-start | bytes 6291460
  52.9 30.2 %copy-start.3 = (bf16[256,1024]{1,0:T(8,128)(2,1)}, bf16[256,1024]{1,0:T(8,128)(2,1)S(1)}, u32[]{:S(2)}) copy-start(bf16[256,1024]{1,0:T(8,128)(2,1)S(1)} %get-tuple-element.37.mixed) | copy-start | bytes 1572868
  52.9 19.1 %copy-start.16 = (bf16[256,1024]{1,0:T(8,128)(2,1)S(1)}, bf16[256,1024]{1,0:T(8,128)(2,1)}, u32[]{:S(2)}) copy-start(bf16[256,1024]{1,0:T(8,128)(2,1)} %copy-done.15) | copy-start | bytes 1572868
  52.9 19.1 %copy-start.29 = (bf16[1,1,256,1024]{3,2,1,0:T(8,128)(2,1)S(1)}, bf16[1,1,256,1024]{3,2,1,0:T(8,128)(2,1)}, u32[]{:S(2)}) copy-start(bf16[1,1,256,1024]{3,2,1,0:T(8,128)(2,1)} %param.16) | copy-start | bytes 1572868
  71.4 6.5 %copy-start.2 = (f32[256,1024]{1,0:T(8,128)}, f32[256,1024]{1,0:T(8,128)S(1)}, u32[]{:S(2)}) copy-start(f32[256,1024]{1,0:T(8,128)S(1)} %get-tuple-element.47.grad_residual) | copy-start | bytes 3145732
  71.4 20.7 %collective-permute-start.7 = (bf16[256,4096]{1,0:T(8,128)(2,1)}, bf16[256,4096]{1,0:T(8,128)(2,1)}, u32[]{:S(2)}, u32[]{:S(2)}) collective-permute-start(bf16[256,4096]{1,0:T(8,128)(2,1)} %get-tuple-element.46), channel_id=1, source_target_pairs={{0,1},{1,0},{2,3},{3,2},{4,5},{5,4},{6,7},{7,6},{8,9},{9,8},{10,11... | collective-permute-start | bytes 6291464 | tf_op jit(solution)/shard_map/ppermute | solution.py:62
  74.4 11.8 %collective-permute-start.4 = (bf16[2048,256]{1,0:T(8,128)(2,1)}, bf16[2048,256]{1,0:T(8,128)(2,1)}, u32[]{:S(2)}, u32[]{:S(2)}) collective-permute-start(bf16[2048,256]{1,0:T(8,128)(2,1)} %get-tuple-element.43), channel_id=1, source_target_pairs={{0,1},{1,0},{2,3},{3,2},{4,5},{5,4},{6,7},{7,6},{8,9},{9,8},{10,11... | collective-permute-start | bytes 3145736 | tf_op jit(solution)/shard_map/ppermute | solution.py:62
  78.0 6.4 %collective-permute-start.9 = (bf16[256,1024]{1,0:T(8,128)(2,1)S(1)}, bf16[256,1024]{1,0:T(8,128)(2,1)S(1)}, u32[]{:S(2)}, u32[]{:S(2)}) collective-permute-start(bf16[256,1024]{1,0:T(8,128)(2,1)S(1)} %convert_element_type.69), channel_id=1, source_target_pairs={{0,1},{1,0},{2,3},{3,2},{4,5},{5,4},{6,7},{7,6},{8,9},{9,8},{10,11... | collective-permute-start | bytes 1572872 | tf_op jit(solution)/shard_map/ppermute | solution.py:62
  79.2 4.6 %collective-permute-start.8 = (bf16[512,256]{0,1:T(8,128)(2,1)S(1)}, bf16[512,256]{0,1:T(8,128)(2,1)S(1)}, u32[]{:S(2)}, u32[]{:S(2)}) collective-permute-start(bf16[512,256]{0,1:T(8,128)(2,1)S(1)} %fusion.24), channel_id=1, source_target_pairs={{0,1},{1,0},{2,3},{3,2},{4,5},{5,4},{6,7},{7,6},{8,9},{9,8},{10,11... | collective-permute-start | bytes 786440 | tf_op jit(solution)/shard_map/ppermute | solution.py:62
  83.8 14.2 %collective-permute-start.10 = (bf16[1024,256]{1,0:T(8,128)(2,1)S(1)}, bf16[1024,256]{1,0:T(8,128)(2,1)S(1)}, u32[]{:S(2)}, u32[]{:S(2)}) collective-permute-start(bf16[1024,256]{1,0:T(8,128)(2,1)S(1)} %copy-done.33), channel_id=1, source_target_pairs={{0,1},{1,0},{2,3},{3,2},{4,5},{5,4},{6,7},{7,6},{8,9},{9,8},{10,11... | collective-permute-start | bytes 1572872 | tf_op jit(solution)/shard_map/ppermute | solution.py:62
  84.3 7.7 %collective-permute-start.6 = (bf16[512,256]{1,0:T(8,128)(2,1)S(1)}, bf16[512,256]{1,0:T(8,128)(2,1)S(1)}, u32[]{:S(2)}, u32[]{:S(2)}) collective-permute-start(bf16[512,256]{1,0:T(8,128)(2,1)S(1)} %get-tuple-element.45), channel_id=1, source_target_pairs={{0,1},{1,0},{2,3},{3,2},{4,5},{5,4},{6,7},{7,6},{8,9},{9,8},{10,11... | collective-permute-start | bytes 786440 | tf_op jit(solution)/shard_map/ppermute | solution.py:62
  194.6 6.5 %copy-start.23 = (f32[16,1024]{1,0:T(8,128)S(1)}, f32[16,1024]{1,0:T(8,128)}, u32[]{:S(2)}) copy-start(f32[16,1024]{1,0:T(8,128)} %get-tuple-element.55) | copy-start | bytes 196612
  194.6 7.1 %copy-start.22 = (f32[16,1024]{1,0:T(8,128)S(1)}, f32[16,1024]{1,0:T(8,128)}, u32[]{:S(2)}) copy-start(f32[16,1024]{1,0:T(8,128)} %get-tuple-element.56) | copy-start | bytes 196612
  194.6 7.7 %copy-start.21 = (f32[16,1024]{1,0:T(8,128)S(1)}, f32[16,1024]{1,0:T(8,128)}, u32[]{:S(2)}) copy-start(f32[16,1024]{1,0:T(8,128)} %get-tuple-element.57) | copy-start | bytes 196612
  194.6 8.3 %copy-start.19 = (f32[16,4096]{1,0:T(8,128)S(1)}, f32[16,4096]{1,0:T(8,128)}, u32[]{:S(2)}) copy-start(f32[16,4096]{1,0:T(8,128)} %get-tuple-element.58) | copy-start | bytes 786436
  194.6 9.0 %copy-start.18 = (f32[64,1024]{1,0:T(8,128)S(1)}, f32[64,1024]{1,0:T(8,128)}, u32[]{:S(2)}) copy-start(f32[64,1024]{1,0:T(8,128)} %get-tuple-element.59) | copy-start | bytes 786436
  (21 other events, 74.5 us)

commit v6 on v5

v6 whole, which is shorter than its diff:
```python
import functools

import jax
import jax.numpy as jnp
from jax.experimental import pallas as pl
from jax.experimental.pallas import tpu as pltpu
from jax import lax
from jax.sharding import PartitionSpec as P

HEADS = 16
LOG2E = 1.4426950408889634
LN2 = 0.6931471805599453


EPS = 1e-05


def from_partner(value, axis, stride):
    mask = 2**stride
    pairs = [(source, source ^ mask) for source in range(lax.axis_size(axis))]
    return lax.ppermute(value, axis, pairs)


def project(left, right):
    return jnp.dot(left, right, preferred_element_type=jnp.float32)


def rows_product(left, right):
    return lax.dot_general(
        left, right, (((0,), (0,)), ((), ())), preferred_element_type=jnp.float32
    )


def back_product(left, right):
    return lax.dot_general(
        left, right, (((1,), (1,)), ((), ())), preferred_element_type=jnp.float32
    )


def norm_forward(hidden, gain, bias):
    center = hidden - jnp.mean(hidden, axis=-1, keepdims=True)
    variance = jnp.mean(center * center, axis=-1, keepdims=True)
    inverse = lax.rsqrt(variance + EPS)
    return center * inverse * gain + bias


def segment_tables(lengths_row, spans_row, places):
    ends = jnp.cumsum(lengths_row, dtype=jnp.int32)
    starts = ends - lengths_row
    segment = jnp.sum((places[:, None] >= ends[None, :]).astype(jnp.int32), axis=1)
    lower = starts + spans_row[:, 0]
    upper = starts + spans_row[:, 1]
    inside = jnp.any(
        (places[:, None] >= lower[None, :]) & (places[:, None] < upper[None, :]), axis=1
    )
    return (segment, inside)


def partner_of(value, axis, mask):
    pairs = [(source, source ^ mask) for source in range(lax.axis_size(axis))]
    return lax.ppermute(value, axis, pairs)


def core_selector(core, rows):
    piece = rows // 32
    target = jnp.arange(rows // 2, dtype=jnp.int32)
    source = (target // piece) * (2 * piece) + core * piece + target % piece
    return (source[:, None] == jnp.arange(rows, dtype=jnp.int32)[None, :]).astype(jnp.bfloat16)


def swap_core(value):
    return partner_of(value, "seq", 1)


def low(value):
    return value.astype(jnp.bfloat16)


MESH = pl.DeviceIdType.MESH
NEAR, WRAP = (0, 3, 1, 2), (0, 1, 3, 2)
QUARTERS = (("x", NEAR), ("x", WRAP), ("z", NEAR), ("z", WRAP))


def flip(value, mask):
    if mask == 1:
        return value + 1 - 2 * lax.rem(value, 2)
    if mask == 2:
        return lax.rem(value + 2, 4)
    if mask == 3:
        return 3 - value
    return value


def block_place(quarter, outer, inner, x, z):
    first, order = QUARTERS[quarter]
    if first == "x":
        return flip(z, order[inner]) * 4 + flip(x, order[outer])
    return flip(z, order[outer]) * 4 + flip(x, order[inner])


def stage_partner(quarter, stage, x, z, seq):
    if stage == 4:
        return {"seq": lax.rem(seq + 2, 4)}
    first, order = QUARTERS[quarter]
    mask = order[2] if stage % 2 == 0 else order[1]
    if (first == "x") == (stage < 2):
        return {"dp": z * 4 + flip(x, mask)}
    return {"dp": flip(z, mask) * 4 + x}


def remote(source, target, send, recv, device):
    return pltpu.make_async_remote_copy(
        src_ref=source,
        dst_ref=target,
        send_sem=send,
        recv_sem=recv,
        device_id=device,
        device_id_type=MESH,
    )


def enter(devices):
    barrier = pltpu.get_barrier_semaphore()
    for device in devices:
        pl.semaphore_signal(barrier, inc=1, device_id=device, device_id_type=MESH)
    pl.semaphore_wait(barrier, len(devices))


def add_blocks(count, total, other):
    def one(index, carry):
        total[index] = (
            total[index].astype(jnp.float32) + other[index].astype(jnp.float32)
        ).astype(jnp.bfloat16)
        return carry

    lax.fori_loop(0, count, one, 0)


def place_here():
    dp, seq = lax.axis_index("dp"), lax.axis_index("seq")
    return lax.div(dp, 4), lax.rem(dp, 4), seq


def ring_partners(z, x, seq):
    pairs = ((0, 0), (0, 1), (2, 0), (2, 1), (0, 4))
    return [stage_partner(quarter, stage, x, z, seq) for quarter, stage in pairs]


def either(one, two):
    return 2 * lax.rem(lax.div(one, 2) + lax.div(two, 2), 2) + lax.rem(one + two, 2)


def relative_place(quarter, z, x, there):
    first, order = QUARTERS[quarter]

    def position(value):
        if order == NEAR:
            return 2 * value - lax.div(value, 2) - 4 * lax.div(value, 3)
        return value + lax.div(value, 2) * (1 - 2 * lax.rem(value, 2))

    z_place = position(either(z, lax.div(there, 4)))
    x_place = position(either(x, lax.rem(there, 4)))
    return x_place * 4 + z_place if first == "x" else z_place * 4 + x_place


class Halving:
    def __init__(self, shapes, results, scratch):
        self.shapes, self.results = shapes, results
        scratch = list(scratch)
        count = len(shapes)
        self.work = scratch[:count]
        self.landings = [scratch[count + 5 * job : count + 5 * job + 5] for job in range(count)]
        self.send_sem, self.recv_sem = scratch[6 * count :]
        self.z, self.x, self.seq = place_here()
        self.y = lax.div(self.seq, 2)

    @staticmethod
    def scratch(shapes):
        shapes_of = [(4, 16, 2 * rows, width // 4) for rows, width in shapes]
        for rows, width in shapes:
            shapes_of += [(4, blocks, 2 * rows, width // 4) for blocks in (8, 4, 2, 1)]
            shapes_of.append((4, rows, width // 4))
        sems = pltpu.SemaphoreType.DMA((len(shapes), 4, 5))
        return [pltpu.VMEM(shape, jnp.bfloat16) for shape in shapes_of] + [sems, sems]

    def put(self, job, quarter, there, value):
        place = relative_place(quarter, self.z, self.x, there)
        self.work[job][quarter, place] = value.astype(jnp.bfloat16)
        return place

    def put_and_send(self, job, quarter, there, value):
        place = self.put(job, quarter, there, value)

        @pl.when(place >= 8)
        def _():
            remote(
                self.work[job].at[quarter, place],
                self.landings[job][0].at[quarter, place - 8],
                self.send_sem.at[job, quarter, 0],
                self.recv_sem.at[job, quarter, 0],
                stage_partner(quarter, 0, self.x, self.z, self.seq),
            ).start()

    def store(self, job, quarter, value):
        rows = 2 * self.shapes[job][0]
        for index in range(16):
            self.put(job, quarter, index, value[index * rows : (index + 1) * rows])
        self.copy(job, quarter, 0).start()

    def copy(self, job, quarter, stage):
        rows = self.shapes[job][0]
        if stage < 4:
            size = 8 >> stage
            source = self.work[job].at[quarter, pl.ds(size, size)]
        else:
            away = pl.multiple_of((1 - self.y) * rows, 16)
            source = self.work[job].at[quarter, 0, pl.ds(away, rows)]
        return remote(
            source,
            self.landings[job][stage].at[quarter],
            self.send_sem.at[job, quarter, stage],
            self.recv_sem.at[job, quarter, stage],
            stage_partner(quarter, stage, self.x, self.z, self.seq),
        )

    def finish(self, job, stage):
        rows, width = self.shapes[job]
        for quarter in range(4):
            work = self.work[job].at[quarter]
            landing = self.landings[job][stage].at[quarter]
            self.copy(job, quarter, stage).wait_recv()
            if stage < 4:
                add_blocks(8 >> stage, work, landing)
                self.copy(job, quarter, stage + 1).start()
            else:
                mine = pl.multiple_of(self.y * rows, 16)
                total = work[0, pl.ds(mine, rows)].astype(jnp.float32)
                first = quarter * width // 4
                result = self.results[job][first // 4096 if width == 4096 else first // 1024]
                result[:, pl.ds(first % result.shape[1], width // 4)] = total + landing[
                    ...
                ].astype(jnp.float32)

    def drain(self):
        for job in range(len(self.shapes)):
            for quarter in range(4):
                for stage in range(5):
                    self.copy(job, quarter, stage).wait_send()


def attention_backward_pair(query, keys, values, share, inverse, grad, mixed, lows):
    span = keys.shape[0]
    here = query.shape[0]
    chunk = 128
    lane = lax.broadcasted_iota(jnp.int32, query.shape, 1)
    zero = jnp.zeros(query.shape, query.dtype)
    queries = jnp.concatenate(
        [jnp.where(lane < 64, query, zero), jnp.where(lane >= 64, query, zero)], axis=0
    )
    turned = grad.astype(jnp.float32).T
    product = turned * mixed.astype(jnp.float32).T
    first = turned[:64] * inverse[:, :here]
    second = turned[64:] * inverse[:, here:]
    none = jnp.zeros_like(first)
    grads = jnp.concatenate(
        [jnp.concatenate([first, none], axis=1), jnp.concatenate([none, second], axis=1)], axis=0
    ).astype(jnp.bfloat16)
    grads_back = grads.T
    centre = inverse * jnp.concatenate(
        [
            jnp.sum(product[:64], axis=0, keepdims=True),
            jnp.sum(product[64:], axis=0, keepdims=True),
        ],
        axis=1,
    )
    grad_keys, grad_values = [], []
    for index in range(span // chunk):
        rows = pl.ds(index * chunk, chunk)
        part = share[rows]
        grad_share = project(values[rows], grads)
        grad_score = (part.astype(jnp.float32) * (grad_share - centre)).astype(jnp.bfloat16)
        lows[rows] = grad_score
        grad_keys.append((project(grad_score, queries) * LN2).astype(jnp.bfloat16))
        grad_values.append(project(part, grads_back).astype(jnp.bfloat16))
    out = rows_product(keys[...], lows[...])
    out = jnp.concatenate([out[:64, :here], out[64:, here:]], axis=0)
    return (out.T * 0.125).astype(jnp.bfloat16), grad_keys, grad_values


def attention_forward_kernel(
    query, keys, values, key_places, key_segments, query_places, query_segments, slopes,
    shares, mixed, inverses, distance, scores,
):
    span = keys.shape[0]
    chunk = 128
    here = query.shape[0]

    @pl.when(pl.program_id(0) == 0)
    def _():
        gap = jnp.abs(query_places[...] - key_places[...]).astype(jnp.float32)
        same = query_segments[...] == key_segments[...]
        distance[...] = jnp.where(same, gap, 1e30)

    lane = lax.broadcasted_iota(jnp.int32, query.shape, 1)
    zero = jnp.zeros(query.shape, query.dtype)
    both = jnp.concatenate(
        [jnp.where(lane < 64, query[...], zero), jnp.where(lane >= 64, query[...], zero)], axis=0
    )
    slope = slopes[0]

    def raw(index, top):
        rows = pl.ds(pl.multiple_of(index * chunk, chunk), chunk)
        part = back_product(keys[rows], both)
        gap = distance[rows]
        part = part - slope * jnp.concatenate([gap, gap], axis=1)
        scores[rows] = part
        return jnp.maximum(top, jnp.max(part.reshape(chunk // 8, 8, 2 * here), axis=0))

    top = lax.fori_loop(
        0, span // chunk, raw, jnp.full((8, 2 * here), -jnp.inf, jnp.float32), unroll=True
    )
    top = jnp.max(top, axis=0, keepdims=True)

    def exponent(index, carry):
        rows = pl.ds(pl.multiple_of(index * chunk, chunk), chunk)
        shares[0, rows] = jnp.exp2(scores[rows] - top).astype(jnp.bfloat16)
        return carry

    lax.fori_loop(0, span // chunk, exponent, 0, unroll=True)
    turned = jnp.concatenate([values[...].T, jnp.ones((16, span), jnp.bfloat16)], axis=0)
    out = project(turned, shares[0])
    inverse = 1.0 / out[128:129]
    inverses[0] = inverse
    out = out[:128] * inverse
    out = jnp.concatenate([out[:64, :here], out[64:, here:]], axis=0)
    mixed[...] = out.T.astype(jnp.bfloat16)


def attention_forward(query, keys, values, tables, slopes):
    here, width = query.shape
    span = keys.shape[0]
    pairs = width // 128
    whole = lambda a: pl.BlockSpec(a.shape, lambda i: (0,) * a.ndim)
    return pl.pallas_call(
        attention_forward_kernel,
        grid=(pairs,),
        in_specs=[
            pl.BlockSpec((here, 128), lambda i: (0, i)),
            pl.BlockSpec((span, 128), lambda i: (0, i)),
            pl.BlockSpec((span, 128), lambda i: (0, i)),
            *[whole(table) for table in tables],
            pl.BlockSpec((1, 1, 2 * here), lambda i: (i, 0, 0)),
        ],
        out_specs=[
            pl.BlockSpec((1, span, 2 * here), lambda i: (i, 0, 0)),
            pl.BlockSpec((here, 128), lambda i: (0, i)),
            pl.BlockSpec((1, 1, 2 * here), lambda i: (i, 0, 0)),
        ],
        out_shape=[
            jax.ShapeDtypeStruct((pairs, span, 2 * here), jnp.bfloat16),
            jax.ShapeDtypeStruct((here, width), jnp.bfloat16),
            jax.ShapeDtypeStruct((pairs, 1, 2 * here), jnp.float32),
        ],
        scratch_shapes=[
            pltpu.VMEM((span, here), jnp.float32),
            pltpu.VMEM((span, 2 * here), jnp.float32),
        ],
        compiler_params=pltpu.CompilerParams(vmem_limit_bytes=40 * 2**20),
    )(query, keys, values, *tables, slopes)


def split_cores(core, source, kept, sent, rows):
    for index in range(source.shape[0] // (2 * rows)):
        mine = pl.multiple_of(index * 2 * rows + core * rows, rows)
        away = pl.multiple_of(index * 2 * rows + (1 - core) * rows, rows)
        kept(index * rows, source[pl.ds(mine, rows)])
        sent(index * rows, source[pl.ds(away, rows)])


def backward_kernel(
    shapes, query, keys, values, shares, inverses, mixed, grad_low, hidden, w_out, w_up, w_down,
    w_query, w_key, w_value, w_skip, normed_own, normed_near, normed_far, normed_far_near,
    joined_kept, joined_other, gain_one, gain_two, bias_two,
    output, grad_own, grad_stored, vectors, *refs,
):
    refs = list(refs)
    take = lambda n: [refs.pop(0) for _ in range(n)]
    results = [take(1), take(1), take(1), take(1), take(2), take(1)]
    lows, held, held_sem, parts, free_sem, swap_send, swap_recv = take(7)
    grad_query, query_landing, side_send, side_recv = take(4)
    columns_two, heads, load_sem, units, residuals = take(5)
    grad_normed, normed_send, normed_landing, grad_hidden, hidden_landing = take(5)
    stored_send, stored_landing, vector_landing, vector_send, vector_recv = take(5)
    turned, inverse_two, block_sem, pair_send, pair_recv, act_recv, part_sem = take(7)
    grad = grad_hidden
    halving = Halving(shapes, results, refs)
    z, x, seq = place_here()
    core_index = lax.rem(seq, 2)
    core = {"seq": flip(seq, 1)}
    far = {"seq": flip(seq, 2)}
    section = {"section": 1 - lax.axis_index("section")}
    pairs = shares.shape[0]
    here, width = query.shape
    block = 512
    blocks = w_up.shape[1] // block
    half = width // 2

    def fetch(pair):
        slot = lax.rem(pair, 2)
        return pltpu.make_async_copy(shares.at[pair], held.at[slot], held_sem.at[slot])

    def load(index):
        source, target = (
            (keys, columns_two.at[pl.ds(0, width)]),
            (values, columns_two.at[pl.ds(width, width)]),
            (w_query, heads.at[0]),
            (w_key, heads.at[1]),
            (w_value, heads.at[2]),
            (hidden, units),
            (hidden, residuals),
            (w_skip, columns_two),
            (joined_kept, held.at[0, :, pl.ds(0, here)]),
            (joined_other, held.at[0, :, pl.ds(here, here)]),
            (w_out.at[:, pl.ds(0, half)], held.at[0]),
            (w_out.at[:, pl.ds(half, half)], held.at[1]),
        )[index]
        return pltpu.make_async_copy(source, target, load_sem.at[index])

    def load_part(part, index):
        return pltpu.make_async_copy(
            (normed_own, normed_near, normed_far, normed_far_near)[part].at[
                :, pl.ds(index * half, half)
            ],
            held.at[index, pl.ds(part * here, here)],
            part_sem.at[part, index],
        )

    def load_block(step):
        slot = lax.rem(step, 2)
        place = pl.ds(pl.multiple_of(step * block, block), block)
        there = pl.ds(pl.multiple_of(slot * block, block), block)
        return (
            pltpu.make_async_copy(
                w_up.at[:, place], columns_two.at[pl.ds(width, width), there], block_sem.at[slot, 0]
            ),
            pltpu.make_async_copy(
                w_down.at[place], columns_two.at[there], block_sem.at[slot, 1]
            ),
        )

    def side(index):
        source, target, device = (
            (parts.at[0], parts.at[1], core),
            (parts.at[2], parts.at[3], core),
            (grad_query, query_landing, core),
            (normed_send, normed_landing, far),
            (grad_hidden, hidden_landing, core),
            (stored_send, stored_landing, section),
            (grad_low, parts.at[0, :, pl.ds(0, width)], core),
            (parts.at[1, :, pl.ds(0, width)], parts.at[0, :, pl.ds(width, width)], core),
        )[index]
        return remote(source, target, side_send.at[index], side_recv.at[index], device)

    def pair_half(index, part):
        lanes = pl.ds((1 - index) * here, here)
        return remote(
            parts.at[3, :, pl.ds((2 * index + part) * here, here)],
            lows.at[pl.ds(half + part * here, here), lanes],
            pair_send.at[index],
            pair_recv.at[index],
            core,
        )

    def pair_whole(index):
        if index == 2:
            source = target = parts.at[2]
        elif index == 3:
            source = target = heads.at[1]
        else:
            source = target = lows.at[pl.ds(half, half), pl.ds((1 - index) * here, here)]
        return remote(source, target, pair_send.at[index], pair_recv.at[index], core)

    def act_place(step, base):
        rows = pl.ds(pl.multiple_of(base + lax.rem(step, 2) * here, here), here)
        return rows, pl.ds(pl.multiple_of(lax.div(step, 2) * here, here), here)

    def act_copy(step):
        rows, lanes = act_place(step, half)
        return remote(
            parts.at[2, :, pl.ds(pl.multiple_of(step * here, here), here)],
            heads.at[2, rows, lanes],
            pair_send.at[2],
            act_recv.at[step],
            core,
        )

    def up_copy(step):
        rows = pl.ds(pl.multiple_of(lax.div(step, 2) * here, here), here)
        lanes = pl.ds(pl.multiple_of(lax.rem(step, 2) * block, block), block)
        return remote(
            heads.at[0, rows, lanes],
            heads.at[1, rows, lanes],
            pair_send.at[3],
            pair_recv.at[3],
            core,
        )

    vector_devices = [core] + [stage_partner(0, stage, x, z, seq) for stage in range(5)]

    def vector_copy(step):
        return remote(
            vectors,
            vector_landing.at[step],
            vector_send.at[step],
            vector_recv.at[step],
            vector_devices[step],
        )

    def vector_finish(step):
        vector_copy(step).wait()
        vectors[...] += vector_landing[step]
        if step < 5:
            vector_copy(step + 1).start()

    for index in (6, 10, 11):
        load(index).start()
    for copy in load_block(0):
        copy.start()
    enter(ring_partners(z, x, seq) + [core, section])
    side(6).start()

    def share_rows(index):
        def kept(row, value):
            lows[pl.ds(row, 16), pl.ds((1 - index) * here, here)] = value

        def sent(row, value):
            lanes = pl.ds((2 * index + row // here) * here, here)
            parts[3, pl.ds(row % here, 16), lanes] = value

        split_cores(core_index, turned, kept, sent, 16)
        pair_half(index, 0).start()
        pair_half(index, 1).start()

    turned[...] = mixed[...].T
    share_rows(0)
    load(6).wait()
    for index in range(2):
        load(10 + index).wait()
        columns = pl.ds(index * half, half)
        residuals[:, columns] += project(mixed[...], held[index])

    def norm_two_rows(index, carry):
        rows = pl.ds(pl.multiple_of(index * 32, 32), 32)
        value = residuals[rows]
        center = value - mean_rows(value)
        scale = lax.rsqrt(mean_rows(center * center) + EPS)
        center = center * scale
        units[rows] = center
        inverse_two[rows] = scale
        stored_send[rows] = (center * gain_two[...] + bias_two[...]).astype(jnp.bfloat16)
        grad_normed[rows] = jnp.zeros_like(value)
        return carry

    lax.fori_loop(0, here // 32, norm_two_rows, 0)
    turned[...] = stored_send[...].T
    share_rows(1)
    side(6).wait_recv()

    def down_share(step):
        act_copy(step).wait_recv()
        rows, lanes = act_place(step, 0)
        rows_other, _ = act_place(step, half)
        value = project(heads[2, rows, lanes], grad_low[...]) + project(
            heads[2, rows_other, lanes], parts[0, :, pl.ds(0, width)]
        )
        for index in range(2):
            for quarter in range(4):
                halving.put_and_send(
                    0,
                    quarter,
                    2 * step + index,
                    value[index * 128 : index * 128 + 128, quarter * 256 : quarter * 256 + 256],
                )

    def one_block(step, carry):
        @pl.when(step + 1 < blocks)
        def _():
            for copy in load_block(step + 1):
                copy.start()

        for copy in load_block(step):
            copy.wait()
        there = pl.ds(pl.multiple_of(lax.rem(step, 2) * block, block), block)
        up_part = columns_two.at[pl.ds(width, width), there]
        down_part = columns_two.at[there]
        upward = project(stored_send[...], up_part[...])
        cdf = 0.5 * (1.0 + lax.erf(upward * 0.7071067811865476))
        act = (upward * cdf).astype(jnp.bfloat16)
        density = jnp.exp(upward * upward * -0.5) * 0.3989422804014327
        slope = cdf + upward * density
        grad_up = (back_product(grad_low[...], down_part[...]) * slope).astype(jnp.bfloat16)
        residuals[...] += project(act, down_part[...])
        grad_normed[...] += back_product(grad_up, up_part[...])
        up_rows = pl.ds(pl.multiple_of(lax.div(step, 2) * here, here), here)
        heads[0, up_rows, there] = grad_up
        up_copy(step).start()
        turned[pl.ds(0, block)] = act.T
        rows, lanes = act_place(step, 0)
        first = lax.rem(step, 2) * here
        sent_lanes = pl.ds(pl.multiple_of(step * here, here), here)

        def kept(row, value):
            heads[2, pl.ds(pl.multiple_of(first + row, 64), 64), lanes] = value

        def sent(row, value):
            parts[2, pl.ds(row, 64), sent_lanes] = value

        split_cores(core_index, turned.at[pl.ds(0, block)], kept, sent, 64)
        act_copy(step).start()

        @pl.when(step > 0)
        def _():
            down_share(step - 1)

        return carry

    lax.fori_loop(0, blocks, one_block, 0)
    load(0).start()
    load(1).start()

    def norm_back(ones, grads, gain, inverse):
        scaled = grads * gain
        value = scaled - mean_rows(scaled) - ones * mean_rows(scaled * ones)
        return (
            inverse * value,
            jnp.sum(grads * ones, axis=0, keepdims=True),
            jnp.sum(grads, axis=0, keepdims=True),
        )

    def norm_two_back(index, sums):
        rows = pl.ds(pl.multiple_of(index * 32, 32), 32)
        value, gain_part, bias_part = norm_back(
            units[rows], grad_normed[rows], gain_two[...], inverse_two[rows]
        )
        output[rows] = residuals[rows].astype(jnp.bfloat16)
        value = grad_low[rows].astype(jnp.float32) + value
        residuals[rows] = value
        parts[1, rows, pl.ds(0, width)] = value.astype(jnp.bfloat16)
        return sums[0] + gain_part, sums[1] + bias_part

    nothing = jnp.zeros((1, width), jnp.float32)
    gain_sum, bias_sum = lax.fori_loop(0, here // 32, norm_two_back, (nothing, nothing))
    side(7).start()
    load(5).start()
    vectors[pl.ds(2, 1)] = gain_sum
    vectors[pl.ds(3, 1)] = bias_sum
    vectors[pl.ds(4, 4)] = jnp.zeros((4, width), jnp.float32)
    down_share(blocks - 1)
    for index in range(2):
        columns = pl.ds(index * half, half)
        part = back_product(parts[1, :, columns], held[index])
        grad_normed[...] = part if index == 0 else grad_normed[...] + part
    grad[...] = grad_normed[...].astype(jnp.bfloat16)
    fetch(0).start()
    pair_whole(1).wait_recv()
    pair_whole(3).wait_recv()
    for quarter in range(4):
        rows = pl.ds(quarter * here, here)
        halving.store(
            1,
            quarter,
            project(lows[pl.ds(0, half), pl.ds(0, here)], heads[0, rows])
            + project(lows[pl.ds(half, half), pl.ds(0, here)], heads[1, rows]),
        )
    pair_whole(3).wait_send()
    pl.semaphore_signal(free_sem.at[0], inc=1, device_id=core, device_id_type=MESH)
    pair_whole(0).wait_recv()
    side(7).wait_recv()
    for quarter in range(4):
        halving.store(
            2,
            quarter,
            project(
                lows[pl.ds(0, half), pl.ds(here, here)], parts[1, :, pl.ds(quarter * 256, 256)]
            )
            + project(
                lows[pl.ds(half, half), pl.ds(here, here)],
                parts[0, :, pl.ds(width + quarter * 256, 256)],
            ),
        )
    for index in range(3):
        pair_whole(index).wait_send()
    side(7).wait_send()
    for index in range(3, 5):
        load(index).start()
    pl.semaphore_wait(free_sem.at[0], 1)
    halving.finish(0, 0)
    load(0).wait()
    load(1).wait()

    def one_pair(pair, carry):
        @pl.when(pair + 1 < pairs)
        def _():
            fetch(pair + 1).start()

        fetch(pair).wait()
        columns = pl.ds(pl.multiple_of(pair * 128, 128), 128)
        others = pl.ds(pl.multiple_of(width + pair * 128, 128), 128)
        out, grad_keys, grad_values = attention_backward_pair(
            query[:, columns],
            columns_two.at[pl.ds(0, width), columns],
            columns_two.at[pl.ds(width, width), columns],
            held.at[lax.rem(pair, 2)],
            inverses[pair],
            grad[:, columns],
            mixed[:, columns],
            lows,
        )
        grad_query[:, columns] = out
        for index, (one, two) in enumerate(zip(grad_keys, grad_values)):
            part, rows = index * 128 // here, pl.ds(index * 128 % here, 128)
            parts[part, rows, columns] = one
            parts[part, rows, others] = two
        for step in range(2):
            for index, place in enumerate((columns, others)):
                remote(
                    parts.at[2 * step + 1, :, place],
                    heads.at[0, pl.ds((2 * step + index) * here, here), columns],
                    swap_send,
                    swap_recv,
                    core,
                ).start()
        return carry

    lax.fori_loop(0, pairs, one_pair, 0)
    side(2).start()
    load(7).start()
    for part in range(4):
        load_part(part, 0).start()
        load_part(part, 1).start()
    swapped = remote(heads.at[0], heads.at[0], swap_send, swap_recv, core)
    swapped.wait()
    pl.semaphore_signal(free_sem.at[1], inc=1, device_id=core, device_id_type=MESH)
    for step in (1, 0):

        def add_rows(index, carry):
            rows = pl.ds(pl.multiple_of(index * 64, 64), 64)
            for index in range(2):
                columns = pl.ds(index * width, width)
                first = pl.multiple_of((2 * step + index) * here + rows.start, 64)
                parts[2 * step, rows, columns] = (
                    parts[2 * step, rows, columns].astype(jnp.float32)
                    + heads[0, pl.ds(first, 64)].astype(jnp.float32)
                ).astype(jnp.bfloat16)
            return carry

        lax.fori_loop(0, here // 64, add_rows, 0)
    load(2).start()
    for index in range(3, 5):
        load(index).wait()

    def from_parts(part, rows):
        return back_product(parts[part, :, pl.ds(0, width)], heads[1, rows]) + back_product(
            parts[part, :, pl.ds(width, width)], heads[2, rows]
        )

    def far_rows(index, carry):
        rows = pl.ds(pl.multiple_of(index * 256, 256), 256)
        normed_send[:, rows] = from_parts(2, rows).astype(jnp.bfloat16)
        return carry

    lax.fori_loop(0, width // 256, far_rows, 0)
    side(3).start()
    pl.semaphore_wait(free_sem.at[1], 1)
    side(0).start()
    side(1).start()
    halving.finish(1, 0)
    halving.finish(2, 0)
    halving.finish(0, 1)

    load(2).wait()

    def own_rows(index, carry):
        rows = pl.ds(pl.multiple_of(index * 256, 256), 256)
        grad_normed[:, rows] = from_parts(0, rows) + back_product(grad_query[...], heads[0, rows])
        return carry

    lax.fori_loop(0, width // 256, own_rows, 0)
    for part in range(4):
        load_part(part, 0).wait()
        load_part(part, 1).wait()

    def select_rows(index, carry):
        first = pl.multiple_of(index * 128, 128)
        row = first + lax.broadcasted_iota(jnp.int32, (128, width), 0)
        lane = lax.broadcasted_iota(jnp.int32, (128, width), 1)
        source = lax.div(row, 16) * 32 + core_index * 16 + lax.rem(row, 16)
        pick = jnp.where(lane == source, 1.0, 0.0).astype(jnp.bfloat16)
        value = back_product(pick[:, :half], held[0]) + back_product(pick[:, half:], held[1])
        value = value.astype(jnp.bfloat16)
        lows[pl.ds(first, 128)] = value[:, :half]
        lows[pl.ds(pl.multiple_of(half + first, 128), 128)] = value[:, half:]
        return carry

    lax.fori_loop(0, half // 128, select_rows, 0)
    load(8).start()
    load(9).start()

    def rows_one(part):
        return lows[pl.ds(part // 2 * half, half), pl.ds(part % 2 * here, here)]

    side(2).wait_recv()
    for quarter in range(4):
        columns = pl.ds(quarter * 256, 256)
        halving.store(
            3,
            quarter,
            project(rows_one(0), grad_query[:, columns])
            + project(rows_one(1), query_landing[:, columns]),
        )
    side(0).wait_recv()
    side(1).wait_recv()
    for quarter in range(4):
        columns = pl.ds(quarter * 512, 512)
        halving.store(
            4,
            quarter,
            project(rows_one(0), parts[0, :, columns])
            + project(rows_one(1), parts[1, :, columns])
            + project(rows_one(2), parts[2, :, columns])
            + project(rows_one(3), parts[3, :, columns]),
        )
    halving.finish(0, 2)
    halving.finish(1, 1)
    halving.finish(2, 1)
    load(5).wait()
    side(3).wait_recv()

    def norm_rows(index, sums):
        rows = pl.ds(pl.multiple_of(index * 32, 32), 32)
        grads = grad_normed[rows] + normed_landing[rows].astype(jnp.float32)
        center = units[rows] - mean_rows(units[rows])
        scale = lax.rsqrt(mean_rows(center * center) + EPS)
        value, gain_part, bias_part = norm_back(center * scale, grads, gain_one[...], scale)
        grad_hidden[rows] = (residuals[rows] + value).astype(jnp.bfloat16)
        return sums[0] + gain_part, sums[1] + bias_part

    gain_sum, bias_sum = lax.fori_loop(0, here // 32, norm_rows, (nothing, nothing))
    side(4).start()
    vectors[pl.ds(0, 1)] = gain_sum
    vectors[pl.ds(1, 1)] = bias_sum
    vector_copy(0).start()
    load(7).wait()

    def stored_rows(index, carry):
        rows = pl.ds(pl.multiple_of(index * 256, 256), 256)
        below = pl.ds(pl.multiple_of(width + index * 256, 256), 256)
        stored_send[:, rows] = back_product(grad_hidden[...], columns_two[below]).astype(
            jnp.bfloat16
        )
        return carry

    lax.fori_loop(0, width // 256, stored_rows, 0)
    side(5).start()
    load(8).wait()
    load(9).wait()
    side(4).wait_recv()
    for quarter in range(4):
        columns = pl.ds(quarter * 256, 256)
        halving.store(
            5,
            quarter,
            project(held[0, :, pl.ds(0, here)], grad_hidden[:, columns])
            + project(held[0, :, pl.ds(here, here)], hidden_landing[:, columns]),
        )
    halving.finish(0, 3)
    halving.finish(1, 2)
    halving.finish(2, 2)
    halving.finish(3, 0)
    halving.finish(4, 0)
    vector_finish(0)

    def own_grads(index, carry):
        rows = pl.ds(pl.multiple_of(index * 256, 256), 256)
        grad_own[:, rows] = back_product(grad_hidden[...], columns_two[rows]).astype(jnp.bfloat16)
        return carry

    lax.fori_loop(0, width // 256, own_grads, 0)
    for stage in range(5):
        halving.finish(5, stage)
        if stage == 0:
            halving.finish(0, 4)
        if stage < 2:
            halving.finish(1, stage + 3)
            halving.finish(2, stage + 3)
        if stage < 4:
            halving.finish(3, stage + 1)
            halving.finish(4, stage + 1)
        vector_finish(stage + 1)
    side(5).wait_recv()
    grad_stored[...] = stored_landing[...]
    halving.drain()
    for index in range(7):
        side(index).wait_send()


def backward(inputs, large, small, collective_id):
    query = inputs[0]
    keys = large[0]
    here, width = query.shape
    span = keys.shape[0]
    shapes = [(width // 16, width), (width // 64, 4 * width), (width // 64, width)]
    shapes += [(width // 64, width), (width // 64, 2 * width), (width // 32, width)]
    inside = pl.BlockSpec(memory_space=pltpu.VMEM)
    outside = pl.BlockSpec(memory_space=pl.ANY)
    result_shapes = shapes[:4] + [shapes[3], shapes[3]] + shapes[5:]
    rows_shape = (here, width)
    low_rows = pltpu.VMEM(rows_shape, jnp.bfloat16)
    full_rows = pltpu.VMEM(rows_shape, jnp.float32)
    dma = pltpu.SemaphoreType.DMA
    operands = [query, *large[:3], *inputs[1:], *large[3:], *small]
    specs = [inside] + [outside] * 3 + [inside] * 3 + [outside] * (len(large) - 3)
    specs += [inside] * len(small)
    return pl.pallas_call(
        functools.partial(backward_kernel, shapes),
        in_specs=specs,
        out_specs=[inside] * (4 + len(result_shapes)),
        out_shape=[jax.ShapeDtypeStruct(rows_shape, jnp.bfloat16)] * 3
        + [jax.ShapeDtypeStruct((8, width), jnp.float32)]
        + [jax.ShapeDtypeStruct(shape, jnp.float32) for shape in result_shapes],
        scratch_shapes=[
            pltpu.VMEM((span, 2 * here), jnp.bfloat16),
            pltpu.VMEM((2, span, 2 * here), jnp.bfloat16),
            dma((2,)),
            pltpu.VMEM((4, here, 2 * width), jnp.bfloat16),
            pltpu.SemaphoreType.REGULAR((2,)),
            dma,
            dma,
            low_rows,
            low_rows,
            dma((8,)),
            dma((8,)),
            pltpu.VMEM((2 * width, width), jnp.bfloat16),
            pltpu.VMEM((3, width, width), jnp.bfloat16),
            dma((12,)),
            full_rows,
            full_rows,
            full_rows,
            low_rows,
            low_rows,
            low_rows,
            low_rows,
            low_rows,
            low_rows,
            pltpu.VMEM((6, 8, width), jnp.float32),
            dma((6,)),
            dma((6,)),
            pltpu.VMEM((width, here), jnp.bfloat16),
            pltpu.VMEM((here, 1), jnp.float32),
            dma((2, 2)),
            dma((4,)),
            dma((4,)),
            dma((8,)),
            dma((4, 2)),
        ]
        + Halving.scratch(shapes),
        compiler_params=pltpu.CompilerParams(
            collective_id=collective_id,
            has_side_effects=True,
            vmem_limit_bytes=62 * 2**20,
        ),
    )(*operands)


def mean_rows(value):
    return jnp.mean(value, axis=-1, keepdims=True)


def copy_kernel(*refs):
    count = (len(refs) - 1) // 3
    ways = []
    for index in range(count):
        source, target, stop = refs[index], refs[count + index], refs[2 * count + index]
        ways.append(
            (
                pltpu.make_async_copy(source, stop, refs[-1].at[0, index]),
                pltpu.make_async_copy(stop, target, refs[-1].at[1, index]),
            )
        )
    for into, _ in ways:
        into.start()
    for into, out in ways:
        into.wait()
        out.start()
    for _, out in ways:
        out.wait()


def copied(arrays):
    outside = pl.BlockSpec(memory_space=pl.ANY)
    return pl.pallas_call(
        copy_kernel,
        in_specs=[outside] * len(arrays),
        out_specs=[outside] * len(arrays),
        out_shape=[jax.ShapeDtypeStruct(array.shape, array.dtype) for array in arrays],
        scratch_shapes=[pltpu.VMEM(array.shape, array.dtype) for array in arrays]
        + [pltpu.SemaphoreType.DMA((2, len(arrays)))],
    )(*arrays)


def on_device(
    states,
    mirror,
    w_skip,
    norm1_gain,
    norm1_bias,
    w_query,
    w_key,
    w_value,
    w_out,
    norm2_gain,
    norm2_bias,
    w_up,
    w_down,
    out_grad,
    lengths,
    infill_spans,
):
    rows_here = states.shape[2]
    model_width = states.shape[3]
    head_count = HEADS
    head_dim = model_width // head_count
    query_scale = head_dim ** (-0.5) * LOG2E
    seq = lax.axis_index("seq")
    own_rows = states.reshape(rows_here, model_width)
    stored = mirror.reshape(rows_here, model_width)
    partner = from_partner(stored, "section", 0)
    lengths_row = lengths.reshape(-1)
    spans_row = infill_spans.reshape(-1, 2)
    row_length = rows_here * lax.axis_size("seq")
    local = jnp.arange(rows_here, dtype=jnp.int32)
    query_place = seq * rows_here + local
    key_place = jnp.concatenate([(seq ^ step) * rows_here + local for step in range(4)])
    query_segment, inside = segment_tables(lengths_row, spans_row, query_place)
    key_segment = segment_tables(lengths_row, spans_row, key_place)[0]
    tables = (key_place[:, None], key_segment[:, None], query_place[None], query_segment[None])
    slopes = 2.0 ** (-8.0 * (jnp.arange(head_count, dtype=jnp.float32) + 1.0) / head_count)
    slopes = jnp.repeat(LOG2E * slopes.reshape(-1, 2), rows_here, axis=1)[:, None, :]
    gain_one = norm1_gain.astype(jnp.float32)
    bias_one = norm1_bias.astype(jnp.float32)
    w_first = w_skip[:model_width]
    w_second = w_skip[model_width:]
    core = seq % 2
    select = jnp.concatenate(
        [core_selector(core, model_width), core_selector(1 - core, model_width)], axis=0
    )

    grad_low = jnp.where(
        inside[:, None], out_grad.reshape(rows_here, model_width), jnp.bfloat16(0)
    )
    hidden = project(own_rows, w_first) + project(partner, w_second)
    normed_one = low(norm_forward(hidden, gain_one, bias_one))
    own_split = low(back_product(select, own_rows))
    partner_split = low(back_product(select, partner))
    half = model_width // 2
    joined_mine = jnp.concatenate([own_split[:half], partner_split[:half]], axis=0)
    joined_other = swap_core(jnp.concatenate([own_split[half:], partner_split[half:]], axis=0))
    far = partner_of(normed_one, "seq", 2)
    near = swap_core(normed_one)
    far_near = swap_core(far)
    normed_all = jnp.concatenate([normed_one, near, far, far_near], axis=0)
    query = low(project(normed_one, w_query) * query_scale)
    keys_all = low(project(normed_all, w_key))
    values_all = low(project(normed_all, w_value))
    shares, mixed_rows, inverses = attention_forward(query, keys_all, values_all, tables, slopes)
    results = backward(
        [query, inverses, mixed_rows, grad_low],
        [
            keys_all,
            values_all,
            shares,
            hidden,
            w_out,
            w_up,
            w_down,
            w_query,
            w_key,
            w_value,
            w_skip,
            normed_one,
            near,
            far,
            far_near,
            joined_mine,
            joined_other,
        ],
        [
            gain_one[None],
            norm2_gain.astype(jnp.float32)[None],
            norm2_bias.astype(jnp.float32)[None],
        ],
        1,
    )
    sums = results[3]
    (
        output,
        grad_own,
        grad_stored,
        down_sum,
        up_sum,
        out_sum,
        query_sum,
        key_sum,
        value_sum,
        skip_sum,
    ) = copied(results[:3] + results[4:])
    shard = lax.axis_index("dp") * 4 + seq
    piece = model_width // 64
    sums = lax.dynamic_slice(sums, (0, shard * piece), (4, piece))
    return (
        output.reshape(states.shape),
        grad_own.reshape(states.shape),
        grad_stored.reshape(states.shape),
        skip_sum[None],
        sums[0][None],
        sums[1][None],
        query_sum[None],
        key_sum[None],
        value_sum[None],
        out_sum[None],
        sums[2][None],
        sums[3][None],
        up_sum[None],
        down_sum[None],
    )


def solution(mesh):
    in_specs = (
        P("section", "dp", "seq", None),
        P("section", "dp", "seq", None),
        P(),
        P(),
        P(),
        P(),
        P(),
        P(),
        P(),
        P(),
        P(),
        P(),
        P(),
        P("section", "dp", "seq", None),
        P("section", "dp", None),
        P("section", "dp", None, None),
    )
    out_specs = (
        P("section", "dp", "seq", None),
        P("section", "dp", "seq", None),
        P("section", "dp", "seq", None),
        P("section", ("dp", "seq"), None),
        P("section", ("dp", "seq")),
        P("section", ("dp", "seq")),
        P("section", ("dp", "seq"), None),
        P("section", ("dp", "seq"), None),
        P("section", ("dp", "seq"), None),
        P("section", ("dp", "seq"), None),
        P("section", ("dp", "seq")),
        P("section", ("dp", "seq")),
        P("section", ("dp", "seq"), None),
        P("section", ("dp", "seq"), None),
    )
    return jax.shard_map(
        on_device, mesh=mesh, in_specs=in_specs, out_specs=out_specs, check_vma=False
    )
```

time: 209 us -> 175 us (0.84); the launches traced: 205 us -> 174 us
  matrix products: 35.4 us -> 12.7 us
  local copies, waits for them, and re-layouts: 12.6 us -> 6.52 us
  waiting for transfers between devices: 15.5 us -> 10.2 us
  Pallas kernels: 126 us -> 129 us
  other arithmetic: 5.99 us -> 8.46 us
    dot_general x8 -> x5, matrix products: 25.5 us -> 10 us  [project(): return jnp.dot(left, right, preferred_element_type=jnp.float32)]
    dot_general x5 -> x2, matrix products: 9.88 us -> 2.71 us  [back_product(): lax.dot_general(left, right, (((1,), (1,)), ((), ())), preferred_element_...]
    unnamed x77 -> x40, local copies, waits for them, and re-layouts: 9.86 us -> 4.62 us
    pallas_call x2, Pallas kernels: 114 us -> 117 us  [the longest x1 115 us: backward(): pl.pallas_call(functools.partial(backward_kernel, shapes), in_specs=specs...]
    ppermute x10 -> x4, waiting for transfers between devices: 10.2 us -> 7.28 us  [partner_of(): return lax.ppermute(value, axis, pairs)]
    ppermute x1, waiting for transfers between devices: 5.33 us -> 2.93 us  [from_partner(): return lax.ppermute(value, axis, pairs)]
    ppermute x10 -> x4, starting transfers between devices: 5.87 us -> 4.03 us  [partner_of(): return lax.ppermute(value, axis, pairs)]
  transfers between devices with their start and end apart: 11 -> 5, of which waited for: 2 -> 2; matrix products, arithmetic and copies ran while one was open for 21% -> 12% of each run, Pallas kernels for 15% -> 7%
where the time goes in v6:
time: 175 us; the launch traced here: 174 us
  Pallas kernels  129 us (74%)
  matrix products  12.7 us (7%)
  waiting for transfers between devices  10.2 us (6%)
  other arithmetic  8.46 us (5%)
  local copies, waits for them, and re-layouts  6.52 us (4%)
  starting transfers between devices  5.77 us (3%)
    pallas_call x1, Pallas kernels, backward(): pl.pallas_call(functools.partial(backward_kernel, shapes), in_specs=specs...  115 us
    pallas_call x1, Pallas kernels, attention_forward(): pl.pallas_call(attention_forward_kernel, grid=(pairs,), in_specs=[pl.Bloc...  11.9 us
    dot_general x5, matrix products, project(): return jnp.dot(left, right, preferred_element_type=jnp.float32)  10 us
    ppermute x4, waiting for transfers between devices, partner_of(): return lax.ppermute(value, axis, pairs)  7.28 us
    unnamed x40, local copies, waits for them, and re-layouts  4.62 us
    ppermute x4, starting transfers between devices, partner_of(): return lax.ppermute(value, axis, pairs)  4.03 us
  transfers between devices with their start and end apart: 5, of which 2 were waited for; matrix products, arithmetic and copies ran while one was open for 12% of the time, Pallas kernels for 7%

profile of v6, /device:TPU:0, one launch (start us, length us, event | category | flops | bytes accessed | tf_op | source)
XLA Modules:
  0.0 174.2 jit_solution(17031420922831070103)
XLA Ops:
  0.7 1.7 collective-permute-start
  2.4 0.8 reduce-window.7
  3.3 0.8 bitcast_add_fusion.1
  4.2 0.7 convert_element_type.34
  4.9 0.7 convert_element_type.35
  5.7 1.9 %bitcast_select_fusion.grad_low = bf16[256,1024]{1,0:T(8,128)(2,1)} fusion(bf16[1,1,256,1024]{3,2,1,0:T(8,128)(2,1)} %param.29, pred[256]{0:T(512)(128)(4,1)S(1)} %and_reduce_fusion), kind=kLoop, calls=%fused_computation.19 | loop fusion | flops 262144 | bytes 1048832 | tf_op jit(solution)/shard_map/jit(_where)/select_n | solution.py:1058
  8.3 0.8 convolution_convert_fusion.3
  9.3 1.6 copy-done.7
  10.9 0.7 fusion.2
  11.6 2.9 %collective-permute-done = bf16[256,1024]{1,0:T(8,128)(2,1)S(1)} collective-permute-done((bf16[256,1024]{1,0:T(8,128)(2,1)}, bf16[256,1024]{1,0:T(8,128)(2,1)S(1)}, u32[]{:S(2)}, u32[]{:S(2)}) %collective-permute-start) | collective-permute-done | bytes 524320 | tf_op jit(solution)/shard_map/ppermute | solution.py:21
  14.5 0.8 fusion.25
  16.4 3.4 %collective-permute-start.2 = (bf16[256,1024]{1,0:T(8,128)(2,1)S(1)}, bf16[256,1024]{1,0:T(8,128)(2,1)}, u32[]{:S(2)}, u32[]{:S(2)}) collective-permute-start(bf16[256,1024]{1,0:T(8,128)(2,1)S(1)} %add_convert_fusion.normed_own), channel_id=1, source_target_pairs={{0,2},{1,3},{2,0},{3,1},{4,6},{5,7},{6,4},{7,5},{8,10},{9,11},{10,... | collective-permute-start | bytes 1572872 | tf_op jit(solution)/shard_map/ppermute | solution.py:61
  21.6 2.0 %convolution_convert_fusion.2 = bf16[1024,256]{1,0:T(8,128)(2,1)S(1)} fusion(bf16[256,1024]{1,0:T(8,128)(2,1)S(1)} %collective-permute-done, pred[512,1024]{1,0:T(32,128)(4,1)} %copy-done.15, pred[512,1024]{1,0:T(32,128)(4,1)} %copy-done.16), kind=kOutput, calls=%fused_computation.12 | convolution fusion | flops 538181632 | bytes 2097152 | tf_op jit(solution)/shard_map/dot_general | solution.py:35
  23.6 7.3 %collective-permute-done.2.normed_far = bf16[256,1024]{1,0:T(8,128)(2,1)} collective-permute-done((bf16[256,1024]{1,0:T(8,128)(2,1)S(1)}, bf16[256,1024]{1,0:T(8,128)(2,1)}, u32[]{:S(2)}, u32[]{:S(2)}) %collective-permute-start.2) | collective-permute-done | bytes 524320 | tf_op jit(solution)/shard_map/ppermute | solution.py:61
  31.5 0.9 pad_maximum_fusion.1.joined_kept
  32.4 0.7 fusion.7.query
  33.3 4.0 %convolution_convert_fusion.values = bf16[1024,1024]{1,0:T(8,128)(2,1)S(1)} fusion(bf16[1024,1024]{1,0:T(8,128)(2,1)S(1)} %copy-done.11, bf16[256,1024]{1,0:T(8,128)(2,1)S(1)} %collective-permute-done.3.normed_far_near, bf16[256,1024]{1,0:T(8,128)(2,1)} %collective-permute-done.2.normed_far, bf16[256,1024]{1,0:T(8,128)(2,1)S(1)} %collective-permute-done.1.normed_near, ...), kind=kOutput, calls=%fused_computation.8 | convolution fusion | flops 2156920832 | bytes 6291456 | tf_op jit(solution)/shard_map/dot_general | solution.py:25
  37.4 3.8 %convolution_convert_fusion.1.keys = bf16[1024,1024]{1,0:T(8,128)(2,1)S(1)} fusion(bf16[1024,1024]{1,0:T(8,128)(2,1)S(1)} %copy-done.10, bf16[256,1024]{1,0:T(8,128)(2,1)S(1)} %collective-permute-done.3.normed_far_near, bf16[256,1024]{1,0:T(8,128)(2,1)} %collective-permute-done.2.normed_far, bf16[256,1024]{1,0:T(8,128)(2,1)S(1)} %collective-permute-done.1.normed_near, ...), kind=kOutput, calls=%fused_computation.9 | convolution fusion | flops 2156920832 | bytes 6291456 | tf_op jit(solution)/shard_map/dot_general | solution.py:25
  41.2 11.9 %shard_map.263 = (bf16[8,1024,512]{2,1,0:T(8,128)(2,1)}, bf16[256,1024]{1,0:T(8,128)(2,1)S(1)}, f32[8,1,512]{2,1,0:T(1,128)S(1)}) custom-call(bf16[256,1024]{1,0:T(8,128)(2,1)S(1)} %fusion.7.query, bf16[1024,1024]{1,0:T(8,128)(2,1)S(1)} %convolution_convert_fusion.1.keys, bf16[1024,1024]{1,0:T(8,128)(2,1)S(1)} %convolution_convert_fusion.values, ...), custom_call_target="tpu_custom_call" | custom-call | tf_op jit(solution)/shard_map/pallas_call | solution.py:344
  53.1 0.8 copy-done.4
  54.5 0.8 copy-done.14
  55.3 114.8 %shard_map.264 = (bf16[256,1024]{1,0:T(8,128)(2,1)}, bf16[256,1024]{1,0:T(8,128)(2,1)}, bf16[256,1024]{1,0:T(8,128)(2,1)}, f32[8,1024]{1,0:T(8,128)}, f32[64,102...) custom-call(bf16[256,1024]{1,0:T(8,128)(2,1)} %copy-done.3, ...), custom_call_target="tpu_custom_call" | custom-call | tf_op jit(solution)/shard_map/pallas_call | solution.py:924
  170.1 0.8 constant_dynamic-slice_fusion
  171.4 2.6 %shard_map.265 = (bf16[256,1024]{1,0:T(8,128)(2,1)}, bf16[256,1024]{1,0:T(8,128)(2,1)}, bf16[256,1024]{1,0:T(8,128)(2,1)}, f32[64,1024]{1,0:T(8,128)}, f32[16,40...) custom-call(bf16[256,1024]{1,0:T(8,128)(2,1)} %get-tuple-element.41., ...), custom_call_target="tpu_custom_call" | custom-call | tf_op jit(solution)/shard_map/pallas_call | solution.py:1001
  (68 shorter events, 6.0 us)
Async XLA Ops:
  0.6 7.7 %copy-start = (bf16[1,1,256,1024]{3,2,1,0:T(8,128)(2,1)S(1)}, bf16[1,1,256,1024]{3,2,1,0:T(8,128)(2,1)}, u32[]{:S(2)}) copy-start(bf16[1,1,256,1024]{3,2,1,0:T(8,128)(2,1)} %param.16) | copy-start | bytes 1572868
  0.7 13.9 %collective-permute-start = (bf16[256,1024]{1,0:T(8,128)(2,1)}, bf16[256,1024]{1,0:T(8,128)(2,1)S(1)}, u32[]{:S(2)}, u32[]{:S(2)}) collective-permute-start(bf16[256,1024]{1,0:T(8,128)(2,1)} %bitcast.55), channel_id=1, source_target_pairs={{0,64},{64,0},{1,65},{65,1},{2,66},{66,2},{3,67},{67,3},{4,68},{68... | collective-permute-start | bytes 1572872 | tf_op jit(solution)/shard_map/ppermute | solution.py:21
  4.9 10.7 %copy-start.17 = (f32[1024]{0:T(1024)}, f32[1024]{0:T(1024)S(1)}, u32[]{:S(2)}) copy-start(f32[1024]{0:T(1024)S(1)} %convert_element_type.34) | copy-start | bytes 12292
  8.3 0.8 copy-start.15
  8.3 1.0 copy-start.16
  8.3 2.6 %copy-start.7 = (bf16[2048,1024]{1,0:T(8,128)(2,1)S(1)}, bf16[2048,1024]{1,0:T(8,128)(2,1)}, u32[]{:S(2)}) copy-start(bf16[2048,1024]{1,0:T(8,128)(2,1)} %w_skip.1) | copy-start | bytes 12582916
  15.3 1.0 copy-start.6
  15.3 4.4 %copy-start.18 = (bf16[1024]{0:T(1024)(128)(2,1)S(1)}, bf16[1024]{0:T(1024)(128)(2,1)}, u32[]{:S(2)}) copy-start(bf16[1024]{0:T(1024)(128)(2,1)} %param.25) | copy-start | bytes 6148
  15.3 5.0 %copy-start.19 = (bf16[1024]{0:T(1024)(128)(2,1)S(1)}, bf16[1024]{0:T(1024)(128)(2,1)}, u32[]{:S(2)}) copy-start(bf16[1024]{0:T(1024)(128)(2,1)} %param.26) | copy-start | bytes 6148
  16.4 21.0 %copy-start.8 = (bf16[256,1024]{1,0:T(8,128)(2,1)}, bf16[256,1024]{1,0:T(8,128)(2,1)S(1)}, u32[]{:S(2)}) copy-start(bf16[256,1024]{1,0:T(8,128)(2,1)S(1)} %add_convert_fusion.normed_own) | copy-start | bytes 1572868
  16.4 14.5 %collective-permute-start.2 = (bf16[256,1024]{1,0:T(8,128)(2,1)S(1)}, bf16[256,1024]{1,0:T(8,128)(2,1)}, u32[]{:S(2)}, u32[]{:S(2)}) collective-permute-start(bf16[256,1024]{1,0:T(8,128)(2,1)S(1)} %add_convert_fusion.normed_own), channel_id=1, source_target_pairs={{0,2},{1,3},{2,0},{3,1},{4,6},{5,7},{6,4},{7,5},{8,10},{9,11},{10,... | collective-permute-start | bytes 1572872 | tf_op jit(solution)/shard_map/ppermute | solution.py:61
  21.5 11.6 %collective-permute-start.1 = (bf16[256,1024]{1,0:T(8,128)(2,1)S(1)}, bf16[256,1024]{1,0:T(8,128)(2,1)S(1)}, u32[]{:S(2)}, u32[]{:S(2)}) collective-permute-start(bf16[256,1024]{1,0:T(8,128)(2,1)S(1)} %add_convert_fusion.normed_own), channel_id=1, source_target_pairs={{0,1},{1,0},{2,3},{3,2},{4,5},{5,4},{6,7},{7,6},{8,9},{9,8},{10,11... | collective-permute-start | bytes 1572872 | tf_op jit(solution)/shard_map/ppermute | solution.py:61
  23.6 8.8 %copy-start.9 = (bf16[1024,1024]{1,0:T(8,128)(2,1)S(1)}, bf16[1024,1024]{1,0:T(8,128)(2,1)}, u32[]{:S(2)}) copy-start(bf16[1024,1024]{1,0:T(8,128)(2,1)} %w_query.1) | copy-start | bytes 6291460
  30.9 2.3 %collective-permute-start.3 = (bf16[256,1024]{1,0:T(8,128)(2,1)}, bf16[256,1024]{1,0:T(8,128)(2,1)S(1)}, u32[]{:S(2)}, u32[]{:S(2)}) collective-permute-start(bf16[256,1024]{1,0:T(8,128)(2,1)} %collective-permute-done.2.normed_far), channel_id=1, source_target_pairs={{0,1},{1,0},{2,3},{3,2},{4,5},{5,4},{6,7},{7,6},{8,9},{9,8},{10,11... | collective-permute-start | bytes 1572872 | tf_op jit(solution)/shard_map/ppermute | solution.py:61
  30.9 23.6 %collective-permute-start.4 = (bf16[1024,256]{1,0:T(8,128)(2,1)S(1)}, bf16[1024,256]{1,0:T(8,128)(2,1)S(1)}, u32[]{:S(2)}, u32[]{:S(2)}) collective-permute-start(bf16[1024,256]{1,0:T(8,128)(2,1)S(1)} %pad_maximum_fusion.2), channel_id=1, source_target_pairs={{0,1},{1,0},{2,3},{3,2},{4,5},{5,4},{6,7},{7,6},{8,9},{9,8},{10,11... | collective-permute-start | bytes 1572872 | tf_op jit(solution)/shard_map/ppermute | solution.py:61
  31.5 1.8 %copy-start.11 = (bf16[1024,1024]{1,0:T(8,128)(2,1)S(1)}, bf16[1024,1024]{1,0:T(8,128)(2,1)}, u32[]{:S(2)}) copy-start(bf16[1024,1024]{1,0:T(8,128)(2,1)} %w_value.1) | copy-start | bytes 6291460
  33.1 8.1 %copy-start.3 = (bf16[256,1024]{1,0:T(8,128)(2,1)}, bf16[256,1024]{1,0:T(8,128)(2,1)S(1)}, u32[]{:S(2)}) copy-start(bf16[256,1024]{1,0:T(8,128)(2,1)S(1)} %fusion.7.query) | copy-start | bytes 1572868
  33.1 4.3 %copy-start.10 = (bf16[1024,1024]{1,0:T(8,128)(2,1)S(1)}, bf16[1024,1024]{1,0:T(8,128)(2,1)}, u32[]{:S(2)}) copy-start(bf16[1024,1024]{1,0:T(8,128)(2,1)} %w_key.1) | copy-start | bytes 6291460
  33.1 4.2 %copy-start.12 = (bf16[256,1024]{1,0:T(8,128)(2,1)}, bf16[256,1024]{1,0:T(8,128)(2,1)S(1)}, u32[]{:S(2)}) copy-start(bf16[256,1024]{1,0:T(8,128)(2,1)S(1)} %collective-permute-done.1.normed_near) | copy-start | bytes 1572868
  33.3 4.1 %copy-start.13 = (bf16[256,1024]{1,0:T(8,128)(2,1)}, bf16[256,1024]{1,0:T(8,128)(2,1)S(1)}, u32[]{:S(2)}) copy-start(bf16[256,1024]{1,0:T(8,128)(2,1)S(1)} %collective-permute-done.3.normed_far_near) | copy-start | bytes 1572868
  37.4 3.8 %copy-start.1 = (bf16[1024,1024]{1,0:T(8,128)(2,1)}, bf16[1024,1024]{1,0:T(8,128)(2,1)S(1)}, u32[]{:S(2)}) copy-start(bf16[1024,1024]{1,0:T(8,128)(2,1)S(1)} %convolution_convert_fusion.values) | copy-start | bytes 6291460
  41.2 11.9 %copy-start.2 = (bf16[1024,1024]{1,0:T(8,128)(2,1)}, bf16[1024,1024]{1,0:T(8,128)(2,1)S(1)}, u32[]{:S(2)}) copy-start(bf16[1024,1024]{1,0:T(8,128)(2,1)S(1)} %convolution_convert_fusion.1.keys) | copy-start | bytes 6291460
  53.1 0.8 copy-start.4
  54.5 0.8 copy-start.14
  (1 other events, 0.6 us)

commit v7 on v6

--- a/solution.py
+++ b/solution.py
@@ -7,18 +7,11 @@
 from jax import lax
 from jax.sharding import PartitionSpec as P
 
-HEADS = 16
 LOG2E = 1.4426950408889634
 LN2 = 0.6931471805599453
 
 
 EPS = 1e-05
-
-
-def from_partner(value, axis, stride):
-    mask = 2**stride
-    pairs = [(source, source ^ mask) for source in range(lax.axis_size(axis))]
-    return lax.ppermute(value, axis, pairs)
 
 
 def project(left, right):
@@ -35,45 +28,6 @@
     return lax.dot_general(
         left, right, (((1,), (1,)), ((), ())), preferred_element_type=jnp.float32
     )
-
-
-def norm_forward(hidden, gain, bias):
-    center = hidden - jnp.mean(hidden, axis=-1, keepdims=True)
-    variance = jnp.mean(center * center, axis=-1, keepdims=True)
-    inverse = lax.rsqrt(variance + EPS)
-    return center * inverse * gain + bias
-
-
-def segment_tables(lengths_row, spans_row, places):
-    ends = jnp.cumsum(lengths_row, dtype=jnp.int32)
-    starts = ends - lengths_row
-    segment = jnp.sum((places[:, None] >= ends[None, :]).astype(jnp.int32), axis=1)
-    lower = starts + spans_row[:, 0]
-    upper = starts + spans_row[:, 1]
-    inside = jnp.any(
-        (places[:, None] >= lower[None, :]) & (places[:, None] < upper[None, :]), axis=1
-    )
-    return (segment, inside)
-
-
-def partner_of(value, axis, mask):
-    pairs = [(source, source ^ mask) for source in range(lax.axis_size(axis))]
-    return lax.ppermute(value, axis, pairs)
-
-
-def core_selector(core, rows):
-    piece = rows // 32
-    target = jnp.arange(rows // 2, dtype=jnp.int32)
-    source = (target // piece) * (2 * piece) + core * piece + target % piece
-    return (source[:, None] == jnp.arange(rows, dtype=jnp.int32)[None, :]).astype(jnp.bfloat16)
-
-
-def swap_core(value):
-    return partner_of(value, "seq", 1)
-
-
-def low(value):
-    return value.astype(jnp.bfloat16)
 
 
 MESH = pl.DeviceIdType.MESH
@@ -141,11 +95,6 @@
     return lax.div(dp, 4), lax.rem(dp, 4), seq
 
 
-def ring_partners(z, x, seq):
-    pairs = ((0, 0), (0, 1), (2, 0), (2, 1), (0, 4))
-    return [stage_partner(quarter, stage, x, z, seq) for quarter, stage in pairs]
-
-
 def either(one, two):
     return 2 * lax.rem(lax.div(one, 2) + lax.div(two, 2), 2) + lax.rem(one + two, 2)
 
@@ -170,16 +119,22 @@
         count = len(shapes)
         self.work = scratch[:count]
         self.landings = [scratch[count + 5 * job : count + 5 * job + 5] for job in range(count)]
-        self.send_sem, self.recv_sem = scratch[6 * count :]
+        self.landings[-1] = self.landings[-1][:3]
+        self.send_sem, self.recv_sem = scratch[-2:]
         self.z, self.x, self.seq = place_here()
         self.y = lax.div(self.seq, 2)
 
     @staticmethod
     def scratch(shapes):
         shapes_of = [(4, 16, 2 * rows, width // 4) for rows, width in shapes]
-        for rows, width in shapes:
-            shapes_of += [(4, blocks, 2 * rows, width // 4) for blocks in (8, 4, 2, 1)]
-            shapes_of.append((4, rows, width // 4))
+        for job, (rows, width) in enumerate(shapes):
+            direct = job == len(shapes) - 1
+            shapes_of += [(4, blocks, 2 * rows, width // 4) for blocks in (8, 4)]
+            if direct:
+                shapes_of.append((4, 7, rows, width // 4))
+            else:
+                shapes_of += [(4, blocks, 2 * rows, width // 4) for blocks in (2, 1)]
+                shapes_of.append((4, rows, width // 4))
         sems = pltpu.SemaphoreType.DMA((len(shapes), 4, 5))
         return [pltpu.VMEM(shape, jnp.bfloat16) for shape in shapes_of] + [sems, sems]
 
@@ -241,10 +196,52 @@
                     ...
                 ].astype(jnp.float32)
 
+    def direct(self, job, quarter, step):
+        rows = self.shapes[job][0]
+        first, order = QUARTERS[quarter]
+        inner, away = step // 2, step % 2
+        if first == "x":
+            dp = flip(self.z, order[inner]) * 4 + self.x
+        else:
+            dp = self.z * 4 + flip(self.x, order[inner])
+        part = pl.multiple_of((1 - self.y if away else self.y) * rows, 16)
+        return remote(
+            self.work[job].at[quarter, inner, pl.ds(part, rows)],
+            self.landings[job][2].at[quarter, step - 1],
+            self.send_sem.at[job, quarter, 2],
+            self.recv_sem.at[job, quarter, 2],
+            {"dp": dp, "seq": flip(self.seq, 2) if away else self.seq},
+        )
+
+    def finish_direct(self, job, stage):
+        rows, width = self.shapes[job]
+        for quarter in range(4):
+            work = self.work[job].at[quarter]
+            landing = self.landings[job][stage].at[quarter]
+            if stage < 2:
+                self.copy(job, quarter, stage).wait_recv()
+                add_blocks(8 >> stage, work, landing)
+                if stage == 0:
+                    self.copy(job, quarter, 1).start()
+                else:
+                    for step in range(1, 8):
+                        self.direct(job, quarter, step).start()
+            else:
+                remote(
+                    landing, landing, self.send_sem.at[job, quarter, 2],
+                    self.recv_sem.at[job, quarter, 2], {"seq": flip(self.seq, 2)},
+                ).wait()
+                mine = pl.multiple_of(self.y * rows, 16)
+                total = work[0, pl.ds(mine, rows)].astype(jnp.float32)
+                for step in range(7):
+                    total = total + landing[step].astype(jnp.float32)
+                self.results[job][0][:, pl.ds(quarter * width // 4, width // 4)] = total
+
     def drain(self):
-        for job in range(len(self.shapes)):
+        last = len(self.shapes) - 1
+        for job in range(last + 1):
             for quarter in range(4):
-                for stage in range(5):
+                for stage in range(2 if job == last else 5):
                     self.copy(job, quarter, stage).wait_send()
 
 
@@ -259,24 +256,29 @@
     )
     turned = grad.astype(jnp.float32).T
     product = turned * mixed.astype(jnp.float32).T
-    first = turned[:64] * inverse[:, :here]
-    second = turned[64:] * inverse[:, here:]
-    none = jnp.zeros_like(first)
-    grads = jnp.concatenate(
-        [jnp.concatenate([first, none], axis=1), jnp.concatenate([none, second], axis=1)], axis=0
-    ).astype(jnp.bfloat16)
-    grads_back = grads.T
-    centre = inverse * jnp.concatenate(
+    centre = jnp.concatenate(
         [
             jnp.sum(product[:64], axis=0, keepdims=True),
             jnp.sum(product[64:], axis=0, keepdims=True),
         ],
         axis=1,
     )
+    none = jnp.zeros((64, here), jnp.float32)
+    sets = []
+    for part in range(2):
+        factor = inverse[part : part + 1]
+        first = turned[:64] * factor[:, :here]
+        second = turned[64:] * factor[:, here:]
+        grads = jnp.concatenate(
+            [jnp.concatenate([first, none], axis=1), jnp.concatenate([none, second], axis=1)],
+            axis=0,
+        ).astype(jnp.bfloat16)
+        sets.append((grads, grads.T, centre * factor))
     grad_keys, grad_values = [], []
     for index in range(span // chunk):
         rows = pl.ds(index * chunk, chunk)
         part = share[rows]
+        grads, grads_back, centre = sets[2 * index // (span // chunk)]
         grad_share = project(values[rows], grads)
         grad_score = (part.astype(jnp.float32) * (grad_share - centre)).astype(jnp.bfloat16)
         lows[rows] = grad_score
@@ -287,86 +289,266 @@
     return (out.T * 0.125).astype(jnp.bfloat16), grad_keys, grad_values
 
 
-def attention_forward_kernel(
-    query, keys, values, key_places, key_segments, query_places, query_segments, slopes,
-    shares, mixed, inverses, distance, scores,
+def flat(vector):
+    return vector[...].astype(jnp.float32).reshape(1, vector.shape[0])
+
+
+def forward_kernel(
+    lengths, spans, own, stored, out_grad, gain_one, bias_one, w_skip, w_query, w_key, w_value,
+    hidden, query, inverses, mixed, grad_low, kept, shares, keys_out, values_out, normed_out, other,
+    partner, normed, joined_sent, joined_landing, turned, w_rows, heads, keys, values,
+    distance, scores, exponents, outs, tops, load_sem, send_sem, recv_sem, share_sem,
 ):
+    seq = lax.axis_index("seq")
+    core_index = lax.rem(seq, 2)
+    core, far = {"seq": flip(seq, 1)}, {"seq": flip(seq, 2)}
+    section = {"section": 1 - lax.axis_index("section")}
+    here, width = own.shape
     span = keys.shape[0]
-    chunk = 128
-    here = query.shape[0]
-
-    @pl.when(pl.program_id(0) == 0)
-    def _():
-        gap = jnp.abs(query_places[...] - key_places[...]).astype(jnp.float32)
-        same = query_segments[...] == key_segments[...]
-        distance[...] = jnp.where(same, gap, 1e30)
-
-    lane = lax.broadcasted_iota(jnp.int32, query.shape, 1)
-    zero = jnp.zeros(query.shape, query.dtype)
-    both = jnp.concatenate(
-        [jnp.where(lane < 64, query[...], zero), jnp.where(lane >= 64, query[...], zero)], axis=0
-    )
-    slope = slopes[0]
-
-    def raw(index, top):
-        rows = pl.ds(pl.multiple_of(index * chunk, chunk), chunk)
-        part = back_product(keys[rows], both)
-        gap = distance[rows]
-        part = part - slope * jnp.concatenate([gap, gap], axis=1)
-        scores[rows] = part
-        return jnp.maximum(top, jnp.max(part.reshape(chunk // 8, 8, 2 * here), axis=0))
-
-    top = lax.fori_loop(
-        0, span // chunk, raw, jnp.full((8, 2 * here), -jnp.inf, jnp.float32), unroll=True
-    )
-    top = jnp.max(top, axis=0, keepdims=True)
-
-    def exponent(index, carry):
-        rows = pl.ds(pl.multiple_of(index * chunk, chunk), chunk)
-        shares[0, rows] = jnp.exp2(scores[rows] - top).astype(jnp.bfloat16)
+    half = width // 2
+    pairs = width // 128
+    piece = here // 2
+
+    loads = [
+        pltpu.make_async_copy(source, target, load_sem.at[index])
+        for index, (source, target) in enumerate(
+            (
+                (w_skip, w_rows),
+                (w_query, heads.at[0]),
+                (w_key, heads.at[1]),
+                (w_value, heads.at[2]),
+                (keys, keys_out),
+                (values, values_out),
+                (normed, normed_out),
+                (joined_landing, other),
+            )
+        )
+    ]
+
+    def send(index, part):
+        rows = pl.ds(part * piece, piece)
+        source, target, device = (
+            (stored.at[rows], partner.at[rows], section),
+            (normed.at[rows], normed.at[pl.ds(here + part * piece, piece)], core),
+            (normed.at[rows], normed.at[pl.ds(2 * here + part * piece, piece)], far),
+            (
+                normed.at[pl.ds(2 * here + part * piece, piece)],
+                normed.at[pl.ds(3 * here + part * piece, piece)],
+                core,
+            ),
+            (
+                joined_sent.at[pl.ds(part * half, half)],
+                joined_landing.at[pl.ds(part * half, half)],
+                core,
+            ),
+        )[index]
+        return remote(source, target, send_sem.at[index, part], recv_sem.at[index, part], device)
+
+    for index in range(4):
+        loads[index].start()
+    enter([core, far, section])
+    send(0, 0).start()
+    send(0, 1).start()
+
+    bounds = []
+    start = jnp.int32(0)
+    for index in range(4):
+        bounds.append((start, start + lengths[0, 0, index]))
+        start = start + lengths[0, 0, index]
+
+    def segment(places):
+        return sum((places >= bounds[index][1]).astype(jnp.int32) for index in range(4))
+
+    place = seq * here + lax.broadcasted_iota(jnp.int32, (here, 1), 0)
+    inside = jnp.zeros((here, 1), jnp.int32)
+    for index in range(4):
+        low_end = bounds[index][0] + spans[0, 0, index, 0]
+        high_end = bounds[index][0] + spans[0, 0, index, 1]
+        inside += (place >= low_end).astype(jnp.int32) * (place < high_end).astype(jnp.int32)
+    grad_low[...] = jnp.where(
+        inside > 0, out_grad[...].astype(jnp.float32), 0.0
+    ).astype(jnp.bfloat16)
+    query_place = seq * here + lax.broadcasted_iota(jnp.int32, (1, here), 1)
+    query_segment = segment(query_place)
+    for index in range(4):
+        key_place = flip(seq, index) * here + lax.broadcasted_iota(jnp.int32, (here, 1), 0)
+        gap = jnp.abs(query_place - key_place).astype(jnp.float32)
+        distance[pl.ds(index * here, here)] = jnp.where(
+            segment(key_place) == query_segment, gap, 1e30
+        )
+
+    def joined_rows(part, source):
+        turned[...] = source[...].T
+
+        def keep(row, value):
+            kept[pl.ds(part * half + row, 32)] = value
+
+        def pass_on(row, value):
+            joined_sent[pl.ds(part * half + row, 32)] = value
+
+        split_cores(core_index, turned, keep, pass_on, 32)
+        send(4, part).start()
+
+    joined_rows(0, own)
+    loads[0].wait()
+    hidden[...] = project(own[...], w_rows[pl.ds(0, width)])
+    gain, bias = flat(gain_one), flat(bias_one)
+    for part in range(2):
+        rows = pl.ds(part * piece, piece)
+        send(0, part).wait_recv()
+        value = hidden[rows] + project(partner[rows], w_rows[pl.ds(width, width)])
+        hidden[rows] = value
+        center = value - mean_rows(value)
+        scale = lax.rsqrt(mean_rows(center * center) + EPS)
+        normed[rows] = (center * scale * gain + bias).astype(jnp.bfloat16)
+        send(2, part).start()
+        send(1, part).start()
+    for index in range(1, 4):
+        loads[index].wait()
+    scale = 0.125 * LOG2E
+    query[...] = (project(normed[pl.ds(0, here)], heads[0]) * scale).astype(jnp.bfloat16)
+
+    def both(first, count):
+        rows = pl.ds(first, count)
+        keys[rows] = project(normed[rows], heads[1]).astype(jnp.bfloat16)
+        values[rows] = project(normed[rows], heads[2]).astype(jnp.bfloat16)
+
+    def attend(part, pair):
+        columns = pl.ds(pl.multiple_of(pair * 128, 128), 128)
+        base = part * 2 * here
+        value = query[:, columns]
+        lane = lax.broadcasted_iota(jnp.int32, value.shape, 1)
+        zero = jnp.zeros(value.shape, value.dtype)
+        stacked = jnp.concatenate(
+            [jnp.where(lane < 64, value, zero), jnp.where(lane >= 64, value, zero)], axis=0
+        )
+        head = 2 * pair + 1 + lax.div(lax.broadcasted_iota(jnp.int32, (1, 2 * here), 1), here)
+        slope = LOG2E * jnp.exp2(head.astype(jnp.float32) * -0.5)
+        top = jnp.full((8, 2 * here), -jnp.inf, jnp.float32)
+        for index in range(4):
+            rows = pl.ds(base + index * 128, 128)
+            score = back_product(keys[rows, columns], stacked)
+            gap = distance[rows]
+            score = score - slope * jnp.concatenate([gap, gap], axis=1)
+            scores[pl.ds(index * 128, 128)] = score
+            top = jnp.maximum(top, jnp.max(score.reshape(16, 8, 2 * here), axis=0))
+        top = jnp.max(top, axis=0, keepdims=True)
+        for index in range(4):
+            rows = pl.ds(index * 128, 128)
+            exponents[pair, pl.ds(base + index * 128, 128)] = jnp.exp2(
+                scores[rows] - top
+            ).astype(jnp.bfloat16)
+        rows = pl.ds(base, 2 * here)
+        pltpu.make_async_copy(
+            exponents.at[pair, rows], shares.at[pair, rows], share_sem
+        ).start()
+        back = jnp.concatenate(
+            [values[rows, columns].T, jnp.ones((16, 2 * here), jnp.bfloat16)], axis=0
+        )
+        return project(back, exponents[pair, rows]), top
+
+    send(1, 0).wait_recv()
+    send(1, 1).wait_recv()
+    both(0, 2 * here)
+    joined_rows(1, partner)
+
+    def near(pair, carry):
+        out, top = attend(0, pair)
+        outs[pair] = out
+        tops[pair] = top
         return carry
 
-    lax.fori_loop(0, span // chunk, exponent, 0, unroll=True)
-    turned = jnp.concatenate([values[...].T, jnp.ones((16, span), jnp.bfloat16)], axis=0)
-    out = project(turned, shares[0])
-    inverse = 1.0 / out[128:129]
-    inverses[0] = inverse
-    out = out[:128] * inverse
-    out = jnp.concatenate([out[:64, :here], out[64:, here:]], axis=0)
-    mixed[...] = out.T.astype(jnp.bfloat16)
-
-
-def attention_forward(query, keys, values, tables, slopes):
-    here, width = query.shape
-    span = keys.shape[0]
+    lax.fori_loop(0, pairs, near, 0)
+    for part in range(2):
+        send(2, part).wait_recv()
+        send(3, part).start()
+    both(2 * here, here)
+    send(3, 0).wait_recv()
+    send(3, 1).wait_recv()
+    both(3 * here, here)
+    for index in range(4, 7):
+        loads[index].start()
+
+    def away(pair, carry):
+        out, top = attend(1, pair)
+        first, first_top = outs[pair], tops[pair]
+        best = jnp.maximum(top, first_top)
+        one, two = jnp.exp2(first_top - best), jnp.exp2(top - best)
+        total = 1.0 / (one * first[128:129] + two * out[128:129])
+        one, two = one * total, two * total
+        inverses[pair, pl.ds(0, 1)] = one
+        inverses[pair, pl.ds(1, 1)] = two
+        out = first[:128] * one + out[:128] * two
+        out = jnp.concatenate([out[:64, :here], out[64:, here:]], axis=0)
+        columns = pl.ds(pl.multiple_of(pair * 128, 128), 128)
+        mixed[:, columns] = out.T.astype(jnp.bfloat16)
+        return carry
+
+    lax.fori_loop(0, pairs, away, 0)
+    for part in range(2):
+        send(4, part).wait_recv()
+    loads[7].start()
+    pltpu.make_async_copy(exponents, shares, share_sem).wait()
+    for index in range(4, 8):
+        loads[index].wait()
+    for index in range(5):
+        for part in range(2):
+            send(index, part).wait_send()
+
+
+def forward(lengths, spans, own, stored, out_grad, norms, weights, collective_id):
+    here, width = own.shape
+    span = 4 * here
     pairs = width // 128
-    whole = lambda a: pl.BlockSpec(a.shape, lambda i: (0,) * a.ndim)
+    inside = pl.BlockSpec(memory_space=pltpu.VMEM)
+    outside = pl.BlockSpec(memory_space=pl.ANY)
+    scalars = pl.BlockSpec(memory_space=pltpu.SMEM)
+    low_shape = lambda *shape: jax.ShapeDtypeStruct(shape, jnp.bfloat16)
+    low_rows = lambda *shape: pltpu.VMEM(shape, jnp.bfloat16)
+    dma = pltpu.SemaphoreType.DMA
     return pl.pallas_call(
-        attention_forward_kernel,
-        grid=(pairs,),
-        in_specs=[
-            pl.BlockSpec((here, 128), lambda i: (0, i)),
-            pl.BlockSpec((span, 128), lambda i: (0, i)),
-            pl.BlockSpec((span, 128), lambda i: (0, i)),
-            *[whole(table) for table in tables],
-            pl.BlockSpec((1, 1, 2 * here), lambda i: (i, 0, 0)),
-        ],
-        out_specs=[
-            pl.BlockSpec((1, span, 2 * here), lambda i: (i, 0, 0)),
-            pl.BlockSpec((here, 128), lambda i: (0, i)),
-            pl.BlockSpec((1, 1, 2 * here), lambda i: (i, 0, 0)),
-        ],
+        forward_kernel,
+        in_specs=[scalars, scalars] + [inside] * 5 + [outside] * 4,
+        out_specs=[inside] * 6 + [outside] * 5,
         out_shape=[
-            jax.ShapeDtypeStruct((pairs, span, 2 * here), jnp.bfloat16),
-            jax.ShapeDtypeStruct((here, width), jnp.bfloat16),
-            jax.ShapeDtypeStruct((pairs, 1, 2 * here), jnp.float32),
+            jax.ShapeDtypeStruct((here, width), jnp.float32),
+            low_shape(here, width),
+            jax.ShapeDtypeStruct((pairs, 2, 2 * here), jnp.float32),
+            low_shape(here, width),
+            low_shape(here, width),
+            low_shape(width, here),
+            low_shape(pairs, span, 2 * here),
+            low_shape(span, width),
+            low_shape(span, width),
+            low_shape(span, width),
+            low_shape(width, here),
         ],
         scratch_shapes=[
+            low_rows(here, width),
+            low_rows(span, width),
+            low_rows(width, here),
+            low_rows(width, here),
+            low_rows(width, here),
+            low_rows(2 * width, width),
+            low_rows(3, width, width),
+            low_rows(span, width),
+            low_rows(span, width),
             pltpu.VMEM((span, here), jnp.float32),
-            pltpu.VMEM((span, 2 * here), jnp.float32),
+            pltpu.VMEM((2 * here, 2 * here), jnp.float32),
+            low_rows(pairs, span, 2 * here),
+            pltpu.VMEM((pairs, 144, 2 * here), jnp.float32),
+            pltpu.VMEM((pairs, 1, 2 * here), jnp.float32),
+            dma((8,)),
+            dma((5, 2)),
+            dma((5, 2)),
+            dma,
         ],
-        compiler_params=pltpu.CompilerParams(vmem_limit_bytes=40 * 2**20),
-    )(query, keys, values, *tables, slopes)
+        compiler_params=pltpu.CompilerParams(
+            collective_id=collective_id,
+            has_side_effects=True,
+            vmem_limit_bytes=56 * 2**20,
+        ),
+    )(lengths, spans, own, stored, out_grad, *norms, *weights)
 
 
 def split_cores(core, source, kept, sent, rows):
@@ -379,8 +561,7 @@
 
 def backward_kernel(
     shapes, query, keys, values, shares, inverses, mixed, grad_low, hidden, w_out, w_up, w_down,
-    w_query, w_key, w_value, w_skip, normed_own, normed_near, normed_far, normed_far_near,
-    joined_kept, joined_other, gain_one, gain_two, bias_two,
+    w_query, w_key, w_value, w_skip, normed_all, joined_kept, joined_other, gain_one, gain_two, bias_two,
     output, grad_own, grad_stored, vectors, *refs,
 ):
     refs = list(refs)
@@ -426,13 +607,9 @@
         )[index]
         return pltpu.make_async_copy(source, target, load_sem.at[index])
 
-    def load_part(part, index):
+    def load_part(index):
         return pltpu.make_async_copy(
-            (normed_own, normed_near, normed_far, normed_far_near)[part].at[
-                :, pl.ds(index * half, half)
-            ],
-            held.at[index, pl.ds(part * here, here)],
-            part_sem.at[part, index],
+            normed_all.at[:, pl.ds(index * half, half)], held.at[index], part_sem.at[index]
         )
 
     def load_block(step):
@@ -505,28 +682,48 @@
             core,
         )
 
-    vector_devices = [core] + [stage_partner(0, stage, x, z, seq) for stage in range(5)]
-
-    def vector_copy(step):
-        return remote(
-            vectors,
-            vector_landing.at[step],
-            vector_send.at[step],
-            vector_recv.at[step],
-            vector_devices[step],
-        )
+    vector_steps = [
+        [core],
+        [{"dp": z * 4 + flip(x, mask)} for mask in (1, 2, 3)],
+        [{"dp": flip(z, mask) * 4 + x} for mask in (1, 2, 3)],
+        [far],
+    ]
+    vector_slots = (0, 1, 4, 7)
+
+    def vector_copies(step):
+        return [
+            remote(
+                vectors,
+                vector_landing.at[slot],
+                vector_send.at[slot],
+                vector_recv.at[slot],
+                device,
+            )
+            for slot, device in enumerate(vector_steps[step], vector_slots[step])
+        ]
+
+    def vector_start(step):
+        for copy in vector_copies(step):
+            copy.start()
 
     def vector_finish(step):
-        vector_copy(step).wait()
-        vectors[...] += vector_landing[step]
-        if step < 5:
-            vector_copy(step + 1).start()
+        copies = vector_copies(step)
+        for copy in copies:
+            copy.wait()
+        for index in range(len(copies)):
+            vectors[...] += vector_landing[vector_slots[step] + index]
+        if step < 3:
+            vector_start(step + 1)
 
     for index in (6, 10, 11):
         load(index).start()
     for copy in load_block(0):
         copy.start()
-    enter(ring_partners(z, x, seq) + [core, section])
+    devices = [core, far, section]
+    for mask in (1, 2, 3):
+        for dp in (z * 4 + flip(x, mask), flip(z, mask) * 4 + x):
+            devices += [{"dp": dp}, {"dp": dp, "seq": flip(seq, 2)}]
+    enter(devices)
     side(6).start()
 
     def share_rows(index):
@@ -557,7 +754,7 @@
         center = center * scale
         units[rows] = center
         inverse_two[rows] = scale
-        stored_send[rows] = (center * gain_two[...] + bias_two[...]).astype(jnp.bfloat16)
+        stored_send[rows] = (center * flat(gain_two) + flat(bias_two)).astype(jnp.bfloat16)
         grad_normed[rows] = jnp.zeros_like(value)
         return carry
 
@@ -640,7 +837,7 @@
     def norm_two_back(index, sums):
         rows = pl.ds(pl.multiple_of(index * 32, 32), 32)
         value, gain_part, bias_part = norm_back(
-            units[rows], grad_normed[rows], gain_two[...], inverse_two[rows]
+            units[rows], grad_normed[rows], flat(gain_two), inverse_two[rows]
         )
         output[rows] = residuals[rows].astype(jnp.bfloat16)
         value = grad_low[rows].astype(jnp.float32) + value
@@ -735,9 +932,8 @@
     lax.fori_loop(0, pairs, one_pair, 0)
     side(2).start()
     load(7).start()
-    for part in range(4):
-        load_part(part, 0).start()
-        load_part(part, 1).start()
+    load_part(0).start()
+    load_part(1).start()
     swapped = remote(heads.at[0], heads.at[0], swap_send, swap_recv, core)
     swapped.wait()
     pl.semaphore_signal(free_sem.at[1], inc=1, device_id=core, device_id_type=MESH)
@@ -786,9 +982,8 @@
         return carry
 
     lax.fori_loop(0, width // 256, own_rows, 0)
-    for part in range(4):
-        load_part(part, 0).wait()
-        load_part(part, 1).wait()
+    load_part(0).wait()
+    load_part(1).wait()
 
     def select_rows(index, carry):
         first = pl.multiple_of(index * 128, 128)
@@ -841,7 +1036,7 @@
         grads = grad_normed[rows] + normed_landing[rows].astype(jnp.float32)
         center = units[rows] - mean_rows(units[rows])
         scale = lax.rsqrt(mean_rows(center * center) + EPS)
-        value, gain_part, bias_part = norm_back(center * scale, grads, gain_one[...], scale)
+        value, gain_part, bias_part = norm_back(center * scale, grads, flat(gain_one), scale)
         grad_hidden[rows] = (residuals[rows] + value).astype(jnp.bfloat16)
         return sums[0] + gain_part, sums[1] + bias_part
 
@@ -849,7 +1044,7 @@
     side(4).start()
     vectors[pl.ds(0, 1)] = gain_sum
     vectors[pl.ds(1, 1)] = bias_sum
-    vector_copy(0).start()
+    vector_start(0)
     load(7).wait()
 
     def stored_rows(index, carry):
@@ -886,17 +1081,25 @@
         return carry
 
     lax.fori_loop(0, width // 256, own_grads, 0)
-    for stage in range(5):
-        halving.finish(5, stage)
-        if stage == 0:
-            halving.finish(0, 4)
-        if stage < 2:
-            halving.finish(1, stage + 3)
-            halving.finish(2, stage + 3)
-        if stage < 4:
-            halving.finish(3, stage + 1)
-            halving.finish(4, stage + 1)
-        vector_finish(stage + 1)
+    halving.finish_direct(5, 0)
+    halving.finish(0, 4)
+    for job in (1, 2):
+        halving.finish(job, 3)
+    for job in (3, 4):
+        halving.finish(job, 1)
+    vector_finish(1)
+    halving.finish_direct(5, 1)
+    for job in (1, 2):
+        halving.finish(job, 4)
+    for job in (3, 4):
+        halving.finish(job, 2)
+    vector_finish(2)
+    for job in (3, 4):
+        halving.finish(job, 3)
+    halving.finish_direct(5, 2)
+    for job in (3, 4):
+        halving.finish(job, 4)
+    vector_finish(3)
     side(5).wait_recv()
     grad_stored[...] = stored_landing[...]
     halving.drain()
@@ -952,16 +1155,16 @@
             low_rows,
             low_rows,
             low_rows,
-            pltpu.VMEM((6, 8, width), jnp.float32),
-            dma((6,)),
-            dma((6,)),
+            pltpu.VMEM((8, 8, width), jnp.float32),
+            dma((8,)),
+            dma((8,)),
             pltpu.VMEM((width, here), jnp.bfloat16),
             pltpu.VMEM((here, 1), jnp.float32),
             dma((2, 2)),
             dma((4,)),
             dma((4,)),
             dma((8,)),
-            dma((4, 2)),
+            dma((2,)),
         ]
         + Halving.scratch(shapes),
         compiler_params=pltpu.CompilerParams(
@@ -1028,51 +1231,29 @@
 ):
     rows_here = states.shape[2]
     model_width = states.shape[3]
-    head_count = HEADS
-    head_dim = model_width // head_count
-    query_scale = head_dim ** (-0.5) * LOG2E
     seq = lax.axis_index("seq")
-    own_rows = states.reshape(rows_here, model_width)
-    stored = mirror.reshape(rows_here, model_width)
-    partner = from_partner(stored, "section", 0)
-    lengths_row = lengths.reshape(-1)
-    spans_row = infill_spans.reshape(-1, 2)
-    row_length = rows_here * lax.axis_size("seq")
-    local = jnp.arange(rows_here, dtype=jnp.int32)
-    query_place = seq * rows_here + local
-    key_place = jnp.concatenate([(seq ^ step) * rows_here + local for step in range(4)])
-    query_segment, inside = segment_tables(lengths_row, spans_row, query_place)
-    key_segment = segment_tables(lengths_row, spans_row, key_place)[0]
-    tables = (key_place[:, None], key_segment[:, None], query_place[None], query_segment[None])
-    slopes = 2.0 ** (-8.0 * (jnp.arange(head_count, dtype=jnp.float32) + 1.0) / head_count)
-    slopes = jnp.repeat(LOG2E * slopes.reshape(-1, 2), rows_here, axis=1)[:, None, :]
-    gain_one = norm1_gain.astype(jnp.float32)
-    bias_one = norm1_bias.astype(jnp.float32)
-    w_first = w_skip[:model_width]
-    w_second = w_skip[model_width:]
-    core = seq % 2
-    select = jnp.concatenate(
-        [core_selector(core, model_width), core_selector(1 - core, model_width)], axis=0
+    (
+        hidden,
+        query,
+        inverses,
+        mixed_rows,
+        grad_low,
+        joined_mine,
+        shares,
+        keys_all,
+        values_all,
+        normed_all,
+        joined_other,
+    ) = forward(
+        lengths,
+        infill_spans,
+        states.reshape(rows_here, model_width),
+        mirror.reshape(rows_here, model_width),
+        out_grad.reshape(rows_here, model_width),
+        [norm1_gain, norm1_bias],
+        (w_skip, w_query, w_key, w_value),
+        2,
     )
-
-    grad_low = jnp.where(
-        inside[:, None], out_grad.reshape(rows_here, model_width), jnp.bfloat16(0)
-    )
-    hidden = project(own_rows, w_first) + project(partner, w_second)
-    normed_one = low(norm_forward(hidden, gain_one, bias_one))
-    own_split = low(back_product(select, own_rows))
-    partner_split = low(back_product(select, partner))
-    half = model_width // 2
-    joined_mine = jnp.concatenate([own_split[:half], partner_split[:half]], axis=0)
-    joined_other = swap_core(jnp.concatenate([own_split[half:], partner_split[half:]], axis=0))
-    far = partner_of(normed_one, "seq", 2)
-    near = swap_core(normed_one)
-    far_near = swap_core(far)
-    normed_all = jnp.concatenate([normed_one, near, far, far_near], axis=0)
-    query = low(project(normed_one, w_query) * query_scale)
-    keys_all = low(project(normed_all, w_key))
-    values_all = low(project(normed_all, w_value))
-    shares, mixed_rows, inverses = attention_forward(query, keys_all, values_all, tables, slopes)
     results = backward(
         [query, inverses, mixed_rows, grad_low],
         [
@@ -1087,18 +1268,11 @@
             w_key,
             w_value,
             w_skip,
-            normed_one,
-            near,
-            far,
-            far_near,
+            normed_all,
             joined_mine,
             joined_other,
         ],
-        [
-            gain_one[None],
-            norm2_gain.astype(jnp.float32)[None],
-            norm2_bias.astype(jnp.float32)[None],
-        ],
+        [norm1_gain, norm2_gain, norm2_bias],
         1,
     )
     sums = results[3]

time: 175 us -> 158 us (0.903)
  Pallas kernels: 129 us -> 155 us
  matrix products: 12.7 us -> 0 us
  waiting for transfers between devices: 10.2 us -> 0 us
  other arithmetic: 8.46 us -> 0 us
  starting transfers between devices: 5.77 us -> 0 us
  local copies, waits for them, and re-layouts: 6.52 us -> 2.62 us
    pallas_call x1, Pallas kernels: 11.9 us -> 40.5 us  [forward(): pl.pallas_call(forward_kernel, in_specs=[scalars, scalars] + [inside] * 5...]
    dot_general x7 -> x0, matrix products: 12.7 us -> none  [the longest x5 10 us: project(): return jnp.dot(left, right, preferred_element_type=jnp.float32)]
    ppermute x5 -> x0, waiting for transfers between devices: 10.2 us -> none  [the longest x4 7.28 us: partner_of(): return lax.ppermute(value, axis, pairs)]
    ppermute x5 -> x0, starting transfers between devices: 5.77 us -> none  [the longest x4 4.03 us: partner_of(): return lax.ppermute(value, axis, pairs)]
    unnamed x40 -> x1, local copies, waits for them, and re-layouts: 4.62 us -> 1.34 us
    pallas_call x1, Pallas kernels: 115 us -> 112 us  [backward(): pl.pallas_call(functools.partial(backward_kernel, shapes), in_specs=specs...]
    select_n x1 -> x0, other arithmetic: 1.94 us -> none  [on_device(): jnp.where(inside[:, None], out_grad.reshape(rows_here, model_width), jnp....]
  transfers between devices with their start and end apart: 5 -> 0, of which waited for: 2 -> 0; matrix products, arithmetic and copies ran while one was open for 12% -> 0% of each run, Pallas kernels for 7% -> 0%
where the time goes in v7:
time: 158 us
  Pallas kernels  155 us (98%)
  local copies, waits for them, and re-layouts  2.62 us (2%)
    pallas_call x1, Pallas kernels, backward(): pl.pallas_call(functools.partial(backward_kernel, shapes), in_specs=specs...  112 us
    pallas_call x1, Pallas kernels, forward(): pl.pallas_call(forward_kernel, in_specs=[scalars, scalars] + [inside] * 5...  40.5 us

profile of v7, /device:TPU:0, one launch (start us, length us, event | category | flops | bytes accessed | tf_op | source)
XLA Modules:
  0.0 158.1 jit_solution(7220962058915412563)
XLA Ops:
  0.6 1.3 copy.30.spans
  2.0 40.5 %shard_map.263 = (f32[256,1024]{1,0:T(8,128)}, bf16[256,1024]{1,0:T(8,128)(2,1)}, f32[8,2,512]{2,1,0:T(2,128)}, bf16[256,1024]{1,0:T(8,128)(2,1)}, bf16[256,1024...) custom-call(s32[1,1,4]{2,1,0:T(1,128)} %lengths.1, ...), custom_call_target="tpu_custom_call" | custom-call | tf_op jit(solution)/shard_map/pallas_call | solution.py:509
  42.4 111.7 %shard_map.264 = (bf16[256,1024]{1,0:T(8,128)(2,1)}, bf16[256,1024]{1,0:T(8,128)(2,1)}, bf16[256,1024]{1,0:T(8,128)(2,1)}, f32[8,1024]{1,0:T(8,128)}, f32[64,102...) custom-call(bf16[256,1024]{1,0:T(8,128)(2,1)} %get-tuple-element.46., ...), custom_call_target="tpu_custom_call" | custom-call | tf_op jit(solution)/shard_map/pallas_call | solution.py:1127
  154.1 2.7 %shard_map.265 = (bf16[256,1024]{1,0:T(8,128)(2,1)}, bf16[256,1024]{1,0:T(8,128)(2,1)}, bf16[256,1024]{1,0:T(8,128)(2,1)}, f32[64,1024]{1,0:T(8,128)}, f32[16,40...) custom-call(bf16[256,1024]{1,0:T(8,128)(2,1)} %get-tuple-element.57., ...), custom_call_target="tpu_custom_call" | custom-call | tf_op jit(solution)/shard_map/pallas_call | solution.py:1204
  156.8 0.8 constant_dynamic-slice_fusion
  157.6 0.5 fusion

commit v8 on v7

--- a/solution.py
+++ b/solution.py
@@ -73,11 +73,15 @@
     )
 
 
+def greet(devices):
+    for device in devices:
+        pl.semaphore_signal(
+            pltpu.get_barrier_semaphore(), inc=1, device_id=device, device_id_type=MESH
+        )
+
+
 def enter(devices):
-    barrier = pltpu.get_barrier_semaphore()
-    for device in devices:
-        pl.semaphore_signal(barrier, inc=1, device_id=device, device_id_type=MESH)
-    pl.semaphore_wait(barrier, len(devices))
+    pl.semaphore_wait(pltpu.get_barrier_semaphore(), len(devices))
 
 
 def add_blocks(count, total, other):
@@ -248,7 +252,7 @@
 def attention_backward_pair(query, keys, values, share, inverse, grad, mixed, lows):
     span = keys.shape[0]
     here = query.shape[0]
-    chunk = 128
+    chunk = span // 2
     lane = lax.broadcasted_iota(jnp.int32, query.shape, 1)
     zero = jnp.zeros(query.shape, query.dtype)
     queries = jnp.concatenate(
@@ -278,7 +282,7 @@
     for index in range(span // chunk):
         rows = pl.ds(index * chunk, chunk)
         part = share[rows]
-        grads, grads_back, centre = sets[2 * index // (span // chunk)]
+        grads, grads_back, centre = sets[index]
         grad_share = project(values[rows], grads)
         grad_score = (part.astype(jnp.float32) * (grad_share - centre)).astype(jnp.bfloat16)
         lows[rows] = grad_score
@@ -307,7 +311,8 @@
     span = keys.shape[0]
     half = width // 2
     pairs = width // 128
-    piece = here // 2
+    parts = 4
+    piece = here // parts
 
     loads = [
         pltpu.make_async_copy(source, target, load_sem.at[index])
@@ -337,18 +342,19 @@
                 core,
             ),
             (
-                joined_sent.at[pl.ds(part * half, half)],
-                joined_landing.at[pl.ds(part * half, half)],
+                joined_sent.at[pl.ds(part % 2 * half, half)],
+                joined_landing.at[pl.ds(part % 2 * half, half)],
                 core,
             ),
         )[index]
         return remote(source, target, send_sem.at[index, part], recv_sem.at[index, part], device)
 
+    greet([core, far, section])
     for index in range(4):
         loads[index].start()
     enter([core, far, section])
-    send(0, 0).start()
-    send(0, 1).start()
+    for part in range(parts):
+        send(0, part).start()
 
     bounds = []
     start = jnp.int32(0)
@@ -362,8 +368,8 @@
     place = seq * here + lax.broadcasted_iota(jnp.int32, (here, 1), 0)
     inside = jnp.zeros((here, 1), jnp.int32)
     for index in range(4):
-        low_end = bounds[index][0] + spans[0, 0, index, 0]
-        high_end = bounds[index][0] + spans[0, 0, index, 1]
+        low_end = bounds[index][0] + spans[0, 0, pl.ds(index, 1), pl.ds(0, 1)]
+        high_end = bounds[index][0] + spans[0, 0, pl.ds(index, 1), pl.ds(1, 1)]
         inside += (place >= low_end).astype(jnp.int32) * (place < high_end).astype(jnp.int32)
     grad_low[...] = jnp.where(
         inside > 0, out_grad[...].astype(jnp.float32), 0.0
@@ -393,7 +399,7 @@
     loads[0].wait()
     hidden[...] = project(own[...], w_rows[pl.ds(0, width)])
     gain, bias = flat(gain_one), flat(bias_one)
-    for part in range(2):
+    for part in range(parts):
         rows = pl.ds(part * piece, piece)
         send(0, part).wait_recv()
         value = hidden[rows] + project(partner[rows], w_rows[pl.ds(width, width)])
@@ -424,21 +430,14 @@
         )
         head = 2 * pair + 1 + lax.div(lax.broadcasted_iota(jnp.int32, (1, 2 * here), 1), here)
         slope = LOG2E * jnp.exp2(head.astype(jnp.float32) * -0.5)
-        top = jnp.full((8, 2 * here), -jnp.inf, jnp.float32)
-        for index in range(4):
-            rows = pl.ds(base + index * 128, 128)
-            score = back_product(keys[rows, columns], stacked)
-            gap = distance[rows]
-            score = score - slope * jnp.concatenate([gap, gap], axis=1)
-            scores[pl.ds(index * 128, 128)] = score
-            top = jnp.maximum(top, jnp.max(score.reshape(16, 8, 2 * here), axis=0))
+        rows = pl.ds(base, 2 * here)
+        gap = distance[rows]
+        score = back_product(keys[rows, columns], stacked)
+        score = score - slope * jnp.concatenate([gap, gap], axis=1)
+        scores[...] = score
+        top = jnp.max(score.reshape(here // 4, 8, 2 * here), axis=0)
         top = jnp.max(top, axis=0, keepdims=True)
-        for index in range(4):
-            rows = pl.ds(index * 128, 128)
-            exponents[pair, pl.ds(base + index * 128, 128)] = jnp.exp2(
-                scores[rows] - top
-            ).astype(jnp.bfloat16)
-        rows = pl.ds(base, 2 * here)
+        exponents[pair, rows] = jnp.exp2(scores[...] - top).astype(jnp.bfloat16)
         pltpu.make_async_copy(
             exponents.at[pair, rows], shares.at[pair, rows], share_sem
         ).start()
@@ -447,8 +446,8 @@
         )
         return project(back, exponents[pair, rows]), top
 
-    send(1, 0).wait_recv()
-    send(1, 1).wait_recv()
+    for part in range(parts):
+        send(1, part).wait_recv()
     both(0, 2 * here)
     joined_rows(1, partner)
 
@@ -458,13 +457,16 @@
         tops[pair] = top
         return carry
 
-    lax.fori_loop(0, pairs, near, 0)
-    for part in range(2):
+    lax.fori_loop(0, pairs - 3, near, 0)
+    for part in range(parts - 1):
         send(2, part).wait_recv()
         send(3, part).start()
+    lax.fori_loop(pairs - 3, pairs, near, 0)
+    send(2, parts - 1).wait_recv()
+    send(3, parts - 1).start()
     both(2 * here, here)
-    send(3, 0).wait_recv()
-    send(3, 1).wait_recv()
+    for part in range(parts):
+        send(3, part).wait_recv()
     both(3 * here, here)
     for index in range(4, 7):
         loads[index].start()
@@ -492,7 +494,7 @@
     for index in range(4, 8):
         loads[index].wait()
     for index in range(5):
-        for part in range(2):
+        for part in range(parts if index < 4 else 2):
             send(index, part).wait_send()
 
 
@@ -508,7 +510,7 @@
     dma = pltpu.SemaphoreType.DMA
     return pl.pallas_call(
         forward_kernel,
-        in_specs=[scalars, scalars] + [inside] * 5 + [outside] * 4,
+        in_specs=[scalars, inside, inside, outside, inside, inside, inside] + [outside] * 4,
         out_specs=[inside] * 6 + [outside] * 5,
         out_shape=[
             jax.ShapeDtypeStruct((here, width), jnp.float32),
@@ -539,8 +541,8 @@
             pltpu.VMEM((pairs, 144, 2 * here), jnp.float32),
             pltpu.VMEM((pairs, 1, 2 * here), jnp.float32),
             dma((8,)),
-            dma((5, 2)),
-            dma((5, 2)),
+            dma((5, 4)),
+            dma((5, 4)),
             dma,
         ],
         compiler_params=pltpu.CompilerParams(
@@ -715,16 +717,15 @@
         if step < 3:
             vector_start(step + 1)
 
+    devices = [core, far, section]
+    for mask in (1, 2, 3):
+        for dp in (z * 4 + flip(x, mask), flip(z, mask) * 4 + x):
+            devices += [{"dp": dp}, {"dp": dp, "seq": flip(seq, 2)}]
+    greet(devices)
     for index in (6, 10, 11):
         load(index).start()
     for copy in load_block(0):
         copy.start()
-    devices = [core, far, section]
-    for mask in (1, 2, 3):
-        for dp in (z * 4 + flip(x, mask), flip(z, mask) * 4 + x):
-            devices += [{"dp": dp}, {"dp": dp, "seq": flip(seq, 2)}]
-    enter(devices)
-    side(6).start()
 
     def share_rows(index):
         def kept(row, value):
@@ -735,8 +736,6 @@
             parts[3, pl.ds(row % here, 16), lanes] = value
 
         split_cores(core_index, turned, kept, sent, 16)
-        pair_half(index, 0).start()
-        pair_half(index, 1).start()
 
     turned[...] = mixed[...].T
     share_rows(0)
@@ -761,7 +760,11 @@
     lax.fori_loop(0, here // 32, norm_two_rows, 0)
     turned[...] = stored_send[...].T
     share_rows(1)
-    side(6).wait_recv()
+    enter(devices)
+    side(6).start()
+    for index in range(2):
+        pair_half(index, 0).start()
+        pair_half(index, 1).start()
 
     def down_share(step):
         act_copy(step).wait_recv()
@@ -814,6 +817,10 @@
 
         split_cores(core_index, turned.at[pl.ds(0, block)], kept, sent, 64)
         act_copy(step).start()
+
+        @pl.when(step == 1)
+        def _():
+            side(6).wait_recv()
 
         @pl.when(step > 0)
         def _():
@@ -891,7 +898,6 @@
     for index in range(3, 5):
         load(index).start()
     pl.semaphore_wait(free_sem.at[0], 1)
-    halving.finish(0, 0)
     load(0).wait()
     load(1).wait()
 
@@ -914,10 +920,10 @@
             lows,
         )
         grad_query[:, columns] = out
-        for index, (one, two) in enumerate(zip(grad_keys, grad_values)):
-            part, rows = index * 128 // here, pl.ds(index * 128 % here, 128)
-            parts[part, rows, columns] = one
-            parts[part, rows, others] = two
+        for part in range(4):
+            first = part % 2 * here
+            parts[part, :, columns] = grad_keys[part // 2][first : first + here]
+            parts[part, :, others] = grad_values[part // 2][first : first + here]
         for step in range(2):
             for index, place in enumerate((columns, others)):
                 remote(
@@ -929,7 +935,9 @@
                 ).start()
         return carry
 
-    lax.fori_loop(0, pairs, one_pair, 0)
+    lax.fori_loop(0, 3, one_pair, 0)
+    halving.finish(0, 0)
+    lax.fori_loop(3, pairs, one_pair, 0)
     side(2).start()
     load(7).start()
     load_part(0).start()
@@ -1057,6 +1065,9 @@
 
     lax.fori_loop(0, width // 256, stored_rows, 0)
     side(5).start()
+    halving.finish(3, 0)
+    halving.finish(4, 0)
+    vector_finish(0)
     load(8).wait()
     load(9).wait()
     side(4).wait_recv()
@@ -1068,12 +1079,6 @@
             project(held[0, :, pl.ds(0, here)], grad_hidden[:, columns])
             + project(held[0, :, pl.ds(here, here)], hidden_landing[:, columns]),
         )
-    halving.finish(0, 3)
-    halving.finish(1, 2)
-    halving.finish(2, 2)
-    halving.finish(3, 0)
-    halving.finish(4, 0)
-    vector_finish(0)
 
     def own_grads(index, carry):
         rows = pl.ds(pl.multiple_of(index * 256, 256), 256)
@@ -1081,25 +1086,20 @@
         return carry
 
     lax.fori_loop(0, width // 256, own_grads, 0)
+    for job, stage in ((0, 3), (1, 2), (2, 2), (3, 1), (4, 1)):
+        halving.finish(job, stage)
+    vector_finish(1)
     halving.finish_direct(5, 0)
-    halving.finish(0, 4)
-    for job in (1, 2):
-        halving.finish(job, 3)
-    for job in (3, 4):
-        halving.finish(job, 1)
-    vector_finish(1)
+    for job, stage in ((3, 2), (4, 2), (0, 4), (1, 3), (2, 3)):
+        halving.finish(job, stage)
+    vector_finish(2)
     halving.finish_direct(5, 1)
-    for job in (1, 2):
-        halving.finish(job, 4)
-    for job in (3, 4):
-        halving.finish(job, 2)
-    vector_finish(2)
-    for job in (3, 4):
-        halving.finish(job, 3)
+    for job, stage in ((3, 3), (4, 3), (1, 4), (2, 4)):
+        halving.finish(job, stage)
+    vector_finish(3)
     halving.finish_direct(5, 2)
     for job in (3, 4):
         halving.finish(job, 4)
-    vector_finish(3)
     side(5).wait_recv()
     grad_stored[...] = stored_landing[...]
     halving.drain()
@@ -1179,11 +1179,12 @@
     return jnp.mean(value, axis=-1, keepdims=True)
 
 
-def copy_kernel(*refs):
-    count = (len(refs) - 1) // 3
+def copy_kernel(count, vectors, *refs):
+    sources, targets, pieces, stops = (
+        refs[:count], refs[count : 2 * count], refs[2 * count : 2 * count + 4], refs[2 * count + 4 : -1]
+    )
     ways = []
-    for index in range(count):
-        source, target, stop = refs[index], refs[count + index], refs[2 * count + index]
+    for index, (source, target, stop) in enumerate(zip(sources, targets, stops)):
         ways.append(
             (
                 pltpu.make_async_copy(source, stop, refs[-1].at[0, index]),
@@ -1192,6 +1193,12 @@
         )
     for into, _ in ways:
         into.start()
+    width = vectors.shape[1]
+    size = width // 64
+    shard = lax.axis_index("dp") * 4 + lax.axis_index("seq")
+    turned = pltpu.roll(vectors[...], lax.rem(width - shard * size, width), 1)
+    for index, piece in enumerate(pieces):
+        piece[...] = turned[index : index + 1, :size]
     for into, out in ways:
         into.wait()
         out.start()
@@ -1199,16 +1206,19 @@
         out.wait()
 
 
-def copied(arrays):
+def copied(vectors, arrays):
     outside = pl.BlockSpec(memory_space=pl.ANY)
+    inside = pl.BlockSpec(memory_space=pltpu.VMEM)
+    piece = jax.ShapeDtypeStruct((1, vectors.shape[1] // 64), jnp.float32)
     return pl.pallas_call(
-        copy_kernel,
-        in_specs=[outside] * len(arrays),
-        out_specs=[outside] * len(arrays),
-        out_shape=[jax.ShapeDtypeStruct(array.shape, array.dtype) for array in arrays],
+        functools.partial(copy_kernel, len(arrays)),
+        in_specs=[inside] + [outside] * len(arrays),
+        out_specs=[outside] * len(arrays) + [inside] * 4,
+        out_shape=[jax.ShapeDtypeStruct(array.shape, array.dtype) for array in arrays]
+        + [piece] * 4,
         scratch_shapes=[pltpu.VMEM(array.shape, array.dtype) for array in arrays]
         + [pltpu.SemaphoreType.DMA((2, len(arrays)))],
-    )(*arrays)
+    )(vectors, *arrays)
 
 
 def on_device(
@@ -1275,7 +1285,6 @@
         [norm1_gain, norm2_gain, norm2_bias],
         1,
     )
-    sums = results[3]
     (
         output,
         grad_own,
@@ -1287,23 +1296,24 @@
         key_sum,
         value_sum,
         skip_sum,
-    ) = copied(results[:3] + results[4:])
-    shard = lax.axis_index("dp") * 4 + seq
-    piece = model_width // 64
-    sums = lax.dynamic_slice(sums, (0, shard * piece), (4, piece))
+        gain_one_sum,
+        bias_one_sum,
+        gain_two_sum,
+        bias_two_sum,
+    ) = copied(results[3], results[:3] + results[4:])
     return (
         output.reshape(states.shape),
         grad_own.reshape(states.shape),
         grad_stored.reshape(states.shape),
         skip_sum[None],
-        sums[0][None],
-        sums[1][None],
+        gain_one_sum,
+        bias_one_sum,
         query_sum[None],
         key_sum[None],
         value_sum[None],
         out_sum[None],
-        sums[2][None],
-        sums[3][None],
+        gain_two_sum,
+        bias_two_sum,
         up_sum[None],
         down_sum[None],
     )

time: 158 us -> 156 us (0.987)
  Pallas kernels: 155 us -> 153 us
    pallas_call x1, Pallas kernels: 112 us -> 108 us  [backward(): pl.pallas_call(functools.partial(backward_kernel, shapes), in_specs=specs...]
    pallas_call x2, Pallas kernels: 43.1 us -> 45.1 us  [the longest x1 41.1 us: forward(): pl.pallas_call(forward_kernel, in_specs=[scalars, inside, inside, outside...]
where the time goes in v8:
time: 156 us
  Pallas kernels  153 us (98%)
    pallas_call x1, Pallas kernels, backward(): pl.pallas_call(functools.partial(backward_kernel, shapes), in_specs=specs...  108 us
    pallas_call x1, Pallas kernels, forward(): pl.pallas_call(forward_kernel, in_specs=[scalars, inside, inside, outside...  41.1 us
    pallas_call x1, Pallas kernels, copied(): pl.pallas_call(functools.partial(copy_kernel, len(arrays)), in_specs=[ins...  3.94 us

profile of v8, /device:TPU:0, one launch (start us, length us, event | category | flops | bytes accessed | tf_op | source)
XLA Modules:
  0.0 155.7 jit_solution(15632489330831756499)
XLA Ops:
  0.6 1.3 copy.30.spans
  2.0 41.1 %shard_map.263 = (f32[256,1024]{1,0:T(8,128)}, bf16[256,1024]{1,0:T(8,128)(2,1)}, f32[8,2,512]{2,1,0:T(2,128)}, bf16[256,1024]{1,0:T(8,128)(2,1)}, bf16[256,1024...) custom-call(s32[1,1,4]{2,1,0:T(1,128)} %lengths.1, ...), custom_call_target="tpu_custom_call" | custom-call | tf_op jit(solution)/shard_map/pallas_call | solution.py:511
  43.1 108.4 %shard_map.264 = (bf16[256,1024]{1,0:T(8,128)(2,1)}, bf16[256,1024]{1,0:T(8,128)(2,1)}, bf16[256,1024]{1,0:T(8,128)(2,1)}, f32[8,1024]{1,0:T(8,128)}, f32[64,102...) custom-call(bf16[256,1024]{1,0:T(8,128)(2,1)} %get-tuple-element.50., ...), custom_call_target="tpu_custom_call" | custom-call | tf_op jit(solution)/shard_map/pallas_call | solution.py:1127
  151.6 3.9 %shard_map.265 = (bf16[256,1024]{1,0:T(8,128)(2,1)}, bf16[256,1024]{1,0:T(8,128)(2,1)}, bf16[256,1024]{1,0:T(8,128)(2,1)}, f32[64,1024]{1,0:T(8,128)}, f32[16,40...) custom-call(f32[8,1024]{1,0:T(8,128)} %get-tuple-element.61.vectors,, ...), custom_call_target="tpu_custom_call" | custom-call | tf_op jit(solution)/shard_map/pallas_call | solution.py:1213

commit v9 on v8

--- a/solution.py
+++ b/solution.py
@@ -311,7 +311,7 @@
     span = keys.shape[0]
     half = width // 2
     pairs = width // 128
-    parts = 4
+    parts = 2
     piece = here // parts
 
     loads = [
@@ -368,8 +368,8 @@
     place = seq * here + lax.broadcasted_iota(jnp.int32, (here, 1), 0)
     inside = jnp.zeros((here, 1), jnp.int32)
     for index in range(4):
-        low_end = bounds[index][0] + spans[0, 0, pl.ds(index, 1), pl.ds(0, 1)]
-        high_end = bounds[index][0] + spans[0, 0, pl.ds(index, 1), pl.ds(1, 1)]
+        low_end = bounds[index][0] + spans[2 * index]
+        high_end = bounds[index][0] + spans[2 * index + 1]
         inside += (place >= low_end).astype(jnp.int32) * (place < high_end).astype(jnp.int32)
     grad_low[...] = jnp.where(
         inside > 0, out_grad[...].astype(jnp.float32), 0.0
@@ -510,7 +510,7 @@
     dma = pltpu.SemaphoreType.DMA
     return pl.pallas_call(
         forward_kernel,
-        in_specs=[scalars, inside, inside, outside, inside, inside, inside] + [outside] * 4,
+        in_specs=[scalars, scalars, inside, outside, inside, inside, inside] + [outside] * 4,
         out_specs=[inside] * 6 + [outside] * 5,
         out_shape=[
             jax.ShapeDtypeStruct((here, width), jnp.float32),
@@ -994,18 +994,18 @@
     load_part(1).wait()
 
     def select_rows(index, carry):
-        first = pl.multiple_of(index * 128, 128)
-        row = first + lax.broadcasted_iota(jnp.int32, (128, width), 0)
-        lane = lax.broadcasted_iota(jnp.int32, (128, width), 1)
+        first = pl.multiple_of(index * 256, 256)
+        row = first + lax.broadcasted_iota(jnp.int32, (256, width), 0)
+        lane = lax.broadcasted_iota(jnp.int32, (256, width), 1)
         source = lax.div(row, 16) * 32 + core_index * 16 + lax.rem(row, 16)
         pick = jnp.where(lane == source, 1.0, 0.0).astype(jnp.bfloat16)
         value = back_product(pick[:, :half], held[0]) + back_product(pick[:, half:], held[1])
         value = value.astype(jnp.bfloat16)
-        lows[pl.ds(first, 128)] = value[:, :half]
-        lows[pl.ds(pl.multiple_of(half + first, 128), 128)] = value[:, half:]
+        lows[pl.ds(first, 256)] = value[:, :half]
+        lows[pl.ds(pl.multiple_of(half + first, 256), 256)] = value[:, half:]
         return carry
 
-    lax.fori_loop(0, half // 128, select_rows, 0)
+    lax.fori_loop(0, half // 256, select_rows, 0)
     load(8).start()
     load(9).start()
 
@@ -1180,28 +1180,31 @@
 
 
 def copy_kernel(count, vectors, *refs):
-    sources, targets, pieces, stops = (
-        refs[:count], refs[count : 2 * count], refs[2 * count : 2 * count + 4], refs[2 * count + 4 : -1]
-    )
+    sources, targets = refs[:count], refs[count : 2 * count]
+    pieces, stops = refs[2 * count : 2 * count + 4], refs[2 * count + 4 : -2]
+    held, sems = refs[-2:]
+    fetch = pltpu.make_async_copy(vectors, held, sems.at[0, count])
+    fetch.start()
     ways = []
     for index, (source, target, stop) in enumerate(zip(sources, targets, stops)):
         ways.append(
             (
-                pltpu.make_async_copy(source, stop, refs[-1].at[0, index]),
-                pltpu.make_async_copy(stop, target, refs[-1].at[1, index]),
+                pltpu.make_async_copy(source, stop, sems.at[0, index]),
+                pltpu.make_async_copy(stop, target, sems.at[1, index]),
             )
         )
     for into, _ in ways:
         into.start()
+    for into, out in ways:
+        into.wait()
+        out.start()
+    fetch.wait()
     width = vectors.shape[1]
     size = width // 64
     shard = lax.axis_index("dp") * 4 + lax.axis_index("seq")
-    turned = pltpu.roll(vectors[...], lax.rem(width - shard * size, width), 1)
+    turned = pltpu.roll(held[...], lax.rem(width - shard * size, width), 1)
     for index, piece in enumerate(pieces):
         piece[...] = turned[index : index + 1, :size]
-    for into, out in ways:
-        into.wait()
-        out.start()
     for _, out in ways:
         out.wait()
 
@@ -1212,12 +1215,15 @@
     piece = jax.ShapeDtypeStruct((1, vectors.shape[1] // 64), jnp.float32)
     return pl.pallas_call(
         functools.partial(copy_kernel, len(arrays)),
-        in_specs=[inside] + [outside] * len(arrays),
+        in_specs=[outside] * (1 + len(arrays)),
         out_specs=[outside] * len(arrays) + [inside] * 4,
         out_shape=[jax.ShapeDtypeStruct(array.shape, array.dtype) for array in arrays]
         + [piece] * 4,
         scratch_shapes=[pltpu.VMEM(array.shape, array.dtype) for array in arrays]
-        + [pltpu.SemaphoreType.DMA((2, len(arrays)))],
+        + [
+            pltpu.VMEM(vectors.shape, vectors.dtype),
+            pltpu.SemaphoreType.DMA((2, len(arrays) + 1)),
+        ],
     )(vectors, *arrays)
 
 
@@ -1256,7 +1262,7 @@
         joined_other,
     ) = forward(
         lengths,
-        infill_spans,
+        infill_spans.reshape(-1),
         states.reshape(rows_here, model_width),
         mirror.reshape(rows_here, model_width),
         out_grad.reshape(rows_here, model_width),

time: 156 us -> 154 us (0.987)
  no operation moved by 1% of the time
where the time goes in v9:
time: 154 us
  Pallas kernels  152 us (99%)
    pallas_call x1, Pallas kernels, backward(): pl.pallas_call(functools.partial(backward_kernel, shapes), in_specs=specs...  108 us
    pallas_call x1, Pallas kernels, forward(): pl.pallas_call(forward_kernel, in_specs=[scalars, scalars, inside, outsid...  40.7 us
    pallas_call x1, Pallas kernels, copied(): pl.pallas_call(functools.partial(copy_kernel, len(arrays)), in_specs=[out...  3.22 us

profile of v9, /device:TPU:0, one launch (start us, length us, event | category | flops | bytes accessed | tf_op | source)
XLA Modules:
  0.0 154.1 jit_solution(16130839991740192619)
XLA Ops:
  0.6 0.8 copy.31
  1.4 0.6 reshape.49.spans
  2.0 40.7 %shard_map.263 = (f32[256,1024]{1,0:T(8,128)}, bf16[256,1024]{1,0:T(8,128)(2,1)}, f32[8,2,512]{2,1,0:T(2,128)}, bf16[256,1024]{1,0:T(8,128)(2,1)}, bf16[256,1024...) custom-call(s32[1,1,4]{2,1,0:T(1,128)} %lengths.1, ...), custom_call_target="tpu_custom_call" | custom-call | tf_op jit(solution)/shard_map/pallas_call | solution.py:511
  42.7 108.0 %shard_map.264 = (bf16[256,1024]{1,0:T(8,128)(2,1)}, bf16[256,1024]{1,0:T(8,128)(2,1)}, bf16[256,1024]{1,0:T(8,128)(2,1)}, f32[8,1024]{1,0:T(8,128)}, f32[64,102...) custom-call(bf16[256,1024]{1,0:T(8,128)(2,1)} %get-tuple-element.50., ...), custom_call_target="tpu_custom_call" | custom-call | tf_op jit(solution)/shard_map/pallas_call | solution.py:1127
  150.7 3.2 %shard_map.265 = (bf16[256,1024]{1,0:T(8,128)(2,1)}, bf16[256,1024]{1,0:T(8,128)(2,1)}, bf16[256,1024]{1,0:T(8,128)(2,1)}, f32[64,1024]{1,0:T(8,128)}, f32[16,40...) custom-call(f32[8,1024]{1,0:T(8,128)} %get-tuple-element.61.vectors,, ...), custom_call_target="tpu_custom_call" | custom-call | tf_op jit(solution)/shard_map/pallas_call | solution.py:1216

commit v10 on v9

--- a/solution.py
+++ b/solution.py
@@ -122,8 +122,10 @@
         scratch = list(scratch)
         count = len(shapes)
         self.work = scratch[:count]
-        self.landings = [scratch[count + 5 * job : count + 5 * job + 5] for job in range(count)]
-        self.landings[-1] = self.landings[-1][:3]
+        first = [count + 5 * job for job in range(count - 1)] + [6 * count - 7]
+        self.landings = [
+            scratch[start : start + (5 if job < count - 2 else 3)] for job, start in enumerate(first)
+        ]
         self.send_sem, self.recv_sem = scratch[-2:]
         self.z, self.x, self.seq = place_here()
         self.y = lax.div(self.seq, 2)
@@ -132,7 +134,7 @@
     def scratch(shapes):
         shapes_of = [(4, 16, 2 * rows, width // 4) for rows, width in shapes]
         for job, (rows, width) in enumerate(shapes):
-            direct = job == len(shapes) - 1
+            direct = job >= len(shapes) - 2
             shapes_of += [(4, blocks, 2 * rows, width // 4) for blocks in (8, 4)]
             if direct:
                 shapes_of.append((4, 7, rows, width // 4))
@@ -239,13 +241,14 @@
                 total = work[0, pl.ds(mine, rows)].astype(jnp.float32)
                 for step in range(7):
                     total = total + landing[step].astype(jnp.float32)
-                self.results[job][0][:, pl.ds(quarter * width // 4, width // 4)] = total
+                start = quarter * width // 4
+                self.results[job][start // 1024][:, pl.ds(start % 1024, width // 4)] = total
 
     def drain(self):
         last = len(self.shapes) - 1
         for job in range(last + 1):
             for quarter in range(4):
-                for stage in range(2 if job == last else 5):
+                for stage in range(2 if job >= last - 1 else 5):
                     self.copy(job, quarter, stage).wait_send()
 
 
@@ -368,8 +371,8 @@
     place = seq * here + lax.broadcasted_iota(jnp.int32, (here, 1), 0)
     inside = jnp.zeros((here, 1), jnp.int32)
     for index in range(4):
-        low_end = bounds[index][0] + spans[2 * index]
-        high_end = bounds[index][0] + spans[2 * index + 1]
+        low_end = bounds[index][0] + spans[0, 0, 0, index]
+        high_end = bounds[index][0] + spans[0, 0, 1, index]
         inside += (place >= low_end).astype(jnp.int32) * (place < high_end).astype(jnp.int32)
     grad_low[...] = jnp.where(
         inside > 0, out_grad[...].astype(jnp.float32), 0.0
@@ -1066,7 +1069,7 @@
     lax.fori_loop(0, width // 256, stored_rows, 0)
     side(5).start()
     halving.finish(3, 0)
-    halving.finish(4, 0)
+    halving.finish_direct(4, 0)
     vector_finish(0)
     load(8).wait()
     load(9).wait()
@@ -1086,20 +1089,21 @@
         return carry
 
     lax.fori_loop(0, width // 256, own_grads, 0)
-    for job, stage in ((0, 3), (1, 2), (2, 2), (3, 1), (4, 1)):
+    for job, stage in ((0, 3), (1, 2), (2, 2), (3, 1)):
         halving.finish(job, stage)
+    halving.finish_direct(4, 1)
     vector_finish(1)
     halving.finish_direct(5, 0)
-    for job, stage in ((3, 2), (4, 2), (0, 4), (1, 3), (2, 3)):
+    for job, stage in ((3, 2), (0, 4), (1, 3), (2, 3)):
         halving.finish(job, stage)
     vector_finish(2)
     halving.finish_direct(5, 1)
-    for job, stage in ((3, 3), (4, 3), (1, 4), (2, 4)):
+    for job, stage in ((3, 3), (1, 4), (2, 4)):
         halving.finish(job, stage)
+    halving.finish_direct(4, 2)
     vector_finish(3)
     halving.finish_direct(5, 2)
-    for job in (3, 4):
-        halving.finish(job, 4)
+    halving.finish(3, 4)
     side(5).wait_recv()
     grad_stored[...] = stored_landing[...]
     halving.drain()
@@ -1262,7 +1266,7 @@
         joined_other,
     ) = forward(
         lengths,
-        infill_spans.reshape(-1),
+        infill_spans.swapaxes(2, 3),
         states.reshape(rows_here, model_width),
         mirror.reshape(rows_here, model_width),
         out_grad.reshape(rows_here, model_width),

time: 154 us -> 153 us (level)
  no operation moved by 1% of the time
where the time goes in v10:
time: 153 us
  Pallas kernels  152 us (99%)
    pallas_call x1, Pallas kernels, backward(): pl.pallas_call(functools.partial(backward_kernel, shapes), in_specs=specs...  108 us
    pallas_call x1, Pallas kernels, forward(): pl.pallas_call(forward_kernel, in_specs=[scalars, scalars, inside, outsid...  40.8 us
    pallas_call x1, Pallas kernels, copied(): pl.pallas_call(functools.partial(copy_kernel, len(arrays)), in_specs=[out...  3.22 us

profile of v10, /device:TPU:0, one launch (start us, length us, event | category | flops | bytes accessed | tf_op | source)
XLA Modules:
  0.0 152.5 jit_solution(15067607321994493673)
XLA Ops:
  0.6 40.8 %shard_map.263 = (f32[256,1024]{1,0:T(8,128)}, bf16[256,1024]{1,0:T(8,128)(2,1)}, f32[8,2,512]{2,1,0:T(2,128)}, bf16[256,1024]{1,0:T(8,128)(2,1)}, bf16[256,1024...) custom-call(s32[1,1,4]{2,1,0:T(1,128)} %lengths.1, ...), custom_call_target="tpu_custom_call" | custom-call | tf_op jit(solution)/shard_map/pallas_call | solution.py:514
  41.4 107.7 %shard_map.264 = (bf16[256,1024]{1,0:T(8,128)(2,1)}, bf16[256,1024]{1,0:T(8,128)(2,1)}, bf16[256,1024]{1,0:T(8,128)(2,1)}, f32[8,1024]{1,0:T(8,128)}, f32[64,102...) custom-call(bf16[256,1024]{1,0:T(8,128)(2,1)} %get-tuple-element.50., ...), custom_call_target="tpu_custom_call" | custom-call | tf_op jit(solution)/shard_map/pallas_call | solution.py:1131
  149.1 3.2 %shard_map.265 = (bf16[256,1024]{1,0:T(8,128)(2,1)}, bf16[256,1024]{1,0:T(8,128)(2,1)}, bf16[256,1024]{1,0:T(8,128)(2,1)}, f32[64,1024]{1,0:T(8,128)}, f32[16,40...) custom-call(f32[8,1024]{1,0:T(8,128)} %get-tuple-element.61.vectors,, ...), custom_call_target="tpu_custom_call" | custom-call | tf_op jit(solution)/shard_map/pallas_call | solution.py:1220
